TPU v7x, 32 devices: a whole 2x2x4 slice. The times are simulated.
32 devices in a mesh: groups: 2 (over x), tensor: 16 (over z, y, core).
Axes of the slice: x: 2, y: 2, z: 4, core: 2. Of those that a mesh axis runs over, the one named last changes fastest.
Arguments:
- attended: bfloat16 [512, 8192], P('groups', 'tensor'), parts along dimension 0, may hold values from -6 to 6
- out_weight: bfloat16 [8192, 8192], P('tensor'), may hold values from -0.09375 to 0.09375
- adapter_down: bfloat16 [32, 8192, 64], P(('groups', 'tensor')), parts along dimension 0, may hold values from -0.0625 to 0.0625
- adapter_up: bfloat16 [32, 64, 8192], P(('groups', 'tensor')), parts along dimension 0, may hold values from -0.75 to 0.75
- row_adapter: int32 [512], P('groups'), parts along dimension 0, may hold values from 0 to 15, as said below
- adapter_slot: int32 [32], P('groups'), parts along dimension 0, may hold values from 0 to 15, as said below
Outputs:
- projected: bfloat16 [512, 8192], P('groups', 'tensor'), parts along dimension 0
There are 2 independent parts, one for each index of `groups`. A program takes and returns all parts, laid end to end along the dimension named above; an argument that names none is the same for every part. Nothing has to cross between parts.
Inputs may be any that keep to these rules, and one draw needn't show every extreme that they name: adapter_slot is a permutation: adapter a is stored at position adapter_slot[a]; positions s with equal s // 1 lie on one device of the tensor axis. `row_adapter`: at most 32 rows have adapters stored on one device of the tensor axis, and exactly 32 on some device.
All inputs are finite; a program needn't handle non-finite values.
Results may differ from a plain program's by a relative error of at most 0.0046.
Values may be sent and summed in bfloat16 or wider, within the bound.
No kernel may reach another device: no remote copies, remote signals or barrier semaphores. Data moves between devices by JAX's collectives and lax.ppermute only.
A program may use at most 192 MiB of HBM per device.

v0:
```python
import jax
import jax.numpy as jnp
from jax import lax
from jax.sharding import PartitionSpec as P

CAP = 32


def shards(attended, out_weight, adapter_down, adapter_up, row_adapter, adapter_slot):
    tensor_size = lax.axis_size("tensor")
    device = lax.axis_index("tensor")
    row_count = attended.shape[0]
    held_count = adapter_down.shape[0]
    storage = adapter_slot[row_adapter]
    partial_value = jnp.dot(attended, out_weight, preferred_element_type=jnp.float32)
    base_out = lax.psum_scatter(partial_value, "tensor", scatter_dimension=1, tiled=True)
    owner_of = storage // held_count
    local_index = storage % held_count
    owner_hot = (owner_of[:, None] == jnp.arange(tensor_size, dtype=jnp.int32)[None, :]).astype(
        jnp.int32
    )
    position = jnp.sum(jnp.cumsum(owner_hot, axis=0) * owner_hot, axis=1) - 1
    target = owner_of * CAP + position
    slot_row = (
        jnp.full((tensor_size * CAP,), row_count, jnp.int32)
        .at[target]
        .set(jnp.arange(row_count, dtype=jnp.int32))
    )
    padded = jnp.concatenate([attended, jnp.zeros((1, attended.shape[1]), attended.dtype)], axis=0)
    outgoing = padded[slot_row]
    arrived = lax.all_to_all(outgoing, "tensor", split_axis=0, concat_axis=1, tiled=True)
    own_slots = lax.dynamic_slice_in_dim(slot_row, device * CAP, CAP)
    slot_local = jnp.concatenate([local_index, jnp.zeros((1,), jnp.int32)])[own_slots]
    selector = (slot_local[None, :] == jnp.arange(held_count, dtype=jnp.int32)[:, None]).astype(
        jnp.float32
    )
    all_shrunk = jnp.einsum(
        "cd,adk->ack", arrived, adapter_down, preferred_element_type=jnp.float32
    )
    shrunk = jnp.sum(all_shrunk * selector[:, :, None], axis=0).astype(jnp.bfloat16)
    picked = (selector[:, :, None] * shrunk[None].astype(jnp.float32)).astype(jnp.bfloat16)
    expanded = jnp.einsum(
        "ack,akd->cd", picked, adapter_up, preferred_element_type=jnp.float32
    ).astype(jnp.bfloat16)
    returned = lax.all_to_all(expanded, "tensor", split_axis=1, concat_axis=0, tiled=True)
    delta_out = returned[target]
    return (base_out + delta_out.astype(jnp.float32)).astype(jnp.bfloat16)


def solution(mesh):
    placed = (
        P("groups", "tensor"),
        P("tensor", None),
        P(("groups", "tensor"), None, None),
        P(("groups", "tensor"), None, None),
        P("groups"),
        P("groups"),
    )
    return jax.shard_map(
        shards, mesh=mesh, in_specs=placed, out_specs=P("groups", "tensor"), check_vma=False
    )
```

profile of v0, /device:TPU:0, one launch (start us, length us, event | category | flops | bytes accessed | tf_op | source)
XLA Modules:
  0.0 150.2 jit_solution(9353145701340766999)
XLA Ops:
  6.5 0.0 copy-start
  6.5 0.0 reduce-scatter.2.cloned.1.call-start
  6.5 9.1 %fusion.17 = f32[256,8192]{1,0:T(8,128)} fusion(bf16[256,512]{1,0:T(8,128)(2,1)} %param.6, bf16[512,8192]{1,0:T(8,128)(2,1)} %param.7), kind=kOutput, calls=%fused_computation.52 | convolution fusion | flops 2147483648 | bytes 17039360 | tf_op jit(solution)/shard_map/dot_general | solution.py:15
  15.7 0.0 copy-start.1
  15.7 0.0 copy-start.3
  15.7 0.0 copy-start.4
  15.7 0.0 copy-start.2
  15.7 0.0 reduce-scatter.2.cloned.1.call-update
  15.7 0.9 copy-done.1
  16.6 0.0 copy-done.3
  16.7 0.7 fusion.16
  17.4 0.0 copy-done.4
  17.4 9.7 %fusion.21 = s32[2,128]{1,0:T(2,128)S(1)} fusion(s32[]{:T(128)} %bitcast.15, s32[]{:T(128)} %bitcast.14, s32[]{:T(128)} %bitcast.13, s32[]{:T(128)} %bitcast.12, s32[]{:T(128)} %bitcast.11, s32[]{:T(128)} %bitcast.10, s32[]{:T(128)} %bitcast.9, s32[]{:T(128)} %bitcast.8, s32[]{:T(128)} %bitcast.7, s32[]{:T(128)} %bitcast.6, s32[]{:T(128)} %bitcast.5, ...), kind=kLoop, calls=%fused_computation.53 | loop fusion | flops 8448 | bytes 2112 | tf_op jit(solution)/shard_map/eq | solution.py:19
  27.1 0.6 reduce-window.6
  27.7 0.2 slice_reduce_fusion
  27.9 9.8 %compare_select_fusion.4 = s32[256]{0:T(256)S(1)} fusion(s32[256]{0:T(256)S(1)} %copy-done.4, s32[]{:T(128)} %bitcast, s32[]{:T(128)} %bitcast.1, s32[]{:T(128)} %bitcast.2, s32[]{:T(128)} %bitcast.3, s32[]{:T(128)} %bitcast.4, s32[]{:T(128)} %bitcast.5, s32[]{:T(128)} %bitcast.6, s32[]{:T(128)} %bitcast.7, s32[]{:T(128)} %bitcast.8, s32[]{:T(128)} %bitcast.9, ...), kind=kLoop, calls=%fused_computation.32 | loop fusion | flops 8448 | bytes 2112 | tf_op jit(solution)/shard_map/gather | solution.py:14
  37.7 0.1 fusion.11
  37.8 9.7 %add_add_fusion = s32[256]{0:T(256)S(1)} fusion(s32[256]{0:T(256)S(1)} %fusion.11, s32[]{:T(128)} %bitcast.15, s32[]{:T(128)} %bitcast.14, s32[]{:T(128)} %bitcast.13, s32[]{:T(128)} %bitcast.12, s32[]{:T(128)} %bitcast.11, s32[]{:T(128)} %bitcast.10, s32[]{:T(128)} %bitcast.9, s32[]{:T(128)} %bitcast.8, s32[]{:T(128)} %bitcast.7, s32[]{:T(128)} %bitcast.6, ...), kind=kLoop, calls=%fused_computation.48 | loop fusion | flops 9216 | bytes 3136 | tf_op jit(solution)/shard_map/add | solution.py:23
  47.6 1.4 scatter_custom_fusion
  49.0 2.6 %gather_fusion.1 = bf16[512,512]{1,0:T(8,128)(2,1)} fusion(bf16[257,512]{1,0:T(8,128)(2,1)S(1)} %concatenate.7, s32[1024]{0:T(1024)S(1)} %pad_clamp_fusion.1), kind=kCustom, calls=%fused_computation.1 | custom fusion | bytes 1050624 | tf_op jit(solution)/shard_map/gather | solution.py:30
  51.6 7.4 %all-to-all-start = ((bf16[16,32,512]{2,1,0:T(8,128)(2,1)}), bf16[16,32,512]{2,1,0:T(8,128)(2,1)S(1)}, u32[]{:S(2)}, u32[]{:S(2)}) async-start(bf16[16,32,512]{2,1,0:T(8,128)(2,1)} %bitcast.20), calls=%async_computation.1 | async-start | bytes 1048576 | tf_op jit(solution)/shard_map/all_to_all | solution.py:31
  59.1 0.1 compare_select_fusion.3
  59.1 0.7 gather_fusion
  59.9 22.2 %all-to-all-done = bf16[16,32,512]{2,1,0:T(8,128)(2,1)S(1)} async-done(((bf16[16,32,512]{2,1,0:T(8,128)(2,1)}), bf16[16,32,512]{2,1,0:T(8,128)(2,1)S(1)}, u32[]{:S(2)}, u32[]{:S(2)}) %all-to-all-start) | async-done | bytes 524320 | tf_op jit(solution)/shard_map/all_to_all | solution.py:31
  82.1 0.0 copy-done
  82.1 0.0 copy-done.2
  82.1 0.9 convolution_convert_fusion
  83.1 0.9 copy.19
  84.0 9.8 %all-to-all-start.1 = ((bf16[32,16,512]{2,0,1:T(8,128)(2,1)}), bf16[32,16,512]{2,0,1:T(8,128)(2,1)S(1)}, u32[]{:S(2)}, u32[]{:S(2)}) async-start(bf16[32,16,512]{2,0,1:T(8,128)(2,1)} %bitcast.80), calls=%async_computation.2 | async-start | bytes 1048576 | tf_op jit(solution)/shard_map/all_to_all | solution.py:45
  93.8 14.5 %all-to-all-done.1 = bf16[32,16,512]{2,0,1:T(8,128)(2,1)S(1)} async-done(((bf16[32,16,512]{2,0,1:T(8,128)(2,1)}), bf16[32,16,512]{2,0,1:T(8,128)(2,1)S(1)}, u32[]{:S(2)}, u32[]{:S(2)}) %all-to-all-start.1) | async-done | bytes 524320 | tf_op jit(solution)/shard_map/all_to_all | solution.py:45
  108.3 1.2 gather_fusion.2
  109.4 32.1 %reduce-scatter.2.cloned.1.call-done = f32[256,512]{1,0:T(8,128)} async-done(((f32[256,8192]{1,0:T(8,128)}), f32[256,512]{1,0:T(8,128)}) %reduce-scatter.2.cloned.1.call-update) | async-done | bytes 524304 | tf_op jit(solution)/shard_map/reduce_scatter | solution.py:16
  141.5 1.8 %add_convert_fusion = bf16[256,512]{1,0:T(8,128)(2,1)} fusion(f32[256,512]{1,0:T(8,128)} %reduce-scatter.2.cloned.1.call-done, bf16[256,512]{1,0:T(8,128)(2,1)S(1)} %gather_fusion.2), kind=kLoop, calls=%fused_computation.15 | loop fusion | flops 393216 | bytes 1048576 | tf_op jit(solution)/shard_map/convert_element_type | solution.py:47
  (13 shorter events, 0.1 us)
Async XLA Ops:
  6.5 75.6 %copy-start = (bf16[1,64,8192]{2,1,0:T(8,128)(2,1)S(1)}, bf16[1,64,8192]{2,1,0:T(8,128)(2,1)}, u32[]{:S(2)}) copy-start(bf16[1,64,8192]{2,1,0:T(8,128)(2,1)} %param.9) | copy-start | bytes 3145732
  6.5 135.0 %reduce-scatter.2.cloned.1.call-start = ((), (), s32[]{:S(2)}) async-start(), calls=%async_computation.3 | async-start | bytes 8912896 | tf_op jit(solution)/shard_map/reduce_scatter | solution.py:16
  15.7 0.9 copy-start.1
  15.7 1.0 copy-start.3
  15.7 1.7 %copy-start.4 = (s32[256]{0:T(256)S(1)}, s32[256]{0:T(256)}, u32[]{:S(2)}) copy-start(s32[256]{0:T(256)} %param.10) | copy-start | bytes 3076
  15.7 66.5 %copy-start.2 = (bf16[1,8192,64]{1,2,0:T(8,128)(2,1)S(1)}, bf16[1,8192,64]{1,2,0:T(8,128)(2,1)}, u32[]{:S(2)}) copy-start(bf16[1,8192,64]{1,2,0:T(8,128)(2,1)} %param.8) | copy-start | bytes 3145732
  51.6 30.4 %all-to-all-start = ((bf16[16,32,512]{2,1,0:T(8,128)(2,1)}), bf16[16,32,512]{2,1,0:T(8,128)(2,1)S(1)}, u32[]{:S(2)}, u32[]{:S(2)}) async-start(bf16[16,32,512]{2,1,0:T(8,128)(2,1)} %bitcast.20), calls=%async_computation.1 | async-start | bytes 1048576 | tf_op jit(solution)/shard_map/all_to_all | solution.py:31
  84.0 24.3 %all-to-all-start.1 = ((bf16[32,16,512]{2,0,1:T(8,128)(2,1)}), bf16[32,16,512]{2,0,1:T(8,128)(2,1)S(1)}, u32[]{:S(2)}, u32[]{:S(2)}) async-start(bf16[32,16,512]{2,0,1:T(8,128)(2,1)} %bitcast.80), calls=%async_computation.2 | async-start | bytes 1048576 | tf_op jit(solution)/shard_map/all_to_all | solution.py:45
Sparse Core Ops, SparseCore 0:
  15.8 125.6 reduce-scatter.1
where the time goes:
time: 151 us; the launch traced here: 150 us
  waiting for transfers between devices  68.8 us (46%)
  other arithmetic  31.9 us (21%)
  starting transfers between devices  17.2 us (11%)
  between operations  13.5 us (9%)
  matrix products  10 us (7%)
  local copies, waits for them, and re-layouts  8.71 us (6%)
    reduce_scatter x1, waiting for transfers between devices, shards(): lax.psum_scatter(partial_value, 'tensor', scatter_dimension=1, tiled=True)  32.1 us
    all_to_all x1, waiting for transfers between devices, shards(): lax.all_to_all(outgoing, 'tensor', split_axis=0, concat_axis=1, tiled=True)  22.2 us
    all_to_all x1, waiting for transfers between devices, shards(): lax.all_to_all(expanded, 'tensor', split_axis=1, concat_axis=0, tiled=True)  14.5 us
    gather x1, other arithmetic, shards(): storage = adapter_slot[row_adapter]  9.77 us
    all_to_all x1, starting transfers between devices, shards(): lax.all_to_all(expanded, 'tensor', split_axis=1, concat_axis=0, tiled=True)  9.77 us
    add x1, other arithmetic, shards(): target = owner_of * CAP + position  9.74 us
    eq x1, other arithmetic, shards(): owner_of[:, None] == jnp.arange(tensor_size, dtype=jnp.int32)[None, :]  9.73 us
    dot_general x1, matrix products, shards(): jnp.dot(attended, out_weight, preferred_element_type=jnp.float32)  9.13 us
  transfers between devices with their start and end apart: 3, of which 3 were waited for; matrix products, arithmetic and copies ran while one was open for 26% of the time, Pallas kernels for 0%

commit v1 on v0

--- a/solution.py
+++ b/solution.py
@@ -1,12 +1,210 @@
+import functools
+
 import jax
 import jax.numpy as jnp
 from jax import lax
+from jax.experimental import pallas as pl
+from jax.experimental.pallas import tpu as pltpu
 from jax.sharding import PartitionSpec as P
 
 CAP = 32
-
-
-def shards(attended, out_weight, adapter_down, adapter_up, row_adapter, adapter_slot):
+VMEM = pltpu.VMEM
+SMEM = pltpu.SMEM
+
+
+def params(mib):
+    return pltpu.CompilerParams(vmem_limit_bytes=mib * 1024 * 1024)
+
+
+def cost(flops, moved):
+    return pl.CostEstimate(flops=flops, bytes_accessed=moved, transcendentals=0)
+
+
+def swap(value, mask, count):
+    return lax.ppermute(value, "tensor", [(t, t ^ mask) for t in range(count)])
+
+
+def route_kernel(count, me_ref, slot_ref, row_ref, attended_ref, outgoing_ref, picks_ref):
+    rows = attended_ref.shape[0]
+    ids = row_ref[...]
+    owner = jnp.zeros_like(ids)
+    for a in range(slot_ref.shape[0]):
+        owner = jnp.where(ids == a, slot_ref[a], owner)
+    hot = (lax.broadcasted_iota(jnp.int32, (count, rows), 0) == owner).astype(jnp.float32)
+    earlier = (
+        lax.broadcasted_iota(jnp.int32, (rows, rows), 0)
+        < lax.broadcasted_iota(jnp.int32, (rows, rows), 1)
+    ).astype(jnp.bfloat16)
+    ahead = jnp.dot(hot.astype(jnp.bfloat16), earlier, preferred_element_type=jnp.float32)
+    place = jnp.sum(ahead * hot, axis=0, keepdims=True).astype(jnp.int32)
+    target = owner * CAP + place
+    slots = lax.broadcasted_iota(jnp.int32, (count * CAP, rows), 0)
+    select = (slots == target).astype(jnp.bfloat16)
+    outgoing_ref[...] = jnp.dot(
+        select, attended_ref[...], preferred_element_type=jnp.float32
+    ).astype(jnp.bfloat16)
+    me = me_ref[0]
+    local = lax.broadcasted_iota(jnp.int32, (CAP, rows), 0)
+    picks_ref[:CAP, :] = (local + me * CAP == target).astype(jnp.bfloat16)
+    picks_ref[CAP:, :] = (local + (me ^ 1) * CAP == target).astype(jnp.bfloat16)
+
+
+def route(me, adapter_slot, row_adapter, attended, count):
+    rows, width = attended.shape
+    return pl.pallas_call(
+        functools.partial(route_kernel, count),
+        out_shape=(
+            jax.ShapeDtypeStruct((count * CAP, width), jnp.bfloat16),
+            jax.ShapeDtypeStruct((2 * CAP, rows), jnp.bfloat16),
+        ),
+        in_specs=[
+            pl.BlockSpec(memory_space=SMEM),
+            pl.BlockSpec(memory_space=SMEM),
+            pl.BlockSpec(memory_space=VMEM),
+            pl.BlockSpec(memory_space=VMEM),
+        ],
+        out_specs=(pl.BlockSpec(memory_space=VMEM), pl.BlockSpec(memory_space=VMEM)),
+        compiler_params=params(16),
+        cost_estimate=cost(2 * count * CAP * rows * width, 2 * (count * CAP + rows) * width),
+        name="route",
+    )(me, adapter_slot, row_adapter[None, :], attended)
+
+
+def away_kernel(me_ref, attended_ref, weight_ref, out_ref):
+    out_ref[0] = jnp.dot(
+        attended_ref[...], weight_ref[...], preferred_element_type=jnp.float32
+    ).astype(jnp.bfloat16)
+
+
+def away(me, attended, out_weight, kz, width):
+    rows, depth = attended.shape
+    return pl.pallas_call(
+        away_kernel,
+        out_shape=jax.ShapeDtypeStruct((2, rows, width), jnp.bfloat16),
+        grid_spec=pltpu.PrefetchScalarGridSpec(
+            num_scalar_prefetch=1,
+            grid=(2,),
+            in_specs=[
+                pl.BlockSpec((rows, depth), lambda i, me: (0, 0)),
+                pl.BlockSpec((depth, width), lambda i, me: (0, me[0] ^ (kz * 4 + i * 2 + 1))),
+            ],
+            out_specs=pl.BlockSpec((1, rows, width), lambda i, me: (i, 0, 0)),
+        ),
+        compiler_params=params(16),
+        cost_estimate=cost(4 * rows * depth * width, 4 * depth * width + 4 * rows * width),
+        name="away",
+    )(me, attended, out_weight)
+
+
+def adapter_kernel(count, me_ref, arrived_ref, down_ref, up_ref, near_ref, far_ref):
+    width = arrived_ref.shape[2]
+    total = jnp.zeros((CAP, down_ref.shape[0]), jnp.float32)
+    for t in range(count):
+        total += lax.dot_general(
+            arrived_ref[t],
+            down_ref[:, t * width : (t + 1) * width],
+            (((1,), (1,)), ((), ())),
+            preferred_element_type=jnp.float32,
+        )
+    shrunk = total.astype(jnp.bfloat16)
+    for m in range(count):
+        start = pl.multiple_of((me_ref[0] ^ m) * width, width)
+        grown = jnp.dot(
+            shrunk, up_ref[:, pl.ds(start, width)], preferred_element_type=jnp.float32
+        ).astype(jnp.bfloat16)
+        if m % 2:
+            far_ref[m // 2] = grown
+        else:
+            near_ref[m // 2] = grown
+
+
+def adapter(me, arrived, down, up):
+    count, cap, width = arrived.shape
+    half = jax.ShapeDtypeStruct((count // 2, cap, width), jnp.bfloat16)
+    vmem = pl.BlockSpec(memory_space=VMEM)
+    return pl.pallas_call(
+        functools.partial(adapter_kernel, count),
+        out_shape=(half, half),
+        in_specs=[pl.BlockSpec(memory_space=SMEM), vmem, vmem, vmem],
+        out_specs=(vmem, vmem),
+        compiler_params=params(24),
+        cost_estimate=cost(4 * cap * down.size, 2 * (down.size + up.size + 2 * arrived.size)),
+        name="adapter",
+    )(me, arrived, down, up)
+
+
+def pair_kernel(
+    me_ref, attended_ref, stay_w_ref, go_w_ref, other_ref, picks_ref, near_ref, far_ref, stay_ref, go_ref
+):
+    def block(weight_ref, j):
+        total = jnp.dot(attended_ref[...], weight_ref[...], preferred_element_type=jnp.float32)
+        own = lax.dot_general(
+            picks_ref[:CAP, :], near_ref[j], (((0,), (0,)), ((), ())), preferred_element_type=jnp.float32
+        )
+        others = lax.dot_general(
+            picks_ref[CAP:, :], far_ref[j], (((0,), (0,)), ((), ())), preferred_element_type=jnp.float32
+        )
+        return total + other_ref[j].astype(jnp.float32) + (own + others)
+
+    go_ref[...] = block(go_w_ref, 1).astype(jnp.bfloat16)
+    stay_ref[...] = block(stay_w_ref, 0)
+
+
+def pair(me, attended, out_weight, other, picks, near, far, kz):
+    rows, depth = attended.shape
+    width = other.shape[2]
+    cap = near.shape[1]
+    whole = lambda i, me: (0, 0)
+    return pl.pallas_call(
+        pair_kernel,
+        out_shape=(
+            jax.ShapeDtypeStruct((rows, width), jnp.float32),
+            jax.ShapeDtypeStruct((rows, width), jnp.bfloat16),
+        ),
+        grid_spec=pltpu.PrefetchScalarGridSpec(
+            num_scalar_prefetch=1,
+            grid=(1,),
+            in_specs=[
+                pl.BlockSpec((rows, depth), whole),
+                pl.BlockSpec((depth, width), lambda i, me: (0, me[0] ^ (kz * 4))),
+                pl.BlockSpec((depth, width), lambda i, me: (0, me[0] ^ (kz * 4 + 2))),
+                pl.BlockSpec((2, rows, width), lambda i, me: (0, 0, 0)),
+                pl.BlockSpec((2 * cap, rows), whole),
+                pl.BlockSpec((2, cap, width), lambda i, me: (kz, 0, 0)),
+                pl.BlockSpec((2, cap, width), lambda i, me: (kz, 0, 0)),
+            ],
+            out_specs=(pl.BlockSpec((rows, width), whole), pl.BlockSpec((rows, width), whole)),
+        ),
+        compiler_params=params(24),
+        cost_estimate=cost(4 * rows * depth * width, 4 * depth * width + 12 * rows * width),
+        name="pair",
+    )(me, attended, out_weight, out_weight, other, picks, near, far)
+
+
+def staged(attended, out_weight, adapter_down, adapter_up, row_adapter, adapter_slot):
+    count = lax.axis_size("tensor")
+    me = lax.axis_index("tensor").astype(jnp.int32)[None]
+    width = out_weight.shape[1] // count
+    outgoing, picks = route(me, adapter_slot, row_adapter, attended, count)
+    arrived = lax.all_to_all(
+        outgoing.reshape(count, CAP, outgoing.shape[1]), "tensor", split_axis=0, concat_axis=0, tiled=True
+    )
+    order = (3, 2, 1, 0)
+    others = {kz: swap(away(me, attended, out_weight, kz, width), 1, count) for kz in order}
+    near, far = adapter(me, arrived, jnp.swapaxes(adapter_down, 1, 2)[0], adapter_up[0])
+    far = swap(far, 1, count)
+    total = None
+    for kz in order:
+        stay, go = pair(me, attended, out_weight, others[kz], picks, near, far, kz)
+        came = swap(go, 2, count)
+        both = stay + came.astype(jnp.float32)
+        if kz:
+            both = swap(both.astype(jnp.bfloat16), 4 * kz, count).astype(jnp.float32)
+        total = both if total is None else total + both
+    return total.astype(jnp.bfloat16)
+
+
+def general(attended, out_weight, adapter_down, adapter_up, row_adapter, adapter_slot):
     tensor_size = lax.axis_size("tensor")
     device = lax.axis_index("tensor")
     row_count = attended.shape[0]
@@ -47,6 +245,12 @@
     return (base_out + delta_out.astype(jnp.float32)).astype(jnp.bfloat16)
 
 
+def shards(*arrays):
+    if lax.axis_size("tensor") == 16 and arrays[2].shape[0] == 1:
+        return staged(*arrays)
+    return general(*arrays)
+
+
 def solution(mesh):
     placed = (
         P("groups", "tensor"),

time: 151 us -> 69.4 us (0.46)
  waiting for transfers between devices: 68.8 us -> 25 us
  other arithmetic: 31.9 us -> 1.14 us
  Pallas kernels: 0 us -> 14 us
  between operations: 13.5 us -> 0.1 us
  matrix products: 10 us -> 0 us
    all_to_all x2 -> x1, waiting for transfers between devices: 36.7 us -> 4.19 us  [staged(): lax.all_to_all(outgoing.reshape(count, CAP, outgoing.shape[1]), 'tensor',...]
    reduce_scatter x1 -> x0, waiting for transfers between devices: 32.1 us -> none  [shards(): lax.psum_scatter(partial_value, 'tensor', scatter_dimension=1, tiled=True)]
    ppermute x0 -> x12, waiting for transfers between devices: none -> 20.9 us  [swap(): return lax.ppermute(value, 'tensor', [(t, t ^ mask) for t in range(count)])]
    pallas_call x0 -> x10, Pallas kernels: none -> 14 us  [the longest x4 6.27 us: pair(): pl.pallas_call(pair_kernel, out_shape=(jax.ShapeDtypeStruct((rows, width)...]
    ppermute x0 -> x12, starting transfers between devices: none -> 11.2 us  [swap(): return lax.ppermute(value, 'tensor', [(t, t ^ mask) for t in range(count)])]
    dot_general x2 -> x0, matrix products: 10 us -> none  [the longest x1 9.13 us: shards(): jnp.dot(attended, out_weight, preferred_element_type=jnp.float32)]
    gather x4 -> x0, other arithmetic: 9.79 us -> none  [the longest x1 9.77 us: shards(): storage = adapter_slot[row_adapter]]
    all_to_all x2 -> x1, starting transfers between devices: 17.2 us -> 7.39 us  [staged(): lax.all_to_all(outgoing.reshape(count, CAP, outgoing.shape[1]), 'tensor',...]
  transfers between devices with their start and end apart: 3 -> 13, of which waited for: 3 -> 7; matrix products, arithmetic and copies ran while one was open for 26% -> 0% of each run, Pallas kernels for 0% -> 18%
where the time goes in v1:
time: 69.4 us; the launch traced here: 68.9 us
  waiting for transfers between devices  25 us (36%)
  starting transfers between devices  18.6 us (27%)
  Pallas kernels  14 us (20%)
  local copies, waits for them, and re-layouts  10 us (14%)
  other arithmetic  1.14 us (2%)
    ppermute x12, waiting for transfers between devices, swap(): return lax.ppermute(value, 'tensor', [(t, t ^ mask) for t in range(count)])  20.9 us
    ppermute x12, starting transfers between devices, swap(): return lax.ppermute(value, 'tensor', [(t, t ^ mask) for t in range(count)])  11.2 us
    unnamed x18, local copies, waits for them, and re-layouts  10 us
    all_to_all x1, starting transfers between devices, staged(): lax.all_to_all(outgoing.reshape(count, CAP, outgoing.shape[1]), 'tensor',...  7.39 us
    pallas_call x4, Pallas kernels, pair(): pl.pallas_call(pair_kernel, out_shape=(jax.ShapeDtypeStruct((rows, width)...  6.27 us
    pallas_call x4, Pallas kernels, away(): pl.pallas_call(away_kernel, out_shape=jax.ShapeDtypeStruct((2, rows, widt...  5.01 us
    all_to_all x1, waiting for transfers between devices, staged(): lax.all_to_all(outgoing.reshape(count, CAP, outgoing.shape[1]), 'tensor',...  4.19 us
    pallas_call x1, Pallas kernels, route(): pl.pallas_call(functools.partial(route_kernel, count), out_shape=(jax.Sha...  1.81 us
  transfers between devices with their start and end apart: 13, of which 7 were waited for; matrix products, arithmetic and copies ran while one was open for 0% of the time, Pallas kernels for 18%

profile of v1, /device:TPU:0, one launch (start us, length us, event | category | flops | bytes accessed | tf_op | source)
XLA Modules:
  0.0 68.9 jit_solution(4307470833144112916)
XLA Ops:
  0.0 0.0 copy-start.2
  0.0 0.9 %copy-done.2 = bf16[256,512]{1,0:T(8,128)(2,1)S(1)} copy-done((bf16[256,512]{1,0:T(8,128)(2,1)S(1)}, bf16[256,512]{1,0:T(8,128)(2,1)}, u32[]{:S(2)}) %copy-start.2) | copy-done | bytes 262168
  1.0 0.0 copy-start.7
  1.0 0.7 copy-done.7
  1.6 0.0 copy-start.8
  1.6 0.7 copy-done.8
  2.3 1.8 %route.1 = (bf16[512,512]{1,0:T(8,128)(2,1)}, bf16[64,256]{1,0:T(8,128)(2,1)S(1)}) custom-call(s32[1]{0:T(128)} %bitcast.me_ref, s32[16]{0:T(128)S(1)} %copy-done.8, s32[1,256]{1,0:T(1,128)S(1)} %bitcast.9, bf16[256,512]{1,0:T(8,128)(2,1)S(1)} %copy-done.2), custom_call_target="tpu_custom_call" | custom-call | flops 134217728 | bytes 786432 | tf_op jit(solution)/shard_map/route/pallas_call | solution.py:54
  4.1 7.4 %all-to-all-start = ((bf16[16,32,512]{2,1,0:T(8,128)(2,1)}), bf16[16,32,512]{2,1,0:T(8,128)(2,1)S(1)}, u32[]{:S(2)}, u32[]{:S(2)}) async-start(bf16[16,32,512]{2,1,0:T(8,128)(2,1)} %bitcast.2), calls=%async_computation | async-start | bytes 1048576 | tf_op jit(solution)/shard_map/all_to_all | solution.py:189
  11.5 0.0 copy-start
  11.5 3.4 %copy-done = bf16[512,8192]{1,0:T(8,128)(2,1)S(1)} copy-done((bf16[512,8192]{1,0:T(8,128)(2,1)S(1)}, bf16[512,8192]{1,0:T(8,128)(2,1)}, u32[]{:S(2)}) %copy-start) | copy-done | bytes 8388632
  14.9 0.0 copy-start.3
  14.9 0.9 %copy-done.3 = bf16[256,512]{1,0:T(8,128)(2,1)S(1)} copy-done((bf16[256,512]{1,0:T(8,128)(2,1)S(1)}, bf16[256,512]{1,0:T(8,128)(2,1)}, u32[]{:S(2)}) %copy-start.3) | copy-done | bytes 262168
  15.8 1.4 %away.4 = bf16[2,256,512]{2,1,0:T(8,128)(2,1)} custom-call(s32[1]{0:T(128)} %bitcast.me_ref, bf16[256,512]{1,0:T(8,128)(2,1)S(1)} %copy-done.3, bf16[512,8192]{1,0:T(8,128)(2,1)S(1)} %copy-done), custom_call_target="tpu_custom_call" | custom-call | flops 268435456 | bytes 1572864 | tf_op jit(solution)/shard_map/away/pallas_call | solution.py:81
  17.3 0.4 collective-permute-start
  17.7 1.4 %away.5 = bf16[2,256,512]{2,1,0:T(8,128)(2,1)} custom-call(s32[1]{0:T(128)} %bitcast.me_ref, bf16[256,512]{1,0:T(8,128)(2,1)S(1)} %copy-done.3, bf16[512,8192]{1,0:T(8,128)(2,1)S(1)} %copy-done), custom_call_target="tpu_custom_call" | custom-call | flops 268435456 | bytes 1572864 | tf_op jit(solution)/shard_map/away/pallas_call | solution.py:81
  19.1 0.0 copy-start.5
  19.1 0.0 copy-start.6
  19.1 0.0 copy-start.4
  19.1 0.1 collective-permute-start.4
  19.2 1.4 %away.6 = bf16[2,256,512]{2,1,0:T(8,128)(2,1)} custom-call(s32[1]{0:T(128)} %bitcast.me_ref, bf16[256,512]{1,0:T(8,128)(2,1)S(1)} %copy-done.3, bf16[512,8192]{1,0:T(8,128)(2,1)S(1)} %copy-done), custom_call_target="tpu_custom_call" | custom-call | flops 268435456 | bytes 1572864 | tf_op jit(solution)/shard_map/away/pallas_call | solution.py:81
  20.6 0.4 collective-permute-start.7
  21.0 0.7 %away.7 = bf16[2,256,512]{2,1,0:T(8,128)(2,1)S(1)} custom-call(s32[1]{0:T(128)} %bitcast.me_ref, bf16[256,512]{1,0:T(8,128)(2,1)S(1)} %copy-done.3, bf16[512,8192]{1,0:T(8,128)(2,1)S(1)} %copy-done), custom_call_target="tpu_custom_call" | custom-call | flops 268435456 | bytes 1572864 | tf_op jit(solution)/shard_map/away/pallas_call | solution.py:81
  21.8 4.2 %all-to-all-done.arrived_ref = bf16[16,32,512]{2,1,0:T(8,128)(2,1)S(1)} async-done(((bf16[16,32,512]{2,1,0:T(8,128)(2,1)}), bf16[16,32,512]{2,1,0:T(8,128)(2,1)S(1)}, u32[]{:S(2)}, u32[]{:S(2)}) %all-to-all-start) | async-done | bytes 524320 | tf_op jit(solution)/shard_map/all_to_all | solution.py:189
  26.0 0.0 copy-done.5
  26.0 0.0 copy-done.6
  26.0 0.9 %adapter.1 = (bf16[8,32,512]{2,1,0:T(8,128)(2,1)S(1)}, bf16[8,32,512]{2,1,0:T(8,128)(2,1)S(1)}) custom-call(s32[1]{0:T(128)} %bitcast.me_ref, bf16[16,32,512]{2,1,0:T(8,128)(2,1)S(1)} %all-to-all-done.arrived_ref, bf16[64,8192]{1,0:T(8,128)(2,1)S(1)} %bitcast.7, bf16[64,8192]{1,0:T(8,128)(2,1)S(1)} %bitcast.8), custom_call_target="tpu_custom_call" | custom-call | flops 67108864 | bytes 3145728 | tf_op jit(solution)/shard_map/adapter/pallas_call | solution.py:125
  26.9 0.1 collective-permute-start.1
  27.0 0.5 collective-permute-start.10
  27.5 0.0 collective-permute-done.other_ref
  27.5 1.0 %collective-permute-done.1.far_ref = bf16[8,32,512]{2,1,0:T(8,128)(2,1)S(1)} collective-permute-done((bf16[8,32,512]{2,1,0:T(8,128)(2,1)S(1)}, bf16[8,32,512]{2,1,0:T(8,128)(2,1)S(1)}, u32[]{:S(2)}, u32[]{:S(2)}) %collective-permute-start.1) | collective-permute-done | bytes 262176 | tf_op jit(solution)/shard_map/ppermute | solution.py:24
  28.5 0.0 copy-done.4
  28.5 0.0 copy-start.1
  28.5 3.4 %copy-done.1 = bf16[512,8192]{1,0:T(8,128)(2,1)S(1)} copy-done((bf16[512,8192]{1,0:T(8,128)(2,1)S(1)}, bf16[512,8192]{1,0:T(8,128)(2,1)}, u32[]{:S(2)}) %copy-start.1) | copy-done | bytes 8388632
  31.9 1.8 %pair.4 = (f32[256,512]{1,0:T(8,128)S(1)}, bf16[256,512]{1,0:T(8,128)(2,1)S(1)}) custom-call(s32[1]{0:T(128)} %bitcast.me_ref, bf16[256,512]{1,0:T(8,128)(2,1)S(1)} %copy-done.4, bf16[512,8192]{1,0:T(8,128)(2,1)S(1)} %copy-done.1, bf16[512,8192]{1,0:T(8,128)(2,1)S(1)} %copy-done.1, bf16[2,256,512]{2,1,0:T(8,128)(2,1)} %collective-permute-done.other_ref, ...), custom_call_target="tpu_custom_call" | custom-call | flops 268435456 | bytes 2621440 | tf_op jit(solution)/shard_map/pair/pallas_call | solution.py:158
  33.7 0.9 %collective-permute-start.2 = (bf16[256,512]{1,0:T(8,128)(2,1)S(1)}, bf16[256,512]{1,0:T(8,128)(2,1)S(1)}, u32[]{:S(2)}, u32[]{:S(2)}) collective-permute-start(bf16[256,512]{1,0:T(8,128)(2,1)S(1)} %get-tuple-element.22), channel_id=1, source_target_pairs={{0,2},{1,3},{2,0},{3,1},{4,6},{5,7},{6,4},{7,5},{8,10},{9,11},{10,... | collective-permute-start | bytes 786440 | tf_op jit(solution)/shard_map/ppermute | solution.py:24
  34.6 0.0 collective-permute-done.4.other_ref
  34.6 1.8 %pair.5 = (f32[256,512]{1,0:T(8,128)S(1)}, bf16[256,512]{1,0:T(8,128)(2,1)S(1)}) custom-call(s32[1]{0:T(128)} %bitcast.me_ref, bf16[256,512]{1,0:T(8,128)(2,1)S(1)} %copy-done.4, bf16[512,8192]{1,0:T(8,128)(2,1)S(1)} %copy-done.1, bf16[512,8192]{1,0:T(8,128)(2,1)S(1)} %copy-done.1, bf16[2,256,512]{2,1,0:T(8,128)(2,1)} %collective-permute-done.4.other_ref, ...), custom_call_target="tpu_custom_call" | custom-call | flops 268435456 | bytes 2621440 | tf_op jit(solution)/shard_map/pair/pallas_call | solution.py:158
  36.5 1.3 %collective-permute-start.5 = (bf16[256,512]{1,0:T(8,128)(2,1)S(1)}, bf16[256,512]{1,0:T(8,128)(2,1)S(1)}, u32[]{:S(2)}, u32[]{:S(2)}) collective-permute-start(bf16[256,512]{1,0:T(8,128)(2,1)S(1)} %get-tuple-element.24), channel_id=1, source_target_pairs={{0,2},{1,3},{2,0},{3,1},{4,6},{5,7},{6,4},{7,5},{8,10},{9,11},{10,... | collective-permute-start | bytes 786440 | tf_op jit(solution)/shard_map/ppermute | solution.py:24
  37.7 0.0 collective-permute-done.7.other_ref
  37.7 1.8 %pair.6 = (f32[256,512]{1,0:T(8,128)S(1)}, bf16[256,512]{1,0:T(8,128)(2,1)S(1)}) custom-call(s32[1]{0:T(128)} %bitcast.me_ref, bf16[256,512]{1,0:T(8,128)(2,1)S(1)} %copy-done.4, bf16[512,8192]{1,0:T(8,128)(2,1)S(1)} %copy-done.1, bf16[512,8192]{1,0:T(8,128)(2,1)S(1)} %copy-done.1, bf16[2,256,512]{2,1,0:T(8,128)(2,1)} %collective-permute-done.7.other_ref, ...), custom_call_target="tpu_custom_call" | custom-call | flops 268435456 | bytes 2621440 | tf_op jit(solution)/shard_map/pair/pallas_call | solution.py:158
  39.6 0.9 %collective-permute-start.8 = (bf16[256,512]{1,0:T(8,128)(2,1)S(1)}, bf16[256,512]{1,0:T(8,128)(2,1)S(1)}, u32[]{:S(2)}, u32[]{:S(2)}) collective-permute-start(bf16[256,512]{1,0:T(8,128)(2,1)S(1)} %get-tuple-element.26), channel_id=1, source_target_pairs={{0,2},{1,3},{2,0},{3,1},{4,6},{5,7},{6,4},{7,5},{8,10},{9,11},{10,... | collective-permute-start | bytes 786440 | tf_op jit(solution)/shard_map/ppermute | solution.py:24
  40.5 0.0 collective-permute-done.10.other_ref
  40.5 0.7 %pair.7 = (f32[256,512]{1,0:T(8,128)S(1)}, bf16[256,512]{1,0:T(8,128)(2,1)S(1)}) custom-call(s32[1]{0:T(128)} %bitcast.me_ref, bf16[256,512]{1,0:T(8,128)(2,1)S(1)} %copy-done.4, bf16[512,8192]{1,0:T(8,128)(2,1)S(1)} %copy-done.1, bf16[512,8192]{1,0:T(8,128)(2,1)S(1)} %copy-done.1, bf16[2,256,512]{2,1,0:T(8,128)(2,1)S(1)} %collective-permute-done.10.other_ref, ...), custom_call_target="tpu_custom_call" | custom-call | flops 268435456 | bytes 2621440 | tf_op jit(solution)/shard_map/pair/pallas_call | solution.py:158
  41.2 1.3 %collective-permute-start.11 = (bf16[256,512]{1,0:T(8,128)(2,1)S(1)}, bf16[256,512]{1,0:T(8,128)(2,1)S(1)}, u32[]{:S(2)}, u32[]{:S(2)}) collective-permute-start(bf16[256,512]{1,0:T(8,128)(2,1)S(1)} %get-tuple-element.28), channel_id=1, source_target_pairs={{0,2},{1,3},{2,0},{3,1},{4,6},{5,7},{6,4},{7,5},{8,10},{9,11},{10,... | collective-permute-start | bytes 786440 | tf_op jit(solution)/shard_map/ppermute | solution.py:24
  42.5 0.4 collective-permute-done.2
  42.9 0.1 add_convert_fusion.3
  43.0 1.6 %collective-permute-start.3 = (bf16[256,512]{1,0:T(8,128)(2,1)S(1)}, bf16[256,512]{1,0:T(8,128)(2,1)S(1)}, u32[]{:S(2)}, u32[]{:S(2)}) collective-permute-start(bf16[256,512]{1,0:T(8,128)(2,1)S(1)} %add_convert_fusion.3), channel_id=1, source_target_pairs={{0,12},{1,13},{2,14},{3,15},{4,8},{5,9},{6,10},{7,11},{8,4},{9,5},... | collective-permute-start | bytes 786440 | tf_op jit(solution)/shard_map/ppermute | solution.py:24
  44.7 3.9 %collective-permute-done.5 = bf16[256,512]{1,0:T(8,128)(2,1)S(1)} collective-permute-done((bf16[256,512]{1,0:T(8,128)(2,1)S(1)}, bf16[256,512]{1,0:T(8,128)(2,1)S(1)}, u32[]{:S(2)}, u32[]{:S(2)}) %collective-permute-start.5) | collective-permute-done | bytes 262176 | tf_op jit(solution)/shard_map/ppermute | solution.py:24
  48.6 0.1 add_convert_fusion.2
  48.6 2.3 %collective-permute-start.6 = (bf16[256,512]{1,0:T(8,128)(2,1)S(1)}, bf16[256,512]{1,0:T(8,128)(2,1)S(1)}, u32[]{:S(2)}, u32[]{:S(2)}) collective-permute-start(bf16[256,512]{1,0:T(8,128)(2,1)S(1)} %add_convert_fusion.2), channel_id=1, source_target_pairs={{0,8},{1,9},{2,10},{3,11},{4,12},{5,13},{6,14},{7,15},{8,0},{9,1},... | collective-permute-start | bytes 786440 | tf_op jit(solution)/shard_map/ppermute | solution.py:24
  51.0 3.2 %collective-permute-done.8 = bf16[256,512]{1,0:T(8,128)(2,1)S(1)} collective-permute-done((bf16[256,512]{1,0:T(8,128)(2,1)S(1)}, bf16[256,512]{1,0:T(8,128)(2,1)S(1)}, u32[]{:S(2)}, u32[]{:S(2)}) %collective-permute-start.8) | collective-permute-done | bytes 262176 | tf_op jit(solution)/shard_map/ppermute | solution.py:24
  54.2 0.1 add_convert_fusion.1
  54.3 1.4 %collective-permute-start.9 = (bf16[256,512]{1,0:T(8,128)(2,1)S(1)}, bf16[256,512]{1,0:T(8,128)(2,1)S(1)}, u32[]{:S(2)}, u32[]{:S(2)}) collective-permute-start(bf16[256,512]{1,0:T(8,128)(2,1)S(1)} %add_convert_fusion.1), channel_id=1, source_target_pairs={{0,4},{1,5},{2,6},{3,7},{4,0},{5,1},{6,2},{7,3},{8,12},{9,13},{10,... | collective-permute-start | bytes 786440 | tf_op jit(solution)/shard_map/ppermute | solution.py:24
  55.7 3.3 %collective-permute-done.11 = bf16[256,512]{1,0:T(8,128)(2,1)S(1)} collective-permute-done((bf16[256,512]{1,0:T(8,128)(2,1)S(1)}, bf16[256,512]{1,0:T(8,128)(2,1)S(1)}, u32[]{:S(2)}, u32[]{:S(2)}) %collective-permute-start.11) | collective-permute-done | bytes 262176 | tf_op jit(solution)/shard_map/ppermute | solution.py:24
  59.0 0.0 collective-permute-done.3
  59.0 9.0 %collective-permute-done.6 = bf16[256,512]{1,0:T(8,128)(2,1)S(1)} collective-permute-done((bf16[256,512]{1,0:T(8,128)(2,1)S(1)}, bf16[256,512]{1,0:T(8,128)(2,1)S(1)}, u32[]{:S(2)}, u32[]{:S(2)}) %collective-permute-start.6) | collective-permute-done | bytes 262176 | tf_op jit(solution)/shard_map/ppermute | solution.py:24
  68.0 0.0 collective-permute-done.9
  68.0 0.9 %add_convert_fusion = bf16[256,512]{1,0:T(8,128)(2,1)} fusion(f32[256,512]{1,0:T(8,128)S(1)} %get-tuple-element.27, bf16[256,512]{1,0:T(8,128)(2,1)S(1)} %collective-permute-done.11, bf16[256,512]{1,0:T(8,128)(2,1)S(1)} %collective-permute-done.9, bf16[256,512]{1,0:T(8,128)(2,1)S(1)} %collective-permute-done.6, bf16[256,512]{1,0:T(8,128)(2,1)S(1)} %collective-permute-done.3), kind=kLoop, calls=%fused_computation | loop fusion | flops 1179648 | bytes 1835008 | tf_op jit(solution)/shard_map/convert_element_type | solution.py:204
Async XLA Ops:
  0.0 0.9 %copy-start.2 = (bf16[256,512]{1,0:T(8,128)(2,1)S(1)}, bf16[256,512]{1,0:T(8,128)(2,1)}, u32[]{:S(2)}) copy-start(bf16[256,512]{1,0:T(8,128)(2,1)} %attended_ref.17) | copy-start | bytes 786436
  1.0 0.7 copy-start.7
  1.6 0.7 copy-start.8
  4.1 21.9 %all-to-all-start = ((bf16[16,32,512]{2,1,0:T(8,128)(2,1)}), bf16[16,32,512]{2,1,0:T(8,128)(2,1)S(1)}, u32[]{:S(2)}, u32[]{:S(2)}) async-start(bf16[16,32,512]{2,1,0:T(8,128)(2,1)} %bitcast.2), calls=%async_computation | async-start | bytes 1048576 | tf_op jit(solution)/shard_map/all_to_all | solution.py:189
  11.5 3.4 %copy-start = (bf16[512,8192]{1,0:T(8,128)(2,1)S(1)}, bf16[512,8192]{1,0:T(8,128)(2,1)}, u32[]{:S(2)}) copy-start(bf16[512,8192]{1,0:T(8,128)(2,1)} %go_w_ref.7) | copy-start | bytes 25165828
  14.9 0.9 %copy-start.3 = (bf16[256,512]{1,0:T(8,128)(2,1)S(1)}, bf16[256,512]{1,0:T(8,128)(2,1)}, u32[]{:S(2)}) copy-start(bf16[256,512]{1,0:T(8,128)(2,1)} %attended_ref.17) | copy-start | bytes 786436
  17.3 10.2 %collective-permute-start = (bf16[2,256,512]{2,1,0:T(8,128)(2,1)}, bf16[2,256,512]{2,1,0:T(8,128)(2,1)}, u32[]{:S(2)}, u32[]{:S(2)}) collective-permute-start(bf16[2,256,512]{2,1,0:T(8,128)(2,1)} %away.4), channel_id=1, source_target_pairs={{0,1},{1,0},{2,3},{3,2},{4,5},{5,4},{6,7},{7,6},{8,9},{9,8},{10,11... | collective-permute-start | bytes 1572872 | tf_op jit(solution)/shard_map/ppermute | solution.py:24
  19.1 6.9 %copy-start.5 = (bf16[1,8192,64]{1,2,0:T(8,128)(2,1)S(1)}, bf16[1,8192,64]{1,2,0:T(8,128)(2,1)}, u32[]{:S(2)}) copy-start(bf16[1,8192,64]{1,2,0:T(8,128)(2,1)} %param.8) | copy-start | bytes 3145732
  19.1 6.9 %copy-start.6 = (bf16[1,64,8192]{2,1,0:T(8,128)(2,1)S(1)}, bf16[1,64,8192]{2,1,0:T(8,128)(2,1)}, u32[]{:S(2)}) copy-start(bf16[1,64,8192]{2,1,0:T(8,128)(2,1)} %param.9) | copy-start | bytes 3145732
  19.1 9.4 %copy-start.4 = (bf16[256,512]{1,0:T(8,128)(2,1)S(1)}, bf16[256,512]{1,0:T(8,128)(2,1)}, u32[]{:S(2)}) copy-start(bf16[256,512]{1,0:T(8,128)(2,1)} %attended_ref.17) | copy-start | bytes 786436
  19.1 15.5 %collective-permute-start.4 = (bf16[2,256,512]{2,1,0:T(8,128)(2,1)}, bf16[2,256,512]{2,1,0:T(8,128)(2,1)}, u32[]{:S(2)}, u32[]{:S(2)}) collective-permute-start(bf16[2,256,512]{2,1,0:T(8,128)(2,1)} %away.5), channel_id=1, source_target_pairs={{0,1},{1,0},{2,3},{3,2},{4,5},{5,4},{6,7},{7,6},{8,9},{9,8},{10,11... | collective-permute-start | bytes 1572872 | tf_op jit(solution)/shard_map/ppermute | solution.py:24
  20.6 17.1 %collective-permute-start.7 = (bf16[2,256,512]{2,1,0:T(8,128)(2,1)}, bf16[2,256,512]{2,1,0:T(8,128)(2,1)}, u32[]{:S(2)}, u32[]{:S(2)}) collective-permute-start(bf16[2,256,512]{2,1,0:T(8,128)(2,1)} %away.6), channel_id=1, source_target_pairs={{0,1},{1,0},{2,3},{3,2},{4,5},{5,4},{6,7},{7,6},{8,9},{9,8},{10,11... | collective-permute-start | bytes 1572872 | tf_op jit(solution)/shard_map/ppermute | solution.py:24
  26.9 1.6 %collective-permute-start.1 = (bf16[8,32,512]{2,1,0:T(8,128)(2,1)S(1)}, bf16[8,32,512]{2,1,0:T(8,128)(2,1)S(1)}, u32[]{:S(2)}, u32[]{:S(2)}) collective-permute-start(bf16[8,32,512]{2,1,0:T(8,128)(2,1)S(1)} %get-tuple-element.20), channel_id=1, source_target_pairs={{0,1},{1,0},{2,3},{3,2},{4,5},{5,4},{6,7},{7,6},{8,9},{9,8},{10,11... | collective-permute-start | bytes 786440 | tf_op jit(solution)/shard_map/ppermute | solution.py:24
  27.0 13.5 %collective-permute-start.10 = (bf16[2,256,512]{2,1,0:T(8,128)(2,1)S(1)}, bf16[2,256,512]{2,1,0:T(8,128)(2,1)S(1)}, u32[]{:S(2)}, u32[]{:S(2)}) collective-permute-start(bf16[2,256,512]{2,1,0:T(8,128)(2,1)S(1)} %away.7), channel_id=1, source_target_pairs={{0,1},{1,0},{2,3},{3,2},{4,5},{5,4},{6,7},{7,6},{8,9},{9,8},{10,11... | collective-permute-start | bytes 1572872 | tf_op jit(solution)/shard_map/ppermute | solution.py:24
  28.5 3.4 %copy-start.1 = (bf16[512,8192]{1,0:T(8,128)(2,1)S(1)}, bf16[512,8192]{1,0:T(8,128)(2,1)}, u32[]{:S(2)}) copy-start(bf16[512,8192]{1,0:T(8,128)(2,1)} %go_w_ref.7) | copy-start | bytes 25165828
  33.7 9.2 %collective-permute-start.2 = (bf16[256,512]{1,0:T(8,128)(2,1)S(1)}, bf16[256,512]{1,0:T(8,128)(2,1)S(1)}, u32[]{:S(2)}, u32[]{:S(2)}) collective-permute-start(bf16[256,512]{1,0:T(8,128)(2,1)S(1)} %get-tuple-element.22), channel_id=1, source_target_pairs={{0,2},{1,3},{2,0},{3,1},{4,6},{5,7},{6,4},{7,5},{8,10},{9,11},{10,... | collective-permute-start | bytes 786440 | tf_op jit(solution)/shard_map/ppermute | solution.py:24
  36.5 12.1 %collective-permute-start.5 = (bf16[256,512]{1,0:T(8,128)(2,1)S(1)}, bf16[256,512]{1,0:T(8,128)(2,1)S(1)}, u32[]{:S(2)}, u32[]{:S(2)}) collective-permute-start(bf16[256,512]{1,0:T(8,128)(2,1)S(1)} %get-tuple-element.24), channel_id=1, source_target_pairs={{0,2},{1,3},{2,0},{3,1},{4,6},{5,7},{6,4},{7,5},{8,10},{9,11},{10,... | collective-permute-start | bytes 786440 | tf_op jit(solution)/shard_map/ppermute | solution.py:24
  39.6 14.6 %collective-permute-start.8 = (bf16[256,512]{1,0:T(8,128)(2,1)S(1)}, bf16[256,512]{1,0:T(8,128)(2,1)S(1)}, u32[]{:S(2)}, u32[]{:S(2)}) collective-permute-start(bf16[256,512]{1,0:T(8,128)(2,1)S(1)} %get-tuple-element.26), channel_id=1, source_target_pairs={{0,2},{1,3},{2,0},{3,1},{4,6},{5,7},{6,4},{7,5},{8,10},{9,11},{10,... | collective-permute-start | bytes 786440 | tf_op jit(solution)/shard_map/ppermute | solution.py:24
  41.2 17.8 %collective-permute-start.11 = (bf16[256,512]{1,0:T(8,128)(2,1)S(1)}, bf16[256,512]{1,0:T(8,128)(2,1)S(1)}, u32[]{:S(2)}, u32[]{:S(2)}) collective-permute-start(bf16[256,512]{1,0:T(8,128)(2,1)S(1)} %get-tuple-element.28), channel_id=1, source_target_pairs={{0,2},{1,3},{2,0},{3,1},{4,6},{5,7},{6,4},{7,5},{8,10},{9,11},{10,... | collective-permute-start | bytes 786440 | tf_op jit(solution)/shard_map/ppermute | solution.py:24
  43.0 16.0 %collective-permute-start.3 = (bf16[256,512]{1,0:T(8,128)(2,1)S(1)}, bf16[256,512]{1,0:T(8,128)(2,1)S(1)}, u32[]{:S(2)}, u32[]{:S(2)}) collective-permute-start(bf16[256,512]{1,0:T(8,128)(2,1)S(1)} %add_convert_fusion.3), channel_id=1, source_target_pairs={{0,12},{1,13},{2,14},{3,15},{4,8},{5,9},{6,10},{7,11},{8,4},{9,5},... | collective-permute-start | bytes 786440 | tf_op jit(solution)/shard_map/ppermute | solution.py:24
  48.6 19.3 %collective-permute-start.6 = (bf16[256,512]{1,0:T(8,128)(2,1)S(1)}, bf16[256,512]{1,0:T(8,128)(2,1)S(1)}, u32[]{:S(2)}, u32[]{:S(2)}) collective-permute-start(bf16[256,512]{1,0:T(8,128)(2,1)S(1)} %add_convert_fusion.2), channel_id=1, source_target_pairs={{0,8},{1,9},{2,10},{3,11},{4,12},{5,13},{6,14},{7,15},{8,0},{9,1},... | collective-permute-start | bytes 786440 | tf_op jit(solution)/shard_map/ppermute | solution.py:24
  54.3 13.7 %collective-permute-start.9 = (bf16[256,512]{1,0:T(8,128)(2,1)S(1)}, bf16[256,512]{1,0:T(8,128)(2,1)S(1)}, u32[]{:S(2)}, u32[]{:S(2)}) collective-permute-start(bf16[256,512]{1,0:T(8,128)(2,1)S(1)} %add_convert_fusion.1), channel_id=1, source_target_pairs={{0,4},{1,5},{2,6},{3,7},{4,0},{5,1},{6,2},{7,3},{8,12},{9,13},{10,... | collective-permute-start | bytes 786440 | tf_op jit(solution)/shard_map/ppermute | solution.py:24

commit v2 on v0

--- a/solution.py
+++ b/solution.py
@@ -1,12 +1,242 @@
+import functools
+
 import jax
 import jax.numpy as jnp
 from jax import lax
+from jax.experimental import pallas as pl
+from jax.experimental.pallas import tpu as pltpu
 from jax.sharding import PartitionSpec as P
 
 CAP = 32
-
-
-def shards(attended, out_weight, adapter_down, adapter_up, row_adapter, adapter_slot):
+IN_VMEM = pl.BlockSpec(memory_space=pltpu.VMEM)
+IN_HBM = pl.BlockSpec(memory_space=pltpu.HBM)
+DMA = pltpu.SemaphoreType.DMA
+
+
+def params(mib):
+    return pltpu.CompilerParams(vmem_limit_bytes=mib * 1024 * 1024)
+
+
+def cost(flops, moved):
+    return pl.CostEstimate(flops=flops, bytes_accessed=moved, transcendentals=0)
+
+
+def shape(dims, dtype=jnp.bfloat16):
+    return jax.ShapeDtypeStruct(dims, dtype)
+
+
+def dot(a, b):
+    return jnp.dot(a, b, preferred_element_type=jnp.float32)
+
+
+def swap(value, mask):
+    count = lax.axis_size("tensor")
+    return lax.ppermute(value, "tensor", [(t, t ^ mask) for t in range(count)])
+
+
+def route_kernel(chips, slot_hbm, row_ref, own_ref, other_ref, target_ref, *rest):
+    out_refs, slot_ref, slot_sem = rest[:chips], rest[chips], rest[chips + 1]
+    rows, width = own_ref.shape
+    me = lax.axis_index("tensor")
+    core = me % 2
+    fetch = pltpu.make_async_copy(slot_hbm, slot_ref, slot_sem)
+    fetch.start()
+    fetch.wait()
+    ids = row_ref[...]
+    owner = jnp.zeros_like(ids)
+    for a in range(slot_ref.shape[0]):
+        owner = jnp.where(ids == a, slot_ref[a], owner)
+    hot = (lax.broadcasted_iota(jnp.int32, (2 * chips, rows), 0) == owner).astype(jnp.float32)
+    earlier = (
+        lax.broadcasted_iota(jnp.int32, (rows, rows), 0)
+        < lax.broadcasted_iota(jnp.int32, (rows, rows), 1)
+    ).astype(jnp.bfloat16)
+    ahead = dot(hot.astype(jnp.bfloat16), earlier)
+    place = jnp.sum(ahead * hot, axis=0, keepdims=True).astype(jnp.int32)
+    target = owner * CAP + place
+    target_ref[...] = target
+    j = lax.broadcasted_iota(jnp.int32, (chips * CAP, rows), 0)
+    slots = (me ^ ((j // CAP) * 2)) * CAP + j % CAP
+    select = (slots == target).astype(jnp.bfloat16)
+    own = dot(select, own_ref[...]).astype(jnp.bfloat16)
+    other = dot(select, other_ref[...]).astype(jnp.bfloat16)
+    for m in range(chips):
+        out_refs[m][:, pl.ds(pl.multiple_of(core * width, width), width)] = own[m * CAP : (m + 1) * CAP]
+        out_refs[m][:, pl.ds(pl.multiple_of((1 - core) * width, width), width)] = other[
+            m * CAP : (m + 1) * CAP
+        ]
+
+
+def route(adapter_slot, row_adapter, own, other):
+    rows, width = own.shape
+    chips = lax.axis_size("tensor") // 2
+    found = pl.pallas_call(
+        functools.partial(route_kernel, chips),
+        out_shape=[shape((1, rows), jnp.int32)] + [shape((CAP, 2 * width))] * chips,
+        in_specs=[IN_HBM, IN_VMEM, IN_VMEM, IN_VMEM],
+        out_specs=[IN_VMEM] * (chips + 1),
+        scratch_shapes=[pltpu.SMEM(adapter_slot.shape, jnp.int32), DMA(())],
+        compiler_params=params(16),
+        cost_estimate=cost(4 * chips * CAP * rows * width, 8 * chips * CAP * width),
+        name="route",
+    )(adapter_slot, row_adapter[None, :], own, other)
+    return found[0], found[1:]
+
+
+def product_kernel(chip_masks, attended_hbm, weight_hbm, away_ref, stay_ref, attended_ref, weight_ref, sems):
+    width = stay_ref.shape[2]
+    me = lax.axis_index("tensor")
+    core, chip = me % 2, me // 2
+    fetches = [pltpu.make_async_copy(attended_hbm, attended_ref, sems.at[len(chip_masks)])]
+    for i, m in enumerate(chip_masks):
+        start = pl.multiple_of((chip ^ m) * 2 * width, 2 * width)
+        fetches.append(
+            pltpu.make_async_copy(weight_hbm.at[:, pl.ds(start, 2 * width)], weight_ref.at[i], sems.at[i])
+        )
+    for fetch in fetches:
+        fetch.start()
+    fetches[0].wait()
+    for i in range(len(chip_masks)):
+        fetches[i + 1].wait()
+        there = pl.ds(pl.multiple_of((1 - core) * width, width), width)
+        here = pl.ds(pl.multiple_of(core * width, width), width)
+        away_ref[i] = dot(attended_ref[...], weight_ref[i, :, there]).astype(jnp.bfloat16)
+        stay_ref[i] = dot(attended_ref[...], weight_ref[i, :, here])
+
+
+def product(attended, out_weight, chip_masks):
+    rows, depth = attended.shape
+    width = out_weight.shape[1] // lax.axis_size("tensor")
+    n = len(chip_masks)
+    return pl.pallas_call(
+        functools.partial(product_kernel, chip_masks),
+        out_shape=(shape((n, rows, width)), shape((n, rows, width), jnp.float32)),
+        in_specs=[IN_HBM, IN_HBM],
+        out_specs=(IN_VMEM, IN_VMEM),
+        scratch_shapes=[
+            pltpu.VMEM((rows, depth), jnp.bfloat16),
+            pltpu.VMEM((n, depth, 2 * width), jnp.bfloat16),
+            DMA((n + 1,)),
+        ],
+        compiler_params=params(24),
+        cost_estimate=cost(4 * n * rows * depth * width, n * (4 * depth * width + 6 * rows * width)),
+        name="product",
+    )(attended, out_weight)
+
+
+def shrink_kernel(down_ref, *refs):
+    arrived_refs, out_ref = refs[:-1], refs[-1]
+    chip = lax.axis_index("tensor") // 2
+    total = jnp.zeros(out_ref.shape, jnp.float32)
+    for m, arrived_ref in enumerate(arrived_refs):
+        width = arrived_ref.shape[1]
+        start = pl.multiple_of((chip ^ m) * width, width)
+        total += lax.dot_general(
+            arrived_ref[...],
+            down_ref[:, pl.ds(start, width)],
+            (((1,), (1,)), ((), ())),
+            preferred_element_type=jnp.float32,
+        )
+    out_ref[...] = total.astype(jnp.bfloat16)
+
+
+def shrink(down, arrived):
+    return pl.pallas_call(
+        shrink_kernel,
+        out_shape=shape((CAP, down.shape[0])),
+        in_specs=[IN_VMEM] * (1 + len(arrived)),
+        out_specs=IN_VMEM,
+        compiler_params=params(16),
+        cost_estimate=cost(2 * CAP * down.size, 2 * down.size),
+        name="shrink",
+    )(down, *arrived)
+
+
+def grow_kernel(shrunk_ref, shrunk_other_ref, up_ref, up_other_ref, *out_refs):
+    me = lax.axis_index("tensor")
+    for m, out_ref in enumerate(out_refs):
+        width = out_ref.shape[1]
+        block = pl.ds(pl.multiple_of((me ^ (2 * m)) * width, width), width)
+        out_ref[:CAP, :] = dot(shrunk_ref[...], up_ref[:, block]).astype(jnp.bfloat16)
+        out_ref[CAP:, :] = dot(shrunk_other_ref[...], up_other_ref[:, block]).astype(jnp.bfloat16)
+
+
+def grow(shrunk, shrunk_other, up, up_other):
+    count = lax.axis_size("tensor")
+    width = up.shape[1] // count
+    return pl.pallas_call(
+        grow_kernel,
+        out_shape=[shape((2 * CAP, width))] * (count // 2),
+        in_specs=[IN_VMEM] * 4,
+        out_specs=[IN_VMEM] * (count // 2),
+        compiler_params=params(16),
+        cost_estimate=cost(2 * CAP * up.size, 4 * up.size),
+        name="grow",
+    )(shrunk, shrunk_other, up, up_other)
+
+
+def finish_kernel(target_ref, base_ref, *refs):
+    grown_refs, out_ref = refs[:-1], refs[-1]
+    rows = base_ref.shape[0]
+    me = lax.axis_index("tensor")
+    j = lax.broadcasted_iota(jnp.int32, (2 * CAP, rows), 0)
+    delta = jnp.zeros(out_ref.shape, jnp.float32)
+    for m, grown_ref in enumerate(grown_refs):
+        slots = (me ^ (2 * m) ^ (j // CAP)) * CAP + j % CAP
+        pick = (slots == target_ref[...]).astype(jnp.bfloat16)
+        delta += lax.dot_general(
+            pick, grown_ref[...], (((0,), (0,)), ((), ())), preferred_element_type=jnp.float32
+        )
+    out_ref[...] = (base_ref[...] + delta).astype(jnp.bfloat16)
+
+
+def finish(target, base, grown):
+    return pl.pallas_call(
+        finish_kernel,
+        out_shape=shape(base.shape),
+        in_specs=[IN_VMEM] * (2 + len(grown)),
+        out_specs=IN_VMEM,
+        compiler_params=params(16),
+        cost_estimate=cost(4 * CAP * len(grown) * base.size, 8 * base.size),
+        name="finish",
+    )(target, base, *grown)
+
+
+def staged(attended, out_weight, adapter_down, adapter_up, row_adapter, adapter_slot):
+    f32 = jnp.float32
+    up, down = adapter_up[0], jnp.swapaxes(adapter_down, 1, 2)[0]
+    attended_other = swap(attended, 1)
+    away7, stay7 = product(attended, out_weight, (7,))
+    came7 = swap(away7, 1)
+    target, outgoing = route(adapter_slot, row_adapter, attended, attended_other)
+    arrived = {m: swap(outgoing[m], 2 * m) for m in (7, 6, 5, 4, 3, 2, 1)}
+    arrived[0] = outgoing[0]
+    up_other = swap(up, 1)
+    go3 = (stay7[0] + came7[0].astype(f32)).astype(jnp.bfloat16)
+    y3 = swap(go3, 2)
+    away_far, stay_far = product(attended, out_weight, (5, 3, 1))
+    came_far = swap(away_far, 1)
+    away_near, stay_near = product(attended, out_weight, (6, 4, 2, 0))
+    came_near = swap(away_near, 1)
+    ys = [y3]
+    for i in range(3):
+        go = (stay_far[i] + came_far[i].astype(f32)).astype(jnp.bfloat16)
+        ys.append(swap(go, 2))
+    sides = [stay_near[i] + came_near[i].astype(f32) + ys[i].astype(f32) for i in range(4)]
+    from3 = swap(sides[0].astype(jnp.bfloat16), 4)
+    from2 = swap((sides[1] + from3.astype(f32)).astype(jnp.bfloat16), 8)
+    from1 = swap(sides[2].astype(jnp.bfloat16), 4)
+    shrunk = shrink(down, [arrived[m] for m in range(8)])
+    shrunk_other = swap(shrunk, 1)
+    grown = grow(shrunk, shrunk_other, up, up_other)
+    back = [grown[0]] + [None] * 7
+    for m in (7, 6, 5, 4, 3, 2, 1):
+        back[m] = swap(grown[m], 2 * m)
+    base = sides[3] + from1.astype(f32) + from2.astype(f32)
+    return finish(target, base, back)
+
+
+def general(attended, out_weight, adapter_down, adapter_up, row_adapter, adapter_slot):
     tensor_size = lax.axis_size("tensor")
     device = lax.axis_index("tensor")
     row_count = attended.shape[0]
@@ -47,6 +277,12 @@
     return (base_out + delta_out.astype(jnp.float32)).astype(jnp.bfloat16)
 
 
+def shards(*arrays):
+    if lax.axis_size("tensor") == 16 and arrays[2].shape[0] == 1:
+        return staged(*arrays)
+    return general(*arrays)
+
+
 def solution(mesh):
     placed = (
         P("groups", "tensor"),

time: 151 us -> 87.9 us (0.58)
  waiting for transfers between devices: 68.8 us -> 32.4 us
  other arithmetic: 31.9 us -> 0.86 us
  starting transfers between devices: 17.2 us -> 41.6 us
  between operations: 13.5 us -> 0.14 us
  matrix products: 10 us -> 0 us
  Pallas kernels: 0 us -> 8.39 us
  local copies, waits for them, and re-layouts: 8.71 us -> 4.35 us
    ppermute x0 -> x27, starting transfers between devices: none -> 41.6 us  [swap(): return lax.ppermute(value, 'tensor', [(t, t ^ mask) for t in range(count)])]
    all_to_all x2 -> x0, waiting for transfers between devices: 36.7 us -> none  [the longest x1 22.2 us: shards(): lax.all_to_all(outgoing, 'tensor', split_axis=0, concat_axis=1, tiled=True)]
    ppermute x0 -> x27, waiting for transfers between devices: none -> 32.4 us  [swap(): return lax.ppermute(value, 'tensor', [(t, t ^ mask) for t in range(count)])]
    reduce_scatter x1 -> x0, waiting for transfers between devices: 32.1 us -> none  [shards(): lax.psum_scatter(partial_value, 'tensor', scatter_dimension=1, tiled=True)]
    all_to_all x2 -> x0, starting transfers between devices: 17.2 us -> none  [the longest x1 9.77 us: shards(): lax.all_to_all(expanded, 'tensor', split_axis=1, concat_axis=0, tiled=True)]
    dot_general x2 -> x0, matrix products: 10 us -> none  [the longest x1 9.13 us: shards(): jnp.dot(attended, out_weight, preferred_element_type=jnp.float32)]
    gather x4 -> x0, other arithmetic: 9.79 us -> none  [the longest x1 9.77 us: shards(): storage = adapter_slot[row_adapter]]
    eq x1 -> x0, other arithmetic: 9.73 us -> none  [shards(): owner_of[:, None] == jnp.arange(tensor_size, dtype=jnp.int32)[None, :]]
  transfers between devices with their start and end apart: 3 -> 27, of which waited for: 3 -> 11; matrix products, arithmetic and copies ran while one was open for 26% -> 1% of each run, Pallas kernels for 0% -> 6%
where the time goes in v2:
time: 87.9 us; the launch traced here: 87.8 us
  starting transfers between devices  41.6 us (47%)
  waiting for transfers between devices  32.4 us (37%)
  Pallas kernels  8.39 us (10%)
  local copies, waits for them, and re-layouts  4.35 us (5%)
    ppermute x27, starting transfers between devices, swap(): return lax.ppermute(value, 'tensor', [(t, t ^ mask) for t in range(count)])  41.6 us
    ppermute x27, waiting for transfers between devices, swap(): return lax.ppermute(value, 'tensor', [(t, t ^ mask) for t in range(count)])  32.4 us
    pallas_call x3, Pallas kernels, product(): pl.pallas_call(functools.partial(product_kernel, chip_masks), out_shape=(...  5.25 us
    unnamed x12, local copies, waits for them, and re-layouts  4.35 us
  transfers between devices with their start and end apart: 27, of which 11 were waited for; matrix products, arithmetic and copies ran while one was open for 1% of the time, Pallas kernels for 6%

profile of v2, /device:TPU:0, one launch (start us, length us, event | category | flops | bytes accessed | tf_op | source)
XLA Modules:
  0.0 87.8 jit_solution(7061316856947448420)
XLA Ops:
  0.0 3.4 %copy-done = bf16[512,8192]{1,0:T(8,128)(2,1)S(1)} copy-done((bf16[512,8192]{1,0:T(8,128)(2,1)S(1)}, bf16[512,8192]{1,0:T(8,128)(2,1)}, u32[]{:S(2)}) %copy-start) | copy-done | bytes 8388632
  3.4 0.9 %copy-done.1 = bf16[256,512]{1,0:T(8,128)(2,1)S(1)} copy-done((bf16[256,512]{1,0:T(8,128)(2,1)S(1)}, bf16[256,512]{1,0:T(8,128)(2,1)}, u32[]{:S(2)}) %copy-start.1) | copy-done | bytes 262168
  4.3 2.0 %product.4 = (bf16[3,256,512]{2,1,0:T(8,128)(2,1)S(1)}, f32[3,256,512]{2,1,0:T(8,128)S(1)}) custom-call(bf16[256,512]{1,0:T(8,128)(2,1)S(1)} %copy-done.1, bf16[512,8192]{1,0:T(8,128)(2,1)S(1)} %copy-done), custom_call_target="tpu_custom_call" | custom-call | flops 805306368 | bytes 5505024 | tf_op jit(solution)/shard_map/product/pallas_call | solution.py:111
  6.3 0.5 collective-permute-start.2
  6.8 2.6 %product.3 = (bf16[4,256,512]{2,1,0:T(8,128)(2,1)S(1)}, f32[4,256,512]{2,1,0:T(8,128)S(1)}) custom-call(bf16[256,512]{1,0:T(8,128)(2,1)S(1)} %copy-done.1, bf16[512,8192]{1,0:T(8,128)(2,1)S(1)} %copy-done), custom_call_target="tpu_custom_call" | custom-call | flops 1073741824 | bytes 7340032 | tf_op jit(solution)/shard_map/product/pallas_call | solution.py:111
  9.4 0.1 collective-permute-start.1
  9.6 0.7 product.5
  10.2 0.5 collective-permute-start.7
  10.8 1.8 %collective-permute-done.7 = bf16[1,256,512]{2,1,0:T(8,128)(2,1)S(1)} collective-permute-done((bf16[1,256,512]{2,1,0:T(8,128)(2,1)S(1)}, bf16[1,256,512]{2,1,0:T(8,128)(2,1)S(1)}, u32[]{:S(2)}, u32[]{:S(2)}) %collective-permute-start.7) | collective-permute-done | bytes 262176 | tf_op jit(solution)/shard_map/ppermute | solution.py:34
  12.5 0.1 fusion.9
  12.6 2.7 %collective-permute-start.8 = (bf16[256,512]{1,0:T(8,128)(2,1)S(1)}, bf16[256,512]{1,0:T(8,128)(2,1)S(1)}, u32[]{:S(2)}, u32[]{:S(2)}) collective-permute-start(bf16[256,512]{1,0:T(8,128)(2,1)S(1)} %fusion.9), channel_id=1, source_target_pairs={{0,2},{1,3},{2,0},{3,1},{4,6},{5,7},{6,4},{7,5},{8,10},{9,11},{10,... | collective-permute-start | bytes 786440 | tf_op jit(solution)/shard_map/ppermute | solution.py:34
  15.3 0.0 collective-permute-done.2
  15.3 0.3 fusion.6
  15.6 0.0 copy-start.4
  15.6 0.0 copy-start.5
  15.6 0.1 collective-permute-start.4
  15.7 0.1 collective-permute-start.19
  15.9 0.4 collective-permute-start
  16.3 6.2 %collective-permute-done.8 = bf16[256,512]{1,0:T(8,128)(2,1)S(1)} collective-permute-done((bf16[256,512]{1,0:T(8,128)(2,1)S(1)}, bf16[256,512]{1,0:T(8,128)(2,1)S(1)}, u32[]{:S(2)}, u32[]{:S(2)}) %collective-permute-start.8) | collective-permute-done | bytes 262176 | tf_op jit(solution)/shard_map/ppermute | solution.py:34
  22.5 2.0 %collective-permute-start.6 = (bf16[256,512]{1,0:T(8,128)(2,1)S(1)}, bf16[256,512]{1,0:T(8,128)(2,1)S(1)}, u32[]{:S(2)}, u32[]{:S(2)}) collective-permute-start(bf16[256,512]{1,0:T(8,128)(2,1)S(1)} %get-tuple-element.54), channel_id=1, source_target_pairs={{0,2},{1,3},{2,0},{3,1},{4,6},{5,7},{6,4},{7,5},{8,10},{9,11},{10,... | collective-permute-start | bytes 786440 | tf_op jit(solution)/shard_map/ppermute | solution.py:34
  24.5 3.6 %collective-permute-done.4 = bf16[256,512]{1,0:T(8,128)(2,1)S(1)} collective-permute-done((bf16[256,512]{1,0:T(8,128)(2,1)S(1)}, bf16[256,512]{1,0:T(8,128)(2,1)S(1)}, u32[]{:S(2)}, u32[]{:S(2)}) %collective-permute-start.4) | collective-permute-done | bytes 262176 | tf_op jit(solution)/shard_map/ppermute | solution.py:34
  28.1 0.0 collective-permute-done.1
  28.1 0.2 fusion.3
  28.3 2.1 %collective-permute-start.9 = (bf16[256,512]{1,0:T(8,128)(2,1)S(1)}, bf16[256,512]{1,0:T(8,128)(2,1)S(1)}, u32[]{:S(2)}, u32[]{:S(2)}) collective-permute-start(bf16[256,512]{1,0:T(8,128)(2,1)S(1)} %get-tuple-element.52), channel_id=1, source_target_pairs={{0,4},{1,5},{2,6},{3,7},{4,0},{5,1},{6,2},{7,3},{8,12},{9,13},{10,... | collective-permute-start | bytes 786440 | tf_op jit(solution)/shard_map/ppermute | solution.py:34
  30.4 0.0 collective-permute-done.other_ref
  30.5 1.0 %route.1 = (s32[1,256]{1,0:T(1,128)S(1)}, bf16[32,1024]{1,0:T(8,128)(2,1)S(1)}, bf16[32,1024]{1,0:T(8,128)(2,1)S(1)}, bf16[32,1024]{1,0:T(8,128)(2,1)S(1)}, bf16...) custom-call(s32[16]{0:T(128)S(1)} %copy-done.5, ...), custom_call_target="tpu_custom_call" | custom-call | flops 134217728 | bytes 1048576 | tf_op jit(solution)/shard_map/route/pallas_call | solution.py:73
  31.5 1.6 %collective-permute-start.11 = (bf16[32,1024]{1,0:T(8,128)(2,1)S(1)}, bf16[32,1024]{1,0:T(8,128)(2,1)S(1)}, u32[]{:S(2)}, u32[]{:S(2)}) collective-permute-start(bf16[32,1024]{1,0:T(8,128)(2,1)S(1)} %get-tuple-element.36), channel_id=1, source_target_pairs={{0,2},{1,3},{2,0},{3,1},{4,6},{5,7},{6,4},{7,5},{8,10},{9,11},{10,... | collective-permute-start | bytes 196616 | tf_op jit(solution)/shard_map/ppermute | solution.py:34
  33.1 0.5 collective-permute-start.12
  33.5 2.3 %collective-permute-done.11.refs_1_ = bf16[32,1024]{1,0:T(8,128)(2,1)S(1)} collective-permute-done((bf16[32,1024]{1,0:T(8,128)(2,1)S(1)}, bf16[32,1024]{1,0:T(8,128)(2,1)S(1)}, u32[]{:S(2)}, u32[]{:S(2)}) %collective-permute-start.11) | collective-permute-done | bytes 65568 | tf_op jit(solution)/shard_map/ppermute | solution.py:34
  35.8 1.8 %collective-permute-start.13 = (bf16[32,1024]{1,0:T(8,128)(2,1)S(1)}, bf16[32,1024]{1,0:T(8,128)(2,1)S(1)}, u32[]{:S(2)}, u32[]{:S(2)}) collective-permute-start(bf16[32,1024]{1,0:T(8,128)(2,1)S(1)} %get-tuple-element.38), channel_id=1, source_target_pairs={{0,6},{1,7},{2,4},{3,5},{4,2},{5,3},{6,0},{7,1},{8,14},{9,15},{10,... | collective-permute-start | bytes 196616 | tf_op jit(solution)/shard_map/ppermute | solution.py:34
  37.6 0.0 collective-permute-done.12.refs_2_
  37.6 2.6 %collective-permute-start.14 = (bf16[32,1024]{1,0:T(8,128)(2,1)S(1)}, bf16[32,1024]{1,0:T(8,128)(2,1)S(1)}, u32[]{:S(2)}, u32[]{:S(2)}) collective-permute-start(bf16[32,1024]{1,0:T(8,128)(2,1)S(1)} %get-tuple-element.39), channel_id=1, source_target_pairs={{0,8},{1,9},{2,10},{3,11},{4,12},{5,13},{6,14},{7,15},{8,0},{9,1},... | collective-permute-start | bytes 196616 | tf_op jit(solution)/shard_map/ppermute | solution.py:34
  40.2 1.5 %collective-permute-done.13.refs_3_ = bf16[32,1024]{1,0:T(8,128)(2,1)S(1)} collective-permute-done((bf16[32,1024]{1,0:T(8,128)(2,1)S(1)}, bf16[32,1024]{1,0:T(8,128)(2,1)S(1)}, u32[]{:S(2)}, u32[]{:S(2)}) %collective-permute-start.13) | collective-permute-done | bytes 65568 | tf_op jit(solution)/shard_map/ppermute | solution.py:34
  41.7 2.8 %collective-permute-start.15 = (bf16[32,1024]{1,0:T(8,128)(2,1)S(1)}, bf16[32,1024]{1,0:T(8,128)(2,1)S(1)}, u32[]{:S(2)}, u32[]{:S(2)}) collective-permute-start(bf16[32,1024]{1,0:T(8,128)(2,1)S(1)} %get-tuple-element.40), channel_id=1, source_target_pairs={{0,10},{1,11},{2,8},{3,9},{4,14},{5,15},{6,12},{7,13},{8,2},{9,3},... | collective-permute-start | bytes 196616 | tf_op jit(solution)/shard_map/ppermute | solution.py:34
  44.5 0.0 collective-permute-done.6
  44.5 0.5 collective-permute-start.3
  45.0 0.0 collective-permute-done.9
  45.0 1.1 %collective-permute-start.5 = (bf16[256,512]{1,0:T(8,128)(2,1)S(1)}, bf16[256,512]{1,0:T(8,128)(2,1)S(1)}, u32[]{:S(2)}, u32[]{:S(2)}) collective-permute-start(bf16[256,512]{1,0:T(8,128)(2,1)S(1)} %get-tuple-element.51), channel_id=1, source_target_pairs={{0,4},{1,5},{2,6},{3,7},{4,0},{5,1},{6,2},{7,3},{8,12},{9,13},{10,... | collective-permute-start | bytes 786440 | tf_op jit(solution)/shard_map/ppermute | solution.py:34
  46.1 0.1 fusion.2
  46.2 0.0 collective-permute-done.14.refs_4_
  46.2 0.1 collective-permute-start.10
  46.4 2.1 %collective-permute-done.15.refs_5_ = bf16[32,1024]{1,0:T(8,128)(2,1)S(1)} collective-permute-done((bf16[32,1024]{1,0:T(8,128)(2,1)S(1)}, bf16[32,1024]{1,0:T(8,128)(2,1)S(1)}, u32[]{:S(2)}, u32[]{:S(2)}) %collective-permute-start.15) | collective-permute-done | bytes 65568 | tf_op jit(solution)/shard_map/ppermute | solution.py:34
  48.5 3.3 %collective-permute-start.16 = (bf16[32,1024]{1,0:T(8,128)(2,1)S(1)}, bf16[32,1024]{1,0:T(8,128)(2,1)S(1)}, u32[]{:S(2)}, u32[]{:S(2)}) collective-permute-start(bf16[32,1024]{1,0:T(8,128)(2,1)S(1)} %get-tuple-element.41), channel_id=1, source_target_pairs={{0,12},{1,13},{2,14},{3,15},{4,8},{5,9},{6,10},{7,11},{8,4},{9,5},... | collective-permute-start | bytes 196616 | tf_op jit(solution)/shard_map/ppermute | solution.py:34
  51.8 6.6 %collective-permute-done.16.refs_6_ = bf16[32,1024]{1,0:T(8,128)(2,1)S(1)} collective-permute-done((bf16[32,1024]{1,0:T(8,128)(2,1)S(1)}, bf16[32,1024]{1,0:T(8,128)(2,1)S(1)}, u32[]{:S(2)}, u32[]{:S(2)}) %collective-permute-start.16) | collective-permute-done | bytes 65568 | tf_op jit(solution)/shard_map/ppermute | solution.py:34
  58.4 4.1 %collective-permute-start.17 = (bf16[32,1024]{1,0:T(8,128)(2,1)S(1)}, bf16[32,1024]{1,0:T(8,128)(2,1)S(1)}, u32[]{:S(2)}, u32[]{:S(2)}) collective-permute-start(bf16[32,1024]{1,0:T(8,128)(2,1)S(1)} %get-tuple-element.42), channel_id=1, source_target_pairs={{0,14},{1,15},{2,12},{3,13},{4,10},{5,11},{6,8},{7,9},{8,6},{9,7},... | collective-permute-start | bytes 196616 | tf_op jit(solution)/shard_map/ppermute | solution.py:34
  62.5 2.9 %collective-permute-done.17.refs_7_ = bf16[32,1024]{1,0:T(8,128)(2,1)S(1)} collective-permute-done((bf16[32,1024]{1,0:T(8,128)(2,1)S(1)}, bf16[32,1024]{1,0:T(8,128)(2,1)S(1)}, u32[]{:S(2)}, u32[]{:S(2)}) %collective-permute-start.17) | collective-permute-done | bytes 65568 | tf_op jit(solution)/shard_map/ppermute | solution.py:34
  65.3 0.4 shrink.1.shrunk_ref
  65.8 0.0 collective-permute-start.18
  65.8 1.2 %collective-permute-done.18.shrunk_other_ref = bf16[32,64]{1,0:T(8,128)(2,1)S(1)} collective-permute-done((bf16[32,64]{1,0:T(8,128)(2,1)S(1)}, bf16[32,64]{1,0:T(8,128)(2,1)S(1)}, u32[]{:S(2)}, u32[]{:S(2)}) %collective-permute-start.18) | collective-permute-done | bytes 4128 | tf_op jit(solution)/shard_map/ppermute | solution.py:34
  66.9 0.0 collective-permute-done.19.up_other_ref
  66.9 0.3 grow.1
  67.2 1.3 %collective-permute-start.20 = (bf16[64,512]{1,0:T(8,128)(2,1)S(1)}, bf16[64,512]{1,0:T(8,128)(2,1)S(1)}, u32[]{:S(2)}, u32[]{:S(2)}) collective-permute-start(bf16[64,512]{1,0:T(8,128)(2,1)S(1)} %get-tuple-element.44), channel_id=1, source_target_pairs={{0,2},{1,3},{2,0},{3,1},{4,6},{5,7},{6,4},{7,5},{8,10},{9,11},{10,... | collective-permute-start | bytes 196616 | tf_op jit(solution)/shard_map/ppermute | solution.py:34
  68.5 2.8 %collective-permute-start.21 = (bf16[64,512]{1,0:T(8,128)(2,1)S(1)}, bf16[64,512]{1,0:T(8,128)(2,1)S(1)}, u32[]{:S(2)}, u32[]{:S(2)}) collective-permute-start(bf16[64,512]{1,0:T(8,128)(2,1)S(1)} %get-tuple-element.45), channel_id=1, source_target_pairs={{0,4},{1,5},{2,6},{3,7},{4,0},{5,1},{6,2},{7,3},{8,12},{9,13},{10,... | collective-permute-start | bytes 196616 | tf_op jit(solution)/shard_map/ppermute | solution.py:34
  71.3 1.0 %collective-permute-start.22 = (bf16[64,512]{1,0:T(8,128)(2,1)S(1)}, bf16[64,512]{1,0:T(8,128)(2,1)S(1)}, u32[]{:S(2)}, u32[]{:S(2)}) collective-permute-start(bf16[64,512]{1,0:T(8,128)(2,1)S(1)} %get-tuple-element.46), channel_id=1, source_target_pairs={{0,6},{1,7},{2,4},{3,5},{4,2},{5,3},{6,0},{7,1},{8,14},{9,15},{10,... | collective-permute-start | bytes 196616 | tf_op jit(solution)/shard_map/ppermute | solution.py:34
  72.3 2.7 %collective-permute-start.23 = (bf16[64,512]{1,0:T(8,128)(2,1)S(1)}, bf16[64,512]{1,0:T(8,128)(2,1)S(1)}, u32[]{:S(2)}, u32[]{:S(2)}) collective-permute-start(bf16[64,512]{1,0:T(8,128)(2,1)S(1)} %get-tuple-element.47), channel_id=1, source_target_pairs={{0,8},{1,9},{2,10},{3,11},{4,12},{5,13},{6,14},{7,15},{8,0},{9,1},... | collective-permute-start | bytes 196616 | tf_op jit(solution)/shard_map/ppermute | solution.py:34
  75.0 1.7 %collective-permute-start.24 = (bf16[64,512]{1,0:T(8,128)(2,1)S(1)}, bf16[64,512]{1,0:T(8,128)(2,1)S(1)}, u32[]{:S(2)}, u32[]{:S(2)}) collective-permute-start(bf16[64,512]{1,0:T(8,128)(2,1)S(1)} %get-tuple-element.48), channel_id=1, source_target_pairs={{0,10},{1,11},{2,8},{3,9},{4,14},{5,15},{6,12},{7,13},{8,2},{9,3},... | collective-permute-start | bytes 196616 | tf_op jit(solution)/shard_map/ppermute | solution.py:34
  76.8 0.0 collective-permute-done.5
  76.8 2.5 %collective-permute-start.25 = (bf16[64,512]{1,0:T(8,128)(2,1)S(1)}, bf16[64,512]{1,0:T(8,128)(2,1)S(1)}, u32[]{:S(2)}, u32[]{:S(2)}) collective-permute-start(bf16[64,512]{1,0:T(8,128)(2,1)S(1)} %get-tuple-element.49), channel_id=1, source_target_pairs={{0,12},{1,13},{2,14},{3,15},{4,8},{5,9},{6,10},{7,11},{8,4},{9,5},... | collective-permute-start | bytes 196616 | tf_op jit(solution)/shard_map/ppermute | solution.py:34
  79.3 2.7 %collective-permute-start.26 = (bf16[64,512]{1,0:T(8,128)(2,1)S(1)}, bf16[64,512]{1,0:T(8,128)(2,1)S(1)}, u32[]{:S(2)}, u32[]{:S(2)}) collective-permute-start(bf16[64,512]{1,0:T(8,128)(2,1)S(1)} %get-tuple-element.50), channel_id=1, source_target_pairs={{0,14},{1,15},{2,12},{3,13},{4,10},{5,11},{6,8},{7,9},{8,6},{9,7},... | collective-permute-start | bytes 196616 | tf_op jit(solution)/shard_map/ppermute | solution.py:34
  81.9 0.2 fusion.5.base_ref
  82.1 0.0 collective-permute-done.22.refs_3_
  82.1 2.6 %collective-permute-done.24.refs_5_ = bf16[64,512]{1,0:T(8,128)(2,1)S(1)} collective-permute-done((bf16[64,512]{1,0:T(8,128)(2,1)S(1)}, bf16[64,512]{1,0:T(8,128)(2,1)S(1)}, u32[]{:S(2)}, u32[]{:S(2)}) %collective-permute-start.24) | collective-permute-done | bytes 65568 | tf_op jit(solution)/shard_map/ppermute | solution.py:34
  84.7 1.6 %collective-permute-done.26.refs_7_ = bf16[64,512]{1,0:T(8,128)(2,1)S(1)} collective-permute-done((bf16[64,512]{1,0:T(8,128)(2,1)S(1)}, bf16[64,512]{1,0:T(8,128)(2,1)S(1)}, u32[]{:S(2)}, u32[]{:S(2)}) %collective-permute-start.26) | collective-permute-done | bytes 65568 | tf_op jit(solution)/shard_map/ppermute | solution.py:34
  86.3 1.4 %finish.1 = bf16[256,512]{1,0:T(8,128)(2,1)} custom-call(s32[1,256]{1,0:T(1,128)S(1)} %get-tuple-element.28.target_ref, f32[256,512]{1,0:T(8,128)S(1)} %fusion.5.base_ref, bf16[64,512]{1,0:T(8,128)(2,1)S(1)} %get-tuple-element.43.refs_0_, bf16[64,512]{1,0:T(8,128)(2,1)S(1)} %collective-permute-done.20.refs_1_, ...), custom_call_target="tpu_custom_call" | custom-call | flops 134217728 | bytes 1048576 | tf_op jit(solution)/shard_map/finish/pallas_call | solution.py:194
  (14 shorter events, 0.0 us)
Async XLA Ops:
  0.0 3.4 %copy-start = (bf16[512,8192]{1,0:T(8,128)(2,1)S(1)}, bf16[512,8192]{1,0:T(8,128)(2,1)}, u32[]{:S(2)}) copy-start(bf16[512,8192]{1,0:T(8,128)(2,1)} %weight_hbm.5) | copy-start | bytes 25165828
  3.4 0.9 %copy-start.1 = (bf16[256,512]{1,0:T(8,128)(2,1)S(1)}, bf16[256,512]{1,0:T(8,128)(2,1)}, u32[]{:S(2)}) copy-start(bf16[256,512]{1,0:T(8,128)(2,1)} %attended_hbm.5) | copy-start | bytes 786436
  6.3 9.0 %collective-permute-start.2 = (bf16[3,256,512]{2,1,0:T(8,128)(2,1)S(1)}, bf16[3,256,512]{2,1,0:T(8,128)(2,1)S(1)}, u32[]{:S(2)}, u32[]{:S(2)}) collective-permute-start(bf16[3,256,512]{2,1,0:T(8,128)(2,1)S(1)} %get-tuple-element.32), channel_id=1, source_target_pairs={{0,1},{1,0},{2,3},{3,2},{4,5},{5,4},{6,7},{7,6},{8,9},{9,8},{10,11... | collective-permute-start | bytes 2359304 | tf_op jit(solution)/shard_map/ppermute | solution.py:34
  9.4 18.7 %collective-permute-start.1 = (bf16[4,256,512]{2,1,0:T(8,128)(2,1)S(1)}, bf16[4,256,512]{2,1,0:T(8,128)(2,1)S(1)}, u32[]{:S(2)}, u32[]{:S(2)}) collective-permute-start(bf16[4,256,512]{2,1,0:T(8,128)(2,1)S(1)} %get-tuple-element.30), channel_id=1, source_target_pairs={{0,1},{1,0},{2,3},{3,2},{4,5},{5,4},{6,7},{7,6},{8,9},{9,8},{10,11... | collective-permute-start | bytes 3145736 | tf_op jit(solution)/shard_map/ppermute | solution.py:34
  10.2 2.3 %collective-permute-start.7 = (bf16[1,256,512]{2,1,0:T(8,128)(2,1)S(1)}, bf16[1,256,512]{2,1,0:T(8,128)(2,1)S(1)}, u32[]{:S(2)}, u32[]{:S(2)}) collective-permute-start(bf16[1,256,512]{2,1,0:T(8,128)(2,1)S(1)} %get-tuple-element.34), channel_id=1, source_target_pairs={{0,1},{1,0},{2,3},{3,2},{4,5},{5,4},{6,7},{7,6},{8,9},{9,8},{10,11... | collective-permute-start | bytes 786440 | tf_op jit(solution)/shard_map/ppermute | solution.py:34
  12.5 3.2 %copy-start.3 = (bf16[1,64,8192]{2,1,0:T(8,128)(2,1)S(1)}, bf16[1,64,8192]{2,1,0:T(8,128)(2,1)}, u32[]{:S(2)}) copy-start(bf16[1,64,8192]{2,1,0:T(8,128)(2,1)} %param.9) | copy-start | bytes 3145732
  12.6 9.9 %collective-permute-start.8 = (bf16[256,512]{1,0:T(8,128)(2,1)S(1)}, bf16[256,512]{1,0:T(8,128)(2,1)S(1)}, u32[]{:S(2)}, u32[]{:S(2)}) collective-permute-start(bf16[256,512]{1,0:T(8,128)(2,1)S(1)} %fusion.9), channel_id=1, source_target_pairs={{0,2},{1,3},{2,0},{3,1},{4,6},{5,7},{6,4},{7,5},{8,10},{9,11},{10,... | collective-permute-start | bytes 786440 | tf_op jit(solution)/shard_map/ppermute | solution.py:34
  15.6 14.8 %copy-start.4 = (s32[256]{0:T(256)S(1)}, s32[256]{0:T(256)}, u32[]{:S(2)}) copy-start(s32[256]{0:T(256)} %param.10) | copy-start | bytes 3076
  15.6 14.8 %copy-start.5 = (s32[16]{0:T(128)S(1)}, s32[16]{0:T(128)}, u32[]{:S(2)}) copy-start(s32[16]{0:T(128)} %slot_hbm.1) | copy-start | bytes 196
  15.6 12.5 %collective-permute-start.4 = (bf16[256,512]{1,0:T(8,128)(2,1)S(1)}, bf16[256,512]{1,0:T(8,128)(2,1)S(1)}, u32[]{:S(2)}, u32[]{:S(2)}) collective-permute-start(bf16[256,512]{1,0:T(8,128)(2,1)S(1)} %get-tuple-element.55), channel_id=1, source_target_pairs={{0,2},{1,3},{2,0},{3,1},{4,6},{5,7},{6,4},{7,5},{8,10},{9,11},{10,... | collective-permute-start | bytes 786440 | tf_op jit(solution)/shard_map/ppermute | solution.py:34
  15.7 51.2 %collective-permute-start.19 = (bf16[64,8192]{1,0:T(8,128)(2,1)S(1)}, bf16[64,8192]{1,0:T(8,128)(2,1)S(1)}, u32[]{:S(2)}, u32[]{:S(2)}) collective-permute-start(bf16[64,8192]{1,0:T(8,128)(2,1)S(1)} %bitcast.34), channel_id=1, source_target_pairs={{0,1},{1,0},{2,3},{3,2},{4,5},{5,4},{6,7},{7,6},{8,9},{9,8},{10,11... | collective-permute-start | bytes 3145736 | tf_op jit(solution)/shard_map/ppermute | solution.py:34
  15.9 14.6 %collective-permute-start = (bf16[256,512]{1,0:T(8,128)(2,1)S(1)}, bf16[256,512]{1,0:T(8,128)(2,1)S(1)}, u32[]{:S(2)}, u32[]{:S(2)}) collective-permute-start(bf16[256,512]{1,0:T(8,128)(2,1)S(1)} %copy-done.1), channel_id=1, source_target_pairs={{0,1},{1,0},{2,3},{3,2},{4,5},{5,4},{6,7},{7,6},{8,9},{9,8},{10,11... | collective-permute-start | bytes 786440 | tf_op jit(solution)/shard_map/ppermute | solution.py:34
  22.5 22.0 %collective-permute-start.6 = (bf16[256,512]{1,0:T(8,128)(2,1)S(1)}, bf16[256,512]{1,0:T(8,128)(2,1)S(1)}, u32[]{:S(2)}, u32[]{:S(2)}) collective-permute-start(bf16[256,512]{1,0:T(8,128)(2,1)S(1)} %get-tuple-element.54), channel_id=1, source_target_pairs={{0,2},{1,3},{2,0},{3,1},{4,6},{5,7},{6,4},{7,5},{8,10},{9,11},{10,... | collective-permute-start | bytes 786440 | tf_op jit(solution)/shard_map/ppermute | solution.py:34
  28.1 37.2 %copy-start.2 = (bf16[1,8192,64]{1,2,0:T(8,128)(2,1)S(1)}, bf16[1,8192,64]{1,2,0:T(8,128)(2,1)}, u32[]{:S(2)}) copy-start(bf16[1,8192,64]{1,2,0:T(8,128)(2,1)} %param.8) | copy-start | bytes 3145732
  28.3 16.7 %collective-permute-start.9 = (bf16[256,512]{1,0:T(8,128)(2,1)S(1)}, bf16[256,512]{1,0:T(8,128)(2,1)S(1)}, u32[]{:S(2)}, u32[]{:S(2)}) collective-permute-start(bf16[256,512]{1,0:T(8,128)(2,1)S(1)} %get-tuple-element.52), channel_id=1, source_target_pairs={{0,4},{1,5},{2,6},{3,7},{4,0},{5,1},{6,2},{7,3},{8,12},{9,13},{10,... | collective-permute-start | bytes 786440 | tf_op jit(solution)/shard_map/ppermute | solution.py:34
  31.5 4.3 %collective-permute-start.11 = (bf16[32,1024]{1,0:T(8,128)(2,1)S(1)}, bf16[32,1024]{1,0:T(8,128)(2,1)S(1)}, u32[]{:S(2)}, u32[]{:S(2)}) collective-permute-start(bf16[32,1024]{1,0:T(8,128)(2,1)S(1)} %get-tuple-element.36), channel_id=1, source_target_pairs={{0,2},{1,3},{2,0},{3,1},{4,6},{5,7},{6,4},{7,5},{8,10},{9,11},{10,... | collective-permute-start | bytes 196616 | tf_op jit(solution)/shard_map/ppermute | solution.py:34
  33.1 4.5 %collective-permute-start.12 = (bf16[32,1024]{1,0:T(8,128)(2,1)S(1)}, bf16[32,1024]{1,0:T(8,128)(2,1)S(1)}, u32[]{:S(2)}, u32[]{:S(2)}) collective-permute-start(bf16[32,1024]{1,0:T(8,128)(2,1)S(1)} %get-tuple-element.37), channel_id=1, source_target_pairs={{0,4},{1,5},{2,6},{3,7},{4,0},{5,1},{6,2},{7,3},{8,12},{9,13},{10,... | collective-permute-start | bytes 196616 | tf_op jit(solution)/shard_map/ppermute | solution.py:34
  35.8 5.9 %collective-permute-start.13 = (bf16[32,1024]{1,0:T(8,128)(2,1)S(1)}, bf16[32,1024]{1,0:T(8,128)(2,1)S(1)}, u32[]{:S(2)}, u32[]{:S(2)}) collective-permute-start(bf16[32,1024]{1,0:T(8,128)(2,1)S(1)} %get-tuple-element.38), channel_id=1, source_target_pairs={{0,6},{1,7},{2,4},{3,5},{4,2},{5,3},{6,0},{7,1},{8,14},{9,15},{10,... | collective-permute-start | bytes 196616 | tf_op jit(solution)/shard_map/ppermute | solution.py:34
  37.6 8.7 %collective-permute-start.14 = (bf16[32,1024]{1,0:T(8,128)(2,1)S(1)}, bf16[32,1024]{1,0:T(8,128)(2,1)S(1)}, u32[]{:S(2)}, u32[]{:S(2)}) collective-permute-start(bf16[32,1024]{1,0:T(8,128)(2,1)S(1)} %get-tuple-element.39), channel_id=1, source_target_pairs={{0,8},{1,9},{2,10},{3,11},{4,12},{5,13},{6,14},{7,15},{8,0},{9,1},... | collective-permute-start | bytes 196616 | tf_op jit(solution)/shard_map/ppermute | solution.py:34
  41.7 6.8 %collective-permute-start.15 = (bf16[32,1024]{1,0:T(8,128)(2,1)S(1)}, bf16[32,1024]{1,0:T(8,128)(2,1)S(1)}, u32[]{:S(2)}, u32[]{:S(2)}) collective-permute-start(bf16[32,1024]{1,0:T(8,128)(2,1)S(1)} %get-tuple-element.40), channel_id=1, source_target_pairs={{0,10},{1,11},{2,8},{3,9},{4,14},{5,15},{6,12},{7,13},{8,2},{9,3},... | collective-permute-start | bytes 196616 | tf_op jit(solution)/shard_map/ppermute | solution.py:34
  44.5 26.8 %collective-permute-start.3 = (bf16[256,512]{1,0:T(8,128)(2,1)S(1)}, bf16[256,512]{1,0:T(8,128)(2,1)S(1)}, u32[]{:S(2)}, u32[]{:S(2)}) collective-permute-start(bf16[256,512]{1,0:T(8,128)(2,1)S(1)} %get-tuple-element.53), channel_id=1, source_target_pairs={{0,2},{1,3},{2,0},{3,1},{4,6},{5,7},{6,4},{7,5},{8,10},{9,11},{10,... | collective-permute-start | bytes 786440 | tf_op jit(solution)/shard_map/ppermute | solution.py:34
  45.0 31.7 %collective-permute-start.5 = (bf16[256,512]{1,0:T(8,128)(2,1)S(1)}, bf16[256,512]{1,0:T(8,128)(2,1)S(1)}, u32[]{:S(2)}, u32[]{:S(2)}) collective-permute-start(bf16[256,512]{1,0:T(8,128)(2,1)S(1)} %get-tuple-element.51), channel_id=1, source_target_pairs={{0,4},{1,5},{2,6},{3,7},{4,0},{5,1},{6,2},{7,3},{8,12},{9,13},{10,... | collective-permute-start | bytes 786440 | tf_op jit(solution)/shard_map/ppermute | solution.py:34
  46.2 33.0 %collective-permute-start.10 = (bf16[256,512]{1,0:T(8,128)(2,1)S(1)}, bf16[256,512]{1,0:T(8,128)(2,1)S(1)}, u32[]{:S(2)}, u32[]{:S(2)}) collective-permute-start(bf16[256,512]{1,0:T(8,128)(2,1)S(1)} %fusion.2), channel_id=1, source_target_pairs={{0,8},{1,9},{2,10},{3,11},{4,12},{5,13},{6,14},{7,15},{8,0},{9,1},... | collective-permute-start | bytes 786440 | tf_op jit(solution)/shard_map/ppermute | solution.py:34
  48.5 9.9 %collective-permute-start.16 = (bf16[32,1024]{1,0:T(8,128)(2,1)S(1)}, bf16[32,1024]{1,0:T(8,128)(2,1)S(1)}, u32[]{:S(2)}, u32[]{:S(2)}) collective-permute-start(bf16[32,1024]{1,0:T(8,128)(2,1)S(1)} %get-tuple-element.41), channel_id=1, source_target_pairs={{0,12},{1,13},{2,14},{3,15},{4,8},{5,9},{6,10},{7,11},{8,4},{9,5},... | collective-permute-start | bytes 196616 | tf_op jit(solution)/shard_map/ppermute | solution.py:34
  58.4 7.0 %collective-permute-start.17 = (bf16[32,1024]{1,0:T(8,128)(2,1)S(1)}, bf16[32,1024]{1,0:T(8,128)(2,1)S(1)}, u32[]{:S(2)}, u32[]{:S(2)}) collective-permute-start(bf16[32,1024]{1,0:T(8,128)(2,1)S(1)} %get-tuple-element.42), channel_id=1, source_target_pairs={{0,14},{1,15},{2,12},{3,13},{4,10},{5,11},{6,8},{7,9},{8,6},{9,7},... | collective-permute-start | bytes 196616 | tf_op jit(solution)/shard_map/ppermute | solution.py:34
  65.8 1.2 %collective-permute-start.18 = (bf16[32,64]{1,0:T(8,128)(2,1)S(1)}, bf16[32,64]{1,0:T(8,128)(2,1)S(1)}, u32[]{:S(2)}, u32[]{:S(2)}) collective-permute-start(bf16[32,64]{1,0:T(8,128)(2,1)S(1)} %shrink.1.shrunk_ref), channel_id=1, source_target_pairs={{0,1},{1,0},{2,3},{3,2},{4,5},{5,4},{6,7},{7,6},{8,9},{9,8},{10,11... | collective-permute-start | bytes 12296 | tf_op jit(solution)/shard_map/ppermute | solution.py:34
  67.2 5.1 %collective-permute-start.20 = (bf16[64,512]{1,0:T(8,128)(2,1)S(1)}, bf16[64,512]{1,0:T(8,128)(2,1)S(1)}, u32[]{:S(2)}, u32[]{:S(2)}) collective-permute-start(bf16[64,512]{1,0:T(8,128)(2,1)S(1)} %get-tuple-element.44), channel_id=1, source_target_pairs={{0,2},{1,3},{2,0},{3,1},{4,6},{5,7},{6,4},{7,5},{8,10},{9,11},{10,... | collective-permute-start | bytes 196616 | tf_op jit(solution)/shard_map/ppermute | solution.py:34
  68.5 6.5 %collective-permute-start.21 = (bf16[64,512]{1,0:T(8,128)(2,1)S(1)}, bf16[64,512]{1,0:T(8,128)(2,1)S(1)}, u32[]{:S(2)}, u32[]{:S(2)}) collective-permute-start(bf16[64,512]{1,0:T(8,128)(2,1)S(1)} %get-tuple-element.45), channel_id=1, source_target_pairs={{0,4},{1,5},{2,6},{3,7},{4,0},{5,1},{6,2},{7,3},{8,12},{9,13},{10,... | collective-permute-start | bytes 196616 | tf_op jit(solution)/shard_map/ppermute | solution.py:34
  71.3 10.7 %collective-permute-start.22 = (bf16[64,512]{1,0:T(8,128)(2,1)S(1)}, bf16[64,512]{1,0:T(8,128)(2,1)S(1)}, u32[]{:S(2)}, u32[]{:S(2)}) collective-permute-start(bf16[64,512]{1,0:T(8,128)(2,1)S(1)} %get-tuple-element.46), channel_id=1, source_target_pairs={{0,6},{1,7},{2,4},{3,5},{4,2},{5,3},{6,0},{7,1},{8,14},{9,15},{10,... | collective-permute-start | bytes 196616 | tf_op jit(solution)/shard_map/ppermute | solution.py:34
  72.3 9.8 %collective-permute-start.23 = (bf16[64,512]{1,0:T(8,128)(2,1)S(1)}, bf16[64,512]{1,0:T(8,128)(2,1)S(1)}, u32[]{:S(2)}, u32[]{:S(2)}) collective-permute-start(bf16[64,512]{1,0:T(8,128)(2,1)S(1)} %get-tuple-element.47), channel_id=1, source_target_pairs={{0,8},{1,9},{2,10},{3,11},{4,12},{5,13},{6,14},{7,15},{8,0},{9,1},... | collective-permute-start | bytes 196616 | tf_op jit(solution)/shard_map/ppermute | solution.py:34
  75.0 9.6 %collective-permute-start.24 = (bf16[64,512]{1,0:T(8,128)(2,1)S(1)}, bf16[64,512]{1,0:T(8,128)(2,1)S(1)}, u32[]{:S(2)}, u32[]{:S(2)}) collective-permute-start(bf16[64,512]{1,0:T(8,128)(2,1)S(1)} %get-tuple-element.48), channel_id=1, source_target_pairs={{0,10},{1,11},{2,8},{3,9},{4,14},{5,15},{6,12},{7,13},{8,2},{9,3},... | collective-permute-start | bytes 196616 | tf_op jit(solution)/shard_map/ppermute | solution.py:34
  76.8 7.9 %collective-permute-start.25 = (bf16[64,512]{1,0:T(8,128)(2,1)S(1)}, bf16[64,512]{1,0:T(8,128)(2,1)S(1)}, u32[]{:S(2)}, u32[]{:S(2)}) collective-permute-start(bf16[64,512]{1,0:T(8,128)(2,1)S(1)} %get-tuple-element.49), channel_id=1, source_target_pairs={{0,12},{1,13},{2,14},{3,15},{4,8},{5,9},{6,10},{7,11},{8,4},{9,5},... | collective-permute-start | bytes 196616 | tf_op jit(solution)/shard_map/ppermute | solution.py:34
  79.3 7.1 %collective-permute-start.26 = (bf16[64,512]{1,0:T(8,128)(2,1)S(1)}, bf16[64,512]{1,0:T(8,128)(2,1)S(1)}, u32[]{:S(2)}, u32[]{:S(2)}) collective-permute-start(bf16[64,512]{1,0:T(8,128)(2,1)S(1)} %get-tuple-element.50), channel_id=1, source_target_pairs={{0,14},{1,15},{2,12},{3,13},{4,10},{5,11},{6,8},{7,9},{8,6},{9,7},... | collective-permute-start | bytes 196616 | tf_op jit(solution)/shard_map/ppermute | solution.py:34

commit v3 on v0

--- a/solution.py
+++ b/solution.py
@@ -1,12 +1,198 @@
+import functools
+
 import jax
 import jax.numpy as jnp
 from jax import lax
+from jax.experimental import pallas as pl
+from jax.experimental.pallas import tpu as pltpu
 from jax.sharding import PartitionSpec as P
 
 CAP = 32
-
-
-def shards(attended, out_weight, adapter_down, adapter_up, row_adapter, adapter_slot):
+IN_VMEM = pl.BlockSpec(memory_space=pltpu.VMEM)
+IN_HBM = pl.BlockSpec(memory_space=pltpu.HBM)
+DMA = pltpu.SemaphoreType.DMA
+
+
+def params(mib):
+    return pltpu.CompilerParams(vmem_limit_bytes=mib * 1024 * 1024)
+
+
+def cost(flops, moved):
+    return pl.CostEstimate(flops=flops, bytes_accessed=moved, transcendentals=0)
+
+
+def shape(dims, dtype=jnp.bfloat16):
+    return jax.ShapeDtypeStruct(dims, dtype)
+
+
+def dot(a, b):
+    return jnp.dot(a, b, preferred_element_type=jnp.float32)
+
+
+def swap(value, mask):
+    count = lax.axis_size("tensor")
+    return lax.ppermute(value, "tensor", [(t, t ^ mask) for t in range(count)])
+
+
+def route_kernel(chips, slot_hbm, row_ref, own_ref, other_ref, target_ref, *rest):
+    out_refs, slot_ref, slot_sem = rest[:chips], rest[chips], rest[chips + 1]
+    rows, width = own_ref.shape
+    me = lax.axis_index("tensor")
+    core = me % 2
+    fetch = pltpu.make_async_copy(slot_hbm, slot_ref, slot_sem)
+    fetch.start()
+    fetch.wait()
+    ids = row_ref[...]
+    owner = jnp.zeros_like(ids)
+    for a in range(slot_ref.shape[0]):
+        owner = jnp.where(ids == a, slot_ref[a], owner)
+    hot = (lax.broadcasted_iota(jnp.int32, (2 * chips, rows), 0) == owner).astype(jnp.float32)
+    earlier = (
+        lax.broadcasted_iota(jnp.int32, (rows, rows), 0)
+        < lax.broadcasted_iota(jnp.int32, (rows, rows), 1)
+    ).astype(jnp.bfloat16)
+    ahead = dot(hot.astype(jnp.bfloat16), earlier)
+    place = jnp.sum(ahead * hot, axis=0, keepdims=True).astype(jnp.int32)
+    target = owner * CAP + place
+    target_ref[...] = target
+    j = lax.broadcasted_iota(jnp.int32, (chips * CAP, rows), 0)
+    slots = (me ^ ((j // CAP) * 2)) * CAP + j % CAP
+    select = (slots == target).astype(jnp.bfloat16)
+    own = dot(select, own_ref[...]).astype(jnp.bfloat16)
+    other = dot(select, other_ref[...]).astype(jnp.bfloat16)
+    for m in range(chips):
+        out_refs[m][:, pl.ds(pl.multiple_of(core * width, width), width)] = own[m * CAP : (m + 1) * CAP]
+        out_refs[m][:, pl.ds(pl.multiple_of((1 - core) * width, width), width)] = other[
+            m * CAP : (m + 1) * CAP
+        ]
+
+
+def route(adapter_slot, row_adapter, own, other):
+    rows, width = own.shape
+    chips = lax.axis_size("tensor") // 2
+    found = pl.pallas_call(
+        functools.partial(route_kernel, chips),
+        out_shape=[shape((1, rows), jnp.int32)] + [shape((CAP, 2 * width))] * chips,
+        in_specs=[IN_HBM, IN_VMEM, IN_VMEM, IN_VMEM],
+        out_specs=[IN_VMEM] * (chips + 1),
+        scratch_shapes=[pltpu.SMEM(adapter_slot.shape, jnp.int32), DMA(())],
+        compiler_params=params(16),
+        cost_estimate=cost(4 * chips * CAP * rows * width, 8 * chips * CAP * width),
+        name="route",
+    )(adapter_slot, row_adapter[None, :], own, other)
+    return found[0], found[1:]
+
+
+def product_kernel(attended_ref, weight_ref, away_ref, stay_ref):
+    chips, rows, width = stay_ref.shape
+    me = lax.axis_index("tensor")
+    for m in reversed(range(chips)):
+        there = pl.ds(pl.multiple_of((me ^ (2 * m + 1)) * width, width), width)
+        here = pl.ds(pl.multiple_of((me ^ (2 * m)) * width, width), width)
+        away_ref[m] = dot(attended_ref[...], weight_ref[:, there]).astype(jnp.bfloat16)
+        stay_ref[m] = dot(attended_ref[...], weight_ref[:, here])
+
+
+def product(attended, out_weight):
+    rows, depth = attended.shape
+    chips = lax.axis_size("tensor") // 2
+    width = out_weight.shape[1] // (2 * chips)
+    return pl.pallas_call(
+        product_kernel,
+        out_shape=(shape((chips, rows, width)), shape((chips, rows, width), jnp.float32)),
+        in_specs=[IN_VMEM, IN_VMEM],
+        out_specs=(IN_VMEM, IN_VMEM),
+        compiler_params=params(24),
+        cost_estimate=cost(2 * rows * out_weight.size, 2 * out_weight.size + 6 * chips * rows * width),
+        name="product",
+    )(attended, out_weight)
+
+
+def adapter_kernel(chip_masks, down_ref, up_ref, *refs):
+    arrived_refs, near_ref, far_ref = refs[:-2], refs[-2], refs[-1]
+    me = lax.axis_index("tensor")
+    total = jnp.zeros((CAP, down_ref.shape[0]), jnp.float32)
+    for m, arrived_ref in zip(chip_masks, arrived_refs):
+        width = arrived_ref.shape[1]
+        start = pl.multiple_of(((me // 2) ^ m) * width, width)
+        total += lax.dot_general(
+            arrived_ref[...],
+            down_ref[:, pl.ds(start, width)],
+            (((1,), (1,)), ((), ())),
+            preferred_element_type=jnp.float32,
+        )
+    shrunk = total.astype(jnp.bfloat16)
+    width = near_ref.shape[2]
+    for m in range(len(arrived_refs)):
+        near = pl.multiple_of((me ^ (2 * m)) * width, width)
+        far = pl.multiple_of((me ^ (2 * m + 1)) * width, width)
+        near_ref[m] = dot(shrunk, up_ref[:, pl.ds(near, width)]).astype(jnp.bfloat16)
+        far_ref[m] = dot(shrunk, up_ref[:, pl.ds(far, width)]).astype(jnp.bfloat16)
+
+
+def adapter(down, up, arrived):
+    chips = len(arrived)
+    half = shape((chips, CAP, up.shape[1] // (2 * chips)))
+    return pl.pallas_call(
+        functools.partial(adapter_kernel, tuple(arrived)),
+        out_shape=(half, half),
+        in_specs=[IN_VMEM] * (2 + chips),
+        out_specs=(IN_VMEM, IN_VMEM),
+        compiler_params=params(16),
+        cost_estimate=cost(40 * 10**9, 128 * down.size),
+        name="adapter",
+    )(down, up, *arrived.values())
+
+
+def join_kernel(chip_masks, target_ref, stay_ref, came_ref, near_ref, far_ref, *out_refs):
+    rows = target_ref.shape[1]
+    me = lax.axis_index("tensor")
+    j = lax.broadcasted_iota(jnp.int32, (CAP, rows), 0)
+    over = (((0,), (0,)), ((), ()))
+    near_pick = (me * CAP + j == target_ref[...]).astype(jnp.bfloat16)
+    far_pick = ((me ^ 1) * CAP + j == target_ref[...]).astype(jnp.bfloat16)
+    for m, out_ref in zip(chip_masks, out_refs):
+        total = stay_ref[m] + came_ref[m].astype(jnp.float32)
+        total += lax.dot_general(near_pick, near_ref[m], over, preferred_element_type=jnp.float32)
+        total += lax.dot_general(far_pick, far_ref[m], over, preferred_element_type=jnp.float32)
+        out_ref[...] = total.astype(out_ref.dtype)
+
+
+def join(target, stay, came, near, far, chip_masks, dtype):
+    n, (rows, width) = len(chip_masks), stay.shape[1:]
+    return pl.pallas_call(
+        functools.partial(join_kernel, chip_masks),
+        out_shape=[shape((rows, width), dtype)] * n,
+        in_specs=[IN_VMEM] * 5,
+        out_specs=[IN_VMEM] * n,
+        compiler_params=params(24),
+        cost_estimate=cost(4 * n * CAP * rows * width, 10 * n * rows * width),
+        name="join",
+    )(target, stay, came, near, far)
+
+
+def staged(attended, out_weight, adapter_down, adapter_up, row_adapter, adapter_slot):
+    f32, bf16 = jnp.float32, jnp.bfloat16
+    up, down = adapter_up[0], jnp.swapaxes(adapter_down, 1, 2)[0]
+    target, outgoing = route(adapter_slot, row_adapter, attended, swap(attended, 1))
+    arrived = {m: swap(outgoing[m], 2 * m) for m in (1, 2, 4, 5, 6, 7, 3)}
+    arrived[0] = outgoing[0]
+    away, stay = product(attended, out_weight)
+    came = swap(away, 1)
+    near, far = adapter(down, up, arrived)
+    far = swap(far, 1)
+    (go3,) = join(target, stay, came, near, far, (7,), bf16)
+    go2, go1, go0 = join(target, stay, came, near, far, (5, 3, 1), bf16)
+    y3, y2, y1, y0 = swap(go3, 2), swap(go2, 2), swap(go1, 2), swap(go0, 2)
+    side3, side2, side1, side0 = join(target, stay, came, near, far, (6, 4, 2, 0), f32)
+    z3 = swap((side3 + y3.astype(f32)).astype(bf16), 4)
+    z2 = swap((side2 + y2.astype(f32) + z3.astype(f32)).astype(bf16), 8)
+    z1 = swap((side1 + y1.astype(f32)).astype(bf16), 4)
+    total = side0 + y0.astype(f32) + z1.astype(f32) + z2.astype(f32)
+    return total.astype(bf16)
+
+
+def general(attended, out_weight, adapter_down, adapter_up, row_adapter, adapter_slot):
     tensor_size = lax.axis_size("tensor")
     device = lax.axis_index("tensor")
     row_count = attended.shape[0]
@@ -47,6 +233,12 @@
     return (base_out + delta_out.astype(jnp.float32)).astype(jnp.bfloat16)
 
 
+def shards(*arrays):
+    if lax.axis_size("tensor") == 16 and arrays[2].shape[0] == 1:
+        return staged(*arrays)
+    return general(*arrays)
+
+
 def solution(mesh):
     placed = (
         P("groups", "tensor"),

time: 151 us -> 65.8 us (0.44)
  waiting for transfers between devices: 68.8 us -> 28.8 us
  other arithmetic: 31.9 us -> 1.1 us
  between operations: 13.5 us -> 0.14 us
  matrix products: 10 us -> 0 us
  Pallas kernels: 0 us -> 5.97 us
  starting transfers between devices: 17.2 us -> 22.9 us
  local copies, waits for them, and re-layouts: 8.71 us -> 6.62 us
    all_to_all x2 -> x0, waiting for transfers between devices: 36.7 us -> none  [the longest x1 22.2 us: shards(): lax.all_to_all(outgoing, 'tensor', split_axis=0, concat_axis=1, tiled=True)]
    reduce_scatter x1 -> x0, waiting for transfers between devices: 32.1 us -> none  [shards(): lax.psum_scatter(partial_value, 'tensor', scatter_dimension=1, tiled=True)]
    ppermute x0 -> x17, waiting for transfers between devices: none -> 28.8 us  [swap(): return lax.ppermute(value, 'tensor', [(t, t ^ mask) for t in range(count)])]
    ppermute x0 -> x17, starting transfers between devices: none -> 22.9 us  [swap(): return lax.ppermute(value, 'tensor', [(t, t ^ mask) for t in range(count)])]
    all_to_all x2 -> x0, starting transfers between devices: 17.2 us -> none  [the longest x1 9.77 us: shards(): lax.all_to_all(expanded, 'tensor', split_axis=1, concat_axis=0, tiled=True)]
    dot_general x2 -> x0, matrix products: 10 us -> none  [the longest x1 9.13 us: shards(): jnp.dot(attended, out_weight, preferred_element_type=jnp.float32)]
    gather x4 -> x0, other arithmetic: 9.79 us -> none  [the longest x1 9.77 us: shards(): storage = adapter_slot[row_adapter]]
    add x1 -> x0, other arithmetic: 9.74 us -> none  [shards(): target = owner_of * CAP + position]
  transfers between devices with their start and end apart: 3 -> 17, of which waited for: 3 -> 7; matrix products, arithmetic and copies ran while one was open for 26% -> 0% of each run, Pallas kernels for 0% -> 7%
where the time goes in v3:
time: 65.8 us; the launch traced here: 65.5 us
  waiting for transfers between devices  28.8 us (44%)
  starting transfers between devices  22.9 us (35%)
  local copies, waits for them, and re-layouts  6.62 us (10%)
  Pallas kernels  5.97 us (9%)
  other arithmetic  1.1 us (2%)
    ppermute x17, waiting for transfers between devices, swap(): return lax.ppermute(value, 'tensor', [(t, t ^ mask) for t in range(count)])  28.8 us
    ppermute x17, starting transfers between devices, swap(): return lax.ppermute(value, 'tensor', [(t, t ^ mask) for t in range(count)])  22.9 us
    unnamed x14, local copies, waits for them, and re-layouts  6.62 us
    pallas_call x1, Pallas kernels, product(): pl.pallas_call(product_kernel, out_shape=(shape((chips, rows, width)), sh...  2.34 us
    pallas_call x3, Pallas kernels, join(): pl.pallas_call(functools.partial(join_kernel, chip_masks), out_shape=[sha...  1.7 us
  transfers between devices with their start and end apart: 17, of which 7 were waited for; matrix products, arithmetic and copies ran while one was open for 0% of the time, Pallas kernels for 7%

profile of v3, /device:TPU:0, one launch (start us, length us, event | category | flops | bytes accessed | tf_op | source)
XLA Modules:
  0.0 65.5 jit_solution(15906330710285789850)
XLA Ops:
  0.0 0.5 collective-permute-start
  0.5 1.4 %collective-permute-done.other_ref = bf16[256,512]{1,0:T(8,128)(2,1)S(1)} collective-permute-done((bf16[256,512]{1,0:T(8,128)(2,1)}, bf16[256,512]{1,0:T(8,128)(2,1)S(1)}, u32[]{:S(2)}, u32[]{:S(2)}) %collective-permute-start) | collective-permute-done | bytes 262176 | tf_op jit(solution)/shard_map/ppermute | solution.py:34
  1.8 0.0 copy-start.1
  1.8 0.9 %copy-done.1 = bf16[256,512]{1,0:T(8,128)(2,1)S(1)} copy-done((bf16[256,512]{1,0:T(8,128)(2,1)S(1)}, bf16[256,512]{1,0:T(8,128)(2,1)}, u32[]{:S(2)}) %copy-start.1) | copy-done | bytes 262168
  2.8 0.0 copy-start.3
  2.8 0.7 %copy-done.3 = s32[256]{0:T(256)S(1)} copy-done((s32[256]{0:T(256)S(1)}, s32[256]{0:T(256)}, u32[]{:S(2)}) %copy-start.3) | copy-done | bytes 1048
  3.5 0.0 copy-start.4
  3.5 0.7 copy-done.4
  4.1 1.0 %route.1 = (s32[1,256]{1,0:T(1,128)S(1)}, bf16[32,1024]{1,0:T(8,128)(2,1)S(1)}, bf16[32,1024]{1,0:T(8,128)(2,1)S(1)}, bf16[32,1024]{1,0:T(8,128)(2,1)S(1)}, bf16...) custom-call(s32[16]{0:T(128)S(1)} %copy-done.4, ...), custom_call_target="tpu_custom_call" | custom-call | flops 134217728 | bytes 1048576 | tf_op jit(solution)/shard_map/route/pallas_call | solution.py:73
  5.1 3.0 %collective-permute-start.2 = (bf16[32,1024]{1,0:T(8,128)(2,1)S(1)}, bf16[32,1024]{1,0:T(8,128)(2,1)S(1)}, u32[]{:S(2)}, u32[]{:S(2)}) collective-permute-start(bf16[32,1024]{1,0:T(8,128)(2,1)S(1)} %get-tuple-element.28), channel_id=1, source_target_pairs={{0,2},{1,3},{2,0},{3,1},{4,6},{5,7},{6,4},{7,5},{8,10},{9,11},{10,... | collective-permute-start | bytes 196616 | tf_op jit(solution)/shard_map/ppermute | solution.py:34
  8.1 1.6 %collective-permute-start.3 = (bf16[32,1024]{1,0:T(8,128)(2,1)S(1)}, bf16[32,1024]{1,0:T(8,128)(2,1)S(1)}, u32[]{:S(2)}, u32[]{:S(2)}) collective-permute-start(bf16[32,1024]{1,0:T(8,128)(2,1)S(1)} %get-tuple-element.29), channel_id=1, source_target_pairs={{0,4},{1,5},{2,6},{3,7},{4,0},{5,1},{6,2},{7,3},{8,12},{9,13},{10,... | collective-permute-start | bytes 196616 | tf_op jit(solution)/shard_map/ppermute | solution.py:34
  9.7 2.6 %collective-permute-start.4 = (bf16[32,1024]{1,0:T(8,128)(2,1)S(1)}, bf16[32,1024]{1,0:T(8,128)(2,1)S(1)}, u32[]{:S(2)}, u32[]{:S(2)}) collective-permute-start(bf16[32,1024]{1,0:T(8,128)(2,1)S(1)} %get-tuple-element.30), channel_id=1, source_target_pairs={{0,8},{1,9},{2,10},{3,11},{4,12},{5,13},{6,14},{7,15},{8,0},{9,1},... | collective-permute-start | bytes 196616 | tf_op jit(solution)/shard_map/ppermute | solution.py:34
  12.2 0.3 collective-permute-start.5
  12.5 2.5 %collective-permute-start.6 = (bf16[32,1024]{1,0:T(8,128)(2,1)S(1)}, bf16[32,1024]{1,0:T(8,128)(2,1)S(1)}, u32[]{:S(2)}, u32[]{:S(2)}) collective-permute-start(bf16[32,1024]{1,0:T(8,128)(2,1)S(1)} %get-tuple-element.32), channel_id=1, source_target_pairs={{0,12},{1,13},{2,14},{3,15},{4,8},{5,9},{6,10},{7,11},{8,4},{9,5},... | collective-permute-start | bytes 196616 | tf_op jit(solution)/shard_map/ppermute | solution.py:34
  15.0 0.0 collective-permute-done.2.refs_0_
  15.0 2.3 %collective-permute-start.7 = (bf16[32,1024]{1,0:T(8,128)(2,1)S(1)}, bf16[32,1024]{1,0:T(8,128)(2,1)S(1)}, u32[]{:S(2)}, u32[]{:S(2)}) collective-permute-start(bf16[32,1024]{1,0:T(8,128)(2,1)S(1)} %get-tuple-element.33), channel_id=1, source_target_pairs={{0,14},{1,15},{2,12},{3,13},{4,10},{5,11},{6,8},{7,9},{8,6},{9,7},... | collective-permute-start | bytes 196616 | tf_op jit(solution)/shard_map/ppermute | solution.py:34
  17.3 0.0 collective-permute-done.3.refs_1_
  17.3 0.0 collective-permute-start.8
  17.3 0.0 copy-start
  17.3 3.4 %copy-done = bf16[512,8192]{1,0:T(8,128)(2,1)S(1)} copy-done((bf16[512,8192]{1,0:T(8,128)(2,1)S(1)}, bf16[512,8192]{1,0:T(8,128)(2,1)}, u32[]{:S(2)}) %copy-start) | copy-done | bytes 8388632
  20.7 0.0 copy-start.2
  20.7 0.9 %copy-done.2 = bf16[256,512]{1,0:T(8,128)(2,1)S(1)} copy-done((bf16[256,512]{1,0:T(8,128)(2,1)S(1)}, bf16[256,512]{1,0:T(8,128)(2,1)}, u32[]{:S(2)}) %copy-start.2) | copy-done | bytes 262168
  21.6 0.0 copy-start.5
  21.6 0.0 copy-start.6
  21.7 2.3 %product.1 = (bf16[8,256,512]{2,1,0:T(8,128)(2,1)S(1)}, f32[8,256,512]{2,1,0:T(8,128)S(1)}) custom-call(bf16[256,512]{1,0:T(8,128)(2,1)S(1)} %copy-done.2, bf16[512,8192]{1,0:T(8,128)(2,1)S(1)} %copy-done), custom_call_target="tpu_custom_call" | custom-call | flops 2147483648 | bytes 14680064 | tf_op jit(solution)/shard_map/product/pallas_call | solution.py:100
  24.0 0.0 collective-permute-done.4.refs_2_
  24.0 0.1 collective-permute-start.1
  24.1 0.0 collective-permute-done.5.refs_3_
  24.1 0.0 collective-permute-done.6.refs_4_
  24.1 0.0 collective-permute-done.7.refs_5_
  24.1 0.0 collective-permute-done.8.refs_6_
  24.1 0.0 copy-done.5
  24.1 0.0 copy-done.6
  24.1 0.9 %adapter.1 = (bf16[8,32,512]{2,1,0:T(8,128)(2,1)S(1)}, bf16[8,32,512]{2,1,0:T(8,128)(2,1)S(1)}) custom-call(bf16[64,8192]{1,0:T(8,128)(2,1)S(1)} %bitcast.6, bf16[64,8192]{1,0:T(8,128)(2,1)S(1)} %bitcast.7, bf16[32,1024]{1,0:T(8,128)(2,1)S(1)} %collective-permute-done.2.refs_0_, bf16[32,1024]{1,0:T(8,128)(2,1)S(1)} %collective-permute-done.3.refs_1_, ...), custom_call_target="tpu_custom_call" | custom-call | flops 40000000000 | bytes 67108864 | tf_op jit(solution)/shard_map/adapter/pallas_call | solution.py:136
  25.1 0.5 collective-permute-start.9
  25.6 3.0 %collective-permute-done.9.far_ref = bf16[8,32,512]{2,1,0:T(8,128)(2,1)S(1)} collective-permute-done((bf16[8,32,512]{2,1,0:T(8,128)(2,1)S(1)}, bf16[8,32,512]{2,1,0:T(8,128)(2,1)S(1)}, u32[]{:S(2)}, u32[]{:S(2)}) %collective-permute-start.9) | collective-permute-done | bytes 262176 | tf_op jit(solution)/shard_map/ppermute | solution.py:34
  28.6 0.0 collective-permute-done.1.came_ref
  28.6 0.3 join.5
  29.0 0.9 %collective-permute-start.14 = (bf16[256,512]{1,0:T(8,128)(2,1)S(1)}, bf16[256,512]{1,0:T(8,128)(2,1)S(1)}, u32[]{:S(2)}, u32[]{:S(2)}) collective-permute-start(bf16[256,512]{1,0:T(8,128)(2,1)S(1)} %join.5), channel_id=1, source_target_pairs={{0,2},{1,3},{2,0},{3,1},{4,6},{5,7},{6,4},{7,5},{8,10},{9,11},{10,... | collective-permute-start | bytes 786440 | tf_op jit(solution)/shard_map/ppermute | solution.py:34
  29.8 0.6 join.4
  30.4 1.3 %collective-permute-start.13 = (bf16[256,512]{1,0:T(8,128)(2,1)S(1)}, bf16[256,512]{1,0:T(8,128)(2,1)S(1)}, u32[]{:S(2)}, u32[]{:S(2)}) collective-permute-start(bf16[256,512]{1,0:T(8,128)(2,1)S(1)} %get-tuple-element.43), channel_id=1, source_target_pairs={{0,2},{1,3},{2,0},{3,1},{4,6},{5,7},{6,4},{7,5},{8,10},{9,11},{10,... | collective-permute-start | bytes 786440 | tf_op jit(solution)/shard_map/ppermute | solution.py:34
  31.7 0.8 %collective-permute-start.11 = (bf16[256,512]{1,0:T(8,128)(2,1)S(1)}, bf16[256,512]{1,0:T(8,128)(2,1)S(1)}, u32[]{:S(2)}, u32[]{:S(2)}) collective-permute-start(bf16[256,512]{1,0:T(8,128)(2,1)S(1)} %get-tuple-element.41), channel_id=1, source_target_pairs={{0,2},{1,3},{2,0},{3,1},{4,6},{5,7},{6,4},{7,5},{8,10},{9,11},{10,... | collective-permute-start | bytes 786440 | tf_op jit(solution)/shard_map/ppermute | solution.py:34
  32.5 0.8 %join.3 = (f32[256,512]{1,0:T(8,128)S(1)}, f32[256,512]{1,0:T(8,128)S(1)}, f32[256,512]{1,0:T(8,128)S(1)}, f32[256,512]{1,0:T(8,128)S(1)}) custom-call(s32[1,256]{1,0:T(1,128)S(1)} %get-tuple-element.25.target_ref, f32[8,256,512]{2,1,0:T(8,128)S(1)} %get-tuple-element.26.stay_ref, bf16[8,256,512]{2,1,0:T(8,128)(2,1)S(1)} %collective-permute-done.1.came_ref, ...), custom_call_target="tpu_custom_call" | custom-call | flops 67108864 | bytes 5242880 | tf_op jit(solution)/shard_map/join/pallas_call | solution.py:163
  33.3 4.9 %collective-permute-done.14 = bf16[256,512]{1,0:T(8,128)(2,1)S(1)} collective-permute-done((bf16[256,512]{1,0:T(8,128)(2,1)S(1)}, bf16[256,512]{1,0:T(8,128)(2,1)S(1)}, u32[]{:S(2)}, u32[]{:S(2)}) %collective-permute-start.14) | collective-permute-done | bytes 262176 | tf_op jit(solution)/shard_map/ppermute | solution.py:34
  38.2 0.1 add_convert_fusion.2
  38.2 2.0 %collective-permute-start.15 = (bf16[256,512]{1,0:T(8,128)(2,1)S(1)}, bf16[256,512]{1,0:T(8,128)(2,1)S(1)}, u32[]{:S(2)}, u32[]{:S(2)}) collective-permute-start(bf16[256,512]{1,0:T(8,128)(2,1)S(1)} %add_convert_fusion.2), channel_id=1, source_target_pairs={{0,4},{1,5},{2,6},{3,7},{4,0},{5,1},{6,2},{7,3},{8,12},{9,13},{10,... | collective-permute-start | bytes 786440 | tf_op jit(solution)/shard_map/ppermute | solution.py:34
  40.3 1.5 %collective-permute-start.10 = (bf16[256,512]{1,0:T(8,128)(2,1)S(1)}, bf16[256,512]{1,0:T(8,128)(2,1)S(1)}, u32[]{:S(2)}, u32[]{:S(2)}) collective-permute-start(bf16[256,512]{1,0:T(8,128)(2,1)S(1)} %get-tuple-element.39), channel_id=1, source_target_pairs={{0,2},{1,3},{2,0},{3,1},{4,6},{5,7},{6,4},{7,5},{8,10},{9,11},{10,... | collective-permute-start | bytes 786440 | tf_op jit(solution)/shard_map/ppermute | solution.py:34
  41.8 7.6 %collective-permute-done.11 = bf16[256,512]{1,0:T(8,128)(2,1)S(1)} collective-permute-done((bf16[256,512]{1,0:T(8,128)(2,1)S(1)}, bf16[256,512]{1,0:T(8,128)(2,1)S(1)}, u32[]{:S(2)}, u32[]{:S(2)}) %collective-permute-start.11) | collective-permute-done | bytes 262176 | tf_op jit(solution)/shard_map/ppermute | solution.py:34
  49.4 0.1 add_convert_fusion.3
  49.5 2.0 %collective-permute-start.12 = (bf16[256,512]{1,0:T(8,128)(2,1)S(1)}, bf16[256,512]{1,0:T(8,128)(2,1)S(1)}, u32[]{:S(2)}, u32[]{:S(2)}) collective-permute-start(bf16[256,512]{1,0:T(8,128)(2,1)S(1)} %add_convert_fusion.3), channel_id=1, source_target_pairs={{0,4},{1,5},{2,6},{3,7},{4,0},{5,1},{6,2},{7,3},{8,12},{9,13},{10,... | collective-permute-start | bytes 786440 | tf_op jit(solution)/shard_map/ppermute | solution.py:34
  51.5 0.0 collective-permute-done.13
  51.5 0.0 collective-permute-done.15
  51.5 0.1 add_convert_fusion.1
  51.6 1.1 %collective-permute-start.16 = (bf16[256,512]{1,0:T(8,128)(2,1)S(1)}, bf16[256,512]{1,0:T(8,128)(2,1)S(1)}, u32[]{:S(2)}, u32[]{:S(2)}) collective-permute-start(bf16[256,512]{1,0:T(8,128)(2,1)S(1)} %add_convert_fusion.1), channel_id=1, source_target_pairs={{0,8},{1,9},{2,10},{3,11},{4,12},{5,13},{6,14},{7,15},{8,0},{9,1},... | collective-permute-start | bytes 786440 | tf_op jit(solution)/shard_map/ppermute | solution.py:34
  52.8 1.4 %collective-permute-done.10 = bf16[256,512]{1,0:T(8,128)(2,1)S(1)} collective-permute-done((bf16[256,512]{1,0:T(8,128)(2,1)S(1)}, bf16[256,512]{1,0:T(8,128)(2,1)S(1)}, u32[]{:S(2)}, u32[]{:S(2)}) %collective-permute-start.10) | collective-permute-done | bytes 262176 | tf_op jit(solution)/shard_map/ppermute | solution.py:34
  54.2 7.6 %collective-permute-done.12 = bf16[256,512]{1,0:T(8,128)(2,1)S(1)} collective-permute-done((bf16[256,512]{1,0:T(8,128)(2,1)S(1)}, bf16[256,512]{1,0:T(8,128)(2,1)S(1)}, u32[]{:S(2)}, u32[]{:S(2)}) %collective-permute-start.12) | collective-permute-done | bytes 262176 | tf_op jit(solution)/shard_map/ppermute | solution.py:34
  61.8 2.9 %collective-permute-done.16 = bf16[256,512]{1,0:T(8,128)(2,1)S(1)} collective-permute-done((bf16[256,512]{1,0:T(8,128)(2,1)S(1)}, bf16[256,512]{1,0:T(8,128)(2,1)S(1)}, u32[]{:S(2)}, u32[]{:S(2)}) %collective-permute-start.16) | collective-permute-done | bytes 262176 | tf_op jit(solution)/shard_map/ppermute | solution.py:34
  64.7 0.8 %add_convert_fusion = bf16[256,512]{1,0:T(8,128)(2,1)} fusion(bf16[256,512]{1,0:T(8,128)(2,1)S(1)} %collective-permute-done.16, bf16[256,512]{1,0:T(8,128)(2,1)S(1)} %collective-permute-done.12, f32[256,512]{1,0:T(8,128)S(1)} %get-tuple-element.38, bf16[256,512]{1,0:T(8,128)(2,1)S(1)} %collective-permute-done.10), kind=kLoop, calls=%fused_computation | loop fusion | flops 917504 | bytes 1572864 | tf_op jit(solution)/shard_map/convert_element_type | solution.py:192
Async XLA Ops:
  0.0 1.8 %collective-permute-start = (bf16[256,512]{1,0:T(8,128)(2,1)}, bf16[256,512]{1,0:T(8,128)(2,1)S(1)}, u32[]{:S(2)}, u32[]{:S(2)}) collective-permute-start(bf16[256,512]{1,0:T(8,128)(2,1)} %attended_ref.1), channel_id=1, source_target_pairs={{0,1},{1,0},{2,3},{3,2},{4,5},{5,4},{6,7},{7,6},{8,9},{9,8},{10,11... | collective-permute-start | bytes 786440 | tf_op jit(solution)/shard_map/ppermute | solution.py:34
  1.8 0.9 %copy-start.1 = (bf16[256,512]{1,0:T(8,128)(2,1)S(1)}, bf16[256,512]{1,0:T(8,128)(2,1)}, u32[]{:S(2)}) copy-start(bf16[256,512]{1,0:T(8,128)(2,1)} %attended_ref.1) | copy-start | bytes 786436
  2.8 0.7 %copy-start.3 = (s32[256]{0:T(256)S(1)}, s32[256]{0:T(256)}, u32[]{:S(2)}) copy-start(s32[256]{0:T(256)} %param.10) | copy-start | bytes 3076
  3.5 0.7 copy-start.4
  5.1 9.9 %collective-permute-start.2 = (bf16[32,1024]{1,0:T(8,128)(2,1)S(1)}, bf16[32,1024]{1,0:T(8,128)(2,1)S(1)}, u32[]{:S(2)}, u32[]{:S(2)}) collective-permute-start(bf16[32,1024]{1,0:T(8,128)(2,1)S(1)} %get-tuple-element.28), channel_id=1, source_target_pairs={{0,2},{1,3},{2,0},{3,1},{4,6},{5,7},{6,4},{7,5},{8,10},{9,11},{10,... | collective-permute-start | bytes 196616 | tf_op jit(solution)/shard_map/ppermute | solution.py:34
  8.1 9.2 %collective-permute-start.3 = (bf16[32,1024]{1,0:T(8,128)(2,1)S(1)}, bf16[32,1024]{1,0:T(8,128)(2,1)S(1)}, u32[]{:S(2)}, u32[]{:S(2)}) collective-permute-start(bf16[32,1024]{1,0:T(8,128)(2,1)S(1)} %get-tuple-element.29), channel_id=1, source_target_pairs={{0,4},{1,5},{2,6},{3,7},{4,0},{5,1},{6,2},{7,3},{8,12},{9,13},{10,... | collective-permute-start | bytes 196616 | tf_op jit(solution)/shard_map/ppermute | solution.py:34
  9.7 14.3 %collective-permute-start.4 = (bf16[32,1024]{1,0:T(8,128)(2,1)S(1)}, bf16[32,1024]{1,0:T(8,128)(2,1)S(1)}, u32[]{:S(2)}, u32[]{:S(2)}) collective-permute-start(bf16[32,1024]{1,0:T(8,128)(2,1)S(1)} %get-tuple-element.30), channel_id=1, source_target_pairs={{0,8},{1,9},{2,10},{3,11},{4,12},{5,13},{6,14},{7,15},{8,0},{9,1},... | collective-permute-start | bytes 196616 | tf_op jit(solution)/shard_map/ppermute | solution.py:34
  12.2 11.8 %collective-permute-start.5 = (bf16[32,1024]{1,0:T(8,128)(2,1)S(1)}, bf16[32,1024]{1,0:T(8,128)(2,1)S(1)}, u32[]{:S(2)}, u32[]{:S(2)}) collective-permute-start(bf16[32,1024]{1,0:T(8,128)(2,1)S(1)} %get-tuple-element.31), channel_id=1, source_target_pairs={{0,10},{1,11},{2,8},{3,9},{4,14},{5,15},{6,12},{7,13},{8,2},{9,3},... | collective-permute-start | bytes 196616 | tf_op jit(solution)/shard_map/ppermute | solution.py:34
  12.5 11.6 %collective-permute-start.6 = (bf16[32,1024]{1,0:T(8,128)(2,1)S(1)}, bf16[32,1024]{1,0:T(8,128)(2,1)S(1)}, u32[]{:S(2)}, u32[]{:S(2)}) collective-permute-start(bf16[32,1024]{1,0:T(8,128)(2,1)S(1)} %get-tuple-element.32), channel_id=1, source_target_pairs={{0,12},{1,13},{2,14},{3,15},{4,8},{5,9},{6,10},{7,11},{8,4},{9,5},... | collective-permute-start | bytes 196616 | tf_op jit(solution)/shard_map/ppermute | solution.py:34
  15.0 9.1 %collective-permute-start.7 = (bf16[32,1024]{1,0:T(8,128)(2,1)S(1)}, bf16[32,1024]{1,0:T(8,128)(2,1)S(1)}, u32[]{:S(2)}, u32[]{:S(2)}) collective-permute-start(bf16[32,1024]{1,0:T(8,128)(2,1)S(1)} %get-tuple-element.33), channel_id=1, source_target_pairs={{0,14},{1,15},{2,12},{3,13},{4,10},{5,11},{6,8},{7,9},{8,6},{9,7},... | collective-permute-start | bytes 196616 | tf_op jit(solution)/shard_map/ppermute | solution.py:34
  17.3 6.8 %collective-permute-start.8 = (bf16[32,1024]{1,0:T(8,128)(2,1)S(1)}, bf16[32,1024]{1,0:T(8,128)(2,1)S(1)}, u32[]{:S(2)}, u32[]{:S(2)}) collective-permute-start(bf16[32,1024]{1,0:T(8,128)(2,1)S(1)} %get-tuple-element.34), channel_id=1, source_target_pairs={{0,6},{1,7},{2,4},{3,5},{4,2},{5,3},{6,0},{7,1},{8,14},{9,15},{10,... | collective-permute-start | bytes 196616 | tf_op jit(solution)/shard_map/ppermute | solution.py:34
  17.3 3.4 %copy-start = (bf16[512,8192]{1,0:T(8,128)(2,1)S(1)}, bf16[512,8192]{1,0:T(8,128)(2,1)}, u32[]{:S(2)}) copy-start(bf16[512,8192]{1,0:T(8,128)(2,1)} %weight_ref.1) | copy-start | bytes 25165828
  20.7 0.9 %copy-start.2 = (bf16[256,512]{1,0:T(8,128)(2,1)S(1)}, bf16[256,512]{1,0:T(8,128)(2,1)}, u32[]{:S(2)}) copy-start(bf16[256,512]{1,0:T(8,128)(2,1)} %attended_ref.1) | copy-start | bytes 786436
  21.6 2.5 %copy-start.5 = (bf16[1,8192,64]{1,2,0:T(8,128)(2,1)S(1)}, bf16[1,8192,64]{1,2,0:T(8,128)(2,1)}, u32[]{:S(2)}) copy-start(bf16[1,8192,64]{1,2,0:T(8,128)(2,1)} %param.8) | copy-start | bytes 3145732
  21.6 2.5 %copy-start.6 = (bf16[1,64,8192]{2,1,0:T(8,128)(2,1)S(1)}, bf16[1,64,8192]{2,1,0:T(8,128)(2,1)}, u32[]{:S(2)}) copy-start(bf16[1,64,8192]{2,1,0:T(8,128)(2,1)} %param.9) | copy-start | bytes 3145732
  24.0 4.6 %collective-permute-start.1 = (bf16[8,256,512]{2,1,0:T(8,128)(2,1)S(1)}, bf16[8,256,512]{2,1,0:T(8,128)(2,1)S(1)}, u32[]{:S(2)}, u32[]{:S(2)}) collective-permute-start(bf16[8,256,512]{2,1,0:T(8,128)(2,1)S(1)} %get-tuple-element.27), channel_id=1, source_target_pairs={{0,1},{1,0},{2,3},{3,2},{4,5},{5,4},{6,7},{7,6},{8,9},{9,8},{10,11... | collective-permute-start | bytes 6291464 | tf_op jit(solution)/shard_map/ppermute | solution.py:34
  25.1 3.5 %collective-permute-start.9 = (bf16[8,32,512]{2,1,0:T(8,128)(2,1)S(1)}, bf16[8,32,512]{2,1,0:T(8,128)(2,1)S(1)}, u32[]{:S(2)}, u32[]{:S(2)}) collective-permute-start(bf16[8,32,512]{2,1,0:T(8,128)(2,1)S(1)} %get-tuple-element.37), channel_id=1, source_target_pairs={{0,1},{1,0},{2,3},{3,2},{4,5},{5,4},{6,7},{7,6},{8,9},{9,8},{10,11... | collective-permute-start | bytes 786440 | tf_op jit(solution)/shard_map/ppermute | solution.py:34
  29.0 9.2 %collective-permute-start.14 = (bf16[256,512]{1,0:T(8,128)(2,1)S(1)}, bf16[256,512]{1,0:T(8,128)(2,1)S(1)}, u32[]{:S(2)}, u32[]{:S(2)}) collective-permute-start(bf16[256,512]{1,0:T(8,128)(2,1)S(1)} %join.5), channel_id=1, source_target_pairs={{0,2},{1,3},{2,0},{3,1},{4,6},{5,7},{6,4},{7,5},{8,10},{9,11},{10,... | collective-permute-start | bytes 786440 | tf_op jit(solution)/shard_map/ppermute | solution.py:34
  30.4 21.1 %collective-permute-start.13 = (bf16[256,512]{1,0:T(8,128)(2,1)S(1)}, bf16[256,512]{1,0:T(8,128)(2,1)S(1)}, u32[]{:S(2)}, u32[]{:S(2)}) collective-permute-start(bf16[256,512]{1,0:T(8,128)(2,1)S(1)} %get-tuple-element.43), channel_id=1, source_target_pairs={{0,2},{1,3},{2,0},{3,1},{4,6},{5,7},{6,4},{7,5},{8,10},{9,11},{10,... | collective-permute-start | bytes 786440 | tf_op jit(solution)/shard_map/ppermute | solution.py:34
  31.7 17.7 %collective-permute-start.11 = (bf16[256,512]{1,0:T(8,128)(2,1)S(1)}, bf16[256,512]{1,0:T(8,128)(2,1)S(1)}, u32[]{:S(2)}, u32[]{:S(2)}) collective-permute-start(bf16[256,512]{1,0:T(8,128)(2,1)S(1)} %get-tuple-element.41), channel_id=1, source_target_pairs={{0,2},{1,3},{2,0},{3,1},{4,6},{5,7},{6,4},{7,5},{8,10},{9,11},{10,... | collective-permute-start | bytes 786440 | tf_op jit(solution)/shard_map/ppermute | solution.py:34
  38.2 13.3 %collective-permute-start.15 = (bf16[256,512]{1,0:T(8,128)(2,1)S(1)}, bf16[256,512]{1,0:T(8,128)(2,1)S(1)}, u32[]{:S(2)}, u32[]{:S(2)}) collective-permute-start(bf16[256,512]{1,0:T(8,128)(2,1)S(1)} %add_convert_fusion.2), channel_id=1, source_target_pairs={{0,4},{1,5},{2,6},{3,7},{4,0},{5,1},{6,2},{7,3},{8,12},{9,13},{10,... | collective-permute-start | bytes 786440 | tf_op jit(solution)/shard_map/ppermute | solution.py:34
  40.3 13.9 %collective-permute-start.10 = (bf16[256,512]{1,0:T(8,128)(2,1)S(1)}, bf16[256,512]{1,0:T(8,128)(2,1)S(1)}, u32[]{:S(2)}, u32[]{:S(2)}) collective-permute-start(bf16[256,512]{1,0:T(8,128)(2,1)S(1)} %get-tuple-element.39), channel_id=1, source_target_pairs={{0,2},{1,3},{2,0},{3,1},{4,6},{5,7},{6,4},{7,5},{8,10},{9,11},{10,... | collective-permute-start | bytes 786440 | tf_op jit(solution)/shard_map/ppermute | solution.py:34
  49.5 12.3 %collective-permute-start.12 = (bf16[256,512]{1,0:T(8,128)(2,1)S(1)}, bf16[256,512]{1,0:T(8,128)(2,1)S(1)}, u32[]{:S(2)}, u32[]{:S(2)}) collective-permute-start(bf16[256,512]{1,0:T(8,128)(2,1)S(1)} %add_convert_fusion.3), channel_id=1, source_target_pairs={{0,4},{1,5},{2,6},{3,7},{4,0},{5,1},{6,2},{7,3},{8,12},{9,13},{10,... | collective-permute-start | bytes 786440 | tf_op jit(solution)/shard_map/ppermute | solution.py:34
  51.6 13.1 %collective-permute-start.16 = (bf16[256,512]{1,0:T(8,128)(2,1)S(1)}, bf16[256,512]{1,0:T(8,128)(2,1)S(1)}, u32[]{:S(2)}, u32[]{:S(2)}) collective-permute-start(bf16[256,512]{1,0:T(8,128)(2,1)S(1)} %add_convert_fusion.1), channel_id=1, source_target_pairs={{0,8},{1,9},{2,10},{3,11},{4,12},{5,13},{6,14},{7,15},{8,0},{9,1},... | collective-permute-start | bytes 786440 | tf_op jit(solution)/shard_map/ppermute | solution.py:34

commit v4 on v3

--- a/solution.py
+++ b/solution.py
@@ -34,7 +34,7 @@
     return lax.ppermute(value, "tensor", [(t, t ^ mask) for t in range(count)])
 
 
-def route_kernel(chips, slot_hbm, row_ref, own_ref, other_ref, target_ref, *rest):
+def route_kernel(chips, slot_hbm, row_ref, own_ref, other_ref, after_ref, target_ref, *rest):
     out_refs, slot_ref, slot_sem = rest[:chips], rest[chips], rest[chips + 1]
     rows, width = own_ref.shape
     me = lax.axis_index("tensor")
@@ -67,30 +67,43 @@
         ]
 
 
-def route(adapter_slot, row_adapter, own, other):
+def route(adapter_slot, row_adapter, own, other, after):
     rows, width = own.shape
     chips = lax.axis_size("tensor") // 2
     found = pl.pallas_call(
         functools.partial(route_kernel, chips),
         out_shape=[shape((1, rows), jnp.int32)] + [shape((CAP, 2 * width))] * chips,
-        in_specs=[IN_HBM, IN_VMEM, IN_VMEM, IN_VMEM],
+        in_specs=[IN_HBM, IN_VMEM, IN_VMEM, IN_VMEM, IN_VMEM],
         out_specs=[IN_VMEM] * (chips + 1),
         scratch_shapes=[pltpu.SMEM(adapter_slot.shape, jnp.int32), DMA(())],
         compiler_params=params(16),
         cost_estimate=cost(4 * chips * CAP * rows * width, 8 * chips * CAP * width),
         name="route",
-    )(adapter_slot, row_adapter[None, :], own, other)
+    )(adapter_slot, row_adapter[None, :], own, other, after)
     return found[0], found[1:]
 
 
-def product_kernel(attended_ref, weight_ref, away_ref, stay_ref):
+def product_kernel(attended_hbm, weight_hbm, away_ref, stay_ref, token_ref, attended_ref, weight_ref, sems):
     chips, rows, width = stay_ref.shape
     me = lax.axis_index("tensor")
-    for m in reversed(range(chips)):
-        there = pl.ds(pl.multiple_of((me ^ (2 * m + 1)) * width, width), width)
-        here = pl.ds(pl.multiple_of((me ^ (2 * m)) * width, width), width)
-        away_ref[m] = dot(attended_ref[...], weight_ref[:, there]).astype(jnp.bfloat16)
-        stay_ref[m] = dot(attended_ref[...], weight_ref[:, here])
+    core, chip = me % 2, me // 2
+    order = tuple(reversed(range(chips)))
+    fetches = [pltpu.make_async_copy(attended_hbm, attended_ref, sems.at[chips])]
+    for m in order:
+        start = pl.multiple_of((chip ^ m) * 2 * width, 2 * width)
+        fetches.append(
+            pltpu.make_async_copy(weight_hbm.at[:, pl.ds(start, 2 * width)], weight_ref.at[m], sems.at[m])
+        )
+    for fetch in fetches:
+        fetch.start()
+    token_ref[...] = jnp.zeros(token_ref.shape, token_ref.dtype)
+    fetches[0].wait()
+    there = pl.ds(pl.multiple_of((1 - core) * width, width), width)
+    here = pl.ds(pl.multiple_of(core * width, width), width)
+    for i, m in enumerate(order):
+        fetches[i + 1].wait()
+        away_ref[m] = dot(attended_ref[...], weight_ref[m, :, there]).astype(jnp.bfloat16)
+        stay_ref[m] = dot(attended_ref[...], weight_ref[m, :, here])
 
 
 def product(attended, out_weight):
@@ -99,10 +112,19 @@
     width = out_weight.shape[1] // (2 * chips)
     return pl.pallas_call(
         product_kernel,
-        out_shape=(shape((chips, rows, width)), shape((chips, rows, width), jnp.float32)),
-        in_specs=[IN_VMEM, IN_VMEM],
-        out_specs=(IN_VMEM, IN_VMEM),
-        compiler_params=params(24),
+        out_shape=(
+            shape((chips, rows, width)),
+            shape((chips, rows, width), jnp.float32),
+            shape((8, 128), jnp.float32),
+        ),
+        in_specs=[IN_HBM, IN_HBM],
+        out_specs=(IN_VMEM, IN_VMEM, IN_VMEM),
+        scratch_shapes=[
+            pltpu.VMEM((rows, depth), jnp.bfloat16),
+            pltpu.VMEM((chips, depth, 2 * width), jnp.bfloat16),
+            DMA((chips + 1,)),
+        ],
+        compiler_params=params(48),
         cost_estimate=cost(2 * rows * out_weight.size, 2 * out_weight.size + 6 * chips * rows * width),
         name="product",
     )(attended, out_weight)
@@ -171,14 +193,31 @@
     )(target, stay, came, near, far)
 
 
+def later_kernel(side_ref, came_ref, after_ref, out_ref):
+    out_ref[...] = (side_ref[...] + came_ref[...].astype(jnp.float32)).astype(jnp.bfloat16)
+
+
+def later(side, came, after):
+    return pl.pallas_call(
+        later_kernel,
+        out_shape=shape(side.shape),
+        in_specs=[IN_VMEM] * 3,
+        out_specs=IN_VMEM,
+        compiler_params=params(16),
+        cost_estimate=cost(2 * side.size, 8 * side.size),
+        name="later",
+    )(side, came, after)
+
+
 def staged(attended, out_weight, adapter_down, adapter_up, row_adapter, adapter_slot):
     f32, bf16 = jnp.float32, jnp.bfloat16
     up, down = adapter_up[0], jnp.swapaxes(adapter_down, 1, 2)[0]
-    target, outgoing = route(adapter_slot, row_adapter, attended, swap(attended, 1))
+    attended_other = swap(attended, 1)
+    away, stay, token = product(attended, out_weight)
+    came = swap(away, 1)
+    target, outgoing = route(adapter_slot, row_adapter, attended, attended_other, token)
     arrived = {m: swap(outgoing[m], 2 * m) for m in (1, 2, 4, 5, 6, 7, 3)}
     arrived[0] = outgoing[0]
-    away, stay = product(attended, out_weight)
-    came = swap(away, 1)
     near, far = adapter(down, up, arrived)
     far = swap(far, 1)
     (go3,) = join(target, stay, came, near, far, (7,), bf16)
@@ -186,8 +225,9 @@
     y3, y2, y1, y0 = swap(go3, 2), swap(go2, 2), swap(go1, 2), swap(go0, 2)
     side3, side2, side1, side0 = join(target, stay, came, near, far, (6, 4, 2, 0), f32)
     z3 = swap((side3 + y3.astype(f32)).astype(bf16), 4)
-    z2 = swap((side2 + y2.astype(f32) + z3.astype(f32)).astype(bf16), 8)
-    z1 = swap((side1 + y1.astype(f32)).astype(bf16), 4)
+    sum2 = (side2 + y2.astype(f32) + z3.astype(f32)).astype(bf16)
+    z2 = swap(sum2, 8)
+    z1 = swap(later(side1, y1, sum2), 4)
     total = side0 + y0.astype(f32) + z1.astype(f32) + z2.astype(f32)
     return total.astype(bf16)
 

time: 65.8 us -> 62.9 us (0.956)
  local copies, waits for them, and re-layouts: 6.62 us -> 0.97 us
  Pallas kernels: 5.97 us -> 10.7 us
  waiting for transfers between devices: 28.8 us -> 26.7 us
    unnamed x14 -> x12, local copies, waits for them, and re-layouts: 6.62 us -> 0.97 us
    pallas_call x1, Pallas kernels: 2.34 us -> 6.97 us  [product(): pl.pallas_call(product_kernel, out_shape=(shape((chips, rows, width)), sh...]
    ppermute x17, waiting for transfers between devices: 28.8 us -> 26.7 us  [swap(): return lax.ppermute(value, 'tensor', [(t, t ^ mask) for t in range(count)])]
  transfers between devices with their start and end apart: 17 -> 17, of which waited for: 7 -> 11; matrix products, arithmetic and copies ran while one was open for 0% -> 0% of each run, Pallas kernels for 7% -> 15%
where the time goes in v4:
time: 62.9 us; the launch traced here: 62.8 us
  waiting for transfers between devices  26.7 us (42%)
  starting transfers between devices  23.3 us (37%)
  Pallas kernels  10.7 us (17%)
  other arithmetic  1.07 us (2%)
  local copies, waits for them, and re-layouts  0.97 us (2%)
    ppermute x17, waiting for transfers between devices, swap(): return lax.ppermute(value, 'tensor', [(t, t ^ mask) for t in range(count)])  26.7 us
    ppermute x17, starting transfers between devices, swap(): return lax.ppermute(value, 'tensor', [(t, t ^ mask) for t in range(count)])  23.3 us
    pallas_call x1, Pallas kernels, product(): pl.pallas_call(product_kernel, out_shape=(shape((chips, rows, width)), sh...  6.97 us
    pallas_call x3, Pallas kernels, join(): pl.pallas_call(functools.partial(join_kernel, chip_masks), out_shape=[sha...  1.71 us
  transfers between devices with their start and end apart: 17, of which 11 were waited for; matrix products, arithmetic and copies ran while one was open for 0% of the time, Pallas kernels for 15%

profile of v4, /device:TPU:0, one launch (start us, length us, event | category | flops | bytes accessed | tf_op | source)
XLA Modules:
  0.0 62.8 jit_solution(5681554977935024876)
XLA Ops:
  0.0 0.5 collective-permute-start
  0.5 0.0 copy-start.1
  0.5 0.9 %copy-done.1 = bf16[256,512]{1,0:T(8,128)(2,1)S(1)} copy-done((bf16[256,512]{1,0:T(8,128)(2,1)S(1)}, bf16[256,512]{1,0:T(8,128)(2,1)}, u32[]{:S(2)}) %copy-start.1) | copy-done | bytes 262168
  1.4 0.0 copy-start.2
  1.4 0.0 copy-start.3
  1.4 0.0 copy-start.4
  1.4 0.0 copy-start.5
  1.4 7.0 %product.1 = (bf16[8,256,512]{2,1,0:T(8,128)(2,1)S(1)}, f32[8,256,512]{2,1,0:T(8,128)}, f32[8,128]{1,0:T(8,128)S(1)}) custom-call(bf16[256,512]{1,0:T(8,128)(2,1)S(1)} %copy-done.1, bf16[512,8192]{1,0:T(8,128)(2,1)} %weight_hbm.1), custom_call_target="tpu_custom_call" | custom-call | flops 2147483648 | bytes 14680064 | tf_op jit(solution)/shard_map/product/pallas_call | solution.py:113
  8.4 0.0 collective-permute-done.other_ref
  8.4 0.0 copy-done.2
  8.4 0.0 copy-done.3
  8.4 1.0 %route.1 = (s32[1,256]{1,0:T(1,128)S(1)}, bf16[32,1024]{1,0:T(8,128)(2,1)S(1)}, bf16[32,1024]{1,0:T(8,128)(2,1)S(1)}, bf16[32,1024]{1,0:T(8,128)(2,1)S(1)}, bf16...) custom-call(s32[16]{0:T(128)S(1)} %copy-done.3, ...), custom_call_target="tpu_custom_call" | custom-call | flops 134217728 | bytes 1048576 | tf_op jit(solution)/shard_map/route/pallas_call | solution.py:73
  9.4 2.6 %collective-permute-start.2 = (bf16[32,1024]{1,0:T(8,128)(2,1)S(1)}, bf16[32,1024]{1,0:T(8,128)(2,1)S(1)}, u32[]{:S(2)}, u32[]{:S(2)}) collective-permute-start(bf16[32,1024]{1,0:T(8,128)(2,1)S(1)} %get-tuple-element.30), channel_id=1, source_target_pairs={{0,2},{1,3},{2,0},{3,1},{4,6},{5,7},{6,4},{7,5},{8,10},{9,11},{10,... | collective-permute-start | bytes 196616 | tf_op jit(solution)/shard_map/ppermute | solution.py:34
  12.0 1.6 %collective-permute-start.3 = (bf16[32,1024]{1,0:T(8,128)(2,1)S(1)}, bf16[32,1024]{1,0:T(8,128)(2,1)S(1)}, u32[]{:S(2)}, u32[]{:S(2)}) collective-permute-start(bf16[32,1024]{1,0:T(8,128)(2,1)S(1)} %get-tuple-element.31), channel_id=1, source_target_pairs={{0,4},{1,5},{2,6},{3,7},{4,0},{5,1},{6,2},{7,3},{8,12},{9,13},{10,... | collective-permute-start | bytes 196616 | tf_op jit(solution)/shard_map/ppermute | solution.py:34
  13.6 2.6 %collective-permute-start.4 = (bf16[32,1024]{1,0:T(8,128)(2,1)S(1)}, bf16[32,1024]{1,0:T(8,128)(2,1)S(1)}, u32[]{:S(2)}, u32[]{:S(2)}) collective-permute-start(bf16[32,1024]{1,0:T(8,128)(2,1)S(1)} %get-tuple-element.32), channel_id=1, source_target_pairs={{0,8},{1,9},{2,10},{3,11},{4,12},{5,13},{6,14},{7,15},{8,0},{9,1},... | collective-permute-start | bytes 196616 | tf_op jit(solution)/shard_map/ppermute | solution.py:34
  16.2 0.3 collective-permute-start.5
  16.5 2.5 %collective-permute-start.6 = (bf16[32,1024]{1,0:T(8,128)(2,1)S(1)}, bf16[32,1024]{1,0:T(8,128)(2,1)S(1)}, u32[]{:S(2)}, u32[]{:S(2)}) collective-permute-start(bf16[32,1024]{1,0:T(8,128)(2,1)S(1)} %get-tuple-element.34), channel_id=1, source_target_pairs={{0,12},{1,13},{2,14},{3,15},{4,8},{5,9},{6,10},{7,11},{8,4},{9,5},... | collective-permute-start | bytes 196616 | tf_op jit(solution)/shard_map/ppermute | solution.py:34
  18.9 0.0 collective-permute-done.2.refs_0_
  18.9 2.3 %collective-permute-start.7 = (bf16[32,1024]{1,0:T(8,128)(2,1)S(1)}, bf16[32,1024]{1,0:T(8,128)(2,1)S(1)}, u32[]{:S(2)}, u32[]{:S(2)}) collective-permute-start(bf16[32,1024]{1,0:T(8,128)(2,1)S(1)} %get-tuple-element.35), channel_id=1, source_target_pairs={{0,14},{1,15},{2,12},{3,13},{4,10},{5,11},{6,8},{7,9},{8,6},{9,7},... | collective-permute-start | bytes 196616 | tf_op jit(solution)/shard_map/ppermute | solution.py:34
  21.2 0.0 collective-permute-done.3.refs_1_
  21.3 0.0 collective-permute-start.8
  21.3 1.7 %collective-permute-done.4.refs_2_ = bf16[32,1024]{1,0:T(8,128)(2,1)S(1)} collective-permute-done((bf16[32,1024]{1,0:T(8,128)(2,1)S(1)}, bf16[32,1024]{1,0:T(8,128)(2,1)S(1)}, u32[]{:S(2)}, u32[]{:S(2)}) %collective-permute-start.4) | collective-permute-done | bytes 65568 | tf_op jit(solution)/shard_map/ppermute | solution.py:34
  23.0 0.0 collective-permute-start.1
  23.0 3.2 %collective-permute-done.5.refs_3_ = bf16[32,1024]{1,0:T(8,128)(2,1)S(1)} collective-permute-done((bf16[32,1024]{1,0:T(8,128)(2,1)S(1)}, bf16[32,1024]{1,0:T(8,128)(2,1)S(1)}, u32[]{:S(2)}, u32[]{:S(2)}) %collective-permute-start.5) | collective-permute-done | bytes 65568 | tf_op jit(solution)/shard_map/ppermute | solution.py:34
  26.1 0.0 collective-permute-done.6.refs_4_
  26.2 0.0 collective-permute-done.7.refs_5_
  26.2 1.0 %collective-permute-done.8.refs_6_ = bf16[32,1024]{1,0:T(8,128)(2,1)S(1)} collective-permute-done((bf16[32,1024]{1,0:T(8,128)(2,1)S(1)}, bf16[32,1024]{1,0:T(8,128)(2,1)S(1)}, u32[]{:S(2)}, u32[]{:S(2)}) %collective-permute-start.8) | collective-permute-done | bytes 65568 | tf_op jit(solution)/shard_map/ppermute | solution.py:34
  27.2 0.0 copy-done.4
  27.2 0.0 copy-done.5
  27.2 0.0 copy-start
  27.2 0.9 %adapter.1 = (bf16[8,32,512]{2,1,0:T(8,128)(2,1)S(1)}, bf16[8,32,512]{2,1,0:T(8,128)(2,1)S(1)}) custom-call(bf16[64,8192]{1,0:T(8,128)(2,1)S(1)} %bitcast.6, bf16[64,8192]{1,0:T(8,128)(2,1)S(1)} %bitcast.7, bf16[32,1024]{1,0:T(8,128)(2,1)S(1)} %collective-permute-done.2.refs_0_, bf16[32,1024]{1,0:T(8,128)(2,1)S(1)} %collective-permute-done.3.refs_1_, ...), custom_call_target="tpu_custom_call" | custom-call | flops 40000000000 | bytes 67108864 | tf_op jit(solution)/shard_map/adapter/pallas_call | solution.py:158
  28.1 0.1 collective-permute-start.9
  28.2 1.5 %collective-permute-done.9.far_ref = bf16[8,32,512]{2,1,0:T(8,128)(2,1)S(1)} collective-permute-done((bf16[8,32,512]{2,1,0:T(8,128)(2,1)S(1)}, bf16[8,32,512]{2,1,0:T(8,128)(2,1)S(1)}, u32[]{:S(2)}, u32[]{:S(2)}) %collective-permute-start.9) | collective-permute-done | bytes 262176 | tf_op jit(solution)/shard_map/ppermute | solution.py:34
  29.7 0.0 collective-permute-done.1.came_ref
  29.7 0.0 copy-done
  29.7 0.3 join.5
  30.0 1.3 %collective-permute-start.13 = (bf16[256,512]{1,0:T(8,128)(2,1)S(1)}, bf16[256,512]{1,0:T(8,128)(2,1)S(1)}, u32[]{:S(2)}, u32[]{:S(2)}) collective-permute-start(bf16[256,512]{1,0:T(8,128)(2,1)S(1)} %join.5), channel_id=1, source_target_pairs={{0,2},{1,3},{2,0},{3,1},{4,6},{5,7},{6,4},{7,5},{8,10},{9,11},{10,... | collective-permute-start | bytes 786440 | tf_op jit(solution)/shard_map/ppermute | solution.py:34
  31.4 0.6 join.4
  32.0 0.8 %collective-permute-start.12 = (bf16[256,512]{1,0:T(8,128)(2,1)S(1)}, bf16[256,512]{1,0:T(8,128)(2,1)S(1)}, u32[]{:S(2)}, u32[]{:S(2)}) collective-permute-start(bf16[256,512]{1,0:T(8,128)(2,1)S(1)} %get-tuple-element.45), channel_id=1, source_target_pairs={{0,2},{1,3},{2,0},{3,1},{4,6},{5,7},{6,4},{7,5},{8,10},{9,11},{10,... | collective-permute-start | bytes 786440 | tf_op jit(solution)/shard_map/ppermute | solution.py:34
  32.8 0.8 %join.3 = (f32[256,512]{1,0:T(8,128)S(1)}, f32[256,512]{1,0:T(8,128)S(1)}, f32[256,512]{1,0:T(8,128)S(1)}, f32[256,512]{1,0:T(8,128)S(1)}) custom-call(s32[1,256]{1,0:T(1,128)S(1)} %get-tuple-element.27.target_ref, f32[8,256,512]{2,1,0:T(8,128)S(1)} %copy-done, bf16[8,256,512]{2,1,0:T(8,128)(2,1)S(1)} %collective-permute-done.1.came_ref, ...), custom_call_target="tpu_custom_call" | custom-call | flops 67108864 | bytes 5242880 | tf_op jit(solution)/shard_map/join/pallas_call | solution.py:185
  33.6 5.7 %collective-permute-done.13 = bf16[256,512]{1,0:T(8,128)(2,1)S(1)} collective-permute-done((bf16[256,512]{1,0:T(8,128)(2,1)S(1)}, bf16[256,512]{1,0:T(8,128)(2,1)S(1)}, u32[]{:S(2)}, u32[]{:S(2)}) %collective-permute-start.13) | collective-permute-done | bytes 262176 | tf_op jit(solution)/shard_map/ppermute | solution.py:34
  39.3 0.1 add_convert_fusion.2
  39.3 2.1 %collective-permute-start.14 = (bf16[256,512]{1,0:T(8,128)(2,1)S(1)}, bf16[256,512]{1,0:T(8,128)(2,1)S(1)}, u32[]{:S(2)}, u32[]{:S(2)}) collective-permute-start(bf16[256,512]{1,0:T(8,128)(2,1)S(1)} %add_convert_fusion.2), channel_id=1, source_target_pairs={{0,4},{1,5},{2,6},{3,7},{4,0},{5,1},{6,2},{7,3},{8,12},{9,13},{10,... | collective-permute-start | bytes 786440 | tf_op jit(solution)/shard_map/ppermute | solution.py:34
  41.4 1.3 %collective-permute-start.11 = (bf16[256,512]{1,0:T(8,128)(2,1)S(1)}, bf16[256,512]{1,0:T(8,128)(2,1)S(1)}, u32[]{:S(2)}, u32[]{:S(2)}) collective-permute-start(bf16[256,512]{1,0:T(8,128)(2,1)S(1)} %get-tuple-element.43), channel_id=1, source_target_pairs={{0,2},{1,3},{2,0},{3,1},{4,6},{5,7},{6,4},{7,5},{8,10},{9,11},{10,... | collective-permute-start | bytes 786440 | tf_op jit(solution)/shard_map/ppermute | solution.py:34
  42.7 0.7 %collective-permute-start.10 = (bf16[256,512]{1,0:T(8,128)(2,1)S(1)}, bf16[256,512]{1,0:T(8,128)(2,1)S(1)}, u32[]{:S(2)}, u32[]{:S(2)}) collective-permute-start(bf16[256,512]{1,0:T(8,128)(2,1)S(1)} %get-tuple-element.41), channel_id=1, source_target_pairs={{0,2},{1,3},{2,0},{3,1},{4,6},{5,7},{6,4},{7,5},{8,10},{9,11},{10,... | collective-permute-start | bytes 786440 | tf_op jit(solution)/shard_map/ppermute | solution.py:34
  43.4 1.5 %collective-permute-done.12 = bf16[256,512]{1,0:T(8,128)(2,1)S(1)} collective-permute-done((bf16[256,512]{1,0:T(8,128)(2,1)S(1)}, bf16[256,512]{1,0:T(8,128)(2,1)S(1)}, u32[]{:S(2)}, u32[]{:S(2)}) %collective-permute-start.12) | collective-permute-done | bytes 262176 | tf_op jit(solution)/shard_map/ppermute | solution.py:34
  44.9 1.5 %collective-permute-done.14 = bf16[256,512]{1,0:T(8,128)(2,1)S(1)} collective-permute-done((bf16[256,512]{1,0:T(8,128)(2,1)S(1)}, bf16[256,512]{1,0:T(8,128)(2,1)S(1)}, u32[]{:S(2)}, u32[]{:S(2)}) %collective-permute-start.14) | collective-permute-done | bytes 262176 | tf_op jit(solution)/shard_map/ppermute | solution.py:34
  46.4 0.1 add_convert_fusion.1.after_ref
  46.5 2.8 %collective-permute-start.16 = (bf16[256,512]{1,0:T(8,128)(2,1)S(1)}, bf16[256,512]{1,0:T(8,128)(2,1)S(1)}, u32[]{:S(2)}, u32[]{:S(2)}) collective-permute-start(bf16[256,512]{1,0:T(8,128)(2,1)S(1)} %add_convert_fusion.1.after_ref), channel_id=1, source_target_pairs={{0,8},{1,9},{2,10},{3,11},{4,12},{5,13},{6,14},{7,15},{8,0},{9,1},... | collective-permute-start | bytes 786440 | tf_op jit(solution)/shard_map/ppermute | solution.py:34
  49.3 1.4 %collective-permute-done.11.came_ref = bf16[256,512]{1,0:T(8,128)(2,1)S(1)} collective-permute-done((bf16[256,512]{1,0:T(8,128)(2,1)S(1)}, bf16[256,512]{1,0:T(8,128)(2,1)S(1)}, u32[]{:S(2)}, u32[]{:S(2)}) %collective-permute-start.11) | collective-permute-done | bytes 262176 | tf_op jit(solution)/shard_map/ppermute | solution.py:34
  50.6 0.1 later.1
  50.7 1.9 %collective-permute-start.15 = (bf16[256,512]{1,0:T(8,128)(2,1)S(1)}, bf16[256,512]{1,0:T(8,128)(2,1)S(1)}, u32[]{:S(2)}, u32[]{:S(2)}) collective-permute-start(bf16[256,512]{1,0:T(8,128)(2,1)S(1)} %later.1), channel_id=1, source_target_pairs={{0,4},{1,5},{2,6},{3,7},{4,0},{5,1},{6,2},{7,3},{8,12},{9,13},{10,... | collective-permute-start | bytes 786440 | tf_op jit(solution)/shard_map/ppermute | solution.py:34
  52.6 2.7 %collective-permute-done.10 = bf16[256,512]{1,0:T(8,128)(2,1)S(1)} collective-permute-done((bf16[256,512]{1,0:T(8,128)(2,1)S(1)}, bf16[256,512]{1,0:T(8,128)(2,1)S(1)}, u32[]{:S(2)}, u32[]{:S(2)}) %collective-permute-start.10) | collective-permute-done | bytes 262176 | tf_op jit(solution)/shard_map/ppermute | solution.py:34
  55.3 3.9 %collective-permute-done.16 = bf16[256,512]{1,0:T(8,128)(2,1)S(1)} collective-permute-done((bf16[256,512]{1,0:T(8,128)(2,1)S(1)}, bf16[256,512]{1,0:T(8,128)(2,1)S(1)}, u32[]{:S(2)}, u32[]{:S(2)}) %collective-permute-start.16) | collective-permute-done | bytes 262176 | tf_op jit(solution)/shard_map/ppermute | solution.py:34
  59.2 2.7 %collective-permute-done.15 = bf16[256,512]{1,0:T(8,128)(2,1)S(1)} collective-permute-done((bf16[256,512]{1,0:T(8,128)(2,1)S(1)}, bf16[256,512]{1,0:T(8,128)(2,1)S(1)}, u32[]{:S(2)}, u32[]{:S(2)}) %collective-permute-start.15) | collective-permute-done | bytes 262176 | tf_op jit(solution)/shard_map/ppermute | solution.py:34
  61.9 0.9 %add_convert_fusion = bf16[256,512]{1,0:T(8,128)(2,1)} fusion(bf16[256,512]{1,0:T(8,128)(2,1)S(1)} %collective-permute-done.16, bf16[256,512]{1,0:T(8,128)(2,1)S(1)} %collective-permute-done.15, f32[256,512]{1,0:T(8,128)S(1)} %get-tuple-element.40, bf16[256,512]{1,0:T(8,128)(2,1)S(1)} %collective-permute-done.10), kind=kLoop, calls=%fused_computation | loop fusion | flops 917504 | bytes 1572864 | tf_op jit(solution)/shard_map/convert_element_type | solution.py:232
Async XLA Ops:
  0.0 8.4 %collective-permute-start = (bf16[256,512]{1,0:T(8,128)(2,1)}, bf16[256,512]{1,0:T(8,128)(2,1)S(1)}, u32[]{:S(2)}, u32[]{:S(2)}) collective-permute-start(bf16[256,512]{1,0:T(8,128)(2,1)} %own_ref.1), channel_id=1, source_target_pairs={{0,1},{1,0},{2,3},{3,2},{4,5},{5,4},{6,7},{7,6},{8,9},{9,8},{10,11... | collective-permute-start | bytes 786440 | tf_op jit(solution)/shard_map/ppermute | solution.py:34
  0.5 0.9 %copy-start.1 = (bf16[256,512]{1,0:T(8,128)(2,1)S(1)}, bf16[256,512]{1,0:T(8,128)(2,1)}, u32[]{:S(2)}) copy-start(bf16[256,512]{1,0:T(8,128)(2,1)} %own_ref.1) | copy-start | bytes 786436
  1.4 7.0 %copy-start.2 = (s32[256]{0:T(256)S(1)}, s32[256]{0:T(256)}, u32[]{:S(2)}) copy-start(s32[256]{0:T(256)} %param.10) | copy-start | bytes 3076
  1.4 7.0 %copy-start.3 = (s32[16]{0:T(128)S(1)}, s32[16]{0:T(128)}, u32[]{:S(2)}) copy-start(s32[16]{0:T(128)} %slot_hbm.1) | copy-start | bytes 196
  1.4 25.7 %copy-start.4 = (bf16[1,8192,64]{1,2,0:T(8,128)(2,1)S(1)}, bf16[1,8192,64]{1,2,0:T(8,128)(2,1)}, u32[]{:S(2)}) copy-start(bf16[1,8192,64]{1,2,0:T(8,128)(2,1)} %param.8) | copy-start | bytes 3145732
  1.4 25.7 %copy-start.5 = (bf16[1,64,8192]{2,1,0:T(8,128)(2,1)S(1)}, bf16[1,64,8192]{2,1,0:T(8,128)(2,1)}, u32[]{:S(2)}) copy-start(bf16[1,64,8192]{2,1,0:T(8,128)(2,1)} %param.9) | copy-start | bytes 3145732
  9.4 9.5 %collective-permute-start.2 = (bf16[32,1024]{1,0:T(8,128)(2,1)S(1)}, bf16[32,1024]{1,0:T(8,128)(2,1)S(1)}, u32[]{:S(2)}, u32[]{:S(2)}) collective-permute-start(bf16[32,1024]{1,0:T(8,128)(2,1)S(1)} %get-tuple-element.30), channel_id=1, source_target_pairs={{0,2},{1,3},{2,0},{3,1},{4,6},{5,7},{6,4},{7,5},{8,10},{9,11},{10,... | collective-permute-start | bytes 196616 | tf_op jit(solution)/shard_map/ppermute | solution.py:34
  12.0 9.2 %collective-permute-start.3 = (bf16[32,1024]{1,0:T(8,128)(2,1)S(1)}, bf16[32,1024]{1,0:T(8,128)(2,1)S(1)}, u32[]{:S(2)}, u32[]{:S(2)}) collective-permute-start(bf16[32,1024]{1,0:T(8,128)(2,1)S(1)} %get-tuple-element.31), channel_id=1, source_target_pairs={{0,4},{1,5},{2,6},{3,7},{4,0},{5,1},{6,2},{7,3},{8,12},{9,13},{10,... | collective-permute-start | bytes 196616 | tf_op jit(solution)/shard_map/ppermute | solution.py:34
  13.6 9.4 %collective-permute-start.4 = (bf16[32,1024]{1,0:T(8,128)(2,1)S(1)}, bf16[32,1024]{1,0:T(8,128)(2,1)S(1)}, u32[]{:S(2)}, u32[]{:S(2)}) collective-permute-start(bf16[32,1024]{1,0:T(8,128)(2,1)S(1)} %get-tuple-element.32), channel_id=1, source_target_pairs={{0,8},{1,9},{2,10},{3,11},{4,12},{5,13},{6,14},{7,15},{8,0},{9,1},... | collective-permute-start | bytes 196616 | tf_op jit(solution)/shard_map/ppermute | solution.py:34
  16.2 10.0 %collective-permute-start.5 = (bf16[32,1024]{1,0:T(8,128)(2,1)S(1)}, bf16[32,1024]{1,0:T(8,128)(2,1)S(1)}, u32[]{:S(2)}, u32[]{:S(2)}) collective-permute-start(bf16[32,1024]{1,0:T(8,128)(2,1)S(1)} %get-tuple-element.33), channel_id=1, source_target_pairs={{0,10},{1,11},{2,8},{3,9},{4,14},{5,15},{6,12},{7,13},{8,2},{9,3},... | collective-permute-start | bytes 196616 | tf_op jit(solution)/shard_map/ppermute | solution.py:34
  16.5 9.7 %collective-permute-start.6 = (bf16[32,1024]{1,0:T(8,128)(2,1)S(1)}, bf16[32,1024]{1,0:T(8,128)(2,1)S(1)}, u32[]{:S(2)}, u32[]{:S(2)}) collective-permute-start(bf16[32,1024]{1,0:T(8,128)(2,1)S(1)} %get-tuple-element.34), channel_id=1, source_target_pairs={{0,12},{1,13},{2,14},{3,15},{4,8},{5,9},{6,10},{7,11},{8,4},{9,5},... | collective-permute-start | bytes 196616 | tf_op jit(solution)/shard_map/ppermute | solution.py:34
  18.9 7.2 %collective-permute-start.7 = (bf16[32,1024]{1,0:T(8,128)(2,1)S(1)}, bf16[32,1024]{1,0:T(8,128)(2,1)S(1)}, u32[]{:S(2)}, u32[]{:S(2)}) collective-permute-start(bf16[32,1024]{1,0:T(8,128)(2,1)S(1)} %get-tuple-element.35), channel_id=1, source_target_pairs={{0,14},{1,15},{2,12},{3,13},{4,10},{5,11},{6,8},{7,9},{8,6},{9,7},... | collective-permute-start | bytes 196616 | tf_op jit(solution)/shard_map/ppermute | solution.py:34
  21.3 5.9 %collective-permute-start.8 = (bf16[32,1024]{1,0:T(8,128)(2,1)S(1)}, bf16[32,1024]{1,0:T(8,128)(2,1)S(1)}, u32[]{:S(2)}, u32[]{:S(2)}) collective-permute-start(bf16[32,1024]{1,0:T(8,128)(2,1)S(1)} %get-tuple-element.36), channel_id=1, source_target_pairs={{0,6},{1,7},{2,4},{3,5},{4,2},{5,3},{6,0},{7,1},{8,14},{9,15},{10,... | collective-permute-start | bytes 196616 | tf_op jit(solution)/shard_map/ppermute | solution.py:34
  23.0 6.7 %collective-permute-start.1 = (bf16[8,256,512]{2,1,0:T(8,128)(2,1)S(1)}, bf16[8,256,512]{2,1,0:T(8,128)(2,1)S(1)}, u32[]{:S(2)}, u32[]{:S(2)}) collective-permute-start(bf16[8,256,512]{2,1,0:T(8,128)(2,1)S(1)} %get-tuple-element.29), channel_id=1, source_target_pairs={{0,1},{1,0},{2,3},{3,2},{4,5},{5,4},{6,7},{7,6},{8,9},{9,8},{10,11... | collective-permute-start | bytes 6291464 | tf_op jit(solution)/shard_map/ppermute | solution.py:34
  27.2 2.5 %copy-start = (f32[8,256,512]{2,1,0:T(8,128)S(1)}, f32[8,256,512]{2,1,0:T(8,128)}, u32[]{:S(2)}) copy-start(f32[8,256,512]{2,1,0:T(8,128)} %get-tuple-element.28.stay_ref) | copy-start | bytes 12582916
  28.1 1.6 %collective-permute-start.9 = (bf16[8,32,512]{2,1,0:T(8,128)(2,1)S(1)}, bf16[8,32,512]{2,1,0:T(8,128)(2,1)S(1)}, u32[]{:S(2)}, u32[]{:S(2)}) collective-permute-start(bf16[8,32,512]{2,1,0:T(8,128)(2,1)S(1)} %get-tuple-element.39), channel_id=1, source_target_pairs={{0,1},{1,0},{2,3},{3,2},{4,5},{5,4},{6,7},{7,6},{8,9},{9,8},{10,11... | collective-permute-start | bytes 786440 | tf_op jit(solution)/shard_map/ppermute | solution.py:34
  30.0 9.2 %collective-permute-start.13 = (bf16[256,512]{1,0:T(8,128)(2,1)S(1)}, bf16[256,512]{1,0:T(8,128)(2,1)S(1)}, u32[]{:S(2)}, u32[]{:S(2)}) collective-permute-start(bf16[256,512]{1,0:T(8,128)(2,1)S(1)} %join.5), channel_id=1, source_target_pairs={{0,2},{1,3},{2,0},{3,1},{4,6},{5,7},{6,4},{7,5},{8,10},{9,11},{10,... | collective-permute-start | bytes 786440 | tf_op jit(solution)/shard_map/ppermute | solution.py:34
  32.0 12.9 %collective-permute-start.12 = (bf16[256,512]{1,0:T(8,128)(2,1)S(1)}, bf16[256,512]{1,0:T(8,128)(2,1)S(1)}, u32[]{:S(2)}, u32[]{:S(2)}) collective-permute-start(bf16[256,512]{1,0:T(8,128)(2,1)S(1)} %get-tuple-element.45), channel_id=1, source_target_pairs={{0,2},{1,3},{2,0},{3,1},{4,6},{5,7},{6,4},{7,5},{8,10},{9,11},{10,... | collective-permute-start | bytes 786440 | tf_op jit(solution)/shard_map/ppermute | solution.py:34
  39.3 7.0 %collective-permute-start.14 = (bf16[256,512]{1,0:T(8,128)(2,1)S(1)}, bf16[256,512]{1,0:T(8,128)(2,1)S(1)}, u32[]{:S(2)}, u32[]{:S(2)}) collective-permute-start(bf16[256,512]{1,0:T(8,128)(2,1)S(1)} %add_convert_fusion.2), channel_id=1, source_target_pairs={{0,4},{1,5},{2,6},{3,7},{4,0},{5,1},{6,2},{7,3},{8,12},{9,13},{10,... | collective-permute-start | bytes 786440 | tf_op jit(solution)/shard_map/ppermute | solution.py:34
  41.4 9.2 %collective-permute-start.11 = (bf16[256,512]{1,0:T(8,128)(2,1)S(1)}, bf16[256,512]{1,0:T(8,128)(2,1)S(1)}, u32[]{:S(2)}, u32[]{:S(2)}) collective-permute-start(bf16[256,512]{1,0:T(8,128)(2,1)S(1)} %get-tuple-element.43), channel_id=1, source_target_pairs={{0,2},{1,3},{2,0},{3,1},{4,6},{5,7},{6,4},{7,5},{8,10},{9,11},{10,... | collective-permute-start | bytes 786440 | tf_op jit(solution)/shard_map/ppermute | solution.py:34
  42.7 12.6 %collective-permute-start.10 = (bf16[256,512]{1,0:T(8,128)(2,1)S(1)}, bf16[256,512]{1,0:T(8,128)(2,1)S(1)}, u32[]{:S(2)}, u32[]{:S(2)}) collective-permute-start(bf16[256,512]{1,0:T(8,128)(2,1)S(1)} %get-tuple-element.41), channel_id=1, source_target_pairs={{0,2},{1,3},{2,0},{3,1},{4,6},{5,7},{6,4},{7,5},{8,10},{9,11},{10,... | collective-permute-start | bytes 786440 | tf_op jit(solution)/shard_map/ppermute | solution.py:34
  46.5 12.7 %collective-permute-start.16 = (bf16[256,512]{1,0:T(8,128)(2,1)S(1)}, bf16[256,512]{1,0:T(8,128)(2,1)S(1)}, u32[]{:S(2)}, u32[]{:S(2)}) collective-permute-start(bf16[256,512]{1,0:T(8,128)(2,1)S(1)} %add_convert_fusion.1.after_ref), channel_id=1, source_target_pairs={{0,8},{1,9},{2,10},{3,11},{4,12},{5,13},{6,14},{7,15},{8,0},{9,1},... | collective-permute-start | bytes 786440 | tf_op jit(solution)/shard_map/ppermute | solution.py:34
  50.7 11.2 %collective-permute-start.15 = (bf16[256,512]{1,0:T(8,128)(2,1)S(1)}, bf16[256,512]{1,0:T(8,128)(2,1)S(1)}, u32[]{:S(2)}, u32[]{:S(2)}) collective-permute-start(bf16[256,512]{1,0:T(8,128)(2,1)S(1)} %later.1), channel_id=1, source_target_pairs={{0,4},{1,5},{2,6},{3,7},{4,0},{5,1},{6,2},{7,3},{8,12},{9,13},{10,... | collective-permute-start | bytes 786440 | tf_op jit(solution)/shard_map/ppermute | solution.py:34

commit v5 on v0

--- a/solution.py
+++ b/solution.py
@@ -1,12 +1,293 @@
+import functools
+
 import jax
 import jax.numpy as jnp
 from jax import lax
+from jax.experimental import pallas as pl
+from jax.experimental.pallas import tpu as pltpu
 from jax.sharding import PartitionSpec as P
 
 CAP = 32
-
-
-def shards(attended, out_weight, adapter_down, adapter_up, row_adapter, adapter_slot):
+IN_VMEM = pl.BlockSpec(memory_space=pltpu.VMEM)
+IN_HBM = pl.BlockSpec(memory_space=pltpu.HBM)
+ANYWHERE = pl.BlockSpec(memory_space=pl.ANY)
+DMA = pltpu.SemaphoreType.DMA
+
+
+def params(mib):
+    return pltpu.CompilerParams(vmem_limit_bytes=mib * 1024 * 1024)
+
+
+def cost(flops, moved):
+    return pl.CostEstimate(flops=flops, bytes_accessed=moved, transcendentals=0)
+
+
+def shape(dims, dtype=jnp.bfloat16):
+    return jax.ShapeDtypeStruct(dims, dtype)
+
+
+def dot(a, b):
+    return jnp.dot(a, b, preferred_element_type=jnp.float32)
+
+
+def swap(value, mask):
+    count = lax.axis_size("tensor")
+    return lax.ppermute(value, "tensor", [(t, t ^ mask) for t in range(count)])
+
+
+def route_kernel(count, layers, slot_hbm, row_ref, own_ref, y_ref, *rest):
+    target_ref, out_refs = rest[-4 - layers], rest[-3 - layers : -3]
+    slot_ref, slot_sem = rest[-2:]
+    rows, width = own_ref.shape
+    me = lax.axis_index("tensor")
+    fetch = pltpu.make_async_copy(slot_hbm, slot_ref, slot_sem)
+    fetch.start()
+    fetch.wait()
+    ids = row_ref[...]
+    owner = jnp.zeros_like(ids)
+    for a in range(slot_ref.shape[0]):
+        owner = jnp.where(ids == a, slot_ref[a], owner)
+    hot = (lax.broadcasted_iota(jnp.int32, (count, rows), 0) == owner).astype(jnp.float32)
+    earlier = (
+        lax.broadcasted_iota(jnp.int32, (rows, rows), 0)
+        < lax.broadcasted_iota(jnp.int32, (rows, rows), 1)
+    ).astype(jnp.bfloat16)
+    ahead = dot(hot.astype(jnp.bfloat16), earlier)
+    place = jnp.sum(ahead * hot, axis=0, keepdims=True).astype(jnp.int32)
+    target = owner * CAP + place
+    target_ref[...] = target
+    j = lax.broadcasted_iota(jnp.int32, (2 * CAP, rows), 0)
+    for k in range(layers):
+        slots = (me ^ (4 * k) ^ (j // CAP)) * CAP + j % CAP
+        select = (slots == target).astype(jnp.bfloat16)
+        out_refs[k][:, :width] = dot(select, own_ref[...]).astype(jnp.bfloat16)
+        out_refs[k][:, width:] = dot(select, y_ref[...]).astype(jnp.bfloat16)
+
+
+def route(adapter_slot, row_adapter, own, y, passed, *after):
+    rows, width = own.shape
+    count = lax.axis_size("tensor")
+    layers = count // 4
+    found = pl.pallas_call(
+        functools.partial(route_kernel, count, layers),
+        out_shape=[shape((1, rows), jnp.int32)]
+        + [shape((2 * CAP, 2 * width))] * layers
+        + [shape(passed.shape, passed.dtype)],
+        in_specs=[IN_HBM] + [IN_VMEM] * 3 + [ANYWHERE] * (1 + len(after)),
+        out_specs=[IN_VMEM] * (layers + 1) + [ANYWHERE],
+        input_output_aliases={4: layers + 1},
+        scratch_shapes=[pltpu.SMEM(adapter_slot.shape, jnp.int32), DMA(())],
+        compiler_params=params(16),
+        cost_estimate=cost(8 * layers * CAP * rows * width, 16 * layers * CAP * width),
+        name="route",
+    )(adapter_slot, row_adapter[None, :], own, y, passed, *after)
+    return found[0], found[1:-1], found[-1]
+
+
+def product_kernel(groups, attended_hbm, weight_hbm, *refs):
+    token_ref, attended_ref, weight_ref, sems = refs[-4:]
+    chips = [m for group in groups for m in group]
+    width = weight_ref.shape[2] // 2
+    me = lax.axis_index("tensor")
+    core, chip = me % 2, me // 2
+    fetches = [pltpu.make_async_copy(attended_hbm, attended_ref, sems.at[len(chips)])]
+    for i, m in enumerate(chips):
+        start = pl.multiple_of((chip ^ m) * 2 * width, 2 * width)
+        fetches.append(
+            pltpu.make_async_copy(weight_hbm.at[:, pl.ds(start, 2 * width)], weight_ref.at[i], sems.at[i])
+        )
+    for fetch in fetches:
+        fetch.start()
+    token_ref[...] = jnp.zeros(token_ref.shape, token_ref.dtype)
+    fetches[0].wait()
+    there = pl.ds(pl.multiple_of((1 - core) * width, width), width)
+    here = pl.ds(pl.multiple_of(core * width, width), width)
+    at = 0
+    for g, group in enumerate(groups):
+        away_ref, stay_ref = refs[2 * g : 2 * g + 2]
+        for i in range(len(group)):
+            fetches[at + 1].wait()
+            away_ref[i] = dot(attended_ref[...], weight_ref[at, :, there]).astype(jnp.bfloat16)
+            stay_ref[i] = dot(attended_ref[...], weight_ref[at, :, here])
+            at += 1
+
+
+def product(attended, out_weight, groups, mib):
+    rows, depth = attended.shape
+    width = out_weight.shape[1] // lax.axis_size("tensor")
+    n = sum(len(group) for group in groups)
+    out_shape = []
+    for group in groups:
+        out_shape.append(shape((len(group), rows, width)))
+        out_shape.append(shape((len(group), rows, width), jnp.float32))
+    out_shape.append(shape((8, 128), jnp.float32))
+    return pl.pallas_call(
+        functools.partial(product_kernel, groups),
+        out_shape=out_shape,
+        in_specs=[IN_HBM, IN_HBM],
+        out_specs=[IN_VMEM] * len(out_shape),
+        scratch_shapes=[
+            pltpu.VMEM((rows, depth), jnp.bfloat16),
+            pltpu.VMEM((n, depth, 2 * width), jnp.bfloat16),
+            DMA((n + 1,)),
+        ],
+        compiler_params=params(mib),
+        cost_estimate=cost(4 * n * rows * depth * width, n * (4 * depth * width + 6 * rows * width)),
+        name="product",
+    )(attended, out_weight)
+
+
+def shrink_kernel(layers, down_ref, other_ref, *refs):
+    arrived_refs, out_ref = refs[:layers], refs[-1]
+    me = lax.axis_index("tensor")
+    width = arrived_refs[0].shape[1] // 2
+    over = (((1,), (1,)), ((), ()))
+    for part, weights_ref in enumerate((down_ref, other_ref)):
+        total = jnp.zeros((CAP, down_ref.shape[0]), jnp.float32)
+        for k, arrived_ref in enumerate(arrived_refs):
+            for side in range(2):
+                block = pl.ds(pl.multiple_of((me ^ (4 * k + 2 * side)) * width, width), width)
+                total += lax.dot_general(
+                    arrived_ref[part * CAP : (part + 1) * CAP, side * width : (side + 1) * width],
+                    weights_ref[:, block],
+                    over,
+                    preferred_element_type=jnp.float32,
+                )
+        out_ref[part * CAP : (part + 1) * CAP, :] = total
+
+
+def shrink(down, other, arrived, *after):
+    return pl.pallas_call(
+        functools.partial(shrink_kernel, len(arrived)),
+        out_shape=shape((2 * CAP, down.shape[0]), jnp.float32),
+        in_specs=[IN_VMEM] * (2 + len(arrived)) + [ANYWHERE] * len(after),
+        out_specs=IN_VMEM,
+        compiler_params=params(16),
+        cost_estimate=cost(40 * 10**9, 4 * down.size),
+        name="shrink",
+    )(down, other, *arrived, *after)
+
+
+def grow_kernel(groups, mine_ref, other_ref, up_ref, up_other_ref, *refs):
+    out_refs = refs[-len(groups) :]
+    me = lax.axis_index("tensor")
+    own = (mine_ref[:CAP, :] + other_ref[CAP:, :]).astype(jnp.bfloat16)
+    others = (mine_ref[CAP:, :] + other_ref[:CAP, :]).astype(jnp.bfloat16)
+    for masks, out_ref in zip(groups, out_refs):
+        width = out_ref.shape[2]
+        for i, mask in enumerate(masks):
+            block = pl.ds(pl.multiple_of((me ^ mask) * width, width), width)
+            out_ref[i, :CAP, :] = dot(own, up_ref[:, block]).astype(jnp.bfloat16)
+            out_ref[i, CAP:, :] = dot(others, up_other_ref[:, block]).astype(jnp.bfloat16)
+
+
+def grow(mine, other, up, up_other, groups, *after):
+    width = up.shape[1] // lax.axis_size("tensor")
+    return pl.pallas_call(
+        functools.partial(grow_kernel, groups),
+        out_shape=[shape((len(masks), 2 * CAP, width)) for masks in groups],
+        in_specs=[IN_VMEM] * 4 + [ANYWHERE] * len(after),
+        out_specs=[IN_VMEM] * len(groups),
+        compiler_params=params(16),
+        cost_estimate=cost(4 * CAP * up.size, 4 * up.size),
+        name="grow",
+    )(mine, other, up, up_other, *after)
+
+
+def join_kernel(terms, target_ref, *refs):
+    out_refs = refs[-len(terms) :]
+    rows = target_ref.shape[1]
+    me = lax.axis_index("tensor")
+    j = lax.broadcasted_iota(jnp.int32, (2 * CAP, rows), 0)
+    picks = {}
+    for (blocks, grown), out_ref in zip(terms, out_refs):
+        total = jnp.zeros(out_ref.shape, jnp.float32)
+        for at, i in blocks:
+            total += refs[at][i].astype(jnp.float32)
+        for at, i, mask in grown:
+            if mask not in picks:
+                slots = (me ^ mask ^ (j // CAP)) * CAP + j % CAP
+                picks[mask] = (slots == target_ref[...]).astype(jnp.bfloat16)
+            total += lax.dot_general(
+                picks[mask], refs[at][i], (((0,), (0,)), ((), ())), preferred_element_type=jnp.float32
+            )
+        out_ref[...] = total.astype(out_ref.dtype)
+
+
+def join(target, operands, terms, dtype):
+    rows, width = target.shape[1], operands[0].shape[2]
+    n = len(terms)
+    return pl.pallas_call(
+        functools.partial(join_kernel, terms),
+        out_shape=[shape((rows, width), dtype)] * n,
+        in_specs=[IN_VMEM] * (1 + len(operands)),
+        out_specs=[IN_VMEM] * n,
+        compiler_params=params(24),
+        cost_estimate=cost(4 * n * CAP * rows * width, 10 * n * rows * width),
+        name="join",
+    )(target, *operands)
+
+
+def later_kernel(side_ref, came_ref, after_ref, out_ref):
+    out_ref[...] = (side_ref[...] + came_ref[...].astype(jnp.float32)).astype(jnp.bfloat16)
+
+
+def later(side, came, after):
+    return pl.pallas_call(
+        later_kernel,
+        out_shape=shape(side.shape),
+        in_specs=[IN_VMEM] * 3,
+        out_specs=IN_VMEM,
+        compiler_params=params(16),
+        cost_estimate=cost(2 * side.size, 8 * side.size),
+        name="later",
+    )(side, came, after)
+
+
+def staged(attended, out_weight, adapter_down, adapter_up, row_adapter, adapter_slot):
+    f32, bf16 = jnp.float32, jnp.bfloat16
+    up, down = adapter_up[0], jnp.swapaxes(adapter_down, 1, 2)[0]
+    from_y = swap(attended, 2)
+    down_other, up_other = swap(down, 1), swap(up, 1)
+    chips = (6, 4, 3, 2, 1, 0)
+    away_first, stay_first, away, stay, token = product(attended, out_weight, ((7, 5), chips), 44)
+    target, outgoing, away_first = route(
+        adapter_slot, row_adapter, attended, from_y, away_first, token, down_other, up_other
+    )
+    arrived = [outgoing[0]] + [None] * 3
+    for k in (2, 3, 1):
+        arrived[k] = swap(outgoing[k], 4 * k)
+    came_first = swap(away_first, 1)
+    go3 = (stay_first[0] + came_first[0].astype(f32)).astype(bf16)
+    go2 = (stay_first[1] + came_first[1].astype(f32)).astype(bf16)
+    y3, y2 = swap(go3, 2)[None], swap(go2, 2)[None]
+    came = swap(away, 1)
+    mine = shrink(down, down_other, arrived)
+    here, over = grow(mine, swap(mine, 1), up, up_other, (tuple(2 * m for m in chips), (14, 10)), y3, y2)
+    over = swap(over, 2)
+    at = {m: i for i, m in enumerate(chips)}
+
+    def blocks(m):
+        return ((0, at[m]), (1, at[m])), ((2, at[m], 0),)
+
+    def early(m, i):
+        base, grown = blocks(m)
+        return base + ((4 + i, 0),), grown + ((3, i, 2),)
+
+    go1, go0 = join(target, [stay, came, here], (blocks(3), blocks(1)), bf16)
+    y1, y0 = swap(go1, 2), swap(go0, 2)
+    (sum3,) = join(target, [stay, came, here, over, y3], (early(6, 0),), bf16)
+    z3 = swap(sum3, 4)
+    (side2,) = join(target, [stay, came, here, over, y3, y2], (early(4, 1),), f32)
+    side1, side0 = join(target, [stay, came, here], (blocks(2), blocks(0)), f32)
+    sum2 = (side2 + z3.astype(f32)).astype(bf16)
+    z2 = swap(sum2, 8)
+    z1 = swap(later(side1, y1, sum2), 4)
+    total = side0 + y0.astype(f32) + z1.astype(f32) + z2.astype(f32)
+    return total.astype(bf16)
+
+
+def general(attended, out_weight, adapter_down, adapter_up, row_adapter, adapter_slot):
     tensor_size = lax.axis_size("tensor")
     device = lax.axis_index("tensor")
     row_count = attended.shape[0]
@@ -47,6 +328,12 @@
     return (base_out + delta_out.astype(jnp.float32)).astype(jnp.bfloat16)
 
 
+def shards(*arrays):
+    if lax.axis_size("tensor") == 16 and arrays[2].shape[0] == 1:
+        return staged(*arrays)
+    return general(*arrays)
+
+
 def solution(mesh):
     placed = (
         P("groups", "tensor"),

time: 151 us -> 58 us (0.38)
  waiting for transfers between devices: 68.8 us -> 26.9 us
  other arithmetic: 31.9 us -> 1.07 us
  between operations: 13.5 us -> 0.13 us
  matrix products: 10 us -> 0 us
  Pallas kernels: 0 us -> 8.13 us
  local copies, waits for them, and re-layouts: 8.71 us -> 1 us
  starting transfers between devices: 17.2 us -> 20.6 us
    all_to_all x2 -> x0, waiting for transfers between devices: 36.7 us -> none  [the longest x1 22.2 us: shards(): lax.all_to_all(outgoing, 'tensor', split_axis=0, concat_axis=1, tiled=True)]
    reduce_scatter x1 -> x0, waiting for transfers between devices: 32.1 us -> none  [shards(): lax.psum_scatter(partial_value, 'tensor', scatter_dimension=1, tiled=True)]
    ppermute x0 -> x17, waiting for transfers between devices: none -> 26.9 us  [swap(): return lax.ppermute(value, 'tensor', [(t, t ^ mask) for t in range(count)])]
    ppermute x0 -> x17, starting transfers between devices: none -> 20.6 us  [swap(): return lax.ppermute(value, 'tensor', [(t, t ^ mask) for t in range(count)])]
    all_to_all x2 -> x0, starting transfers between devices: 17.2 us -> none  [the longest x1 9.77 us: shards(): lax.all_to_all(expanded, 'tensor', split_axis=1, concat_axis=0, tiled=True)]
    dot_general x2 -> x0, matrix products: 10 us -> none  [the longest x1 9.13 us: shards(): jnp.dot(attended, out_weight, preferred_element_type=jnp.float32)]
    gather x4 -> x0, other arithmetic: 9.79 us -> none  [the longest x1 9.77 us: shards(): storage = adapter_slot[row_adapter]]
    add x1 -> x0, other arithmetic: 9.74 us -> none  [shards(): target = owner_of * CAP + position]
  transfers between devices with their start and end apart: 3 -> 17, of which waited for: 3 -> 11; matrix products, arithmetic and copies ran while one was open for 26% -> 0% of each run, Pallas kernels for 0% -> 11%
where the time goes in v5:
time: 58 us; the launch traced here: 57.8 us
  waiting for transfers between devices  26.9 us (46%)
  starting transfers between devices  20.6 us (36%)
  Pallas kernels  8.13 us (14%)
  other arithmetic  1.07 us (2%)
  local copies, waits for them, and re-layouts  1 us (2%)
    ppermute x17, waiting for transfers between devices, swap(): return lax.ppermute(value, 'tensor', [(t, t ^ mask) for t in range(count)])  26.9 us
    ppermute x17, starting transfers between devices, swap(): return lax.ppermute(value, 'tensor', [(t, t ^ mask) for t in range(count)])  20.6 us
    pallas_call x1, Pallas kernels, product(): pl.pallas_call(functools.partial(product_kernel, groups), out_shape=out_s...  4.85 us
    pallas_call x4, Pallas kernels, join(): pl.pallas_call(functools.partial(join_kernel, terms), out_shape=[shape((r...  1.33 us
    pallas_call x1, Pallas kernels, route(): pl.pallas_call(functools.partial(route_kernel, count, layers), out_shape=...  1.21 us
  transfers between devices with their start and end apart: 17, of which 11 were waited for; matrix products, arithmetic and copies ran while one was open for 0% of the time, Pallas kernels for 11%

profile of v5, /device:TPU:0, one launch (start us, length us, event | category | flops | bytes accessed | tf_op | source)
XLA Modules:
  0.0 57.8 jit_solution(10604751609832830364)
XLA Ops:
  0.0 0.5 collective-permute-start.1
  0.5 0.0 copy-start.2
  0.5 0.0 copy-start.3
  0.5 0.1 collective-permute-start.2
  0.5 3.0 %collective-permute-start = (bf16[256,512]{1,0:T(8,128)(2,1)}, bf16[256,512]{1,0:T(8,128)(2,1)S(1)}, u32[]{:S(2)}, u32[]{:S(2)}) collective-permute-start(bf16[256,512]{1,0:T(8,128)(2,1)} %own_ref.1), channel_id=1, source_target_pairs={{0,2},{1,3},{2,0},{3,1},{4,6},{5,7},{6,4},{7,5},{8,10},{9,11},{10,... | collective-permute-start | bytes 786440 | tf_op jit(solution)/shard_map/ppermute | solution.py:35
  3.5 0.0 copy-start
  3.5 1.0 %copy-done = bf16[256,512]{1,0:T(8,128)(2,1)S(1)} copy-done((bf16[256,512]{1,0:T(8,128)(2,1)S(1)}, bf16[256,512]{1,0:T(8,128)(2,1)}, u32[]{:S(2)}) %copy-start) | copy-done | bytes 262168
  4.5 4.9 %product.1 = (bf16[2,256,512]{2,1,0:T(8,128)(2,1)S(1)}, f32[2,256,512]{2,1,0:T(8,128)S(1)}, bf16[6,256,512]{2,1,0:T(8,128)(2,1)S(1)}, f32[6,256,512]{2,1,0:T(8,128)S(1)}, f32[8,128]{1,0:T(8,128)S(1)}) custom-call(bf16[256,512]{1,0:T(8,128)(2,1)S(1)} %copy-done, bf16[512,8192]{1,0:T(8,128)(2,1)} %weight_hbm.1), custom_call_target="tpu_custom_call" | custom-call | flops 2147483648 | bytes 14680064 | tf_op jit(solution)/shard_map/product/pallas_call | solution.py:124
  9.3 0.0 copy-start.4
  9.3 0.9 %collective-permute-done.y_ref = bf16[256,512]{1,0:T(8,128)(2,1)S(1)} collective-permute-done((bf16[256,512]{1,0:T(8,128)(2,1)}, bf16[256,512]{1,0:T(8,128)(2,1)S(1)}, u32[]{:S(2)}, u32[]{:S(2)}) %collective-permute-start) | collective-permute-done | bytes 262176 | tf_op jit(solution)/shard_map/ppermute | solution.py:35
  10.2 0.0 collective-permute-done.1.rest_2_.other_ref
  10.2 0.0 collective-permute-done.2.rest_3_.up_other_ref
  10.2 0.0 copy-done.2
  10.2 0.0 copy-done.3
  10.3 1.2 %route.1 = (s32[1,256]{1,0:T(1,128)S(1)}, bf16[64,1024]{1,0:T(8,128)(2,1)S(1)}, bf16[64,1024]{1,0:T(8,128)(2,1)S(1)}, bf16[64,1024]{1,0:T(8,128)(2,1)S(1)}, bf16...) custom-call(s32[16]{0:T(128)S(1)} %copy-done.3, ...), custom_call_target="tpu_custom_call", output_to_operand_aliasing={{5}: (4, {})} | custom-call | flops 134217728 | bytes 1048576 | tf_op jit(solution)/shard_map/route/pallas_call | solution.py:71
  11.5 0.1 collective-permute-start.8
  11.5 0.5 collective-permute-start.3
  12.0 1.8 %collective-permute-start.4 = (bf16[64,1024]{1,0:T(8,128)(2,1)S(1)}, bf16[64,1024]{1,0:T(8,128)(2,1)S(1)}, u32[]{:S(2)}, u32[]{:S(2)}) collective-permute-start(bf16[64,1024]{1,0:T(8,128)(2,1)S(1)} %get-tuple-element.28), channel_id=1, source_target_pairs={{0,4},{1,5},{2,6},{3,7},{4,0},{5,1},{6,2},{7,3},{8,12},{9,13},{10,... | collective-permute-start | bytes 393224 | tf_op jit(solution)/shard_map/ppermute | solution.py:35
  13.8 2.6 %collective-permute-start.5 = (bf16[64,1024]{1,0:T(8,128)(2,1)S(1)}, bf16[64,1024]{1,0:T(8,128)(2,1)S(1)}, u32[]{:S(2)}, u32[]{:S(2)}) collective-permute-start(bf16[64,1024]{1,0:T(8,128)(2,1)S(1)} %get-tuple-element.29), channel_id=1, source_target_pairs={{0,8},{1,9},{2,10},{3,11},{4,12},{5,13},{6,14},{7,15},{8,0},{9,1},... | collective-permute-start | bytes 393224 | tf_op jit(solution)/shard_map/ppermute | solution.py:35
  16.4 0.0 collective-permute-start.6
  16.4 0.0 collective-permute-done.8
  16.4 0.2 fusion.1
  16.6 1.8 %collective-permute-start.10 = (bf16[256,512]{1,0:T(8,128)(2,1)S(1)}, bf16[256,512]{1,0:T(8,128)(2,1)S(1)}, u32[]{:S(2)}, u32[]{:S(2)}) collective-permute-start(bf16[256,512]{1,0:T(8,128)(2,1)S(1)} %get-tuple-element.39), channel_id=1, source_target_pairs={{0,2},{1,3},{2,0},{3,1},{4,6},{5,7},{6,4},{7,5},{8,10},{9,11},{10,... | collective-permute-start | bytes 786440 | tf_op jit(solution)/shard_map/ppermute | solution.py:35
  18.4 1.0 %collective-permute-done.4.refs_1_ = bf16[64,1024]{1,0:T(8,128)(2,1)S(1)} collective-permute-done((bf16[64,1024]{1,0:T(8,128)(2,1)S(1)}, bf16[64,1024]{1,0:T(8,128)(2,1)S(1)}, u32[]{:S(2)}, u32[]{:S(2)}) %collective-permute-start.4) | collective-permute-done | bytes 131104 | tf_op jit(solution)/shard_map/ppermute | solution.py:35
  19.4 1.7 %collective-permute-start.9 = (bf16[256,512]{1,0:T(8,128)(2,1)S(1)}, bf16[256,512]{1,0:T(8,128)(2,1)S(1)}, u32[]{:S(2)}, u32[]{:S(2)}) collective-permute-start(bf16[256,512]{1,0:T(8,128)(2,1)S(1)} %get-tuple-element.40), channel_id=1, source_target_pairs={{0,2},{1,3},{2,0},{3,1},{4,6},{5,7},{6,4},{7,5},{8,10},{9,11},{10,... | collective-permute-start | bytes 786440 | tf_op jit(solution)/shard_map/ppermute | solution.py:35
  21.1 5.6 %collective-permute-done.5.refs_2_ = bf16[64,1024]{1,0:T(8,128)(2,1)S(1)} collective-permute-done((bf16[64,1024]{1,0:T(8,128)(2,1)S(1)}, bf16[64,1024]{1,0:T(8,128)(2,1)S(1)}, u32[]{:S(2)}, u32[]{:S(2)}) %collective-permute-start.5) | collective-permute-done | bytes 131104 | tf_op jit(solution)/shard_map/ppermute | solution.py:35
  26.8 0.0 collective-permute-done.6.refs_3_
  26.8 0.0 copy-done.4
  26.8 0.0 copy-start.1
  26.8 0.4 shrink.1.mine_ref
  27.2 0.0 collective-permute-start.7
  27.2 1.2 %collective-permute-done.7.other_ref = f32[64,64]{1,0:T(8,128)S(1)} collective-permute-done((f32[64,64]{1,0:T(8,128)S(1)}, f32[64,64]{1,0:T(8,128)S(1)}, u32[]{:S(2)}, u32[]{:S(2)}) %collective-permute-start.7) | collective-permute-done | bytes 16416 | tf_op jit(solution)/shard_map/ppermute | solution.py:35
  28.4 0.0 collective-permute-done.10
  28.4 1.6 %collective-permute-done.9 = bf16[256,512]{1,0:T(8,128)(2,1)S(1)} collective-permute-done((bf16[256,512]{1,0:T(8,128)(2,1)S(1)}, bf16[256,512]{1,0:T(8,128)(2,1)S(1)}, u32[]{:S(2)}, u32[]{:S(2)}) %collective-permute-start.9) | collective-permute-done | bytes 262176 | tf_op jit(solution)/shard_map/ppermute | solution.py:35
  30.0 0.0 copy-done.1
  30.0 0.3 grow.1
  30.3 1.6 %collective-permute-start.13 = (bf16[2,64,512]{2,1,0:T(8,128)(2,1)S(1)}, bf16[2,64,512]{2,1,0:T(8,128)(2,1)S(1)}, u32[]{:S(2)}, u32[]{:S(2)}) collective-permute-start(bf16[2,64,512]{2,1,0:T(8,128)(2,1)S(1)} %get-tuple-element.38), channel_id=1, source_target_pairs={{0,2},{1,3},{2,0},{3,1},{4,6},{5,7},{6,4},{7,5},{8,10},{9,11},{10,... | collective-permute-start | bytes 393224 | tf_op jit(solution)/shard_map/ppermute | solution.py:35
  31.9 0.0 collective-permute-done.3.refs_1_
  31.9 3.4 %collective-permute-done.13.refs_3_ = bf16[2,64,512]{2,1,0:T(8,128)(2,1)S(1)} collective-permute-done((bf16[2,64,512]{2,1,0:T(8,128)(2,1)S(1)}, bf16[2,64,512]{2,1,0:T(8,128)(2,1)S(1)}, u32[]{:S(2)}, u32[]{:S(2)}) %collective-permute-start.13) | collective-permute-done | bytes 131104 | tf_op jit(solution)/shard_map/ppermute | solution.py:35
  35.4 0.3 join.7
  35.7 1.3 %collective-permute-start.14 = (bf16[256,512]{1,0:T(8,128)(2,1)S(1)}, bf16[256,512]{1,0:T(8,128)(2,1)S(1)}, u32[]{:S(2)}, u32[]{:S(2)}) collective-permute-start(bf16[256,512]{1,0:T(8,128)(2,1)S(1)} %join.7), channel_id=1, source_target_pairs={{0,4},{1,5},{2,6},{3,7},{4,0},{5,1},{6,2},{7,3},{8,12},{9,13},{10,... | collective-permute-start | bytes 786440 | tf_op jit(solution)/shard_map/ppermute | solution.py:35
  37.0 0.3 join.5
  37.3 1.6 %collective-permute-start.12 = (bf16[256,512]{1,0:T(8,128)(2,1)S(1)}, bf16[256,512]{1,0:T(8,128)(2,1)S(1)}, u32[]{:S(2)}, u32[]{:S(2)}) collective-permute-start(bf16[256,512]{1,0:T(8,128)(2,1)S(1)} %get-tuple-element.37), channel_id=1, source_target_pairs={{0,2},{1,3},{2,0},{3,1},{4,6},{5,7},{6,4},{7,5},{8,10},{9,11},{10,... | collective-permute-start | bytes 786440 | tf_op jit(solution)/shard_map/ppermute | solution.py:35
  38.9 0.5 collective-permute-start.11
  39.4 0.3 join.4
  39.7 0.3 join.6
  40.1 2.7 %collective-permute-done.14 = bf16[256,512]{1,0:T(8,128)(2,1)S(1)} collective-permute-done((bf16[256,512]{1,0:T(8,128)(2,1)S(1)}, bf16[256,512]{1,0:T(8,128)(2,1)S(1)}, u32[]{:S(2)}, u32[]{:S(2)}) %collective-permute-start.14) | collective-permute-done | bytes 262176 | tf_op jit(solution)/shard_map/ppermute | solution.py:35
  42.7 0.1 add_convert_fusion.1.after_ref
  42.8 2.8 %collective-permute-start.16 = (bf16[256,512]{1,0:T(8,128)(2,1)S(1)}, bf16[256,512]{1,0:T(8,128)(2,1)S(1)}, u32[]{:S(2)}, u32[]{:S(2)}) collective-permute-start(bf16[256,512]{1,0:T(8,128)(2,1)S(1)} %add_convert_fusion.1.after_ref), channel_id=1, source_target_pairs={{0,8},{1,9},{2,10},{3,11},{4,12},{5,13},{6,14},{7,15},{8,0},{9,1},... | collective-permute-start | bytes 786440 | tf_op jit(solution)/shard_map/ppermute | solution.py:35
  45.6 1.0 %collective-permute-done.12.came_ref = bf16[256,512]{1,0:T(8,128)(2,1)S(1)} collective-permute-done((bf16[256,512]{1,0:T(8,128)(2,1)S(1)}, bf16[256,512]{1,0:T(8,128)(2,1)S(1)}, u32[]{:S(2)}, u32[]{:S(2)}) %collective-permute-start.12) | collective-permute-done | bytes 262176 | tf_op jit(solution)/shard_map/ppermute | solution.py:35
  46.7 0.9 %collective-permute-start.15 = (bf16[256,512]{1,0:T(8,128)(2,1)S(1)}, bf16[256,512]{1,0:T(8,128)(2,1)S(1)}, u32[]{:S(2)}, u32[]{:S(2)}) collective-permute-start(bf16[256,512]{1,0:T(8,128)(2,1)S(1)} %later.1), channel_id=1, source_target_pairs={{0,4},{1,5},{2,6},{3,7},{4,0},{5,1},{6,2},{7,3},{8,12},{9,13},{10,... | collective-permute-start | bytes 786440 | tf_op jit(solution)/shard_map/ppermute | solution.py:35
  47.5 2.7 %collective-permute-done.11 = bf16[256,512]{1,0:T(8,128)(2,1)S(1)} collective-permute-done((bf16[256,512]{1,0:T(8,128)(2,1)S(1)}, bf16[256,512]{1,0:T(8,128)(2,1)S(1)}, u32[]{:S(2)}, u32[]{:S(2)}) %collective-permute-start.11) | collective-permute-done | bytes 262176 | tf_op jit(solution)/shard_map/ppermute | solution.py:35
  50.2 6.0 %collective-permute-done.16 = bf16[256,512]{1,0:T(8,128)(2,1)S(1)} collective-permute-done((bf16[256,512]{1,0:T(8,128)(2,1)S(1)}, bf16[256,512]{1,0:T(8,128)(2,1)S(1)}, u32[]{:S(2)}, u32[]{:S(2)}) %collective-permute-start.16) | collective-permute-done | bytes 262176 | tf_op jit(solution)/shard_map/ppermute | solution.py:35
  56.2 0.7 %collective-permute-done.15 = bf16[256,512]{1,0:T(8,128)(2,1)S(1)} collective-permute-done((bf16[256,512]{1,0:T(8,128)(2,1)S(1)}, bf16[256,512]{1,0:T(8,128)(2,1)S(1)}, u32[]{:S(2)}, u32[]{:S(2)}) %collective-permute-start.15) | collective-permute-done | bytes 262176 | tf_op jit(solution)/shard_map/ppermute | solution.py:35
  57.0 0.8 %add_convert_fusion = bf16[256,512]{1,0:T(8,128)(2,1)} fusion(bf16[256,512]{1,0:T(8,128)(2,1)S(1)} %collective-permute-done.16, bf16[256,512]{1,0:T(8,128)(2,1)S(1)} %collective-permute-done.15, f32[256,512]{1,0:T(8,128)S(1)} %get-tuple-element.34, bf16[256,512]{1,0:T(8,128)(2,1)S(1)} %collective-permute-done.11), kind=kLoop, calls=%fused_computation | loop fusion | flops 917504 | bytes 1572864 | tf_op jit(solution)/shard_map/convert_element_type | solution.py:287
  (1 shorter events, 0.0 us)
Async XLA Ops:
  0.0 10.2 %collective-permute-start.1 = (bf16[64,8192]{1,0:T(8,128)(2,1)}, bf16[64,8192]{1,0:T(8,128)(2,1)S(1)}, u32[]{:S(2)}, u32[]{:S(2)}) collective-permute-start(bf16[64,8192]{1,0:T(8,128)(2,1)} %bitcast.19), channel_id=1, source_target_pairs={{0,1},{1,0},{2,3},{3,2},{4,5},{5,4},{6,7},{7,6},{8,9},{9,8},{10,11... | collective-permute-start | bytes 3145736 | tf_op jit(solution)/shard_map/ppermute | solution.py:35
  0.5 9.8 %copy-start.2 = (s32[256]{0:T(256)S(1)}, s32[256]{0:T(256)}, u32[]{:S(2)}) copy-start(s32[256]{0:T(256)} %param.10) | copy-start | bytes 3076
  0.5 9.8 %copy-start.3 = (s32[16]{0:T(128)S(1)}, s32[16]{0:T(128)}, u32[]{:S(2)}) copy-start(s32[16]{0:T(128)} %slot_hbm.1) | copy-start | bytes 196
  0.5 9.8 %collective-permute-start.2 = (bf16[64,8192]{1,0:T(8,128)(2,1)}, bf16[64,8192]{1,0:T(8,128)(2,1)S(1)}, u32[]{:S(2)}, u32[]{:S(2)}) collective-permute-start(bf16[64,8192]{1,0:T(8,128)(2,1)} %bitcast.14), channel_id=1, source_target_pairs={{0,1},{1,0},{2,3},{3,2},{4,5},{5,4},{6,7},{7,6},{8,9},{9,8},{10,11... | collective-permute-start | bytes 3145736 | tf_op jit(solution)/shard_map/ppermute | solution.py:35
  0.5 9.7 %collective-permute-start = (bf16[256,512]{1,0:T(8,128)(2,1)}, bf16[256,512]{1,0:T(8,128)(2,1)S(1)}, u32[]{:S(2)}, u32[]{:S(2)}) collective-permute-start(bf16[256,512]{1,0:T(8,128)(2,1)} %own_ref.1), channel_id=1, source_target_pairs={{0,2},{1,3},{2,0},{3,1},{4,6},{5,7},{6,4},{7,5},{8,10},{9,11},{10,... | collective-permute-start | bytes 786440 | tf_op jit(solution)/shard_map/ppermute | solution.py:35
  3.5 1.0 %copy-start = (bf16[256,512]{1,0:T(8,128)(2,1)S(1)}, bf16[256,512]{1,0:T(8,128)(2,1)}, u32[]{:S(2)}) copy-start(bf16[256,512]{1,0:T(8,128)(2,1)} %own_ref.1) | copy-start | bytes 786436
  9.3 17.4 %copy-start.4 = (bf16[1,8192,64]{1,2,0:T(8,128)(2,1)S(1)}, bf16[1,8192,64]{1,2,0:T(8,128)(2,1)}, u32[]{:S(2)}) copy-start(bf16[1,8192,64]{1,2,0:T(8,128)(2,1)} %param.8) | copy-start | bytes 3145732
  11.5 5.0 %collective-permute-start.8 = (bf16[2,256,512]{2,1,0:T(8,128)(2,1)S(1)}, bf16[2,256,512]{2,1,0:T(8,128)(2,1)S(1)}, u32[]{:S(2)}, u32[]{:S(2)}) collective-permute-start(bf16[2,256,512]{2,1,0:T(8,128)(2,1)S(1)} %get-tuple-element.32), channel_id=1, source_target_pairs={{0,1},{1,0},{2,3},{3,2},{4,5},{5,4},{6,7},{7,6},{8,9},{9,8},{10,11... | collective-permute-start | bytes 1572872 | tf_op jit(solution)/shard_map/ppermute | solution.py:35
  11.5 20.4 %collective-permute-start.3 = (bf16[6,256,512]{2,1,0:T(8,128)(2,1)S(1)}, bf16[6,256,512]{2,1,0:T(8,128)(2,1)S(1)}, u32[]{:S(2)}, u32[]{:S(2)}) collective-permute-start(bf16[6,256,512]{2,1,0:T(8,128)(2,1)S(1)} %get-tuple-element.26), channel_id=1, source_target_pairs={{0,1},{1,0},{2,3},{3,2},{4,5},{5,4},{6,7},{7,6},{8,9},{9,8},{10,11... | collective-permute-start | bytes 4718600 | tf_op jit(solution)/shard_map/ppermute | solution.py:35
  12.0 7.3 %collective-permute-start.4 = (bf16[64,1024]{1,0:T(8,128)(2,1)S(1)}, bf16[64,1024]{1,0:T(8,128)(2,1)S(1)}, u32[]{:S(2)}, u32[]{:S(2)}) collective-permute-start(bf16[64,1024]{1,0:T(8,128)(2,1)S(1)} %get-tuple-element.28), channel_id=1, source_target_pairs={{0,4},{1,5},{2,6},{3,7},{4,0},{5,1},{6,2},{7,3},{8,12},{9,13},{10,... | collective-permute-start | bytes 393224 | tf_op jit(solution)/shard_map/ppermute | solution.py:35
  13.8 12.9 %collective-permute-start.5 = (bf16[64,1024]{1,0:T(8,128)(2,1)S(1)}, bf16[64,1024]{1,0:T(8,128)(2,1)S(1)}, u32[]{:S(2)}, u32[]{:S(2)}) collective-permute-start(bf16[64,1024]{1,0:T(8,128)(2,1)S(1)} %get-tuple-element.29), channel_id=1, source_target_pairs={{0,8},{1,9},{2,10},{3,11},{4,12},{5,13},{6,14},{7,15},{8,0},{9,1},... | collective-permute-start | bytes 393224 | tf_op jit(solution)/shard_map/ppermute | solution.py:35
  16.4 10.3 %collective-permute-start.6 = (bf16[64,1024]{1,0:T(8,128)(2,1)S(1)}, bf16[64,1024]{1,0:T(8,128)(2,1)S(1)}, u32[]{:S(2)}, u32[]{:S(2)}) collective-permute-start(bf16[64,1024]{1,0:T(8,128)(2,1)S(1)} %get-tuple-element.30), channel_id=1, source_target_pairs={{0,12},{1,13},{2,14},{3,15},{4,8},{5,9},{6,10},{7,11},{8,4},{9,5},... | collective-permute-start | bytes 393224 | tf_op jit(solution)/shard_map/ppermute | solution.py:35
  16.6 11.8 %collective-permute-start.10 = (bf16[256,512]{1,0:T(8,128)(2,1)S(1)}, bf16[256,512]{1,0:T(8,128)(2,1)S(1)}, u32[]{:S(2)}, u32[]{:S(2)}) collective-permute-start(bf16[256,512]{1,0:T(8,128)(2,1)S(1)} %get-tuple-element.39), channel_id=1, source_target_pairs={{0,2},{1,3},{2,0},{3,1},{4,6},{5,7},{6,4},{7,5},{8,10},{9,11},{10,... | collective-permute-start | bytes 786440 | tf_op jit(solution)/shard_map/ppermute | solution.py:35
  19.4 10.6 %collective-permute-start.9 = (bf16[256,512]{1,0:T(8,128)(2,1)S(1)}, bf16[256,512]{1,0:T(8,128)(2,1)S(1)}, u32[]{:S(2)}, u32[]{:S(2)}) collective-permute-start(bf16[256,512]{1,0:T(8,128)(2,1)S(1)} %get-tuple-element.40), channel_id=1, source_target_pairs={{0,2},{1,3},{2,0},{3,1},{4,6},{5,7},{6,4},{7,5},{8,10},{9,11},{10,... | collective-permute-start | bytes 786440 | tf_op jit(solution)/shard_map/ppermute | solution.py:35
  26.8 3.3 %copy-start.1 = (bf16[1,64,8192]{2,1,0:T(8,128)(2,1)S(1)}, bf16[1,64,8192]{2,1,0:T(8,128)(2,1)}, u32[]{:S(2)}) copy-start(bf16[1,64,8192]{2,1,0:T(8,128)(2,1)} %param.9) | copy-start | bytes 3145732
  27.2 1.2 %collective-permute-start.7 = (f32[64,64]{1,0:T(8,128)S(1)}, f32[64,64]{1,0:T(8,128)S(1)}, u32[]{:S(2)}, u32[]{:S(2)}) collective-permute-start(f32[64,64]{1,0:T(8,128)S(1)} %shrink.1.mine_ref), channel_id=1, source_target_pairs={{0,1},{1,0},{2,3},{3,2},{4,5},{5,4},{6,7},{7,6},{8,9},{9,8},{10,11... | collective-permute-start | bytes 49160 | tf_op jit(solution)/shard_map/ppermute | solution.py:35
  30.3 5.0 %collective-permute-start.13 = (bf16[2,64,512]{2,1,0:T(8,128)(2,1)S(1)}, bf16[2,64,512]{2,1,0:T(8,128)(2,1)S(1)}, u32[]{:S(2)}, u32[]{:S(2)}) collective-permute-start(bf16[2,64,512]{2,1,0:T(8,128)(2,1)S(1)} %get-tuple-element.38), channel_id=1, source_target_pairs={{0,2},{1,3},{2,0},{3,1},{4,6},{5,7},{6,4},{7,5},{8,10},{9,11},{10,... | collective-permute-start | bytes 393224 | tf_op jit(solution)/shard_map/ppermute | solution.py:35
  35.7 7.0 %collective-permute-start.14 = (bf16[256,512]{1,0:T(8,128)(2,1)S(1)}, bf16[256,512]{1,0:T(8,128)(2,1)S(1)}, u32[]{:S(2)}, u32[]{:S(2)}) collective-permute-start(bf16[256,512]{1,0:T(8,128)(2,1)S(1)} %join.7), channel_id=1, source_target_pairs={{0,4},{1,5},{2,6},{3,7},{4,0},{5,1},{6,2},{7,3},{8,12},{9,13},{10,... | collective-permute-start | bytes 786440 | tf_op jit(solution)/shard_map/ppermute | solution.py:35
  37.3 9.3 %collective-permute-start.12 = (bf16[256,512]{1,0:T(8,128)(2,1)S(1)}, bf16[256,512]{1,0:T(8,128)(2,1)S(1)}, u32[]{:S(2)}, u32[]{:S(2)}) collective-permute-start(bf16[256,512]{1,0:T(8,128)(2,1)S(1)} %get-tuple-element.37), channel_id=1, source_target_pairs={{0,2},{1,3},{2,0},{3,1},{4,6},{5,7},{6,4},{7,5},{8,10},{9,11},{10,... | collective-permute-start | bytes 786440 | tf_op jit(solution)/shard_map/ppermute | solution.py:35
  38.9 11.3 %collective-permute-start.11 = (bf16[256,512]{1,0:T(8,128)(2,1)S(1)}, bf16[256,512]{1,0:T(8,128)(2,1)S(1)}, u32[]{:S(2)}, u32[]{:S(2)}) collective-permute-start(bf16[256,512]{1,0:T(8,128)(2,1)S(1)} %get-tuple-element.35), channel_id=1, source_target_pairs={{0,2},{1,3},{2,0},{3,1},{4,6},{5,7},{6,4},{7,5},{8,10},{9,11},{10,... | collective-permute-start | bytes 786440 | tf_op jit(solution)/shard_map/ppermute | solution.py:35
  42.8 13.4 %collective-permute-start.16 = (bf16[256,512]{1,0:T(8,128)(2,1)S(1)}, bf16[256,512]{1,0:T(8,128)(2,1)S(1)}, u32[]{:S(2)}, u32[]{:S(2)}) collective-permute-start(bf16[256,512]{1,0:T(8,128)(2,1)S(1)} %add_convert_fusion.1.after_ref), channel_id=1, source_target_pairs={{0,8},{1,9},{2,10},{3,11},{4,12},{5,13},{6,14},{7,15},{8,0},{9,1},... | collective-permute-start | bytes 786440 | tf_op jit(solution)/shard_map/ppermute | solution.py:35
  46.7 10.3 %collective-permute-start.15 = (bf16[256,512]{1,0:T(8,128)(2,1)S(1)}, bf16[256,512]{1,0:T(8,128)(2,1)S(1)}, u32[]{:S(2)}, u32[]{:S(2)}) collective-permute-start(bf16[256,512]{1,0:T(8,128)(2,1)S(1)} %later.1), channel_id=1, source_target_pairs={{0,4},{1,5},{2,6},{3,7},{4,0},{5,1},{6,2},{7,3},{8,12},{9,13},{10,... | collective-permute-start | bytes 786440 | tf_op jit(solution)/shard_map/ppermute | solution.py:35

commit v6 on v5

--- a/solution.py
+++ b/solution.py
@@ -35,8 +35,24 @@
     return lax.ppermute(value, "tensor", [(t, t ^ mask) for t in range(count)])
 
 
+def once_kernel(*refs):
+    pass
+
+
+def once(values, *after):
+    return pl.pallas_call(
+        once_kernel,
+        out_shape=[shape(value.shape, value.dtype) for value in values],
+        in_specs=[ANYWHERE] * (len(values) + len(after)),
+        out_specs=[ANYWHERE] * len(values),
+        input_output_aliases={i: i for i in range(len(values))},
+        cost_estimate=cost(0, 0),
+        name="once",
+    )(*values, *after)
+
+
 def route_kernel(count, layers, slot_hbm, row_ref, own_ref, y_ref, *rest):
-    target_ref, out_refs = rest[-4 - layers], rest[-3 - layers : -3]
+    target_ref, out_refs = rest[-3 - layers], rest[-2 - layers : -2]
     slot_ref, slot_sem = rest[-2:]
     rows, width = own_ref.shape
     me = lax.axis_index("tensor")
@@ -64,24 +80,21 @@
         out_refs[k][:, width:] = dot(select, y_ref[...]).astype(jnp.bfloat16)
 
 
-def route(adapter_slot, row_adapter, own, y, passed, *after):
+def route(adapter_slot, row_adapter, own, y, *after):
     rows, width = own.shape
     count = lax.axis_size("tensor")
     layers = count // 4
     found = pl.pallas_call(
         functools.partial(route_kernel, count, layers),
-        out_shape=[shape((1, rows), jnp.int32)]
-        + [shape((2 * CAP, 2 * width))] * layers
-        + [shape(passed.shape, passed.dtype)],
-        in_specs=[IN_HBM] + [IN_VMEM] * 3 + [ANYWHERE] * (1 + len(after)),
-        out_specs=[IN_VMEM] * (layers + 1) + [ANYWHERE],
-        input_output_aliases={4: layers + 1},
+        out_shape=[shape((1, rows), jnp.int32)] + [shape((2 * CAP, 2 * width))] * layers,
+        in_specs=[IN_HBM] + [IN_VMEM] * 3 + [ANYWHERE] * len(after),
+        out_specs=[IN_VMEM] * (layers + 1),
         scratch_shapes=[pltpu.SMEM(adapter_slot.shape, jnp.int32), DMA(())],
         compiler_params=params(16),
         cost_estimate=cost(8 * layers * CAP * rows * width, 16 * layers * CAP * width),
         name="route",
-    )(adapter_slot, row_adapter[None, :], own, y, passed, *after)
-    return found[0], found[1:-1], found[-1]
+    )(adapter_slot, row_adapter[None, :], own, y, *after)
+    return found[0], found[1:]
 
 
 def product_kernel(groups, attended_hbm, weight_hbm, *refs):
@@ -228,61 +241,51 @@
     )(target, *operands)
 
 
-def later_kernel(side_ref, came_ref, after_ref, out_ref):
-    out_ref[...] = (side_ref[...] + came_ref[...].astype(jnp.float32)).astype(jnp.bfloat16)
-
-
-def later(side, came, after):
-    return pl.pallas_call(
-        later_kernel,
-        out_shape=shape(side.shape),
-        in_specs=[IN_VMEM] * 3,
-        out_specs=IN_VMEM,
-        compiler_params=params(16),
-        cost_estimate=cost(2 * side.size, 8 * side.size),
-        name="later",
-    )(side, came, after)
-
-
 def staged(attended, out_weight, adapter_down, adapter_up, row_adapter, adapter_slot):
     f32, bf16 = jnp.float32, jnp.bfloat16
     up, down = adapter_up[0], jnp.swapaxes(adapter_down, 1, 2)[0]
     from_y = swap(attended, 2)
     down_other, up_other = swap(down, 1), swap(up, 1)
-    chips = (6, 4, 3, 2, 1, 0)
-    away_first, stay_first, away, stay, token = product(attended, out_weight, ((7, 5), chips), 44)
-    target, outgoing, away_first = route(
-        adapter_slot, row_adapter, attended, from_y, away_first, token, down_other, up_other
-    )
+    chips = (5, 4, 3, 2, 1, 0)
+    away_first, stay_first, away, stay, token = product(attended, out_weight, ((7, 6), chips), 44)
+    (away_first,) = once((away_first,), from_y, down_other, up_other)
+    came_first = swap(away_first, 1)
+    (away,) = once((away,), came_first)
+    came = swap(away, 1)
+    target, outgoing = route(adapter_slot, row_adapter, attended, from_y, token)
     arrived = [outgoing[0]] + [None] * 3
     for k in (2, 3, 1):
         arrived[k] = swap(outgoing[k], 4 * k)
-    came_first = swap(away_first, 1)
-    go3 = (stay_first[0] + came_first[0].astype(f32)).astype(bf16)
-    go2 = (stay_first[1] + came_first[1].astype(f32)).astype(bf16)
-    y3, y2 = swap(go3, 2)[None], swap(go2, 2)[None]
-    came = swap(away, 1)
+    first = [stay_first[i] + came_first[i].astype(f32) for i in range(2)]
+    y3 = swap(first[0].astype(bf16), 2)
+    y2 = swap((stay[0] + came[0].astype(f32)).astype(bf16), 2)[None]
+    y1 = swap((stay[2] + came[2].astype(f32)).astype(bf16), 2)[None]
+    z3 = swap((first[1] + y3.astype(f32)).astype(bf16), 4)[None]
     mine = shrink(down, down_other, arrived)
-    here, over = grow(mine, swap(mine, 1), up, up_other, (tuple(2 * m for m in chips), (14, 10)), y3, y2)
-    over = swap(over, 2)
-    at = {m: i for i, m in enumerate(chips)}
+    here_chips = (4, 2, 1, 0)
+    groups = (tuple(2 * m for m in here_chips), (10, 6), (12,), (14,))
+    here, over2, over4, over6 = grow(mine, swap(mine, 1), up, up_other, groups, z3, y2, y1)
+    over2, over4, over6 = swap(over2, 2), swap(over4, 4), swap(over6, 6)
 
     def blocks(m):
-        return ((0, at[m]), (1, at[m])), ((2, at[m], 0),)
-
-    def early(m, i):
-        base, grown = blocks(m)
-        return base + ((4 + i, 0),), grown + ((3, i, 2),)
-
-    go1, go0 = join(target, [stay, came, here], (blocks(3), blocks(1)), bf16)
-    y1, y0 = swap(go1, 2), swap(go0, 2)
-    (sum3,) = join(target, [stay, came, here, over, y3], (early(6, 0),), bf16)
-    z3 = swap(sum3, 4)
-    (side2,) = join(target, [stay, came, here, over, y3, y2], (early(4, 1),), f32)
-    side1, side0 = join(target, [stay, came, here], (blocks(2), blocks(0)), f32)
-    sum2 = (side2 + z3.astype(f32)).astype(bf16)
+        return ((0, chips.index(m)), (1, chips.index(m))), ((2, here_chips.index(m), 0),)
+
+    base, grown = blocks(4)
+    (sum2,) = join(
+        target,
+        [stay, came, here, over2, over4, over6, z3, y2],
+        ((base + ((6, 0), (7, 0)), grown + ((3, 0, 2), (4, 0, 4), (5, 0, 6))),),
+        bf16,
+    )
     z2 = swap(sum2, 8)
-    z1 = swap(later(side1, y1, sum2), 4)
+    base, grown = blocks(2)
+    (sum1,) = join(
+        target, [stay, came, here, over2, y1, sum2], ((base + ((4, 0),), grown + ((3, 1, 2),)),), bf16
+    )
+    z1 = swap(sum1, 4)
+    (go0,) = join(target, [stay, came, here], (blocks(1),), bf16)
+    y0 = swap(go0, 2)
+    (side0,) = join(target, [stay, came, here], (blocks(0),), f32)
     total = side0 + y0.astype(f32) + z1.astype(f32) + z2.astype(f32)
     return total.astype(bf16)
 

time: 58 us -> 62.9 us (1.084)
  local copies, waits for them, and re-layouts: 1 us -> 6.41 us
  waiting for transfers between devices: 26.9 us -> 21.7 us
  Pallas kernels: 8.13 us -> 10.6 us
  other arithmetic: 1.07 us -> 3.37 us
    unnamed x10 -> x26, local copies, waits for them, and re-layouts: 1 us -> 6.41 us
    ppermute x17 -> x19, waiting for transfers between devices: 26.9 us -> 21.7 us  [swap(): return lax.ppermute(value, 'tensor', [(t, t ^ mask) for t in range(count)])]
    convert_element_type x2 -> x3, other arithmetic: 0.23 us -> 2.53 us  [the longest x1 1.31 us: staged(): y3 = swap(first[0].astype(bf16), 2)]
    pallas_call x1, Pallas kernels: 0.4 us -> 1.71 us  [shrink(): pl.pallas_call(functools.partial(shrink_kernel, len(arrived)), out_shape=...]
    pallas_call x1, Pallas kernels: 0.29 us -> 1.51 us  [grow(): pl.pallas_call(functools.partial(grow_kernel, groups), out_shape=[shape((...]
    ppermute x17 -> x19, starting transfers between devices: 20.6 us -> 20 us  [swap(): return lax.ppermute(value, 'tensor', [(t, t ^ mask) for t in range(count)])]
  transfers between devices with their start and end apart: 17 -> 19, of which waited for: 11 -> 10; matrix products, arithmetic and copies ran while one was open for 0% -> 4% of each run, Pallas kernels for 11% -> 15%
where the time goes in v6:
time: 62.9 us; the launch traced here: 62.3 us
  waiting for transfers between devices  21.7 us (34%)
  starting transfers between devices  20 us (32%)
  Pallas kernels  10.6 us (17%)
  local copies, waits for them, and re-layouts  6.41 us (10%)
  other arithmetic  3.37 us (5%)
    ppermute x19, waiting for transfers between devices, swap(): return lax.ppermute(value, 'tensor', [(t, t ^ mask) for t in range(count)])  21.7 us
    ppermute x19, starting transfers between devices, swap(): return lax.ppermute(value, 'tensor', [(t, t ^ mask) for t in range(count)])  20 us
    unnamed x26, local copies, waits for them, and re-layouts  6.41 us
    pallas_call x1, Pallas kernels, product(): pl.pallas_call(functools.partial(product_kernel, groups), out_shape=out_s...  4.85 us
    pallas_call x1, Pallas kernels, shrink(): pl.pallas_call(functools.partial(shrink_kernel, len(arrived)), out_shape=...  1.71 us
    pallas_call x1, Pallas kernels, grow(): pl.pallas_call(functools.partial(grow_kernel, groups), out_shape=[shape((...  1.51 us
    pallas_call x4, Pallas kernels, join(): pl.pallas_call(functools.partial(join_kernel, terms), out_shape=[shape((r...  1.32 us
    convert_element_type x1, other arithmetic, staged(): y3 = swap(first[0].astype(bf16), 2)  1.31 us
  transfers between devices with their start and end apart: 19, of which 10 were waited for; matrix products, arithmetic and copies ran while one was open for 4% of the time, Pallas kernels for 15%

profile of v6, /device:TPU:0, one launch (start us, length us, event | category | flops | bytes accessed | tf_op | source)
XLA Modules:
  0.0 62.3 jit_solution(2833631021384413868)
XLA Ops:
  0.0 0.5 collective-permute-start.1
  0.5 0.1 collective-permute-start.2
  0.5 3.0 %collective-permute-start = (bf16[256,512]{1,0:T(8,128)(2,1)}, bf16[256,512]{1,0:T(8,128)(2,1)S(1)}, u32[]{:S(2)}, u32[]{:S(2)}) collective-permute-start(bf16[256,512]{1,0:T(8,128)(2,1)} %own_ref.1), channel_id=1, source_target_pairs={{0,2},{1,3},{2,0},{3,1},{4,6},{5,7},{6,4},{7,5},{8,10},{9,11},{10,... | collective-permute-start | bytes 786440 | tf_op jit(solution)/shard_map/ppermute | solution.py:35
  3.5 1.0 %copy-done.2 = bf16[256,512]{1,0:T(8,128)(2,1)S(1)} copy-done((bf16[256,512]{1,0:T(8,128)(2,1)S(1)}, bf16[256,512]{1,0:T(8,128)(2,1)}, u32[]{:S(2)}) %copy-start.2) | copy-done | bytes 262168
  4.5 4.9 %product.1 = (bf16[2,256,512]{2,1,0:T(8,128)(2,1)S(1)}, f32[2,256,512]{2,1,0:T(8,128)S(1)}, bf16[6,256,512]{2,1,0:T(8,128)(2,1)S(1)}, f32[6,256,512]{2,1,0:T(8,128)S(1)}, f32[8,128]{1,0:T(8,128)S(1)}) custom-call(bf16[256,512]{1,0:T(8,128)(2,1)S(1)} %copy-done.2, bf16[512,8192]{1,0:T(8,128)(2,1)} %weight_hbm.1), custom_call_target="tpu_custom_call" | custom-call | flops 2147483648 | bytes 14680064 | tf_op jit(solution)/shard_map/product/pallas_call | solution.py:137
  9.3 0.0 copy-start
  9.3 1.2 %copy-done = bf16[6,256,512]{2,1,0:T(8,128)(2,1)} copy-done((bf16[6,256,512]{2,1,0:T(8,128)(2,1)}, bf16[6,256,512]{2,1,0:T(8,128)(2,1)S(1)}, u32[]{:S(2)}) %copy-start) | copy-done | bytes 1572888
  10.5 1.0 %copy-done.4 = f32[2,256,512]{2,1,0:T(8,128)} copy-done((f32[2,256,512]{2,1,0:T(8,128)}, f32[2,256,512]{2,1,0:T(8,128)S(1)}, u32[]{:S(2)}) %copy-start.4) | copy-done | bytes 1048600
  11.5 0.8 %copy-done.8 = bf16[2,256,512]{2,1,0:T(8,128)(2,1)} copy-done((bf16[2,256,512]{2,1,0:T(8,128)(2,1)}, bf16[2,256,512]{2,1,0:T(8,128)(2,1)S(1)}, u32[]{:S(2)}) %copy-start.8) | copy-done | bytes 524312
  12.3 0.0 collective-permute-done.y_ref.refs_1_
  12.3 0.0 collective-permute-done.1.refs_2_.other_ref
  12.3 0.0 collective-permute-done.2.refs_3_.up_other_ref
  12.3 0.7 %copy-done.6 = bf16[256,512]{1,0:T(8,128)(2,1)} copy-done((bf16[256,512]{1,0:T(8,128)(2,1)}, bf16[256,512]{1,0:T(8,128)(2,1)S(1)}, u32[]{:S(2)}) %copy-start.6) | copy-done | bytes 262168
  13.0 0.0 collective-permute-start.3
  13.0 2.1 %collective-permute-done.3.refs_1_ = bf16[2,256,512]{2,1,0:T(8,128)(2,1)S(1)} collective-permute-done((bf16[2,256,512]{2,1,0:T(8,128)(2,1)}, bf16[2,256,512]{2,1,0:T(8,128)(2,1)S(1)}, u32[]{:S(2)}, u32[]{:S(2)}) %collective-permute-start.3) | collective-permute-done | bytes 524320 | tf_op jit(solution)/shard_map/ppermute | solution.py:35
  15.1 0.8 %copy-done.12 = bf16[2,256,512]{2,1,0:T(8,128)(2,1)} copy-done((bf16[2,256,512]{2,1,0:T(8,128)(2,1)}, bf16[2,256,512]{2,1,0:T(8,128)(2,1)S(1)}, u32[]{:S(2)}) %copy-start.12) | copy-done | bytes 524312
  16.0 0.2 collective-permute-start.4
  16.2 1.3 %fusion.1 = bf16[256,512]{1,0:T(8,128)(2,1)S(1)} fusion(f32[2,256,512]{2,1,0:T(8,128)} %copy-done.4, bf16[2,256,512]{2,1,0:T(8,128)(2,1)} %copy-done.12), kind=kLoop, calls=%fused_computation.6 | loop fusion | flops 393216 | bytes 1048576 | tf_op jit(solution)/shard_map/convert_element_type | solution.py:260
  17.5 0.1 collective-permute-start.9
  17.5 0.0 copy-done.3
  17.6 0.0 copy-done.9
  17.6 0.0 copy-done.10
  17.6 0.0 copy-start.7
  17.6 0.9 %copy-done.7 = bf16[256,512]{1,0:T(8,128)(2,1)S(1)} copy-done((bf16[256,512]{1,0:T(8,128)(2,1)S(1)}, bf16[256,512]{1,0:T(8,128)(2,1)}, u32[]{:S(2)}) %copy-start.7) | copy-done | bytes 262168
  18.5 1.2 %route.1 = (s32[1,256]{1,0:T(1,128)S(1)}, bf16[64,1024]{1,0:T(8,128)(2,1)S(1)}, bf16[64,1024]{1,0:T(8,128)(2,1)S(1)}, bf16[64,1024]{1,0:T(8,128)(2,1)S(1)}, bf16[64,1024]{1,0:T(8,128)(2,1)S(1)}) custom-call(s32[16]{0:T(128)S(1)} %copy-done.10, s32[1,256]{1,0:T(1,128)S(1)} %bitcast.26, bf16[256,512]{1,0:T(8,128)(2,1)S(1)} %copy-done.3, ...), custom_call_target="tpu_custom_call" | custom-call | flops 134217728 | bytes 1048576 | tf_op jit(solution)/shard_map/route/pallas_call | solution.py:87
  19.7 2.1 %collective-permute-start.5 = (bf16[64,1024]{1,0:T(8,128)(2,1)S(1)}, bf16[64,1024]{1,0:T(8,128)(2,1)S(1)}, u32[]{:S(2)}, u32[]{:S(2)}) collective-permute-start(bf16[64,1024]{1,0:T(8,128)(2,1)S(1)} %get-tuple-element.25), channel_id=1, source_target_pairs={{0,4},{1,5},{2,6},{3,7},{4,0},{5,1},{6,2},{7,3},{8,12},{9,13},{10,... | collective-permute-start | bytes 393224 | tf_op jit(solution)/shard_map/ppermute | solution.py:35
  21.9 2.6 %collective-permute-start.6 = (bf16[64,1024]{1,0:T(8,128)(2,1)S(1)}, bf16[64,1024]{1,0:T(8,128)(2,1)S(1)}, u32[]{:S(2)}, u32[]{:S(2)}) collective-permute-start(bf16[64,1024]{1,0:T(8,128)(2,1)S(1)} %get-tuple-element.26), channel_id=1, source_target_pairs={{0,8},{1,9},{2,10},{3,11},{4,12},{5,13},{6,14},{7,15},{8,0},{9,1},... | collective-permute-start | bytes 393224 | tf_op jit(solution)/shard_map/ppermute | solution.py:35
  24.4 0.0 collective-permute-start.7
  24.4 1.5 %collective-permute-done.9 = bf16[256,512]{1,0:T(8,128)(2,1)S(1)} collective-permute-done((bf16[256,512]{1,0:T(8,128)(2,1)S(1)}, bf16[256,512]{1,0:T(8,128)(2,1)S(1)}, u32[]{:S(2)}, u32[]{:S(2)}) %collective-permute-start.9) | collective-permute-done | bytes 262176 | tf_op jit(solution)/shard_map/ppermute | solution.py:35
  26.0 0.0 copy-done.5
  26.0 1.1 %fusion = bf16[256,512]{1,0:T(8,128)(2,1)S(1)} fusion(bf16[256,512]{1,0:T(8,128)(2,1)S(1)} %collective-permute-done.9, f32[2,256,512]{2,1,0:T(8,128)S(1)} %copy-done.5, bf16[2,256,512]{2,1,0:T(8,128)(2,1)} %copy-done.12), kind=kLoop, calls=%fused_computation.1 | loop fusion | flops 655360 | bytes 1310720 | tf_op jit(solution)/shard_map/convert_element_type | solution.py:263
  27.0 1.6 %collective-permute-start.10 = (bf16[256,512]{1,0:T(8,128)(2,1)S(1)}, bf16[256,512]{1,0:T(8,128)(2,1)S(1)}, u32[]{:S(2)}, u32[]{:S(2)}) collective-permute-start(bf16[256,512]{1,0:T(8,128)(2,1)S(1)} %fusion), channel_id=1, source_target_pairs={{0,4},{1,5},{2,6},{3,7},{4,0},{5,1},{6,2},{7,3},{8,12},{9,13},{10,... | collective-permute-start | bytes 786440 | tf_op jit(solution)/shard_map/ppermute | solution.py:35
  28.7 0.0 collective-permute-done.4.refs_1_
  28.7 0.2 fusion.3
  28.9 0.6 collective-permute-start.12
  29.4 0.0 collective-permute-done.5.refs_1_
  29.4 1.5 %collective-permute-start.11 = (bf16[256,512]{1,0:T(8,128)(2,1)S(1)}, bf16[256,512]{1,0:T(8,128)(2,1)S(1)}, u32[]{:S(2)}, u32[]{:S(2)}) collective-permute-start(bf16[256,512]{1,0:T(8,128)(2,1)S(1)} %get-tuple-element.34), channel_id=1, source_target_pairs={{0,2},{1,3},{2,0},{3,1},{4,6},{5,7},{6,4},{7,5},{8,10},{9,11},{10,... | collective-permute-start | bytes 786440 | tf_op jit(solution)/shard_map/ppermute | solution.py:35
  30.9 3.8 %collective-permute-done.6.refs_2_ = bf16[64,1024]{1,0:T(8,128)(2,1)S(1)} collective-permute-done((bf16[64,1024]{1,0:T(8,128)(2,1)S(1)}, bf16[64,1024]{1,0:T(8,128)(2,1)S(1)}, u32[]{:S(2)}, u32[]{:S(2)}) %collective-permute-start.6) | collective-permute-done | bytes 131104 | tf_op jit(solution)/shard_map/ppermute | solution.py:35
  34.8 0.0 collective-permute-done.7.refs_3_
  34.8 0.0 copy-done.11
  34.8 1.7 %shrink.1.mine_ref = f32[64,64]{1,0:T(8,128)S(1)} custom-call(bf16[64,8192]{1,0:T(8,128)(2,1)S(1)} %bitcast.28, bf16[64,8192]{1,0:T(8,128)(2,1)} %collective-permute-done.1.refs_2_.other_ref, bf16[64,1024]{1,0:T(8,128)(2,1)S(1)} %get-tuple-element.24.refs_0_, bf16[64,1024]{1,0:T(8,128)(2,1)S(1)} %collective-permute-done.5.refs_1_, ...), custom_call_target="tpu_custom_call" | custom-call | flops 40000000000 | bytes 2097152 | tf_op jit(solution)/shard_map/shrink/pallas_call | solution.py:173
  36.5 0.0 collective-permute-start.8
  36.5 1.2 %collective-permute-done.8.other_ref = f32[64,64]{1,0:T(8,128)S(1)} collective-permute-done((f32[64,64]{1,0:T(8,128)S(1)}, f32[64,64]{1,0:T(8,128)S(1)}, u32[]{:S(2)}, u32[]{:S(2)}) %collective-permute-start.8) | collective-permute-done | bytes 16416 | tf_op jit(solution)/shard_map/ppermute | solution.py:35
  37.7 0.5 collective-permute-done.10
  38.2 0.0 collective-permute-done.12
  38.3 3.6 %collective-permute-done.11 = bf16[256,512]{1,0:T(8,128)(2,1)S(1)} collective-permute-done((bf16[256,512]{1,0:T(8,128)(2,1)S(1)}, bf16[256,512]{1,0:T(8,128)(2,1)S(1)}, u32[]{:S(2)}, u32[]{:S(2)}) %collective-permute-start.11) | collective-permute-done | bytes 262176 | tf_op jit(solution)/shard_map/ppermute | solution.py:35
  41.9 1.5 %grow.1 = (bf16[4,64,512]{2,1,0:T(8,128)(2,1)S(1)}, bf16[2,64,512]{2,1,0:T(8,128)(2,1)S(1)}, bf16[1,64,512]{2,1,0:T(8,128)(2,1)S(1)}, bf16[1,64,512]{2,1,0:T(8,128)(2,1)S(1)}) custom-call(f32[64,64]{1,0:T(8,128)S(1)} %shrink.1.mine_ref, f32[64,64]{1,0:T(8,128)S(1)} %collective-permute-done.8.other_ref, bf16[64,8192]{1,0:T(8,128)(2,1)S(1)} %bitcast.19, ...), custom_call_target="tpu_custom_call" | custom-call | flops 67108864 | bytes 2097152 | tf_op jit(solution)/shard_map/grow/pallas_call | solution.py:199
  43.4 0.6 collective-permute-start.14
  44.0 0.5 collective-permute-start.15
  44.5 2.4 %collective-permute-start.16 = (bf16[1,64,512]{2,1,0:T(8,128)(2,1)S(1)}, bf16[1,64,512]{2,1,0:T(8,128)(2,1)S(1)}, u32[]{:S(2)}, u32[]{:S(2)}) collective-permute-start(bf16[1,64,512]{2,1,0:T(8,128)(2,1)S(1)} %get-tuple-element.32), channel_id=1, source_target_pairs={{0,6},{1,7},{2,4},{3,5},{4,2},{5,3},{6,0},{7,1},{8,14},{9,15},{10,... | collective-permute-start | bytes 196616 | tf_op jit(solution)/shard_map/ppermute | solution.py:35
  47.0 0.3 join.5
  47.2 0.6 collective-permute-start.13
  47.8 0.4 collective-permute-done.15.refs_4_
  48.2 1.8 %collective-permute-done.16.refs_5_ = bf16[1,64,512]{2,1,0:T(8,128)(2,1)S(1)} collective-permute-done((bf16[1,64,512]{2,1,0:T(8,128)(2,1)S(1)}, bf16[1,64,512]{2,1,0:T(8,128)(2,1)S(1)}, u32[]{:S(2)}, u32[]{:S(2)}) %collective-permute-start.16) | collective-permute-done | bytes 65568 | tf_op jit(solution)/shard_map/ppermute | solution.py:35
  50.0 0.3 collective-permute-done.14.refs_3_
  50.3 0.5 join.6.refs_5_
  50.8 0.3 join.7
  51.1 1.1 %collective-permute-start.17 = (bf16[256,512]{1,0:T(8,128)(2,1)S(1)}, bf16[256,512]{1,0:T(8,128)(2,1)S(1)}, u32[]{:S(2)}, u32[]{:S(2)}) collective-permute-start(bf16[256,512]{1,0:T(8,128)(2,1)S(1)} %join.7), channel_id=1, source_target_pairs={{0,4},{1,5},{2,6},{3,7},{4,0},{5,1},{6,2},{7,3},{8,12},{9,13},{10,... | collective-permute-start | bytes 786440 | tf_op jit(solution)/shard_map/ppermute | solution.py:35
  52.2 2.6 %collective-permute-start.18 = (bf16[256,512]{1,0:T(8,128)(2,1)S(1)}, bf16[256,512]{1,0:T(8,128)(2,1)S(1)}, u32[]{:S(2)}, u32[]{:S(2)}) collective-permute-start(bf16[256,512]{1,0:T(8,128)(2,1)S(1)} %join.6.refs_5_), channel_id=1, source_target_pairs={{0,8},{1,9},{2,10},{3,11},{4,12},{5,13},{6,14},{7,15},{8,0},{9,1},... | collective-permute-start | bytes 786440 | tf_op jit(solution)/shard_map/ppermute | solution.py:35
  54.8 0.3 join.4
  55.1 0.0 collective-permute-done.13
  55.1 6.3 %collective-permute-done.17 = bf16[256,512]{1,0:T(8,128)(2,1)S(1)} collective-permute-done((bf16[256,512]{1,0:T(8,128)(2,1)S(1)}, bf16[256,512]{1,0:T(8,128)(2,1)S(1)}, u32[]{:S(2)}, u32[]{:S(2)}) %collective-permute-start.17) | collective-permute-done | bytes 262176 | tf_op jit(solution)/shard_map/ppermute | solution.py:35
  61.4 0.0 collective-permute-done.18
  61.4 0.8 %add_convert_fusion = bf16[256,512]{1,0:T(8,128)(2,1)} fusion(bf16[256,512]{1,0:T(8,128)(2,1)S(1)} %collective-permute-done.18, bf16[256,512]{1,0:T(8,128)(2,1)S(1)} %collective-permute-done.17, f32[256,512]{1,0:T(8,128)S(1)} %join.4, bf16[256,512]{1,0:T(8,128)(2,1)S(1)} %collective-permute-done.13), kind=kLoop, calls=%fused_computation.2 | loop fusion | flops 917504 | bytes 1572864 | tf_op jit(solution)/shard_map/convert_element_type | solution.py:290
  (14 shorter events, 0.0 us)
Async XLA Ops:
  0.0 12.3 %collective-permute-start.1 = (bf16[64,8192]{1,0:T(8,128)(2,1)}, bf16[64,8192]{1,0:T(8,128)(2,1)}, u32[]{:S(2)}, u32[]{:S(2)}) collective-permute-start(bf16[64,8192]{1,0:T(8,128)(2,1)} %bitcast.27), channel_id=1, source_target_pairs={{0,1},{1,0},{2,3},{3,2},{4,5},{5,4},{6,7},{7,6},{8,9},{9,8},{10,11... | collective-permute-start | bytes 3145736 | tf_op jit(solution)/shard_map/ppermute | solution.py:35
  0.5 11.9 %collective-permute-start.2 = (bf16[64,8192]{1,0:T(8,128)(2,1)}, bf16[64,8192]{1,0:T(8,128)(2,1)}, u32[]{:S(2)}, u32[]{:S(2)}) collective-permute-start(bf16[64,8192]{1,0:T(8,128)(2,1)} %bitcast.18), channel_id=1, source_target_pairs={{0,1},{1,0},{2,3},{3,2},{4,5},{5,4},{6,7},{7,6},{8,9},{9,8},{10,11... | collective-permute-start | bytes 3145736 | tf_op jit(solution)/shard_map/ppermute | solution.py:35
  0.5 11.8 %collective-permute-start = (bf16[256,512]{1,0:T(8,128)(2,1)}, bf16[256,512]{1,0:T(8,128)(2,1)S(1)}, u32[]{:S(2)}, u32[]{:S(2)}) collective-permute-start(bf16[256,512]{1,0:T(8,128)(2,1)} %own_ref.1), channel_id=1, source_target_pairs={{0,2},{1,3},{2,0},{3,1},{4,6},{5,7},{6,4},{7,5},{8,10},{9,11},{10,... | collective-permute-start | bytes 786440 | tf_op jit(solution)/shard_map/ppermute | solution.py:35
  3.5 1.0 %copy-start.2 = (bf16[256,512]{1,0:T(8,128)(2,1)S(1)}, bf16[256,512]{1,0:T(8,128)(2,1)}, u32[]{:S(2)}) copy-start(bf16[256,512]{1,0:T(8,128)(2,1)} %own_ref.1) | copy-start | bytes 786436
  9.3 1.2 %copy-start = (bf16[6,256,512]{2,1,0:T(8,128)(2,1)}, bf16[6,256,512]{2,1,0:T(8,128)(2,1)S(1)}, u32[]{:S(2)}) copy-start(bf16[6,256,512]{2,1,0:T(8,128)(2,1)S(1)} %get-tuple-element.22.refs_0_) | copy-start | bytes 4718596
  10.5 1.0 %copy-start.4 = (f32[2,256,512]{2,1,0:T(8,128)}, f32[2,256,512]{2,1,0:T(8,128)S(1)}, u32[]{:S(2)}) copy-start(f32[2,256,512]{2,1,0:T(8,128)S(1)} %get-tuple-element.28) | copy-start | bytes 3145732
  11.5 0.8 %copy-start.8 = (bf16[2,256,512]{2,1,0:T(8,128)(2,1)}, bf16[2,256,512]{2,1,0:T(8,128)(2,1)S(1)}, u32[]{:S(2)}) copy-start(bf16[2,256,512]{2,1,0:T(8,128)(2,1)S(1)} %get-tuple-element.23.refs_0_) | copy-start | bytes 1572868
  12.3 0.7 %copy-start.6 = (bf16[256,512]{1,0:T(8,128)(2,1)}, bf16[256,512]{1,0:T(8,128)(2,1)S(1)}, u32[]{:S(2)}) copy-start(bf16[256,512]{1,0:T(8,128)(2,1)S(1)} %collective-permute-done.y_ref.refs_1_) | copy-start | bytes 786436
  13.0 2.1 %collective-permute-start.3 = (bf16[2,256,512]{2,1,0:T(8,128)(2,1)}, bf16[2,256,512]{2,1,0:T(8,128)(2,1)S(1)}, u32[]{:S(2)}, u32[]{:S(2)}) collective-permute-start(bf16[2,256,512]{2,1,0:T(8,128)(2,1)} %once.2), channel_id=1, source_target_pairs={{0,1},{1,0},{2,3},{3,2},{4,5},{5,4},{6,7},{7,6},{8,9},{9,8},{10,11... | collective-permute-start | bytes 1572872 | tf_op jit(solution)/shard_map/ppermute | solution.py:35
  15.1 0.8 %copy-start.12 = (bf16[2,256,512]{2,1,0:T(8,128)(2,1)}, bf16[2,256,512]{2,1,0:T(8,128)(2,1)S(1)}, u32[]{:S(2)}) copy-start(bf16[2,256,512]{2,1,0:T(8,128)(2,1)S(1)} %collective-permute-done.3.refs_1_) | copy-start | bytes 1572868
  15.9 1.6 %copy-start.3 = (bf16[256,512]{1,0:T(8,128)(2,1)S(1)}, bf16[256,512]{1,0:T(8,128)(2,1)}, u32[]{:S(2)}) copy-start(bf16[256,512]{1,0:T(8,128)(2,1)} %own_ref.1) | copy-start | bytes 786436
  15.9 1.6 %copy-start.9 = (s32[256]{0:T(256)S(1)}, s32[256]{0:T(256)}, u32[]{:S(2)}) copy-start(s32[256]{0:T(256)} %param.10) | copy-start | bytes 3076
  15.9 1.6 %copy-start.10 = (s32[16]{0:T(128)S(1)}, s32[16]{0:T(128)}, u32[]{:S(2)}) copy-start(s32[16]{0:T(128)} %slot_hbm.1) | copy-start | bytes 196
  15.9 10.0 %copy-start.5 = (f32[2,256,512]{2,1,0:T(8,128)S(1)}, f32[2,256,512]{2,1,0:T(8,128)}, u32[]{:S(2)}) copy-start(f32[2,256,512]{2,1,0:T(8,128)} %copy-done.4) | copy-start | bytes 3145732
  16.0 12.7 %collective-permute-start.4 = (bf16[6,256,512]{2,1,0:T(8,128)(2,1)}, bf16[6,256,512]{2,1,0:T(8,128)(2,1)S(1)}, u32[]{:S(2)}, u32[]{:S(2)}) collective-permute-start(bf16[6,256,512]{2,1,0:T(8,128)(2,1)} %once.3), channel_id=1, source_target_pairs={{0,1},{1,0},{2,3},{3,2},{4,5},{5,4},{6,7},{7,6},{8,9},{9,8},{10,11... | collective-permute-start | bytes 4718600 | tf_op jit(solution)/shard_map/ppermute | solution.py:35
  17.5 8.5 %collective-permute-start.9 = (bf16[256,512]{1,0:T(8,128)(2,1)S(1)}, bf16[256,512]{1,0:T(8,128)(2,1)S(1)}, u32[]{:S(2)}, u32[]{:S(2)}) collective-permute-start(bf16[256,512]{1,0:T(8,128)(2,1)S(1)} %fusion.1), channel_id=1, source_target_pairs={{0,2},{1,3},{2,0},{3,1},{4,6},{5,7},{6,4},{7,5},{8,10},{9,11},{10,... | collective-permute-start | bytes 786440 | tf_op jit(solution)/shard_map/ppermute | solution.py:35
  17.6 1.0 %copy-start.7 = (bf16[256,512]{1,0:T(8,128)(2,1)S(1)}, bf16[256,512]{1,0:T(8,128)(2,1)}, u32[]{:S(2)}) copy-start(bf16[256,512]{1,0:T(8,128)(2,1)} %copy-done.6) | copy-start | bytes 786436
  19.7 9.7 %collective-permute-start.5 = (bf16[64,1024]{1,0:T(8,128)(2,1)S(1)}, bf16[64,1024]{1,0:T(8,128)(2,1)S(1)}, u32[]{:S(2)}, u32[]{:S(2)}) collective-permute-start(bf16[64,1024]{1,0:T(8,128)(2,1)S(1)} %get-tuple-element.25), channel_id=1, source_target_pairs={{0,4},{1,5},{2,6},{3,7},{4,0},{5,1},{6,2},{7,3},{8,12},{9,13},{10,... | collective-permute-start | bytes 393224 | tf_op jit(solution)/shard_map/ppermute | solution.py:35
  21.9 12.9 %collective-permute-start.6 = (bf16[64,1024]{1,0:T(8,128)(2,1)S(1)}, bf16[64,1024]{1,0:T(8,128)(2,1)S(1)}, u32[]{:S(2)}, u32[]{:S(2)}) collective-permute-start(bf16[64,1024]{1,0:T(8,128)(2,1)S(1)} %get-tuple-element.26), channel_id=1, source_target_pairs={{0,8},{1,9},{2,10},{3,11},{4,12},{5,13},{6,14},{7,15},{8,0},{9,1},... | collective-permute-start | bytes 393224 | tf_op jit(solution)/shard_map/ppermute | solution.py:35
  24.4 10.3 %copy-start.11 = (bf16[1,8192,64]{1,2,0:T(8,128)(2,1)S(1)}, bf16[1,8192,64]{1,2,0:T(8,128)(2,1)}, u32[]{:S(2)}) copy-start(bf16[1,8192,64]{1,2,0:T(8,128)(2,1)} %param.8) | copy-start | bytes 3145732
  24.4 10.3 %collective-permute-start.7 = (bf16[64,1024]{1,0:T(8,128)(2,1)S(1)}, bf16[64,1024]{1,0:T(8,128)(2,1)S(1)}, u32[]{:S(2)}, u32[]{:S(2)}) collective-permute-start(bf16[64,1024]{1,0:T(8,128)(2,1)S(1)} %get-tuple-element.27), channel_id=1, source_target_pairs={{0,12},{1,13},{2,14},{3,15},{4,8},{5,9},{6,10},{7,11},{8,4},{9,5},... | collective-permute-start | bytes 393224 | tf_op jit(solution)/shard_map/ppermute | solution.py:35
  27.0 11.2 %collective-permute-start.10 = (bf16[256,512]{1,0:T(8,128)(2,1)S(1)}, bf16[256,512]{1,0:T(8,128)(2,1)S(1)}, u32[]{:S(2)}, u32[]{:S(2)}) collective-permute-start(bf16[256,512]{1,0:T(8,128)(2,1)S(1)} %fusion), channel_id=1, source_target_pairs={{0,4},{1,5},{2,6},{3,7},{4,0},{5,1},{6,2},{7,3},{8,12},{9,13},{10,... | collective-permute-start | bytes 786440 | tf_op jit(solution)/shard_map/ppermute | solution.py:35
  28.9 9.4 %collective-permute-start.12 = (bf16[256,512]{1,0:T(8,128)(2,1)S(1)}, bf16[256,512]{1,0:T(8,128)(2,1)S(1)}, u32[]{:S(2)}, u32[]{:S(2)}) collective-permute-start(bf16[256,512]{1,0:T(8,128)(2,1)S(1)} %get-tuple-element.33), channel_id=1, source_target_pairs={{0,2},{1,3},{2,0},{3,1},{4,6},{5,7},{6,4},{7,5},{8,10},{9,11},{10,... | collective-permute-start | bytes 786440 | tf_op jit(solution)/shard_map/ppermute | solution.py:35
  29.4 12.4 %collective-permute-start.11 = (bf16[256,512]{1,0:T(8,128)(2,1)S(1)}, bf16[256,512]{1,0:T(8,128)(2,1)S(1)}, u32[]{:S(2)}, u32[]{:S(2)}) collective-permute-start(bf16[256,512]{1,0:T(8,128)(2,1)S(1)} %get-tuple-element.34), channel_id=1, source_target_pairs={{0,2},{1,3},{2,0},{3,1},{4,6},{5,7},{6,4},{7,5},{8,10},{9,11},{10,... | collective-permute-start | bytes 786440 | tf_op jit(solution)/shard_map/ppermute | solution.py:35
  34.8 7.1 %copy-start.1 = (bf16[1,64,8192]{2,1,0:T(8,128)(2,1)S(1)}, bf16[1,64,8192]{2,1,0:T(8,128)(2,1)}, u32[]{:S(2)}) copy-start(bf16[1,64,8192]{2,1,0:T(8,128)(2,1)} %param.9) | copy-start | bytes 3145732
  36.5 1.2 %collective-permute-start.8 = (f32[64,64]{1,0:T(8,128)S(1)}, f32[64,64]{1,0:T(8,128)S(1)}, u32[]{:S(2)}, u32[]{:S(2)}) collective-permute-start(f32[64,64]{1,0:T(8,128)S(1)} %shrink.1.mine_ref), channel_id=1, source_target_pairs={{0,1},{1,0},{2,3},{3,2},{4,5},{5,4},{6,7},{7,6},{8,9},{9,8},{10,11... | collective-permute-start | bytes 49160 | tf_op jit(solution)/shard_map/ppermute | solution.py:35
  43.4 6.9 %collective-permute-start.14 = (bf16[2,64,512]{2,1,0:T(8,128)(2,1)S(1)}, bf16[2,64,512]{2,1,0:T(8,128)(2,1)S(1)}, u32[]{:S(2)}, u32[]{:S(2)}) collective-permute-start(bf16[2,64,512]{2,1,0:T(8,128)(2,1)S(1)} %get-tuple-element.30), channel_id=1, source_target_pairs={{0,2},{1,3},{2,0},{3,1},{4,6},{5,7},{6,4},{7,5},{8,10},{9,11},{10,... | collective-permute-start | bytes 393224 | tf_op jit(solution)/shard_map/ppermute | solution.py:35
  44.0 4.3 %collective-permute-start.15 = (bf16[1,64,512]{2,1,0:T(8,128)(2,1)S(1)}, bf16[1,64,512]{2,1,0:T(8,128)(2,1)S(1)}, u32[]{:S(2)}, u32[]{:S(2)}) collective-permute-start(bf16[1,64,512]{2,1,0:T(8,128)(2,1)S(1)} %get-tuple-element.31), channel_id=1, source_target_pairs={{0,4},{1,5},{2,6},{3,7},{4,0},{5,1},{6,2},{7,3},{8,12},{9,13},{10,... | collective-permute-start | bytes 196616 | tf_op jit(solution)/shard_map/ppermute | solution.py:35
  44.5 5.5 %collective-permute-start.16 = (bf16[1,64,512]{2,1,0:T(8,128)(2,1)S(1)}, bf16[1,64,512]{2,1,0:T(8,128)(2,1)S(1)}, u32[]{:S(2)}, u32[]{:S(2)}) collective-permute-start(bf16[1,64,512]{2,1,0:T(8,128)(2,1)S(1)} %get-tuple-element.32), channel_id=1, source_target_pairs={{0,6},{1,7},{2,4},{3,5},{4,2},{5,3},{6,0},{7,1},{8,14},{9,15},{10,... | collective-permute-start | bytes 196616 | tf_op jit(solution)/shard_map/ppermute | solution.py:35
  47.2 7.9 %collective-permute-start.13 = (bf16[256,512]{1,0:T(8,128)(2,1)S(1)}, bf16[256,512]{1,0:T(8,128)(2,1)S(1)}, u32[]{:S(2)}, u32[]{:S(2)}) collective-permute-start(bf16[256,512]{1,0:T(8,128)(2,1)S(1)} %join.5), channel_id=1, source_target_pairs={{0,2},{1,3},{2,0},{3,1},{4,6},{5,7},{6,4},{7,5},{8,10},{9,11},{10,... | collective-permute-start | bytes 786440 | tf_op jit(solution)/shard_map/ppermute | solution.py:35
  51.1 10.3 %collective-permute-start.17 = (bf16[256,512]{1,0:T(8,128)(2,1)S(1)}, bf16[256,512]{1,0:T(8,128)(2,1)S(1)}, u32[]{:S(2)}, u32[]{:S(2)}) collective-permute-start(bf16[256,512]{1,0:T(8,128)(2,1)S(1)} %join.7), channel_id=1, source_target_pairs={{0,4},{1,5},{2,6},{3,7},{4,0},{5,1},{6,2},{7,3},{8,12},{9,13},{10,... | collective-permute-start | bytes 786440 | tf_op jit(solution)/shard_map/ppermute | solution.py:35
  52.2 9.2 %collective-permute-start.18 = (bf16[256,512]{1,0:T(8,128)(2,1)S(1)}, bf16[256,512]{1,0:T(8,128)(2,1)S(1)}, u32[]{:S(2)}, u32[]{:S(2)}) collective-permute-start(bf16[256,512]{1,0:T(8,128)(2,1)S(1)} %join.6.refs_5_), channel_id=1, source_target_pairs={{0,8},{1,9},{2,10},{3,11},{4,12},{5,13},{6,14},{7,15},{8,0},{9,1},... | collective-permute-start | bytes 786440 | tf_op jit(solution)/shard_map/ppermute | solution.py:35

commit v7 on v6

--- a/solution.py
+++ b/solution.py
@@ -46,6 +46,7 @@
         in_specs=[ANYWHERE] * (len(values) + len(after)),
         out_specs=[ANYWHERE] * len(values),
         input_output_aliases={i: i for i in range(len(values))},
+        compiler_params=params(1),
         cost_estimate=cost(0, 0),
         name="once",
     )(*values, *after)

time: 62.9 us -> 58.7 us (0.933)
  local copies, waits for them, and re-layouts: 6.41 us -> 1 us
  waiting for transfers between devices: 21.7 us -> 25.1 us
  starting transfers between devices: 20 us -> 23.1 us
  Pallas kernels: 10.6 us -> 8.07 us
  other arithmetic: 3.37 us -> 1.2 us
    unnamed x26 -> x10, local copies, waits for them, and re-layouts: 6.41 us -> 1 us
    ppermute x19, waiting for transfers between devices: 21.7 us -> 25.1 us  [swap(): return lax.ppermute(value, 'tensor', [(t, t ^ mask) for t in range(count)])]
    ppermute x19, starting transfers between devices: 20 us -> 23.1 us  [swap(): return lax.ppermute(value, 'tensor', [(t, t ^ mask) for t in range(count)])]
    pallas_call x1, Pallas kernels: 1.71 us -> 0.4 us  [shrink(): pl.pallas_call(functools.partial(shrink_kernel, len(arrived)), out_shape=...]
    convert_element_type x1, other arithmetic: 1.31 us -> 0.07 us  [staged(): y3 = swap(first[0].astype(bf16), 2)]
    pallas_call x1, Pallas kernels: 1.51 us -> 0.29 us  [grow(): pl.pallas_call(functools.partial(grow_kernel, groups), out_shape=[shape((...]
    convert_element_type x1, other arithmetic: 1.05 us -> 0.11 us  [staged(): z3 = swap((first[1] + y3.astype(f32)).astype(bf16), 4)[None]]
  transfers between devices with their start and end apart: 19 -> 19, of which waited for: 10 -> 12; matrix products, arithmetic and copies ran while one was open for 4% -> 1% of each run, Pallas kernels for 15% -> 13%
where the time goes in v7:
time: 58.7 us; the launch traced here: 58.6 us
  waiting for transfers between devices  25.1 us (43%)
  starting transfers between devices  23.1 us (39%)
  Pallas kernels  8.07 us (14%)
  other arithmetic  1.2 us (2%)
  local copies, waits for them, and re-layouts  1 us (2%)
    ppermute x19, waiting for transfers between devices, swap(): return lax.ppermute(value, 'tensor', [(t, t ^ mask) for t in range(count)])  25.1 us
    ppermute x19, starting transfers between devices, swap(): return lax.ppermute(value, 'tensor', [(t, t ^ mask) for t in range(count)])  23.1 us
    pallas_call x1, Pallas kernels, product(): pl.pallas_call(functools.partial(product_kernel, groups), out_shape=out_s...  4.85 us
    pallas_call x4, Pallas kernels, join(): pl.pallas_call(functools.partial(join_kernel, terms), out_shape=[shape((r...  1.32 us
    pallas_call x1, Pallas kernels, route(): pl.pallas_call(functools.partial(route_kernel, count, layers), out_shape=...  1.2 us
  transfers between devices with their start and end apart: 19, of which 12 were waited for; matrix products, arithmetic and copies ran while one was open for 1% of the time, Pallas kernels for 13%

profile of v7, /device:TPU:0, one launch (start us, length us, event | category | flops | bytes accessed | tf_op | source)
XLA Modules:
  0.0 58.6 jit_solution(10777110853091734542)
XLA Ops:
  0.0 0.5 collective-permute-start.1
  0.5 0.1 collective-permute-start.2
  0.5 3.0 %collective-permute-start = (bf16[256,512]{1,0:T(8,128)(2,1)}, bf16[256,512]{1,0:T(8,128)(2,1)S(1)}, u32[]{:S(2)}, u32[]{:S(2)}) collective-permute-start(bf16[256,512]{1,0:T(8,128)(2,1)} %own_ref.1), channel_id=1, source_target_pairs={{0,2},{1,3},{2,0},{3,1},{4,6},{5,7},{6,4},{7,5},{8,10},{9,11},{10,... | collective-permute-start | bytes 786440 | tf_op jit(solution)/shard_map/ppermute | solution.py:35
  3.5 0.0 copy-start.1
  3.5 1.0 %copy-done.1 = bf16[256,512]{1,0:T(8,128)(2,1)S(1)} copy-done((bf16[256,512]{1,0:T(8,128)(2,1)S(1)}, bf16[256,512]{1,0:T(8,128)(2,1)}, u32[]{:S(2)}) %copy-start.1) | copy-done | bytes 262168
  4.5 4.9 %product.1 = (bf16[2,256,512]{2,1,0:T(8,128)(2,1)S(1)}, f32[2,256,512]{2,1,0:T(8,128)S(1)}, bf16[6,256,512]{2,1,0:T(8,128)(2,1)S(1)}, f32[6,256,512]{2,1,0:T(8,128)S(1)}, f32[8,128]{1,0:T(8,128)S(1)}) custom-call(bf16[256,512]{1,0:T(8,128)(2,1)S(1)} %copy-done.1, bf16[512,8192]{1,0:T(8,128)(2,1)} %weight_hbm.1), custom_call_target="tpu_custom_call" | custom-call | flops 2147483648 | bytes 14680064 | tf_op jit(solution)/shard_map/product/pallas_call | solution.py:138
  9.3 0.8 %collective-permute-done.y_ref.refs_1_ = bf16[256,512]{1,0:T(8,128)(2,1)S(1)} collective-permute-done((bf16[256,512]{1,0:T(8,128)(2,1)}, bf16[256,512]{1,0:T(8,128)(2,1)S(1)}, u32[]{:S(2)}, u32[]{:S(2)}) %collective-permute-start) | collective-permute-done | bytes 262176 | tf_op jit(solution)/shard_map/ppermute | solution.py:35
  10.2 0.0 collective-permute-done.1.refs_2_.other_ref
  10.2 0.0 collective-permute-done.2.refs_3_.up_other_ref
  10.2 0.1 collective-permute-start.3
  10.2 1.9 %collective-permute-done.3.refs_1_ = bf16[2,256,512]{2,1,0:T(8,128)(2,1)S(1)} collective-permute-done((bf16[2,256,512]{2,1,0:T(8,128)(2,1)S(1)}, bf16[2,256,512]{2,1,0:T(8,128)(2,1)S(1)}, u32[]{:S(2)}, u32[]{:S(2)}) %collective-permute-start.3) | collective-permute-done | bytes 524320 | tf_op jit(solution)/shard_map/ppermute | solution.py:35
  12.1 0.0 copy-start.2
  12.1 0.0 copy-start.3
  12.1 0.1 collective-permute-start.4
  12.3 0.1 fusion.1
  12.4 1.8 %collective-permute-start.9 = (bf16[256,512]{1,0:T(8,128)(2,1)S(1)}, bf16[256,512]{1,0:T(8,128)(2,1)S(1)}, u32[]{:S(2)}, u32[]{:S(2)}) collective-permute-start(bf16[256,512]{1,0:T(8,128)(2,1)S(1)} %fusion.1), channel_id=1, source_target_pairs={{0,2},{1,3},{2,0},{3,1},{4,6},{5,7},{6,4},{7,5},{8,10},{9,11},{10,... | collective-permute-start | bytes 786440 | tf_op jit(solution)/shard_map/ppermute | solution.py:35
  14.2 0.0 copy-done.2
  14.2 0.0 copy-done.3
  14.2 1.2 %route.1 = (s32[1,256]{1,0:T(1,128)S(1)}, bf16[64,1024]{1,0:T(8,128)(2,1)S(1)}, bf16[64,1024]{1,0:T(8,128)(2,1)S(1)}, bf16[64,1024]{1,0:T(8,128)(2,1)S(1)}, bf16[64,1024]{1,0:T(8,128)(2,1)S(1)}) custom-call(s32[16]{0:T(128)S(1)} %copy-done.3, s32[1,256]{1,0:T(1,128)S(1)} %bitcast.26, bf16[256,512]{1,0:T(8,128)(2,1)S(1)} %copy-done.1, ...), custom_call_target="tpu_custom_call" | custom-call | flops 134217728 | bytes 1048576 | tf_op jit(solution)/shard_map/route/pallas_call | solution.py:88
  15.4 1.6 %collective-permute-start.5 = (bf16[64,1024]{1,0:T(8,128)(2,1)S(1)}, bf16[64,1024]{1,0:T(8,128)(2,1)S(1)}, u32[]{:S(2)}, u32[]{:S(2)}) collective-permute-start(bf16[64,1024]{1,0:T(8,128)(2,1)S(1)} %get-tuple-element.25), channel_id=1, source_target_pairs={{0,4},{1,5},{2,6},{3,7},{4,0},{5,1},{6,2},{7,3},{8,12},{9,13},{10,... | collective-permute-start | bytes 393224 | tf_op jit(solution)/shard_map/ppermute | solution.py:35
  17.0 2.6 %collective-permute-start.6 = (bf16[64,1024]{1,0:T(8,128)(2,1)S(1)}, bf16[64,1024]{1,0:T(8,128)(2,1)S(1)}, u32[]{:S(2)}, u32[]{:S(2)}) collective-permute-start(bf16[64,1024]{1,0:T(8,128)(2,1)S(1)} %get-tuple-element.26), channel_id=1, source_target_pairs={{0,8},{1,9},{2,10},{3,11},{4,12},{5,13},{6,14},{7,15},{8,0},{9,1},... | collective-permute-start | bytes 393224 | tf_op jit(solution)/shard_map/ppermute | solution.py:35
  19.6 0.0 copy-start.4
  19.6 0.2 collective-permute-start.7
  19.8 1.2 %collective-permute-done.9 = bf16[256,512]{1,0:T(8,128)(2,1)S(1)} collective-permute-done((bf16[256,512]{1,0:T(8,128)(2,1)S(1)}, bf16[256,512]{1,0:T(8,128)(2,1)S(1)}, u32[]{:S(2)}, u32[]{:S(2)}) %collective-permute-start.9) | collective-permute-done | bytes 262176 | tf_op jit(solution)/shard_map/ppermute | solution.py:35
  21.0 0.1 fusion
  21.1 1.9 %collective-permute-start.10 = (bf16[256,512]{1,0:T(8,128)(2,1)S(1)}, bf16[256,512]{1,0:T(8,128)(2,1)S(1)}, u32[]{:S(2)}, u32[]{:S(2)}) collective-permute-start(bf16[256,512]{1,0:T(8,128)(2,1)S(1)} %fusion), channel_id=1, source_target_pairs={{0,4},{1,5},{2,6},{3,7},{4,0},{5,1},{6,2},{7,3},{8,12},{9,13},{10,... | collective-permute-start | bytes 786440 | tf_op jit(solution)/shard_map/ppermute | solution.py:35
  23.0 0.0 collective-permute-done.4.refs_1_
  23.0 0.2 fusion.3
  23.1 1.6 %collective-permute-start.12 = (bf16[256,512]{1,0:T(8,128)(2,1)S(1)}, bf16[256,512]{1,0:T(8,128)(2,1)S(1)}, u32[]{:S(2)}, u32[]{:S(2)}) collective-permute-start(bf16[256,512]{1,0:T(8,128)(2,1)S(1)} %get-tuple-element.33), channel_id=1, source_target_pairs={{0,2},{1,3},{2,0},{3,1},{4,6},{5,7},{6,4},{7,5},{8,10},{9,11},{10,... | collective-permute-start | bytes 786440 | tf_op jit(solution)/shard_map/ppermute | solution.py:35
  24.7 0.0 collective-permute-done.5.refs_1_
  24.7 0.5 collective-permute-start.11
  25.2 4.7 %collective-permute-done.6.refs_2_ = bf16[64,1024]{1,0:T(8,128)(2,1)S(1)} collective-permute-done((bf16[64,1024]{1,0:T(8,128)(2,1)S(1)}, bf16[64,1024]{1,0:T(8,128)(2,1)S(1)}, u32[]{:S(2)}, u32[]{:S(2)}) %collective-permute-start.6) | collective-permute-done | bytes 131104 | tf_op jit(solution)/shard_map/ppermute | solution.py:35
  30.0 0.0 collective-permute-done.7.refs_3_
  30.0 0.0 copy-done.4
  30.0 0.0 copy-start
  30.0 0.4 shrink.1.mine_ref
  30.4 0.0 collective-permute-start.8
  30.4 1.2 %collective-permute-done.8.other_ref = f32[64,64]{1,0:T(8,128)S(1)} collective-permute-done((f32[64,64]{1,0:T(8,128)S(1)}, f32[64,64]{1,0:T(8,128)S(1)}, u32[]{:S(2)}, u32[]{:S(2)}) %collective-permute-start.8) | collective-permute-done | bytes 16416 | tf_op jit(solution)/shard_map/ppermute | solution.py:35
  31.6 1.0 %collective-permute-done.10 = bf16[256,512]{1,0:T(8,128)(2,1)S(1)} collective-permute-done((bf16[256,512]{1,0:T(8,128)(2,1)S(1)}, bf16[256,512]{1,0:T(8,128)(2,1)S(1)}, u32[]{:S(2)}, u32[]{:S(2)}) %collective-permute-start.10) | collective-permute-done | bytes 262176 | tf_op jit(solution)/shard_map/ppermute | solution.py:35
  32.6 0.0 collective-permute-done.12
  32.6 3.7 %collective-permute-done.11 = bf16[256,512]{1,0:T(8,128)(2,1)S(1)} collective-permute-done((bf16[256,512]{1,0:T(8,128)(2,1)S(1)}, bf16[256,512]{1,0:T(8,128)(2,1)S(1)}, u32[]{:S(2)}, u32[]{:S(2)}) %collective-permute-start.11) | collective-permute-done | bytes 262176 | tf_op jit(solution)/shard_map/ppermute | solution.py:35
  36.3 0.0 copy-done
  36.3 0.3 grow.1
  36.6 1.6 %collective-permute-start.14 = (bf16[2,64,512]{2,1,0:T(8,128)(2,1)S(1)}, bf16[2,64,512]{2,1,0:T(8,128)(2,1)S(1)}, u32[]{:S(2)}, u32[]{:S(2)}) collective-permute-start(bf16[2,64,512]{2,1,0:T(8,128)(2,1)S(1)} %get-tuple-element.30), channel_id=1, source_target_pairs={{0,2},{1,3},{2,0},{3,1},{4,6},{5,7},{6,4},{7,5},{8,10},{9,11},{10,... | collective-permute-start | bytes 393224 | tf_op jit(solution)/shard_map/ppermute | solution.py:35
  38.2 0.4 collective-permute-start.15
  38.7 1.5 %collective-permute-start.16 = (bf16[1,64,512]{2,1,0:T(8,128)(2,1)S(1)}, bf16[1,64,512]{2,1,0:T(8,128)(2,1)S(1)}, u32[]{:S(2)}, u32[]{:S(2)}) collective-permute-start(bf16[1,64,512]{2,1,0:T(8,128)(2,1)S(1)} %get-tuple-element.32), channel_id=1, source_target_pairs={{0,6},{1,7},{2,4},{3,5},{4,2},{5,3},{6,0},{7,1},{8,14},{9,15},{10,... | collective-permute-start | bytes 196616 | tf_op jit(solution)/shard_map/ppermute | solution.py:35
  40.2 0.3 join.5
  40.4 1.6 %collective-permute-start.13 = (bf16[256,512]{1,0:T(8,128)(2,1)S(1)}, bf16[256,512]{1,0:T(8,128)(2,1)S(1)}, u32[]{:S(2)}, u32[]{:S(2)}) collective-permute-start(bf16[256,512]{1,0:T(8,128)(2,1)S(1)} %join.5), channel_id=1, source_target_pairs={{0,2},{1,3},{2,0},{3,1},{4,6},{5,7},{6,4},{7,5},{8,10},{9,11},{10,... | collective-permute-start | bytes 786440 | tf_op jit(solution)/shard_map/ppermute | solution.py:35
  42.0 0.4 collective-permute-done.15.refs_4_
  42.5 1.5 %collective-permute-done.16.refs_5_ = bf16[1,64,512]{2,1,0:T(8,128)(2,1)S(1)} collective-permute-done((bf16[1,64,512]{2,1,0:T(8,128)(2,1)S(1)}, bf16[1,64,512]{2,1,0:T(8,128)(2,1)S(1)}, u32[]{:S(2)}, u32[]{:S(2)}) %collective-permute-start.16) | collective-permute-done | bytes 65568 | tf_op jit(solution)/shard_map/ppermute | solution.py:35
  43.9 0.2 collective-permute-done.14.refs_3_
  44.1 0.5 join.6.refs_5_
  44.6 0.3 join.7
  44.9 1.4 %collective-permute-start.17 = (bf16[256,512]{1,0:T(8,128)(2,1)S(1)}, bf16[256,512]{1,0:T(8,128)(2,1)S(1)}, u32[]{:S(2)}, u32[]{:S(2)}) collective-permute-start(bf16[256,512]{1,0:T(8,128)(2,1)S(1)} %join.7), channel_id=1, source_target_pairs={{0,4},{1,5},{2,6},{3,7},{4,0},{5,1},{6,2},{7,3},{8,12},{9,13},{10,... | collective-permute-start | bytes 786440 | tf_op jit(solution)/shard_map/ppermute | solution.py:35
  46.4 2.6 %collective-permute-start.18 = (bf16[256,512]{1,0:T(8,128)(2,1)S(1)}, bf16[256,512]{1,0:T(8,128)(2,1)S(1)}, u32[]{:S(2)}, u32[]{:S(2)}) collective-permute-start(bf16[256,512]{1,0:T(8,128)(2,1)S(1)} %join.6.refs_5_), channel_id=1, source_target_pairs={{0,8},{1,9},{2,10},{3,11},{4,12},{5,13},{6,14},{7,15},{8,0},{9,1},... | collective-permute-start | bytes 786440 | tf_op jit(solution)/shard_map/ppermute | solution.py:35
  49.0 0.3 join.4
  49.2 0.0 collective-permute-done.13
  49.2 5.7 %collective-permute-done.17 = bf16[256,512]{1,0:T(8,128)(2,1)S(1)} collective-permute-done((bf16[256,512]{1,0:T(8,128)(2,1)S(1)}, bf16[256,512]{1,0:T(8,128)(2,1)S(1)}, u32[]{:S(2)}, u32[]{:S(2)}) %collective-permute-start.17) | collective-permute-done | bytes 262176 | tf_op jit(solution)/shard_map/ppermute | solution.py:35
  54.9 2.8 %collective-permute-done.18 = bf16[256,512]{1,0:T(8,128)(2,1)S(1)} collective-permute-done((bf16[256,512]{1,0:T(8,128)(2,1)S(1)}, bf16[256,512]{1,0:T(8,128)(2,1)S(1)}, u32[]{:S(2)}, u32[]{:S(2)}) %collective-permute-start.18) | collective-permute-done | bytes 262176 | tf_op jit(solution)/shard_map/ppermute | solution.py:35
  57.7 0.9 %add_convert_fusion = bf16[256,512]{1,0:T(8,128)(2,1)} fusion(bf16[256,512]{1,0:T(8,128)(2,1)S(1)} %collective-permute-done.18, bf16[256,512]{1,0:T(8,128)(2,1)S(1)} %collective-permute-done.17, f32[256,512]{1,0:T(8,128)S(1)} %join.4, bf16[256,512]{1,0:T(8,128)(2,1)S(1)} %collective-permute-done.13), kind=kLoop, calls=%fused_computation.2 | loop fusion | flops 917504 | bytes 1572864 | tf_op jit(solution)/shard_map/convert_element_type | solution.py:291
  (2 shorter events, 0.0 us)
Async XLA Ops:
  0.0 10.2 %collective-permute-start.1 = (bf16[64,8192]{1,0:T(8,128)(2,1)}, bf16[64,8192]{1,0:T(8,128)(2,1)S(1)}, u32[]{:S(2)}, u32[]{:S(2)}) collective-permute-start(bf16[64,8192]{1,0:T(8,128)(2,1)} %bitcast.27), channel_id=1, source_target_pairs={{0,1},{1,0},{2,3},{3,2},{4,5},{5,4},{6,7},{7,6},{8,9},{9,8},{10,11... | collective-permute-start | bytes 3145736 | tf_op jit(solution)/shard_map/ppermute | solution.py:35
  0.5 9.7 %collective-permute-start.2 = (bf16[64,8192]{1,0:T(8,128)(2,1)}, bf16[64,8192]{1,0:T(8,128)(2,1)S(1)}, u32[]{:S(2)}, u32[]{:S(2)}) collective-permute-start(bf16[64,8192]{1,0:T(8,128)(2,1)} %bitcast.18), channel_id=1, source_target_pairs={{0,1},{1,0},{2,3},{3,2},{4,5},{5,4},{6,7},{7,6},{8,9},{9,8},{10,11... | collective-permute-start | bytes 3145736 | tf_op jit(solution)/shard_map/ppermute | solution.py:35
  0.5 9.6 %collective-permute-start = (bf16[256,512]{1,0:T(8,128)(2,1)}, bf16[256,512]{1,0:T(8,128)(2,1)S(1)}, u32[]{:S(2)}, u32[]{:S(2)}) collective-permute-start(bf16[256,512]{1,0:T(8,128)(2,1)} %own_ref.1), channel_id=1, source_target_pairs={{0,2},{1,3},{2,0},{3,1},{4,6},{5,7},{6,4},{7,5},{8,10},{9,11},{10,... | collective-permute-start | bytes 786440 | tf_op jit(solution)/shard_map/ppermute | solution.py:35
  3.5 1.0 %copy-start.1 = (bf16[256,512]{1,0:T(8,128)(2,1)S(1)}, bf16[256,512]{1,0:T(8,128)(2,1)}, u32[]{:S(2)}) copy-start(bf16[256,512]{1,0:T(8,128)(2,1)} %own_ref.1) | copy-start | bytes 786436
  10.2 2.0 %collective-permute-start.3 = (bf16[2,256,512]{2,1,0:T(8,128)(2,1)S(1)}, bf16[2,256,512]{2,1,0:T(8,128)(2,1)S(1)}, u32[]{:S(2)}, u32[]{:S(2)}) collective-permute-start(bf16[2,256,512]{2,1,0:T(8,128)(2,1)S(1)} %once.2), channel_id=1, source_target_pairs={{0,1},{1,0},{2,3},{3,2},{4,5},{5,4},{6,7},{7,6},{8,9},{9,8},{10,11... | collective-permute-start | bytes 1572872 | tf_op jit(solution)/shard_map/ppermute | solution.py:35
  12.1 2.0 %copy-start.2 = (s32[256]{0:T(256)S(1)}, s32[256]{0:T(256)}, u32[]{:S(2)}) copy-start(s32[256]{0:T(256)} %param.10) | copy-start | bytes 3076
  12.1 2.0 %copy-start.3 = (s32[16]{0:T(128)S(1)}, s32[16]{0:T(128)}, u32[]{:S(2)}) copy-start(s32[16]{0:T(128)} %slot_hbm.1) | copy-start | bytes 196
  12.1 10.8 %collective-permute-start.4 = (bf16[6,256,512]{2,1,0:T(8,128)(2,1)S(1)}, bf16[6,256,512]{2,1,0:T(8,128)(2,1)S(1)}, u32[]{:S(2)}, u32[]{:S(2)}) collective-permute-start(bf16[6,256,512]{2,1,0:T(8,128)(2,1)S(1)} %once.3), channel_id=1, source_target_pairs={{0,1},{1,0},{2,3},{3,2},{4,5},{5,4},{6,7},{7,6},{8,9},{9,8},{10,11... | collective-permute-start | bytes 4718600 | tf_op jit(solution)/shard_map/ppermute | solution.py:35
  12.4 8.7 %collective-permute-start.9 = (bf16[256,512]{1,0:T(8,128)(2,1)S(1)}, bf16[256,512]{1,0:T(8,128)(2,1)S(1)}, u32[]{:S(2)}, u32[]{:S(2)}) collective-permute-start(bf16[256,512]{1,0:T(8,128)(2,1)S(1)} %fusion.1), channel_id=1, source_target_pairs={{0,2},{1,3},{2,0},{3,1},{4,6},{5,7},{6,4},{7,5},{8,10},{9,11},{10,... | collective-permute-start | bytes 786440 | tf_op jit(solution)/shard_map/ppermute | solution.py:35
  15.4 9.3 %collective-permute-start.5 = (bf16[64,1024]{1,0:T(8,128)(2,1)S(1)}, bf16[64,1024]{1,0:T(8,128)(2,1)S(1)}, u32[]{:S(2)}, u32[]{:S(2)}) collective-permute-start(bf16[64,1024]{1,0:T(8,128)(2,1)S(1)} %get-tuple-element.25), channel_id=1, source_target_pairs={{0,4},{1,5},{2,6},{3,7},{4,0},{5,1},{6,2},{7,3},{8,12},{9,13},{10,... | collective-permute-start | bytes 393224 | tf_op jit(solution)/shard_map/ppermute | solution.py:35
  17.0 13.0 %collective-permute-start.6 = (bf16[64,1024]{1,0:T(8,128)(2,1)S(1)}, bf16[64,1024]{1,0:T(8,128)(2,1)S(1)}, u32[]{:S(2)}, u32[]{:S(2)}) collective-permute-start(bf16[64,1024]{1,0:T(8,128)(2,1)S(1)} %get-tuple-element.26), channel_id=1, source_target_pairs={{0,8},{1,9},{2,10},{3,11},{4,12},{5,13},{6,14},{7,15},{8,0},{9,1},... | collective-permute-start | bytes 393224 | tf_op jit(solution)/shard_map/ppermute | solution.py:35
  19.6 10.4 %copy-start.4 = (bf16[1,8192,64]{1,2,0:T(8,128)(2,1)S(1)}, bf16[1,8192,64]{1,2,0:T(8,128)(2,1)}, u32[]{:S(2)}) copy-start(bf16[1,8192,64]{1,2,0:T(8,128)(2,1)} %param.8) | copy-start | bytes 3145732
  19.6 10.4 %collective-permute-start.7 = (bf16[64,1024]{1,0:T(8,128)(2,1)S(1)}, bf16[64,1024]{1,0:T(8,128)(2,1)S(1)}, u32[]{:S(2)}, u32[]{:S(2)}) collective-permute-start(bf16[64,1024]{1,0:T(8,128)(2,1)S(1)} %get-tuple-element.27), channel_id=1, source_target_pairs={{0,12},{1,13},{2,14},{3,15},{4,8},{5,9},{6,10},{7,11},{8,4},{9,5},... | collective-permute-start | bytes 393224 | tf_op jit(solution)/shard_map/ppermute | solution.py:35
  21.1 11.5 %collective-permute-start.10 = (bf16[256,512]{1,0:T(8,128)(2,1)S(1)}, bf16[256,512]{1,0:T(8,128)(2,1)S(1)}, u32[]{:S(2)}, u32[]{:S(2)}) collective-permute-start(bf16[256,512]{1,0:T(8,128)(2,1)S(1)} %fusion), channel_id=1, source_target_pairs={{0,4},{1,5},{2,6},{3,7},{4,0},{5,1},{6,2},{7,3},{8,12},{9,13},{10,... | collective-permute-start | bytes 786440 | tf_op jit(solution)/shard_map/ppermute | solution.py:35
  23.1 9.5 %collective-permute-start.12 = (bf16[256,512]{1,0:T(8,128)(2,1)S(1)}, bf16[256,512]{1,0:T(8,128)(2,1)S(1)}, u32[]{:S(2)}, u32[]{:S(2)}) collective-permute-start(bf16[256,512]{1,0:T(8,128)(2,1)S(1)} %get-tuple-element.33), channel_id=1, source_target_pairs={{0,2},{1,3},{2,0},{3,1},{4,6},{5,7},{6,4},{7,5},{8,10},{9,11},{10,... | collective-permute-start | bytes 786440 | tf_op jit(solution)/shard_map/ppermute | solution.py:35
  24.7 11.6 %collective-permute-start.11 = (bf16[256,512]{1,0:T(8,128)(2,1)S(1)}, bf16[256,512]{1,0:T(8,128)(2,1)S(1)}, u32[]{:S(2)}, u32[]{:S(2)}) collective-permute-start(bf16[256,512]{1,0:T(8,128)(2,1)S(1)} %get-tuple-element.34), channel_id=1, source_target_pairs={{0,2},{1,3},{2,0},{3,1},{4,6},{5,7},{6,4},{7,5},{8,10},{9,11},{10,... | collective-permute-start | bytes 786440 | tf_op jit(solution)/shard_map/ppermute | solution.py:35
  30.0 6.3 %copy-start = (bf16[1,64,8192]{2,1,0:T(8,128)(2,1)S(1)}, bf16[1,64,8192]{2,1,0:T(8,128)(2,1)}, u32[]{:S(2)}) copy-start(bf16[1,64,8192]{2,1,0:T(8,128)(2,1)} %param.9) | copy-start | bytes 3145732
  30.4 1.2 %collective-permute-start.8 = (f32[64,64]{1,0:T(8,128)S(1)}, f32[64,64]{1,0:T(8,128)S(1)}, u32[]{:S(2)}, u32[]{:S(2)}) collective-permute-start(f32[64,64]{1,0:T(8,128)S(1)} %shrink.1.mine_ref), channel_id=1, source_target_pairs={{0,1},{1,0},{2,3},{3,2},{4,5},{5,4},{6,7},{7,6},{8,9},{9,8},{10,11... | collective-permute-start | bytes 49160 | tf_op jit(solution)/shard_map/ppermute | solution.py:35
  36.6 7.5 %collective-permute-start.14 = (bf16[2,64,512]{2,1,0:T(8,128)(2,1)S(1)}, bf16[2,64,512]{2,1,0:T(8,128)(2,1)S(1)}, u32[]{:S(2)}, u32[]{:S(2)}) collective-permute-start(bf16[2,64,512]{2,1,0:T(8,128)(2,1)S(1)} %get-tuple-element.30), channel_id=1, source_target_pairs={{0,2},{1,3},{2,0},{3,1},{4,6},{5,7},{6,4},{7,5},{8,10},{9,11},{10,... | collective-permute-start | bytes 393224 | tf_op jit(solution)/shard_map/ppermute | solution.py:35
  38.2 4.3 %collective-permute-start.15 = (bf16[1,64,512]{2,1,0:T(8,128)(2,1)S(1)}, bf16[1,64,512]{2,1,0:T(8,128)(2,1)S(1)}, u32[]{:S(2)}, u32[]{:S(2)}) collective-permute-start(bf16[1,64,512]{2,1,0:T(8,128)(2,1)S(1)} %get-tuple-element.31), channel_id=1, source_target_pairs={{0,4},{1,5},{2,6},{3,7},{4,0},{5,1},{6,2},{7,3},{8,12},{9,13},{10,... | collective-permute-start | bytes 196616 | tf_op jit(solution)/shard_map/ppermute | solution.py:35
  38.7 5.3 %collective-permute-start.16 = (bf16[1,64,512]{2,1,0:T(8,128)(2,1)S(1)}, bf16[1,64,512]{2,1,0:T(8,128)(2,1)S(1)}, u32[]{:S(2)}, u32[]{:S(2)}) collective-permute-start(bf16[1,64,512]{2,1,0:T(8,128)(2,1)S(1)} %get-tuple-element.32), channel_id=1, source_target_pairs={{0,6},{1,7},{2,4},{3,5},{4,2},{5,3},{6,0},{7,1},{8,14},{9,15},{10,... | collective-permute-start | bytes 196616 | tf_op jit(solution)/shard_map/ppermute | solution.py:35
  40.4 8.8 %collective-permute-start.13 = (bf16[256,512]{1,0:T(8,128)(2,1)S(1)}, bf16[256,512]{1,0:T(8,128)(2,1)S(1)}, u32[]{:S(2)}, u32[]{:S(2)}) collective-permute-start(bf16[256,512]{1,0:T(8,128)(2,1)S(1)} %join.5), channel_id=1, source_target_pairs={{0,2},{1,3},{2,0},{3,1},{4,6},{5,7},{6,4},{7,5},{8,10},{9,11},{10,... | collective-permute-start | bytes 786440 | tf_op jit(solution)/shard_map/ppermute | solution.py:35
  44.9 10.0 %collective-permute-start.17 = (bf16[256,512]{1,0:T(8,128)(2,1)S(1)}, bf16[256,512]{1,0:T(8,128)(2,1)S(1)}, u32[]{:S(2)}, u32[]{:S(2)}) collective-permute-start(bf16[256,512]{1,0:T(8,128)(2,1)S(1)} %join.7), channel_id=1, source_target_pairs={{0,4},{1,5},{2,6},{3,7},{4,0},{5,1},{6,2},{7,3},{8,12},{9,13},{10,... | collective-permute-start | bytes 786440 | tf_op jit(solution)/shard_map/ppermute | solution.py:35
  46.4 11.4 %collective-permute-start.18 = (bf16[256,512]{1,0:T(8,128)(2,1)S(1)}, bf16[256,512]{1,0:T(8,128)(2,1)S(1)}, u32[]{:S(2)}, u32[]{:S(2)}) collective-permute-start(bf16[256,512]{1,0:T(8,128)(2,1)S(1)} %join.6.refs_5_), channel_id=1, source_target_pairs={{0,8},{1,9},{2,10},{3,11},{4,12},{5,13},{6,14},{7,15},{8,0},{9,1},... | collective-permute-start | bytes 786440 | tf_op jit(solution)/shard_map/ppermute | solution.py:35

commit v8 on v7

--- a/solution.py
+++ b/solution.py
@@ -151,14 +151,14 @@
     )(attended, out_weight)
 
 
-def shrink_kernel(layers, down_ref, other_ref, *refs):
-    arrived_refs, out_ref = refs[:layers], refs[-1]
+def shrink_kernel(distances, down_ref, other_ref, *refs):
+    arrived_refs, out_ref = refs[: len(distances)], refs[-1]
     me = lax.axis_index("tensor")
     width = arrived_refs[0].shape[1] // 2
     over = (((1,), (1,)), ((), ()))
     for part, weights_ref in enumerate((down_ref, other_ref)):
         total = jnp.zeros((CAP, down_ref.shape[0]), jnp.float32)
-        for k, arrived_ref in enumerate(arrived_refs):
+        for k, arrived_ref in zip(distances, arrived_refs):
             for side in range(2):
                 block = pl.ds(pl.multiple_of((me ^ (4 * k + 2 * side)) * width, width), width)
                 total += lax.dot_general(
@@ -172,14 +172,14 @@
 
 def shrink(down, other, arrived, *after):
     return pl.pallas_call(
-        functools.partial(shrink_kernel, len(arrived)),
+        functools.partial(shrink_kernel, tuple(arrived)),
         out_shape=shape((2 * CAP, down.shape[0]), jnp.float32),
         in_specs=[IN_VMEM] * (2 + len(arrived)) + [ANYWHERE] * len(after),
         out_specs=IN_VMEM,
         compiler_params=params(16),
-        cost_estimate=cost(40 * 10**9, 4 * down.size),
+        cost_estimate=cost(40*10**9, 4 * down.size),
         name="shrink",
-    )(down, other, *arrived, *after)
+    )(down, other, *arrived.values(), *after)
 
 
 def grow_kernel(groups, mine_ref, other_ref, up_ref, up_other_ref, *refs):
@@ -203,7 +203,7 @@
         in_specs=[IN_VMEM] * 4 + [ANYWHERE] * len(after),
         out_specs=[IN_VMEM] * len(groups),
         compiler_params=params(16),
-        cost_estimate=cost(4 * CAP * up.size, 4 * up.size),
+        cost_estimate=cost(4*CAP*up.size, 4 * up.size),
         name="grow",
     )(mine, other, up, up_other, *after)
 
@@ -247,47 +247,48 @@
     up, down = adapter_up[0], jnp.swapaxes(adapter_down, 1, 2)[0]
     from_y = swap(attended, 2)
     down_other, up_other = swap(down, 1), swap(up, 1)
-    chips = (5, 4, 3, 2, 1, 0)
-    away_first, stay_first, away, stay, token = product(attended, out_weight, ((7, 6), chips), 44)
-    (away_first,) = once((away_first,), from_y, down_other, up_other)
-    came_first = swap(away_first, 1)
-    (away,) = once((away,), came_first)
-    came = swap(away, 1)
-    target, outgoing = route(adapter_slot, row_adapter, attended, from_y, token)
-    arrived = [outgoing[0]] + [None] * 3
-    for k in (2, 3, 1):
-        arrived[k] = swap(outgoing[k], 4 * k)
-    first = [stay_first[i] + came_first[i].astype(f32) for i in range(2)]
-    y3 = swap(first[0].astype(bf16), 2)
-    y2 = swap((stay[0] + came[0].astype(f32)).astype(bf16), 2)[None]
-    y1 = swap((stay[2] + came[2].astype(f32)).astype(bf16), 2)[None]
-    z3 = swap((first[1] + y3.astype(f32)).astype(bf16), 4)[None]
+    chips = (6, 4, 3, 2, 1, 0)
+    away_first, stay_first, away, stay, token = product(attended, out_weight, ((7, 5), chips), 44)
+    target, outgoing = route(adapter_slot, row_adapter, attended, from_y, token, down_other, up_other)
+    arrived = {k: swap(outgoing[k], 4 * k) for k in (2,3,1)}
+    arrived[0] = outgoing[0]
+    away_first, away = once((away_first, away), target)
+    came_first, came = swap(away_first, 1), swap(away, 1)
+
+    def base(m):
+        return stay[chips.index(m)] + came[chips.index(m)].astype(f32)
+
+    y3 = swap((stay_first[0] + came_first[0].astype(f32)).astype(bf16), 2)
+    y2 = swap((stay_first[1] + came_first[1].astype(f32)).astype(bf16), 2)[None]
     mine = shrink(down, down_other, arrived)
+    ready3, go1 = once((y3, base(3).astype(bf16)), mine)
+    z3 = swap((base(6) + ready3.astype(f32)).astype(bf16), 4)[None]
+    y1 = swap(go1, 2)[None]
     here_chips = (4, 2, 1, 0)
     groups = (tuple(2 * m for m in here_chips), (10, 6), (12,), (14,))
-    here, over2, over4, over6 = grow(mine, swap(mine, 1), up, up_other, groups, z3, y2, y1)
+    here, over2, over4, over6 = grow(mine, swap(mine, 1), up, up_other, groups, y3, y2)
     over2, over4, over6 = swap(over2, 2), swap(over4, 4), swap(over6, 6)
 
     def blocks(m):
         return ((0, chips.index(m)), (1, chips.index(m))), ((2, here_chips.index(m), 0),)
 
-    base, grown = blocks(4)
+    sums, grown = blocks(4)
     (sum2,) = join(
         target,
         [stay, came, here, over2, over4, over6, z3, y2],
-        ((base + ((6, 0), (7, 0)), grown + ((3, 0, 2), (4, 0, 4), (5, 0, 6))),),
+        ((sums + ((6, 0), (7, 0)), grown + ((3, 0, 2), (4, 0, 4), (5, 0, 6))),),
         bf16,
     )
     z2 = swap(sum2, 8)
-    base, grown = blocks(2)
+    sums, grown = blocks(2)
     (sum1,) = join(
-        target, [stay, came, here, over2, y1, sum2], ((base + ((4, 0),), grown + ((3, 1, 2),)),), bf16
+        target, [stay, came, here, over2, y1, sum2], ((sums + ((4, 0),), grown + ((3, 1, 2),)),), bf16
     )
     z1 = swap(sum1, 4)
-    (go0,) = join(target, [stay, came, here], (blocks(1),), bf16)
+    (go0,) = join(target, [stay, came, here, sum2], (blocks(1),), bf16)
     y0 = swap(go0, 2)
     (side0,) = join(target, [stay, came, here], (blocks(0),), f32)
-    total = side0 + y0.astype(f32) + z1.astype(f32) + z2.astype(f32)
+    total = side0 + y0.astype(f32) + z2.astype(f32) + z1.astype(f32)
     return total.astype(bf16)
 
 

time: 58.7 us -> 60.7 us (1.034)
  waiting for transfers between devices: 25.1 us -> 27 us
    ppermute x19, waiting for transfers between devices: 25.1 us -> 27 us  [swap(): return lax.ppermute(value, 'tensor', [(t, t ^ mask) for t in range(count)])]
  transfers between devices with their start and end apart: 19 -> 19, of which waited for: 12 -> 9; matrix products, arithmetic and copies ran while one was open for 1% -> 0% of each run, Pallas kernels for 13% -> 11%
where the time goes in v8:
time: 60.7 us; the launch traced here: 60.2 us
  waiting for transfers between devices  27 us (44%)
  starting transfers between devices  22.8 us (38%)
  Pallas kernels  8.07 us (13%)
  other arithmetic  1.2 us (2%)
  local copies, waits for them, and re-layouts  1 us (2%)
    ppermute x19, waiting for transfers between devices, swap(): return lax.ppermute(value, 'tensor', [(t, t ^ mask) for t in range(count)])  27 us
    ppermute x19, starting transfers between devices, swap(): return lax.ppermute(value, 'tensor', [(t, t ^ mask) for t in range(count)])  22.8 us
    pallas_call x1, Pallas kernels, product(): pl.pallas_call(functools.partial(product_kernel, groups), out_shape=out_s...  4.85 us
    pallas_call x4, Pallas kernels, join(): pl.pallas_call(functools.partial(join_kernel, terms), out_shape=[shape((r...  1.31 us
  transfers between devices with their start and end apart: 19, of which 9 were waited for; matrix products, arithmetic and copies ran while one was open for 0% of the time, Pallas kernels for 11%

profile of v8, /device:TPU:0, one launch (start us, length us, event | category | flops | bytes accessed | tf_op | source)
XLA Modules:
  0.0 60.2 jit_solution(4065171930313978919)
XLA Ops:
  0.0 0.5 collective-permute-start.1
  0.5 0.0 copy-start.2
  0.5 0.0 copy-start.3
  0.5 0.1 collective-permute-start.2
  0.5 3.0 %collective-permute-start = (bf16[256,512]{1,0:T(8,128)(2,1)}, bf16[256,512]{1,0:T(8,128)(2,1)S(1)}, u32[]{:S(2)}, u32[]{:S(2)}) collective-permute-start(bf16[256,512]{1,0:T(8,128)(2,1)} %own_ref.1), channel_id=1, source_target_pairs={{0,2},{1,3},{2,0},{3,1},{4,6},{5,7},{6,4},{7,5},{8,10},{9,11},{10,... | collective-permute-start | bytes 786440 | tf_op jit(solution)/shard_map/ppermute | solution.py:35
  3.5 0.0 copy-start.1
  3.5 1.0 %copy-done.1 = bf16[256,512]{1,0:T(8,128)(2,1)S(1)} copy-done((bf16[256,512]{1,0:T(8,128)(2,1)S(1)}, bf16[256,512]{1,0:T(8,128)(2,1)}, u32[]{:S(2)}) %copy-start.1) | copy-done | bytes 262168
  4.5 4.9 %product.1 = (bf16[2,256,512]{2,1,0:T(8,128)(2,1)S(1)}, f32[2,256,512]{2,1,0:T(8,128)S(1)}, bf16[6,256,512]{2,1,0:T(8,128)(2,1)S(1)}, f32[6,256,512]{2,1,0:T(8,128)S(1)}, f32[8,128]{1,0:T(8,128)S(1)}) custom-call(bf16[256,512]{1,0:T(8,128)(2,1)S(1)} %copy-done.1, bf16[512,8192]{1,0:T(8,128)(2,1)} %weight_hbm.1), custom_call_target="tpu_custom_call" | custom-call | flops 2147483648 | bytes 14680064 | tf_op jit(solution)/shard_map/product/pallas_call | solution.py:138
  9.3 0.9 %collective-permute-done.y_ref = bf16[256,512]{1,0:T(8,128)(2,1)S(1)} collective-permute-done((bf16[256,512]{1,0:T(8,128)(2,1)}, bf16[256,512]{1,0:T(8,128)(2,1)S(1)}, u32[]{:S(2)}, u32[]{:S(2)}) %collective-permute-start) | collective-permute-done | bytes 262176 | tf_op jit(solution)/shard_map/ppermute | solution.py:35
  10.2 0.0 collective-permute-done.1.rest_1_.other_ref
  10.2 0.0 collective-permute-done.2.rest_2_.up_other_ref
  10.2 0.0 copy-done.2
  10.2 0.0 copy-done.3
  10.3 1.2 %route.1 = (s32[1,256]{1,0:T(1,128)S(1)}, bf16[64,1024]{1,0:T(8,128)(2,1)S(1)}, bf16[64,1024]{1,0:T(8,128)(2,1)S(1)}, bf16[64,1024]{1,0:T(8,128)(2,1)S(1)}, bf16[64,1024]{1,0:T(8,128)(2,1)S(1)}) custom-call(s32[16]{0:T(128)S(1)} %copy-done.3, s32[1,256]{1,0:T(1,128)S(1)} %bitcast.24, bf16[256,512]{1,0:T(8,128)(2,1)S(1)} %copy-done.1, ...), custom_call_target="tpu_custom_call" | custom-call | flops 134217728 | bytes 1048576 | tf_op jit(solution)/shard_map/route/pallas_call | solution.py:88
  11.5 0.0 copy-start.4
  11.5 0.1 collective-permute-start.8
  11.6 2.9 %collective-permute-start.4 = (bf16[64,1024]{1,0:T(8,128)(2,1)S(1)}, bf16[64,1024]{1,0:T(8,128)(2,1)S(1)}, u32[]{:S(2)}, u32[]{:S(2)}) collective-permute-start(bf16[64,1024]{1,0:T(8,128)(2,1)S(1)} %get-tuple-element.29), channel_id=1, source_target_pairs={{0,8},{1,9},{2,10},{3,11},{4,12},{5,13},{6,14},{7,15},{8,0},{9,1},... | collective-permute-start | bytes 393224 | tf_op jit(solution)/shard_map/ppermute | solution.py:35
  14.4 1.3 %collective-permute-start.5 = (bf16[64,1024]{1,0:T(8,128)(2,1)S(1)}, bf16[64,1024]{1,0:T(8,128)(2,1)S(1)}, u32[]{:S(2)}, u32[]{:S(2)}) collective-permute-start(bf16[64,1024]{1,0:T(8,128)(2,1)S(1)} %get-tuple-element.30), channel_id=1, source_target_pairs={{0,12},{1,13},{2,14},{3,15},{4,8},{5,9},{6,10},{7,11},{8,4},{9,5},... | collective-permute-start | bytes 393224 | tf_op jit(solution)/shard_map/ppermute | solution.py:35
  15.8 0.2 collective-permute-start.6
  16.0 0.0 collective-permute-start.3
  16.0 0.0 collective-permute-done.8
  16.0 0.2 fusion.2
  16.2 1.6 %collective-permute-start.10 = (bf16[256,512]{1,0:T(8,128)(2,1)S(1)}, bf16[256,512]{1,0:T(8,128)(2,1)S(1)}, u32[]{:S(2)}, u32[]{:S(2)}) collective-permute-start(bf16[256,512]{1,0:T(8,128)(2,1)S(1)} %get-tuple-element.41), channel_id=1, source_target_pairs={{0,2},{1,3},{2,0},{3,1},{4,6},{5,7},{6,4},{7,5},{8,10},{9,11},{10,... | collective-permute-start | bytes 786440 | tf_op jit(solution)/shard_map/ppermute | solution.py:35
  17.8 6.7 %collective-permute-done.4.refs_0_ = bf16[64,1024]{1,0:T(8,128)(2,1)S(1)} collective-permute-done((bf16[64,1024]{1,0:T(8,128)(2,1)S(1)}, bf16[64,1024]{1,0:T(8,128)(2,1)S(1)}, u32[]{:S(2)}, u32[]{:S(2)}) %collective-permute-start.4) | collective-permute-done | bytes 131104 | tf_op jit(solution)/shard_map/ppermute | solution.py:35
  24.5 1.8 %collective-permute-start.9 = (bf16[256,512]{1,0:T(8,128)(2,1)S(1)}, bf16[256,512]{1,0:T(8,128)(2,1)S(1)}, u32[]{:S(2)}, u32[]{:S(2)}) collective-permute-start(bf16[256,512]{1,0:T(8,128)(2,1)S(1)} %get-tuple-element.42), channel_id=1, source_target_pairs={{0,2},{1,3},{2,0},{3,1},{4,6},{5,7},{6,4},{7,5},{8,10},{9,11},{10,... | collective-permute-start | bytes 786440 | tf_op jit(solution)/shard_map/ppermute | solution.py:35
  26.2 0.0 collective-permute-done.5.refs_1_
  26.2 0.0 collective-permute-done.6.refs_2_
  26.3 0.0 copy-done.4
  26.3 0.0 copy-start
  26.3 0.4 shrink.1.mine_ref.refs_2_
  26.7 0.0 collective-permute-start.7
  26.7 1.2 %collective-permute-done.7.other_ref = f32[64,64]{1,0:T(8,128)S(1)} collective-permute-done((f32[64,64]{1,0:T(8,128)S(1)}, f32[64,64]{1,0:T(8,128)S(1)}, u32[]{:S(2)}, u32[]{:S(2)}) %collective-permute-start.7) | collective-permute-done | bytes 16416 | tf_op jit(solution)/shard_map/ppermute | solution.py:35
  27.9 0.0 collective-permute-done.10
  27.9 4.3 %collective-permute-done.9.refs_0_ = bf16[256,512]{1,0:T(8,128)(2,1)S(1)} collective-permute-done((bf16[256,512]{1,0:T(8,128)(2,1)S(1)}, bf16[256,512]{1,0:T(8,128)(2,1)S(1)}, u32[]{:S(2)}, u32[]{:S(2)}) %collective-permute-start.9) | collective-permute-done | bytes 262176 | tf_op jit(solution)/shard_map/ppermute | solution.py:35
  32.2 0.0 copy-done
  32.2 0.3 grow.1
  32.5 0.0 collective-permute-done.3.refs_1_
  32.6 0.1 fusion.3.refs_1_
  32.6 0.1 fusion
  32.8 1.0 %collective-permute-start.14 = (bf16[256,512]{1,0:T(8,128)(2,1)S(1)}, bf16[256,512]{1,0:T(8,128)(2,1)S(1)}, u32[]{:S(2)}, u32[]{:S(2)}) collective-permute-start(bf16[256,512]{1,0:T(8,128)(2,1)S(1)} %fusion), channel_id=1, source_target_pairs={{0,4},{1,5},{2,6},{3,7},{4,0},{5,1},{6,2},{7,3},{8,12},{9,13},{10,... | collective-permute-start | bytes 786440 | tf_op jit(solution)/shard_map/ppermute | solution.py:35
  33.8 1.5 %collective-permute-start.17 = (bf16[256,512]{1,0:T(8,128)(2,1)S(1)}, bf16[256,512]{1,0:T(8,128)(2,1)S(1)}, u32[]{:S(2)}, u32[]{:S(2)}) collective-permute-start(bf16[256,512]{1,0:T(8,128)(2,1)S(1)} %get-tuple-element.40), channel_id=1, source_target_pairs={{0,2},{1,3},{2,0},{3,1},{4,6},{5,7},{6,4},{7,5},{8,10},{9,11},{10,... | collective-permute-start | bytes 786440 | tf_op jit(solution)/shard_map/ppermute | solution.py:35
  35.3 0.5 collective-permute-start.11
  35.8 1.1 %collective-permute-start.12 = (bf16[1,64,512]{2,1,0:T(8,128)(2,1)S(1)}, bf16[1,64,512]{2,1,0:T(8,128)(2,1)S(1)}, u32[]{:S(2)}, u32[]{:S(2)}) collective-permute-start(bf16[1,64,512]{2,1,0:T(8,128)(2,1)S(1)} %get-tuple-element.37), channel_id=1, source_target_pairs={{0,4},{1,5},{2,6},{3,7},{4,0},{5,1},{6,2},{7,3},{8,12},{9,13},{10,... | collective-permute-start | bytes 196616 | tf_op jit(solution)/shard_map/ppermute | solution.py:35
  36.9 1.9 %collective-permute-start.13 = (bf16[1,64,512]{2,1,0:T(8,128)(2,1)S(1)}, bf16[1,64,512]{2,1,0:T(8,128)(2,1)S(1)}, u32[]{:S(2)}, u32[]{:S(2)}) collective-permute-start(bf16[1,64,512]{2,1,0:T(8,128)(2,1)S(1)} %get-tuple-element.38), channel_id=1, source_target_pairs={{0,6},{1,7},{2,4},{3,5},{4,2},{5,3},{6,0},{7,1},{8,14},{9,15},{10,... | collective-permute-start | bytes 196616 | tf_op jit(solution)/shard_map/ppermute | solution.py:35
  38.8 3.0 %collective-permute-done.12.refs_4_ = bf16[1,64,512]{2,1,0:T(8,128)(2,1)S(1)} collective-permute-done((bf16[1,64,512]{2,1,0:T(8,128)(2,1)S(1)}, bf16[1,64,512]{2,1,0:T(8,128)(2,1)S(1)}, u32[]{:S(2)}, u32[]{:S(2)}) %collective-permute-start.12) | collective-permute-done | bytes 65568 | tf_op jit(solution)/shard_map/ppermute | solution.py:35
  41.8 1.5 %collective-permute-done.13.refs_5_ = bf16[1,64,512]{2,1,0:T(8,128)(2,1)S(1)} collective-permute-done((bf16[1,64,512]{2,1,0:T(8,128)(2,1)S(1)}, bf16[1,64,512]{2,1,0:T(8,128)(2,1)S(1)}, u32[]{:S(2)}, u32[]{:S(2)}) %collective-permute-start.13) | collective-permute-done | bytes 65568 | tf_op jit(solution)/shard_map/ppermute | solution.py:35
  43.3 1.8 %collective-permute-done.11.refs_3_ = bf16[2,64,512]{2,1,0:T(8,128)(2,1)S(1)} collective-permute-done((bf16[2,64,512]{2,1,0:T(8,128)(2,1)S(1)}, bf16[2,64,512]{2,1,0:T(8,128)(2,1)S(1)}, u32[]{:S(2)}, u32[]{:S(2)}) %collective-permute-start.11) | collective-permute-done | bytes 131104 | tf_op jit(solution)/shard_map/ppermute | solution.py:35
  45.1 0.0 collective-permute-done.14
  45.1 0.5 join.5.refs_3_.refs_5_
  45.6 0.3 join.6
  45.9 1.6 %collective-permute-start.15 = (bf16[256,512]{1,0:T(8,128)(2,1)S(1)}, bf16[256,512]{1,0:T(8,128)(2,1)S(1)}, u32[]{:S(2)}, u32[]{:S(2)}) collective-permute-start(bf16[256,512]{1,0:T(8,128)(2,1)S(1)} %join.6), channel_id=1, source_target_pairs={{0,2},{1,3},{2,0},{3,1},{4,6},{5,7},{6,4},{7,5},{8,10},{9,11},{10,... | collective-permute-start | bytes 786440 | tf_op jit(solution)/shard_map/ppermute | solution.py:35
  47.4 0.0 collective-permute-done.17
  47.4 0.3 join.7
  47.8 0.4 collective-permute-start.18
  48.2 3.4 %collective-permute-start.16 = (bf16[256,512]{1,0:T(8,128)(2,1)S(1)}, bf16[256,512]{1,0:T(8,128)(2,1)S(1)}, u32[]{:S(2)}, u32[]{:S(2)}) collective-permute-start(bf16[256,512]{1,0:T(8,128)(2,1)S(1)} %join.5.refs_3_.refs_5_), channel_id=1, source_target_pairs={{0,8},{1,9},{2,10},{3,11},{4,12},{5,13},{6,14},{7,15},{8,0},{9,1},... | collective-permute-start | bytes 786440 | tf_op jit(solution)/shard_map/ppermute | solution.py:35
  51.6 0.3 join.4
  51.8 0.5 collective-permute-done.15
  52.3 7.1 %collective-permute-done.18 = bf16[256,512]{1,0:T(8,128)(2,1)S(1)} collective-permute-done((bf16[256,512]{1,0:T(8,128)(2,1)S(1)}, bf16[256,512]{1,0:T(8,128)(2,1)S(1)}, u32[]{:S(2)}, u32[]{:S(2)}) %collective-permute-start.18) | collective-permute-done | bytes 262176 | tf_op jit(solution)/shard_map/ppermute | solution.py:35
  59.4 0.0 collective-permute-done.16
  59.4 0.9 %add_convert_fusion = bf16[256,512]{1,0:T(8,128)(2,1)} fusion(bf16[256,512]{1,0:T(8,128)(2,1)S(1)} %collective-permute-done.18, bf16[256,512]{1,0:T(8,128)(2,1)S(1)} %collective-permute-done.16, f32[256,512]{1,0:T(8,128)S(1)} %join.4, bf16[256,512]{1,0:T(8,128)(2,1)S(1)} %collective-permute-done.15), kind=kLoop, calls=%fused_computation.2 | loop fusion | flops 917504 | bytes 1572864 | tf_op jit(solution)/shard_map/convert_element_type | solution.py:292
  (2 shorter events, 0.0 us)
Async XLA Ops:
  0.0 10.2 %collective-permute-start.1 = (bf16[64,8192]{1,0:T(8,128)(2,1)}, bf16[64,8192]{1,0:T(8,128)(2,1)S(1)}, u32[]{:S(2)}, u32[]{:S(2)}) collective-permute-start(bf16[64,8192]{1,0:T(8,128)(2,1)} %bitcast.25), channel_id=1, source_target_pairs={{0,1},{1,0},{2,3},{3,2},{4,5},{5,4},{6,7},{7,6},{8,9},{9,8},{10,11... | collective-permute-start | bytes 3145736 | tf_op jit(solution)/shard_map/ppermute | solution.py:35
  0.5 9.8 %copy-start.2 = (s32[256]{0:T(256)S(1)}, s32[256]{0:T(256)}, u32[]{:S(2)}) copy-start(s32[256]{0:T(256)} %param.10) | copy-start | bytes 3076
  0.5 9.8 %copy-start.3 = (s32[16]{0:T(128)S(1)}, s32[16]{0:T(128)}, u32[]{:S(2)}) copy-start(s32[16]{0:T(128)} %slot_hbm.1) | copy-start | bytes 196
  0.5 9.8 %collective-permute-start.2 = (bf16[64,8192]{1,0:T(8,128)(2,1)}, bf16[64,8192]{1,0:T(8,128)(2,1)S(1)}, u32[]{:S(2)}, u32[]{:S(2)}) collective-permute-start(bf16[64,8192]{1,0:T(8,128)(2,1)} %bitcast.18), channel_id=1, source_target_pairs={{0,1},{1,0},{2,3},{3,2},{4,5},{5,4},{6,7},{7,6},{8,9},{9,8},{10,11... | collective-permute-start | bytes 3145736 | tf_op jit(solution)/shard_map/ppermute | solution.py:35
  0.5 9.7 %collective-permute-start = (bf16[256,512]{1,0:T(8,128)(2,1)}, bf16[256,512]{1,0:T(8,128)(2,1)S(1)}, u32[]{:S(2)}, u32[]{:S(2)}) collective-permute-start(bf16[256,512]{1,0:T(8,128)(2,1)} %own_ref.1), channel_id=1, source_target_pairs={{0,2},{1,3},{2,0},{3,1},{4,6},{5,7},{6,4},{7,5},{8,10},{9,11},{10,... | collective-permute-start | bytes 786440 | tf_op jit(solution)/shard_map/ppermute | solution.py:35
  3.5 1.0 %copy-start.1 = (bf16[256,512]{1,0:T(8,128)(2,1)S(1)}, bf16[256,512]{1,0:T(8,128)(2,1)}, u32[]{:S(2)}) copy-start(bf16[256,512]{1,0:T(8,128)(2,1)} %own_ref.1) | copy-start | bytes 786436
  11.5 14.8 %copy-start.4 = (bf16[1,8192,64]{1,2,0:T(8,128)(2,1)S(1)}, bf16[1,8192,64]{1,2,0:T(8,128)(2,1)}, u32[]{:S(2)}) copy-start(bf16[1,8192,64]{1,2,0:T(8,128)(2,1)} %param.8) | copy-start | bytes 3145732
  11.5 4.5 %collective-permute-start.8 = (bf16[2,256,512]{2,1,0:T(8,128)(2,1)S(1)}, bf16[2,256,512]{2,1,0:T(8,128)(2,1)S(1)}, u32[]{:S(2)}, u32[]{:S(2)}) collective-permute-start(bf16[2,256,512]{2,1,0:T(8,128)(2,1)S(1)} %get-tuple-element.34), channel_id=1, source_target_pairs={{0,1},{1,0},{2,3},{3,2},{4,5},{5,4},{6,7},{7,6},{8,9},{9,8},{10,11... | collective-permute-start | bytes 1572872 | tf_op jit(solution)/shard_map/ppermute | solution.py:35
  11.6 12.9 %collective-permute-start.4 = (bf16[64,1024]{1,0:T(8,128)(2,1)S(1)}, bf16[64,1024]{1,0:T(8,128)(2,1)S(1)}, u32[]{:S(2)}, u32[]{:S(2)}) collective-permute-start(bf16[64,1024]{1,0:T(8,128)(2,1)S(1)} %get-tuple-element.29), channel_id=1, source_target_pairs={{0,8},{1,9},{2,10},{3,11},{4,12},{5,13},{6,14},{7,15},{8,0},{9,1},... | collective-permute-start | bytes 393224 | tf_op jit(solution)/shard_map/ppermute | solution.py:35
  14.4 11.8 %collective-permute-start.5 = (bf16[64,1024]{1,0:T(8,128)(2,1)S(1)}, bf16[64,1024]{1,0:T(8,128)(2,1)S(1)}, u32[]{:S(2)}, u32[]{:S(2)}) collective-permute-start(bf16[64,1024]{1,0:T(8,128)(2,1)S(1)} %get-tuple-element.30), channel_id=1, source_target_pairs={{0,12},{1,13},{2,14},{3,15},{4,8},{5,9},{6,10},{7,11},{8,4},{9,5},... | collective-permute-start | bytes 393224 | tf_op jit(solution)/shard_map/ppermute | solution.py:35
  15.8 10.5 %collective-permute-start.6 = (bf16[64,1024]{1,0:T(8,128)(2,1)S(1)}, bf16[64,1024]{1,0:T(8,128)(2,1)S(1)}, u32[]{:S(2)}, u32[]{:S(2)}) collective-permute-start(bf16[64,1024]{1,0:T(8,128)(2,1)S(1)} %get-tuple-element.31), channel_id=1, source_target_pairs={{0,4},{1,5},{2,6},{3,7},{4,0},{5,1},{6,2},{7,3},{8,12},{9,13},{10,... | collective-permute-start | bytes 393224 | tf_op jit(solution)/shard_map/ppermute | solution.py:35
  16.0 16.5 %collective-permute-start.3 = (bf16[6,256,512]{2,1,0:T(8,128)(2,1)S(1)}, bf16[6,256,512]{2,1,0:T(8,128)(2,1)S(1)}, u32[]{:S(2)}, u32[]{:S(2)}) collective-permute-start(bf16[6,256,512]{2,1,0:T(8,128)(2,1)S(1)} %get-tuple-element.28), channel_id=1, source_target_pairs={{0,1},{1,0},{2,3},{3,2},{4,5},{5,4},{6,7},{7,6},{8,9},{9,8},{10,11... | collective-permute-start | bytes 4718600 | tf_op jit(solution)/shard_map/ppermute | solution.py:35
  16.2 11.7 %collective-permute-start.10 = (bf16[256,512]{1,0:T(8,128)(2,1)S(1)}, bf16[256,512]{1,0:T(8,128)(2,1)S(1)}, u32[]{:S(2)}, u32[]{:S(2)}) collective-permute-start(bf16[256,512]{1,0:T(8,128)(2,1)S(1)} %get-tuple-element.41), channel_id=1, source_target_pairs={{0,2},{1,3},{2,0},{3,1},{4,6},{5,7},{6,4},{7,5},{8,10},{9,11},{10,... | collective-permute-start | bytes 786440 | tf_op jit(solution)/shard_map/ppermute | solution.py:35
  24.5 7.8 %collective-permute-start.9 = (bf16[256,512]{1,0:T(8,128)(2,1)S(1)}, bf16[256,512]{1,0:T(8,128)(2,1)S(1)}, u32[]{:S(2)}, u32[]{:S(2)}) collective-permute-start(bf16[256,512]{1,0:T(8,128)(2,1)S(1)} %get-tuple-element.42), channel_id=1, source_target_pairs={{0,2},{1,3},{2,0},{3,1},{4,6},{5,7},{6,4},{7,5},{8,10},{9,11},{10,... | collective-permute-start | bytes 786440 | tf_op jit(solution)/shard_map/ppermute | solution.py:35
  26.3 6.0 %copy-start = (bf16[1,64,8192]{2,1,0:T(8,128)(2,1)S(1)}, bf16[1,64,8192]{2,1,0:T(8,128)(2,1)}, u32[]{:S(2)}) copy-start(bf16[1,64,8192]{2,1,0:T(8,128)(2,1)} %param.9) | copy-start | bytes 3145732
  26.7 1.2 %collective-permute-start.7 = (f32[64,64]{1,0:T(8,128)S(1)}, f32[64,64]{1,0:T(8,128)S(1)}, u32[]{:S(2)}, u32[]{:S(2)}) collective-permute-start(f32[64,64]{1,0:T(8,128)S(1)} %shrink.1.mine_ref.refs_2_), channel_id=1, source_target_pairs={{0,1},{1,0},{2,3},{3,2},{4,5},{5,4},{6,7},{7,6},{8,9},{9,8},{10,11... | collective-permute-start | bytes 49160 | tf_op jit(solution)/shard_map/ppermute | solution.py:35
  32.8 12.4 %collective-permute-start.14 = (bf16[256,512]{1,0:T(8,128)(2,1)S(1)}, bf16[256,512]{1,0:T(8,128)(2,1)S(1)}, u32[]{:S(2)}, u32[]{:S(2)}) collective-permute-start(bf16[256,512]{1,0:T(8,128)(2,1)S(1)} %fusion), channel_id=1, source_target_pairs={{0,4},{1,5},{2,6},{3,7},{4,0},{5,1},{6,2},{7,3},{8,12},{9,13},{10,... | collective-permute-start | bytes 786440 | tf_op jit(solution)/shard_map/ppermute | solution.py:35
  33.8 13.7 %collective-permute-start.17 = (bf16[256,512]{1,0:T(8,128)(2,1)S(1)}, bf16[256,512]{1,0:T(8,128)(2,1)S(1)}, u32[]{:S(2)}, u32[]{:S(2)}) collective-permute-start(bf16[256,512]{1,0:T(8,128)(2,1)S(1)} %get-tuple-element.40), channel_id=1, source_target_pairs={{0,2},{1,3},{2,0},{3,1},{4,6},{5,7},{6,4},{7,5},{8,10},{9,11},{10,... | collective-permute-start | bytes 786440 | tf_op jit(solution)/shard_map/ppermute | solution.py:35
  35.3 9.8 %collective-permute-start.11 = (bf16[2,64,512]{2,1,0:T(8,128)(2,1)S(1)}, bf16[2,64,512]{2,1,0:T(8,128)(2,1)S(1)}, u32[]{:S(2)}, u32[]{:S(2)}) collective-permute-start(bf16[2,64,512]{2,1,0:T(8,128)(2,1)S(1)} %get-tuple-element.36), channel_id=1, source_target_pairs={{0,2},{1,3},{2,0},{3,1},{4,6},{5,7},{6,4},{7,5},{8,10},{9,11},{10,... | collective-permute-start | bytes 393224 | tf_op jit(solution)/shard_map/ppermute | solution.py:35
  35.8 6.0 %collective-permute-start.12 = (bf16[1,64,512]{2,1,0:T(8,128)(2,1)S(1)}, bf16[1,64,512]{2,1,0:T(8,128)(2,1)S(1)}, u32[]{:S(2)}, u32[]{:S(2)}) collective-permute-start(bf16[1,64,512]{2,1,0:T(8,128)(2,1)S(1)} %get-tuple-element.37), channel_id=1, source_target_pairs={{0,4},{1,5},{2,6},{3,7},{4,0},{5,1},{6,2},{7,3},{8,12},{9,13},{10,... | collective-permute-start | bytes 196616 | tf_op jit(solution)/shard_map/ppermute | solution.py:35
  36.9 6.4 %collective-permute-start.13 = (bf16[1,64,512]{2,1,0:T(8,128)(2,1)S(1)}, bf16[1,64,512]{2,1,0:T(8,128)(2,1)S(1)}, u32[]{:S(2)}, u32[]{:S(2)}) collective-permute-start(bf16[1,64,512]{2,1,0:T(8,128)(2,1)S(1)} %get-tuple-element.38), channel_id=1, source_target_pairs={{0,6},{1,7},{2,4},{3,5},{4,2},{5,3},{6,0},{7,1},{8,14},{9,15},{10,... | collective-permute-start | bytes 196616 | tf_op jit(solution)/shard_map/ppermute | solution.py:35
  45.9 6.4 %collective-permute-start.15 = (bf16[256,512]{1,0:T(8,128)(2,1)S(1)}, bf16[256,512]{1,0:T(8,128)(2,1)S(1)}, u32[]{:S(2)}, u32[]{:S(2)}) collective-permute-start(bf16[256,512]{1,0:T(8,128)(2,1)S(1)} %join.6), channel_id=1, source_target_pairs={{0,2},{1,3},{2,0},{3,1},{4,6},{5,7},{6,4},{7,5},{8,10},{9,11},{10,... | collective-permute-start | bytes 786440 | tf_op jit(solution)/shard_map/ppermute | solution.py:35
  47.8 11.6 %collective-permute-start.18 = (bf16[256,512]{1,0:T(8,128)(2,1)S(1)}, bf16[256,512]{1,0:T(8,128)(2,1)S(1)}, u32[]{:S(2)}, u32[]{:S(2)}) collective-permute-start(bf16[256,512]{1,0:T(8,128)(2,1)S(1)} %join.7), channel_id=1, source_target_pairs={{0,4},{1,5},{2,6},{3,7},{4,0},{5,1},{6,2},{7,3},{8,12},{9,13},{10,... | collective-permute-start | bytes 786440 | tf_op jit(solution)/shard_map/ppermute | solution.py:35
  48.2 11.2 %collective-permute-start.16 = (bf16[256,512]{1,0:T(8,128)(2,1)S(1)}, bf16[256,512]{1,0:T(8,128)(2,1)S(1)}, u32[]{:S(2)}, u32[]{:S(2)}) collective-permute-start(bf16[256,512]{1,0:T(8,128)(2,1)S(1)} %join.5.refs_3_.refs_5_), channel_id=1, source_target_pairs={{0,8},{1,9},{2,10},{3,11},{4,12},{5,13},{6,14},{7,15},{8,0},{9,1},... | collective-permute-start | bytes 786440 | tf_op jit(solution)/shard_map/ppermute | solution.py:35

commit v9 on v8

--- a/solution.py
+++ b/solution.py
@@ -52,10 +52,47 @@
     )(*values, *after)
 
 
-def route_kernel(count, layers, slot_hbm, row_ref, own_ref, y_ref, *rest):
+def columns_kernel(down_hbm, other_hbm, out_ref, sems):
+    me = lax.axis_index("tensor")
+    rank = out_ref.shape[0] // 2
+    layers = lax.axis_size("tensor") // 4
+    width = out_ref.shape[1] // layers
+    fetches = []
+    for i, source in enumerate((down_hbm, other_hbm)):
+        for k in range(layers):
+            start = pl.multiple_of((me ^ 2 ^ (4 * k)) * width, width)
+            fetches.append(
+                pltpu.make_async_copy(
+                    source.at[:, pl.ds(start, width)],
+                    out_ref.at[pl.ds(i * rank, rank), pl.ds(k * width, width)],
+                    sems.at[i * layers + k],
+                )
+            )
+    for fetch in fetches:
+        fetch.start()
+    for fetch in fetches:
+        fetch.wait()
+
+
+def columns(down, other):
+    rank, depth = down.shape
+    return pl.pallas_call(
+        columns_kernel,
+        out_shape=shape((2 * rank, depth // 4)),
+        in_specs=[ANYWHERE, ANYWHERE],
+        out_specs=IN_VMEM,
+        scratch_shapes=[DMA((2 * (lax.axis_size("tensor") // 4),))],
+        compiler_params=params(8),
+        cost_estimate=cost(0, 2 * down.size),
+        name="columns",
+    )(down, other)
+
+
+def route_kernel(count, slot_hbm, row_ref, own_ref, *rest):
+    layers = count // 4
     target_ref, out_refs = rest[-3 - layers], rest[-2 - layers : -2]
     slot_ref, slot_sem = rest[-2:]
-    rows, width = own_ref.shape
+    rows = own_ref.shape[0]
     me = lax.axis_index("tensor")
     fetch = pltpu.make_async_copy(slot_hbm, slot_ref, slot_sem)
     fetch.start()
@@ -73,34 +110,32 @@
     place = jnp.sum(ahead * hot, axis=0, keepdims=True).astype(jnp.int32)
     target = owner * CAP + place
     target_ref[...] = target
-    j = lax.broadcasted_iota(jnp.int32, (2 * CAP, rows), 0)
+    j = lax.broadcasted_iota(jnp.int32, (4 * CAP, rows), 0)
     for k in range(layers):
         slots = (me ^ (4 * k) ^ (j // CAP)) * CAP + j % CAP
         select = (slots == target).astype(jnp.bfloat16)
-        out_refs[k][:, :width] = dot(select, own_ref[...]).astype(jnp.bfloat16)
-        out_refs[k][:, width:] = dot(select, y_ref[...]).astype(jnp.bfloat16)
-
-
-def route(adapter_slot, row_adapter, own, y, *after):
+        out_refs[k][...] = dot(select, own_ref[...]).astype(jnp.bfloat16)
+
+
+def route(adapter_slot, row_adapter, own, *after):
     rows, width = own.shape
     count = lax.axis_size("tensor")
     layers = count // 4
     found = pl.pallas_call(
-        functools.partial(route_kernel, count, layers),
-        out_shape=[shape((1, rows), jnp.int32)] + [shape((2 * CAP, 2 * width))] * layers,
-        in_specs=[IN_HBM] + [IN_VMEM] * 3 + [ANYWHERE] * len(after),
+        functools.partial(route_kernel, count),
+        out_shape=[shape((1, rows), jnp.int32)] + [shape((4 * CAP, width))] * layers,
+        in_specs=[IN_HBM] + [IN_VMEM] * 2 + [ANYWHERE] * len(after),
         out_specs=[IN_VMEM] * (layers + 1),
         scratch_shapes=[pltpu.SMEM(adapter_slot.shape, jnp.int32), DMA(())],
         compiler_params=params(16),
         cost_estimate=cost(8 * layers * CAP * rows * width, 16 * layers * CAP * width),
         name="route",
-    )(adapter_slot, row_adapter[None, :], own, y, *after)
+    )(adapter_slot, row_adapter[None, :], own, *after)
     return found[0], found[1:]
 
 
-def product_kernel(groups, attended_hbm, weight_hbm, *refs):
-    token_ref, attended_ref, weight_ref, sems = refs[-4:]
-    chips = [m for group in groups for m in group]
+def product_kernel(chips, attended_hbm, weight_hbm, *refs):
+    away_ref, stay_ref, token_ref, attended_ref, weight_ref, sems = refs[-6:]
     width = weight_ref.shape[2] // 2
     me = lax.axis_index("tensor")
     core, chip = me % 2, me // 2
@@ -116,30 +151,25 @@
     fetches[0].wait()
     there = pl.ds(pl.multiple_of((1 - core) * width, width), width)
     here = pl.ds(pl.multiple_of(core * width, width), width)
-    at = 0
-    for g, group in enumerate(groups):
-        away_ref, stay_ref = refs[2 * g : 2 * g + 2]
-        for i in range(len(group)):
-            fetches[at + 1].wait()
-            away_ref[i] = dot(attended_ref[...], weight_ref[at, :, there]).astype(jnp.bfloat16)
-            stay_ref[i] = dot(attended_ref[...], weight_ref[at, :, here])
-            at += 1
-
-
-def product(attended, out_weight, groups, mib):
+    for i in range(len(chips)):
+        fetches[i + 1].wait()
+        away_ref[i] = dot(attended_ref[...], weight_ref[i, :, there]).astype(jnp.bfloat16)
+        stay_ref[i] = dot(attended_ref[...], weight_ref[i, :, here])
+
+
+def product(attended, out_weight, chips, mib, *after):
     rows, depth = attended.shape
     width = out_weight.shape[1] // lax.axis_size("tensor")
-    n = sum(len(group) for group in groups)
-    out_shape = []
-    for group in groups:
-        out_shape.append(shape((len(group), rows, width)))
-        out_shape.append(shape((len(group), rows, width), jnp.float32))
-    out_shape.append(shape((8, 128), jnp.float32))
-    return pl.pallas_call(
-        functools.partial(product_kernel, groups),
-        out_shape=out_shape,
-        in_specs=[IN_HBM, IN_HBM],
-        out_specs=[IN_VMEM] * len(out_shape),
+    n = len(chips)
+    return pl.pallas_call(
+        functools.partial(product_kernel, chips),
+        out_shape=(
+            shape((n, rows, width)),
+            shape((n, rows, width), jnp.float32),
+            shape((8, 128), jnp.float32),
+        ),
+        in_specs=[IN_HBM, IN_HBM] + [ANYWHERE] * len(after),
+        out_specs=[IN_VMEM] * 3,
         scratch_shapes=[
             pltpu.VMEM((rows, depth), jnp.bfloat16),
             pltpu.VMEM((n, depth, 2 * width), jnp.bfloat16),
@@ -148,38 +178,43 @@
         compiler_params=params(mib),
         cost_estimate=cost(4 * n * rows * depth * width, n * (4 * depth * width + 6 * rows * width)),
         name="product",
-    )(attended, out_weight)
-
-
-def shrink_kernel(distances, down_ref, other_ref, *refs):
-    arrived_refs, out_ref = refs[: len(distances)], refs[-1]
-    me = lax.axis_index("tensor")
-    width = arrived_refs[0].shape[1] // 2
+    )(attended, out_weight, *after)
+
+
+def shrink_kernel(distances, down_ref, other_ref, across_ref, *refs):
+    arrived_refs, out_refs = refs[: len(distances)], refs[-2:]
+    me = lax.axis_index("tensor")
+    rank = down_ref.shape[0]
+    width = arrived_refs[0].shape[1]
     over = (((1,), (1,)), ((), ()))
-    for part, weights_ref in enumerate((down_ref, other_ref)):
-        total = jnp.zeros((CAP, down_ref.shape[0]), jnp.float32)
+    for owner in range(4):
+        total = jnp.zeros((CAP, rank), jnp.float32)
         for k, arrived_ref in zip(distances, arrived_refs):
-            for side in range(2):
-                block = pl.ds(pl.multiple_of((me ^ (4 * k + 2 * side)) * width, width), width)
-                total += lax.dot_general(
-                    arrived_ref[part * CAP : (part + 1) * CAP, side * width : (side + 1) * width],
-                    weights_ref[:, block],
-                    over,
-                    preferred_element_type=jnp.float32,
-                )
-        out_ref[part * CAP : (part + 1) * CAP, :] = total
-
-
-def shrink(down, other, arrived, *after):
+            if owner < 2:
+                block = pl.ds(pl.multiple_of((me ^ (4 * k)) * width, width), width)
+                weights = (down_ref, other_ref)[owner][:, block]
+            else:
+                weights = across_ref[(owner - 2) * rank : (owner - 1) * rank, k * width : (k + 1) * width]
+            total += lax.dot_general(
+                arrived_ref[owner * CAP : (owner + 1) * CAP, :],
+                weights,
+                over,
+                preferred_element_type=jnp.float32,
+            )
+        out_refs[owner // 2][owner % 2 * CAP : (owner % 2 + 1) * CAP, :] = total
+
+
+def shrink(down, other, across, arrived, *after):
+    rank = down.shape[0]
     return pl.pallas_call(
         functools.partial(shrink_kernel, tuple(arrived)),
-        out_shape=shape((2 * CAP, down.shape[0]), jnp.float32),
-        in_specs=[IN_VMEM] * (2 + len(arrived)) + [ANYWHERE] * len(after),
-        out_specs=IN_VMEM,
+        out_shape=[shape((2 * CAP, rank), jnp.float32)] * 2,
+        in_specs=[IN_VMEM] * (3 + len(arrived)) + [ANYWHERE] * len(after),
+        out_specs=[IN_VMEM] * 2,
         compiler_params=params(16),
-        cost_estimate=cost(40*10**9, 4 * down.size),
+        cost_estimate=cost(40 * 10**9, 4 * down.size),
         name="shrink",
-    )(down, other, *arrived.values(), *after)
+    )(down, other, across, *arrived.values(), *after)
 
 
 def grow_kernel(groups, mine_ref, other_ref, up_ref, up_other_ref, *refs):
@@ -203,7 +238,7 @@
         in_specs=[IN_VMEM] * 4 + [ANYWHERE] * len(after),
         out_specs=[IN_VMEM] * len(groups),
         compiler_params=params(16),
-        cost_estimate=cost(4*CAP*up.size, 4 * up.size),
+        cost_estimate=cost(4 * 10**9, 4 * up.size),
         name="grow",
     )(mine, other, up, up_other, *after)
 
@@ -242,53 +277,66 @@
     )(target, *operands)
 
 
+def gather_kernel(side_ref, y_ref, z_ref, out_ref):
+    out_ref[...] = side_ref[...] + y_ref[...].astype(jnp.float32) + z_ref[...].astype(jnp.float32)
+
+
+def gather(side, y, z):
+    return pl.pallas_call(
+        gather_kernel,
+        out_shape=shape(side.shape, jnp.float32),
+        in_specs=[IN_VMEM] * 3,
+        out_specs=IN_VMEM,
+        compiler_params=params(16),
+        cost_estimate=cost(2 * side.size, 12 * side.size),
+        name="gather",
+    )(side, y, z)
+
+
 def staged(attended, out_weight, adapter_down, adapter_up, row_adapter, adapter_slot):
     f32, bf16 = jnp.float32, jnp.bfloat16
     up, down = adapter_up[0], jnp.swapaxes(adapter_down, 1, 2)[0]
-    from_y = swap(attended, 2)
     down_other, up_other = swap(down, 1), swap(up, 1)
-    chips = (6, 4, 3, 2, 1, 0)
-    away_first, stay_first, away, stay, token = product(attended, out_weight, ((7, 5), chips), 44)
-    target, outgoing = route(adapter_slot, row_adapter, attended, from_y, token, down_other, up_other)
-    arrived = {k: swap(outgoing[k], 4 * k) for k in (2,3,1)}
+    firsts, chips = (7, 6, 5), (4, 3, 2, 1, 0)
+    away_first, stay_first, token = product(attended, out_weight, firsts, 44)
+    to_y = columns(down, down_other)
+    across = swap(to_y, 2)
+    target, outgoing = route(adapter_slot, row_adapter, attended, token, to_y, up_other)
+    came_first = swap(away_first, 1)
+    arrived = {k: swap(outgoing[k], 4 * k) for k in (2, 3, 1)}
     arrived[0] = outgoing[0]
-    away_first, away = once((away_first, away), target)
-    came_first, came = swap(away_first, 1), swap(away, 1)
-
-    def base(m):
-        return stay[chips.index(m)] + came[chips.index(m)].astype(f32)
-
-    y3 = swap((stay_first[0] + came_first[0].astype(f32)).astype(bf16), 2)
-    y2 = swap((stay_first[1] + came_first[1].astype(f32)).astype(bf16), 2)[None]
-    mine = shrink(down, down_other, arrived)
-    ready3, go1 = once((y3, base(3).astype(bf16)), mine)
-    z3 = swap((base(6) + ready3.astype(f32)).astype(bf16), 4)[None]
-    y1 = swap(go1, 2)[None]
-    here_chips = (4, 2, 1, 0)
-    groups = (tuple(2 * m for m in here_chips), (10, 6), (12,), (14,))
-    here, over2, over4, over6 = grow(mine, swap(mine, 1), up, up_other, groups, y3, y2)
+    away, stay, _ = product(attended, out_weight, chips, 44, target)
+    came = swap(away, 1)
+    first = [stay_first[i] + came_first[i].astype(f32) for i in range(3)]
+    y3, y2 = swap(first[0].astype(bf16), 2), swap(first[2].astype(bf16), 2)[None]
+    z3 = swap((first[1] + y3.astype(f32)).astype(bf16), 4)[None]
+    mine, theirs = shrink(down, down_other, across, arrived)
+    mine = mine + swap(theirs, 2)
+    here_chips = (4, 3, 2, 1, 0)
+    groups = (tuple(2 * m for m in here_chips), (10,), (12,), (14,))
+    here, over2, over4, over6 = grow(mine, swap(mine, 1), up, up_other, groups, y3, came)
     over2, over4, over6 = swap(over2, 2), swap(over4, 4), swap(over6, 6)
 
     def blocks(m):
         return ((0, chips.index(m)), (1, chips.index(m))), ((2, here_chips.index(m), 0),)
 
-    sums, grown = blocks(4)
+    (ready2,) = join(target, [stay, came, z3, y2], ((((0, 0), (1, 0), (2, 0), (3, 0)), ()),), f32)
+    (go1,) = join(target, [stay, came, here, over2, over4, over6, ready2], (blocks(3),), bf16)
+    y1 = swap(go1, 2)
     (sum2,) = join(
         target,
-        [stay, came, here, over2, over4, over6, z3, y2],
-        ((sums + ((6, 0), (7, 0)), grown + ((3, 0, 2), (4, 0, 4), (5, 0, 6))),),
+        [ready2[None], here, over2, over4, over6],
+        ((((0, 0),), ((1, here_chips.index(4), 0), (2, 0, 2), (3, 0, 4), (4, 0, 6))),),
         bf16,
     )
     z2 = swap(sum2, 8)
-    sums, grown = blocks(2)
-    (sum1,) = join(
-        target, [stay, came, here, over2, y1, sum2], ((sums + ((4, 0),), grown + ((3, 1, 2),)),), bf16
-    )
-    z1 = swap(sum1, 4)
     (go0,) = join(target, [stay, came, here, sum2], (blocks(1),), bf16)
     y0 = swap(go0, 2)
+    sums, grown = blocks(2)
+    (sum1,) = join(target, [stay, came, here, y1[None], sum2], ((sums + ((3, 0),), grown),), bf16)
+    z1 = swap(sum1, 4)
     (side0,) = join(target, [stay, came, here], (blocks(0),), f32)
-    total = side0 + y0.astype(f32) + z2.astype(f32) + z1.astype(f32)
+    total = gather(side0, y0, z2) + z1.astype(f32)
     return total.astype(bf16)
 
 

time: 60.7 us -> 61.6 us (1.015)
  Pallas kernels: 8.07 us -> 10.2 us
  waiting for transfers between devices: 27 us -> 26.2 us
    pallas_call x4 -> x5, Pallas kernels: 6.06 us -> 7.91 us  [the longest x2 6.64 us: product(): pl.pallas_call(functools.partial(product_kernel, chips), out_shape=(shape...]
    ppermute x19 -> x20, waiting for transfers between devices: 27 us -> 26.2 us  [swap(): return lax.ppermute(value, 'tensor', [(t, t ^ mask) for t in range(count)])]
    pallas_call x4 -> x6, Pallas kernels: 1.31 us -> 1.61 us  [join(): pl.pallas_call(functools.partial(join_kernel, terms), out_shape=[shape((r...]
    ppermute x19 -> x20, starting transfers between devices: 22.8 us -> 22.9 us  [swap(): return lax.ppermute(value, 'tensor', [(t, t ^ mask) for t in range(count)])]
  transfers between devices with their start and end apart: 19 -> 20, of which waited for: 9 -> 10; matrix products, arithmetic and copies ran while one was open for 0% -> 0% of each run, Pallas kernels for 11% -> 16%
where the time goes in v9:
time: 61.6 us; the launch traced here: 61.5 us
  waiting for transfers between devices  26.2 us (43%)
  starting transfers between devices  22.9 us (37%)
  Pallas kernels  10.2 us (17%)
  other arithmetic  1.06 us (2%)
  local copies, waits for them, and re-layouts  0.97 us (2%)
    ppermute x20, waiting for transfers between devices, swap(): return lax.ppermute(value, 'tensor', [(t, t ^ mask) for t in range(count)])  26.2 us
    ppermute x20, starting transfers between devices, swap(): return lax.ppermute(value, 'tensor', [(t, t ^ mask) for t in range(count)])  22.9 us
    pallas_call x2, Pallas kernels, product(): pl.pallas_call(functools.partial(product_kernel, chips), out_shape=(shape...  6.64 us
    pallas_call x6, Pallas kernels, join(): pl.pallas_call(functools.partial(join_kernel, terms), out_shape=[shape((r...  1.61 us
  transfers between devices with their start and end apart: 20, of which 10 were waited for; matrix products, arithmetic and copies ran while one was open for 0% of the time, Pallas kernels for 16%

profile of v9, /device:TPU:0, one launch (start us, length us, event | category | flops | bytes accessed | tf_op | source)
XLA Modules:
  0.0 61.5 jit_solution(2110184230824412080)
XLA Ops:
  0.0 0.5 collective-permute-start
  0.5 0.1 collective-permute-start.1
  0.5 0.0 copy-start
  0.5 0.9 %copy-done = bf16[256,512]{1,0:T(8,128)(2,1)S(1)} copy-done((bf16[256,512]{1,0:T(8,128)(2,1)S(1)}, bf16[256,512]{1,0:T(8,128)(2,1)}, u32[]{:S(2)}) %copy-start) | copy-done | bytes 262168
  1.5 2.7 %product.2 = (bf16[3,256,512]{2,1,0:T(8,128)(2,1)S(1)}, f32[3,256,512]{2,1,0:T(8,128)S(1)}, f32[8,128]{1,0:T(8,128)S(1)}) custom-call(bf16[256,512]{1,0:T(8,128)(2,1)S(1)} %copy-done, bf16[512,8192]{1,0:T(8,128)(2,1)} %weight_hbm.3), custom_call_target="tpu_custom_call" | custom-call | flops 805306368 | bytes 5505024 | tf_op jit(solution)/shard_map/product/pallas_call | solution.py:164
  4.2 0.0 copy-start.2
  4.2 0.0 copy-start.3
  4.2 0.5 collective-permute-start.9
  4.7 0.0 collective-permute-done.other_hbm.other_ref
  4.7 0.0 copy-done.1
  4.7 0.2 columns.1.rest_1_
  4.9 2.6 %collective-permute-start.3 = (bf16[128,2048]{1,0:T(8,128)(2,1)S(1)}, bf16[128,2048]{1,0:T(8,128)(2,1)S(1)}, u32[]{:S(2)}, u32[]{:S(2)}) collective-permute-start(bf16[128,2048]{1,0:T(8,128)(2,1)S(1)} %columns.1.rest_1_), channel_id=1, source_target_pairs={{0,2},{1,3},{2,0},{3,1},{4,6},{5,7},{6,4},{7,5},{8,10},{9,11},{10,... | collective-permute-start | bytes 1572872 | tf_op jit(solution)/shard_map/ppermute | solution.py:35
  7.5 0.0 collective-permute-done.1.rest_2_.up_other_ref
  7.5 0.0 copy-done.2
  7.5 0.0 copy-done.3
  7.5 1.0 %route.1 = (s32[1,256]{1,0:T(1,128)S(1)}, bf16[128,512]{1,0:T(8,128)(2,1)S(1)}, bf16[128,512]{1,0:T(8,128)(2,1)S(1)}, bf16[128,512]{1,0:T(8,128)(2,1)S(1)}, bf16[128,512]{1,0:T(8,128)(2,1)S(1)}) custom-call(s32[16]{0:T(128)S(1)} %copy-done.3, s32[1,256]{1,0:T(1,128)S(1)} %bitcast.24, bf16[256,512]{1,0:T(8,128)(2,1)S(1)} %copy-done, ...), custom_call_target="tpu_custom_call" | custom-call | flops 134217728 | bytes 1048576 | tf_op jit(solution)/shard_map/route/pallas_call | solution.py:124
  8.6 2.7 %collective-permute-start.4 = (bf16[128,512]{1,0:T(8,128)(2,1)S(1)}, bf16[128,512]{1,0:T(8,128)(2,1)S(1)}, u32[]{:S(2)}, u32[]{:S(2)}) collective-permute-start(bf16[128,512]{1,0:T(8,128)(2,1)S(1)} %get-tuple-element.25), channel_id=1, source_target_pairs={{0,8},{1,9},{2,10},{3,11},{4,12},{5,13},{6,14},{7,15},{8,0},{9,1},... | collective-permute-start | bytes 393224 | tf_op jit(solution)/shard_map/ppermute | solution.py:35
  11.2 1.4 %collective-permute-start.5 = (bf16[128,512]{1,0:T(8,128)(2,1)S(1)}, bf16[128,512]{1,0:T(8,128)(2,1)S(1)}, u32[]{:S(2)}, u32[]{:S(2)}) collective-permute-start(bf16[128,512]{1,0:T(8,128)(2,1)S(1)} %get-tuple-element.26), channel_id=1, source_target_pairs={{0,12},{1,13},{2,14},{3,15},{4,8},{5,9},{6,10},{7,11},{8,4},{9,5},... | collective-permute-start | bytes 393224 | tf_op jit(solution)/shard_map/ppermute | solution.py:35
  12.6 0.2 collective-permute-start.6
  12.8 0.0 collective-permute-done.9
  12.8 0.2 fusion.2
  13.0 0.6 collective-permute-start.10
  13.5 4.0 %product.3 = (bf16[5,256,512]{2,1,0:T(8,128)(2,1)S(1)}, f32[5,256,512]{2,1,0:T(8,128)S(1)}, f32[8,128]{1,0:T(8,128)}) custom-call(bf16[256,512]{1,0:T(8,128)(2,1)S(1)} %copy-done, bf16[512,8192]{1,0:T(8,128)(2,1)} %weight_hbm.3, s32[1,256]{1,0:T(1,128)S(1)} %get-tuple-element.22.refs_0_.target_ref), custom_call_target="tpu_custom_call" | custom-call | flops 1342177280 | bytes 9175040 | tf_op jit(solution)/shard_map/product/pallas_call | solution.py:164
  17.5 4.0 %collective-permute-done.4.refs_0_ = bf16[128,512]{1,0:T(8,128)(2,1)S(1)} collective-permute-done((bf16[128,512]{1,0:T(8,128)(2,1)S(1)}, bf16[128,512]{1,0:T(8,128)(2,1)S(1)}, u32[]{:S(2)}, u32[]{:S(2)}) %collective-permute-start.4) | collective-permute-done | bytes 131104 | tf_op jit(solution)/shard_map/ppermute | solution.py:35
  21.5 0.0 collective-permute-start.2
  21.5 0.0 collective-permute-done.5.refs_1_
  21.5 0.6 collective-permute-done.6.refs_2_
  22.1 0.0 collective-permute-done.3.across_ref
  22.1 0.4 shrink.1
  22.5 0.5 collective-permute-start.7
  23.0 1.6 %collective-permute-start.12 = (bf16[256,512]{1,0:T(8,128)(2,1)S(1)}, bf16[256,512]{1,0:T(8,128)(2,1)S(1)}, u32[]{:S(2)}, u32[]{:S(2)}) collective-permute-start(bf16[256,512]{1,0:T(8,128)(2,1)S(1)} %get-tuple-element.37), channel_id=1, source_target_pairs={{0,2},{1,3},{2,0},{3,1},{4,6},{5,7},{6,4},{7,5},{8,10},{9,11},{10,... | collective-permute-start | bytes 786440 | tf_op jit(solution)/shard_map/ppermute | solution.py:35
  24.6 2.3 %collective-permute-done.7 = f32[64,64]{1,0:T(8,128)S(1)} collective-permute-done((f32[64,64]{1,0:T(8,128)S(1)}, f32[64,64]{1,0:T(8,128)S(1)}, u32[]{:S(2)}, u32[]{:S(2)}) %collective-permute-start.7) | collective-permute-done | bytes 16416 | tf_op jit(solution)/shard_map/ppermute | solution.py:35
  26.9 0.0 collective-permute-start.8
  26.9 0.0 collective-permute-done.10.refs_0_
  26.9 0.1 fusion
  27.0 2.1 %collective-permute-start.11 = (bf16[256,512]{1,0:T(8,128)(2,1)S(1)}, bf16[256,512]{1,0:T(8,128)(2,1)S(1)}, u32[]{:S(2)}, u32[]{:S(2)}) collective-permute-start(bf16[256,512]{1,0:T(8,128)(2,1)S(1)} %fusion), channel_id=1, source_target_pairs={{0,4},{1,5},{2,6},{3,7},{4,0},{5,1},{6,2},{7,3},{8,12},{9,13},{10,... | collective-permute-start | bytes 786440 | tf_op jit(solution)/shard_map/ppermute | solution.py:35
  29.1 0.0 collective-permute-done.8.other_ref
  29.1 0.0 collective-permute-done.2.refs_1_
  29.1 0.0 copy-done.4
  29.2 0.3 grow.1
  29.5 1.3 %collective-permute-start.13 = (bf16[1,64,512]{2,1,0:T(8,128)(2,1)S(1)}, bf16[1,64,512]{2,1,0:T(8,128)(2,1)S(1)}, u32[]{:S(2)}, u32[]{:S(2)}) collective-permute-start(bf16[1,64,512]{2,1,0:T(8,128)(2,1)S(1)} %get-tuple-element.34), channel_id=1, source_target_pairs={{0,2},{1,3},{2,0},{3,1},{4,6},{5,7},{6,4},{7,5},{8,10},{9,11},{10,... | collective-permute-start | bytes 196616 | tf_op jit(solution)/shard_map/ppermute | solution.py:35
  30.7 1.0 %collective-permute-start.14 = (bf16[1,64,512]{2,1,0:T(8,128)(2,1)S(1)}, bf16[1,64,512]{2,1,0:T(8,128)(2,1)S(1)}, u32[]{:S(2)}, u32[]{:S(2)}) collective-permute-start(bf16[1,64,512]{2,1,0:T(8,128)(2,1)S(1)} %get-tuple-element.35), channel_id=1, source_target_pairs={{0,4},{1,5},{2,6},{3,7},{4,0},{5,1},{6,2},{7,3},{8,12},{9,13},{10,... | collective-permute-start | bytes 196616 | tf_op jit(solution)/shard_map/ppermute | solution.py:35
  31.7 1.3 %collective-permute-start.15 = (bf16[1,64,512]{2,1,0:T(8,128)(2,1)S(1)}, bf16[1,64,512]{2,1,0:T(8,128)(2,1)S(1)}, u32[]{:S(2)}, u32[]{:S(2)}) collective-permute-start(bf16[1,64,512]{2,1,0:T(8,128)(2,1)S(1)} %get-tuple-element.36), channel_id=1, source_target_pairs={{0,6},{1,7},{2,4},{3,5},{4,2},{5,3},{6,0},{7,1},{8,14},{9,15},{10,... | collective-permute-start | bytes 196616 | tf_op jit(solution)/shard_map/ppermute | solution.py:35
  33.0 0.0 collective-permute-done.12
  33.0 3.3 %collective-permute-done.11 = bf16[256,512]{1,0:T(8,128)(2,1)S(1)} collective-permute-done((bf16[256,512]{1,0:T(8,128)(2,1)S(1)}, bf16[256,512]{1,0:T(8,128)(2,1)S(1)}, u32[]{:S(2)}, u32[]{:S(2)}) %collective-permute-start.11) | collective-permute-done | bytes 262176 | tf_op jit(solution)/shard_map/ppermute | solution.py:35
  36.3 0.1 join.7.refs_6_
  36.4 0.0 collective-permute-done.13.refs_2_.refs_3_
  36.4 1.3 %collective-permute-done.14.refs_3_.refs_4_ = bf16[1,64,512]{2,1,0:T(8,128)(2,1)S(1)} collective-permute-done((bf16[1,64,512]{2,1,0:T(8,128)(2,1)S(1)}, bf16[1,64,512]{2,1,0:T(8,128)(2,1)S(1)}, u32[]{:S(2)}, u32[]{:S(2)}) %collective-permute-start.14) | collective-permute-done | bytes 65568 | tf_op jit(solution)/shard_map/ppermute | solution.py:35
  37.7 2.0 %collective-permute-done.15.refs_4_.refs_5_ = bf16[1,64,512]{2,1,0:T(8,128)(2,1)S(1)} collective-permute-done((bf16[1,64,512]{2,1,0:T(8,128)(2,1)S(1)}, bf16[1,64,512]{2,1,0:T(8,128)(2,1)S(1)}, u32[]{:S(2)}, u32[]{:S(2)}) %collective-permute-start.15) | collective-permute-done | bytes 65568 | tf_op jit(solution)/shard_map/ppermute | solution.py:35
  39.7 0.3 join.10
  40.0 0.7 %collective-permute-start.18 = (bf16[256,512]{1,0:T(8,128)(2,1)S(1)}, bf16[256,512]{1,0:T(8,128)(2,1)S(1)}, u32[]{:S(2)}, u32[]{:S(2)}) collective-permute-start(bf16[256,512]{1,0:T(8,128)(2,1)S(1)} %join.10), channel_id=1, source_target_pairs={{0,2},{1,3},{2,0},{3,1},{4,6},{5,7},{6,4},{7,5},{8,10},{9,11},{10,... | collective-permute-start | bytes 786440 | tf_op jit(solution)/shard_map/ppermute | solution.py:35
  40.7 0.5 join.8.refs_3_.refs_4_
  41.2 3.7 %collective-permute-start.17 = (bf16[256,512]{1,0:T(8,128)(2,1)S(1)}, bf16[256,512]{1,0:T(8,128)(2,1)S(1)}, u32[]{:S(2)}, u32[]{:S(2)}) collective-permute-start(bf16[256,512]{1,0:T(8,128)(2,1)S(1)} %join.8.refs_3_.refs_4_), channel_id=1, source_target_pairs={{0,8},{1,9},{2,10},{3,11},{4,12},{5,13},{6,14},{7,15},{8,0},{9,1},... | collective-permute-start | bytes 786440 | tf_op jit(solution)/shard_map/ppermute | solution.py:35
  44.9 0.3 join.9
  45.2 0.3 collective-permute-start.16
  45.4 3.5 %collective-permute-done.18 = bf16[256,512]{1,0:T(8,128)(2,1)S(1)} collective-permute-done((bf16[256,512]{1,0:T(8,128)(2,1)S(1)}, bf16[256,512]{1,0:T(8,128)(2,1)S(1)}, u32[]{:S(2)}, u32[]{:S(2)}) %collective-permute-start.18) | collective-permute-done | bytes 262176 | tf_op jit(solution)/shard_map/ppermute | solution.py:35
  48.9 0.3 join.11
  49.2 2.0 %collective-permute-start.19 = (bf16[256,512]{1,0:T(8,128)(2,1)S(1)}, bf16[256,512]{1,0:T(8,128)(2,1)S(1)}, u32[]{:S(2)}, u32[]{:S(2)}) collective-permute-start(bf16[256,512]{1,0:T(8,128)(2,1)S(1)} %join.11), channel_id=1, source_target_pairs={{0,4},{1,5},{2,6},{3,7},{4,0},{5,1},{6,2},{7,3},{8,12},{9,13},{10,... | collective-permute-start | bytes 786440 | tf_op jit(solution)/shard_map/ppermute | solution.py:35
  51.2 0.3 join.6.side_ref
  51.4 2.1 %collective-permute-done.16.y_ref = bf16[256,512]{1,0:T(8,128)(2,1)S(1)} collective-permute-done((bf16[256,512]{1,0:T(8,128)(2,1)S(1)}, bf16[256,512]{1,0:T(8,128)(2,1)S(1)}, u32[]{:S(2)}, u32[]{:S(2)}) %collective-permute-start.16) | collective-permute-done | bytes 262176 | tf_op jit(solution)/shard_map/ppermute | solution.py:35
  53.6 2.9 %collective-permute-done.17.z_ref = bf16[256,512]{1,0:T(8,128)(2,1)S(1)} collective-permute-done((bf16[256,512]{1,0:T(8,128)(2,1)S(1)}, bf16[256,512]{1,0:T(8,128)(2,1)S(1)}, u32[]{:S(2)}, u32[]{:S(2)}) %collective-permute-start.17) | collective-permute-done | bytes 262176 | tf_op jit(solution)/shard_map/ppermute | solution.py:35
  56.5 0.1 gather.1
  56.6 4.1 %collective-permute-done.19 = bf16[256,512]{1,0:T(8,128)(2,1)S(1)} collective-permute-done((bf16[256,512]{1,0:T(8,128)(2,1)S(1)}, bf16[256,512]{1,0:T(8,128)(2,1)S(1)}, u32[]{:S(2)}, u32[]{:S(2)}) %collective-permute-start.19) | collective-permute-done | bytes 262176 | tf_op jit(solution)/shard_map/ppermute | solution.py:35
  60.7 0.8 %add_convert_fusion = bf16[256,512]{1,0:T(8,128)(2,1)} fusion(f32[256,512]{1,0:T(8,128)S(1)} %gather.1, bf16[256,512]{1,0:T(8,128)(2,1)S(1)} %collective-permute-done.19), kind=kLoop, calls=%fused_computation.2 | loop fusion | flops 393216 | bytes 1048576 | tf_op jit(solution)/shard_map/convert_element_type | solution.py:340
  (3 shorter events, 0.0 us)
Async XLA Ops:
  0.0 4.7 %collective-permute-start = (bf16[64,8192]{1,0:T(8,128)(2,1)}, bf16[64,8192]{1,0:T(8,128)(2,1)S(1)}, u32[]{:S(2)}, u32[]{:S(2)}) collective-permute-start(bf16[64,8192]{1,0:T(8,128)(2,1)} %bitcast.18), channel_id=1, source_target_pairs={{0,1},{1,0},{2,3},{3,2},{4,5},{5,4},{6,7},{7,6},{8,9},{9,8},{10,11... | collective-permute-start | bytes 3145736 | tf_op jit(solution)/shard_map/ppermute | solution.py:35
  0.5 7.1 %collective-permute-start.1 = (bf16[64,8192]{1,0:T(8,128)(2,1)}, bf16[64,8192]{1,0:T(8,128)(2,1)S(1)}, u32[]{:S(2)}, u32[]{:S(2)}) collective-permute-start(bf16[64,8192]{1,0:T(8,128)(2,1)} %bitcast.25), channel_id=1, source_target_pairs={{0,1},{1,0},{2,3},{3,2},{4,5},{5,4},{6,7},{7,6},{8,9},{9,8},{10,11... | collective-permute-start | bytes 3145736 | tf_op jit(solution)/shard_map/ppermute | solution.py:35
  0.5 0.9 %copy-start = (bf16[256,512]{1,0:T(8,128)(2,1)S(1)}, bf16[256,512]{1,0:T(8,128)(2,1)}, u32[]{:S(2)}) copy-start(bf16[256,512]{1,0:T(8,128)(2,1)} %attended_hbm.3) | copy-start | bytes 786436
  1.5 3.2 %copy-start.1 = (bf16[1,8192,64]{1,2,0:T(8,128)(2,1)S(1)}, bf16[1,8192,64]{1,2,0:T(8,128)(2,1)}, u32[]{:S(2)}) copy-start(bf16[1,8192,64]{1,2,0:T(8,128)(2,1)} %param.8) | copy-start | bytes 3145732
  4.2 3.4 %copy-start.2 = (s32[256]{0:T(256)S(1)}, s32[256]{0:T(256)}, u32[]{:S(2)}) copy-start(s32[256]{0:T(256)} %param.10) | copy-start | bytes 3076
  4.2 3.4 %copy-start.3 = (s32[16]{0:T(128)S(1)}, s32[16]{0:T(128)}, u32[]{:S(2)}) copy-start(s32[16]{0:T(128)} %slot_hbm.1) | copy-start | bytes 196
  4.2 8.6 %collective-permute-start.9 = (bf16[3,256,512]{2,1,0:T(8,128)(2,1)S(1)}, bf16[3,256,512]{2,1,0:T(8,128)(2,1)S(1)}, u32[]{:S(2)}, u32[]{:S(2)}) collective-permute-start(bf16[3,256,512]{2,1,0:T(8,128)(2,1)S(1)} %get-tuple-element.32), channel_id=1, source_target_pairs={{0,1},{1,0},{2,3},{3,2},{4,5},{5,4},{6,7},{7,6},{8,9},{9,8},{10,11... | collective-permute-start | bytes 2359304 | tf_op jit(solution)/shard_map/ppermute | solution.py:35
  4.9 17.2 %collective-permute-start.3 = (bf16[128,2048]{1,0:T(8,128)(2,1)S(1)}, bf16[128,2048]{1,0:T(8,128)(2,1)S(1)}, u32[]{:S(2)}, u32[]{:S(2)}) collective-permute-start(bf16[128,2048]{1,0:T(8,128)(2,1)S(1)} %columns.1.rest_1_), channel_id=1, source_target_pairs={{0,2},{1,3},{2,0},{3,1},{4,6},{5,7},{6,4},{7,5},{8,10},{9,11},{10,... | collective-permute-start | bytes 1572872 | tf_op jit(solution)/shard_map/ppermute | solution.py:35
  8.6 13.0 %collective-permute-start.4 = (bf16[128,512]{1,0:T(8,128)(2,1)S(1)}, bf16[128,512]{1,0:T(8,128)(2,1)S(1)}, u32[]{:S(2)}, u32[]{:S(2)}) collective-permute-start(bf16[128,512]{1,0:T(8,128)(2,1)S(1)} %get-tuple-element.25), channel_id=1, source_target_pairs={{0,8},{1,9},{2,10},{3,11},{4,12},{5,13},{6,14},{7,15},{8,0},{9,1},... | collective-permute-start | bytes 393224 | tf_op jit(solution)/shard_map/ppermute | solution.py:35
  11.2 10.3 %collective-permute-start.5 = (bf16[128,512]{1,0:T(8,128)(2,1)S(1)}, bf16[128,512]{1,0:T(8,128)(2,1)S(1)}, u32[]{:S(2)}, u32[]{:S(2)}) collective-permute-start(bf16[128,512]{1,0:T(8,128)(2,1)S(1)} %get-tuple-element.26), channel_id=1, source_target_pairs={{0,12},{1,13},{2,14},{3,15},{4,8},{5,9},{6,10},{7,11},{8,4},{9,5},... | collective-permute-start | bytes 393224 | tf_op jit(solution)/shard_map/ppermute | solution.py:35
  12.6 9.6 %collective-permute-start.6 = (bf16[128,512]{1,0:T(8,128)(2,1)S(1)}, bf16[128,512]{1,0:T(8,128)(2,1)S(1)}, u32[]{:S(2)}, u32[]{:S(2)}) collective-permute-start(bf16[128,512]{1,0:T(8,128)(2,1)S(1)} %get-tuple-element.27), channel_id=1, source_target_pairs={{0,4},{1,5},{2,6},{3,7},{4,0},{5,1},{6,2},{7,3},{8,12},{9,13},{10,... | collective-permute-start | bytes 393224 | tf_op jit(solution)/shard_map/ppermute | solution.py:35
  13.0 13.9 %collective-permute-start.10 = (bf16[256,512]{1,0:T(8,128)(2,1)S(1)}, bf16[256,512]{1,0:T(8,128)(2,1)S(1)}, u32[]{:S(2)}, u32[]{:S(2)}) collective-permute-start(bf16[256,512]{1,0:T(8,128)(2,1)S(1)} %get-tuple-element.38), channel_id=1, source_target_pairs={{0,2},{1,3},{2,0},{3,1},{4,6},{5,7},{6,4},{7,5},{8,10},{9,11},{10,... | collective-permute-start | bytes 786440 | tf_op jit(solution)/shard_map/ppermute | solution.py:35
  21.5 7.6 %collective-permute-start.2 = (bf16[5,256,512]{2,1,0:T(8,128)(2,1)S(1)}, bf16[5,256,512]{2,1,0:T(8,128)(2,1)S(1)}, u32[]{:S(2)}, u32[]{:S(2)}) collective-permute-start(bf16[5,256,512]{2,1,0:T(8,128)(2,1)S(1)} %get-tuple-element.24), channel_id=1, source_target_pairs={{0,1},{1,0},{2,3},{3,2},{4,5},{5,4},{6,7},{7,6},{8,9},{9,8},{10,11... | collective-permute-start | bytes 3932168 | tf_op jit(solution)/shard_map/ppermute | solution.py:35
  22.1 7.0 %copy-start.4 = (bf16[1,64,8192]{2,1,0:T(8,128)(2,1)S(1)}, bf16[1,64,8192]{2,1,0:T(8,128)(2,1)}, u32[]{:S(2)}) copy-start(bf16[1,64,8192]{2,1,0:T(8,128)(2,1)} %param.9) | copy-start | bytes 3145732
  22.5 4.3 %collective-permute-start.7 = (f32[64,64]{1,0:T(8,128)S(1)}, f32[64,64]{1,0:T(8,128)S(1)}, u32[]{:S(2)}, u32[]{:S(2)}) collective-permute-start(f32[64,64]{1,0:T(8,128)S(1)} %get-tuple-element.30), channel_id=1, source_target_pairs={{0,2},{1,3},{2,0},{3,1},{4,6},{5,7},{6,4},{7,5},{8,10},{9,11},{10,... | collective-permute-start | bytes 49160 | tf_op jit(solution)/shard_map/ppermute | solution.py:35
  23.0 10.0 %collective-permute-start.12 = (bf16[256,512]{1,0:T(8,128)(2,1)S(1)}, bf16[256,512]{1,0:T(8,128)(2,1)S(1)}, u32[]{:S(2)}, u32[]{:S(2)}) collective-permute-start(bf16[256,512]{1,0:T(8,128)(2,1)S(1)} %get-tuple-element.37), channel_id=1, source_target_pairs={{0,2},{1,3},{2,0},{3,1},{4,6},{5,7},{6,4},{7,5},{8,10},{9,11},{10,... | collective-permute-start | bytes 786440 | tf_op jit(solution)/shard_map/ppermute | solution.py:35
  26.9 2.3 %collective-permute-start.8 = (f32[64,64]{1,0:T(8,128)S(1)}, f32[64,64]{1,0:T(8,128)S(1)}, u32[]{:S(2)}, u32[]{:S(2)}) collective-permute-start(f32[64,64]{1,0:T(8,128)S(1)} %add.23.mine_ref), channel_id=1, source_target_pairs={{0,1},{1,0},{2,3},{3,2},{4,5},{5,4},{6,7},{7,6},{8,9},{9,8},{10,11... | collective-permute-start | bytes 49160 | tf_op jit(solution)/shard_map/ppermute | solution.py:35
  27.0 9.3 %collective-permute-start.11 = (bf16[256,512]{1,0:T(8,128)(2,1)S(1)}, bf16[256,512]{1,0:T(8,128)(2,1)S(1)}, u32[]{:S(2)}, u32[]{:S(2)}) collective-permute-start(bf16[256,512]{1,0:T(8,128)(2,1)S(1)} %fusion), channel_id=1, source_target_pairs={{0,4},{1,5},{2,6},{3,7},{4,0},{5,1},{6,2},{7,3},{8,12},{9,13},{10,... | collective-permute-start | bytes 786440 | tf_op jit(solution)/shard_map/ppermute | solution.py:35
  29.5 7.0 %collective-permute-start.13 = (bf16[1,64,512]{2,1,0:T(8,128)(2,1)S(1)}, bf16[1,64,512]{2,1,0:T(8,128)(2,1)S(1)}, u32[]{:S(2)}, u32[]{:S(2)}) collective-permute-start(bf16[1,64,512]{2,1,0:T(8,128)(2,1)S(1)} %get-tuple-element.34), channel_id=1, source_target_pairs={{0,2},{1,3},{2,0},{3,1},{4,6},{5,7},{6,4},{7,5},{8,10},{9,11},{10,... | collective-permute-start | bytes 196616 | tf_op jit(solution)/shard_map/ppermute | solution.py:35
  30.7 7.0 %collective-permute-start.14 = (bf16[1,64,512]{2,1,0:T(8,128)(2,1)S(1)}, bf16[1,64,512]{2,1,0:T(8,128)(2,1)S(1)}, u32[]{:S(2)}, u32[]{:S(2)}) collective-permute-start(bf16[1,64,512]{2,1,0:T(8,128)(2,1)S(1)} %get-tuple-element.35), channel_id=1, source_target_pairs={{0,4},{1,5},{2,6},{3,7},{4,0},{5,1},{6,2},{7,3},{8,12},{9,13},{10,... | collective-permute-start | bytes 196616 | tf_op jit(solution)/shard_map/ppermute | solution.py:35
  31.7 8.0 %collective-permute-start.15 = (bf16[1,64,512]{2,1,0:T(8,128)(2,1)S(1)}, bf16[1,64,512]{2,1,0:T(8,128)(2,1)S(1)}, u32[]{:S(2)}, u32[]{:S(2)}) collective-permute-start(bf16[1,64,512]{2,1,0:T(8,128)(2,1)S(1)} %get-tuple-element.36), channel_id=1, source_target_pairs={{0,6},{1,7},{2,4},{3,5},{4,2},{5,3},{6,0},{7,1},{8,14},{9,15},{10,... | collective-permute-start | bytes 196616 | tf_op jit(solution)/shard_map/ppermute | solution.py:35
  40.0 8.9 %collective-permute-start.18 = (bf16[256,512]{1,0:T(8,128)(2,1)S(1)}, bf16[256,512]{1,0:T(8,128)(2,1)S(1)}, u32[]{:S(2)}, u32[]{:S(2)}) collective-permute-start(bf16[256,512]{1,0:T(8,128)(2,1)S(1)} %join.10), channel_id=1, source_target_pairs={{0,2},{1,3},{2,0},{3,1},{4,6},{5,7},{6,4},{7,5},{8,10},{9,11},{10,... | collective-permute-start | bytes 786440 | tf_op jit(solution)/shard_map/ppermute | solution.py:35
  41.2 15.3 %collective-permute-start.17 = (bf16[256,512]{1,0:T(8,128)(2,1)S(1)}, bf16[256,512]{1,0:T(8,128)(2,1)S(1)}, u32[]{:S(2)}, u32[]{:S(2)}) collective-permute-start(bf16[256,512]{1,0:T(8,128)(2,1)S(1)} %join.8.refs_3_.refs_4_), channel_id=1, source_target_pairs={{0,8},{1,9},{2,10},{3,11},{4,12},{5,13},{6,14},{7,15},{8,0},{9,1},... | collective-permute-start | bytes 786440 | tf_op jit(solution)/shard_map/ppermute | solution.py:35
  45.2 8.4 %collective-permute-start.16 = (bf16[256,512]{1,0:T(8,128)(2,1)S(1)}, bf16[256,512]{1,0:T(8,128)(2,1)S(1)}, u32[]{:S(2)}, u32[]{:S(2)}) collective-permute-start(bf16[256,512]{1,0:T(8,128)(2,1)S(1)} %join.9), channel_id=1, source_target_pairs={{0,2},{1,3},{2,0},{3,1},{4,6},{5,7},{6,4},{7,5},{8,10},{9,11},{10,... | collective-permute-start | bytes 786440 | tf_op jit(solution)/shard_map/ppermute | solution.py:35
  49.2 11.5 %collective-permute-start.19 = (bf16[256,512]{1,0:T(8,128)(2,1)S(1)}, bf16[256,512]{1,0:T(8,128)(2,1)S(1)}, u32[]{:S(2)}, u32[]{:S(2)}) collective-permute-start(bf16[256,512]{1,0:T(8,128)(2,1)S(1)} %join.11), channel_id=1, source_target_pairs={{0,4},{1,5},{2,6},{3,7},{4,0},{5,1},{6,2},{7,3},{8,12},{9,13},{10,... | collective-permute-start | bytes 786440 | tf_op jit(solution)/shard_map/ppermute | solution.py:35

commit v10 on v8

--- a/solution.py
+++ b/solution.py
@@ -98,9 +98,8 @@
     return found[0], found[1:]
 
 
-def product_kernel(groups, attended_hbm, weight_hbm, *refs):
-    token_ref, attended_ref, weight_ref, sems = refs[-4:]
-    chips = [m for group in groups for m in group]
+def product_kernel(chips, attended_hbm, weight_hbm, *refs):
+    away_ref, stay_ref, token_ref, attended_ref, weight_ref, sems = refs[-6:]
     width = weight_ref.shape[2] // 2
     me = lax.axis_index("tensor")
     core, chip = me % 2, me // 2
@@ -116,30 +115,25 @@
     fetches[0].wait()
     there = pl.ds(pl.multiple_of((1 - core) * width, width), width)
     here = pl.ds(pl.multiple_of(core * width, width), width)
-    at = 0
-    for g, group in enumerate(groups):
-        away_ref, stay_ref = refs[2 * g : 2 * g + 2]
-        for i in range(len(group)):
-            fetches[at + 1].wait()
-            away_ref[i] = dot(attended_ref[...], weight_ref[at, :, there]).astype(jnp.bfloat16)
-            stay_ref[i] = dot(attended_ref[...], weight_ref[at, :, here])
-            at += 1
-
-
-def product(attended, out_weight, groups, mib):
+    for i in range(len(chips)):
+        fetches[i + 1].wait()
+        away_ref[i] = dot(attended_ref[...], weight_ref[i, :, there]).astype(jnp.bfloat16)
+        stay_ref[i] = dot(attended_ref[...], weight_ref[i, :, here])
+
+
+def product(attended, out_weight, chips, mib, *after):
     rows, depth = attended.shape
     width = out_weight.shape[1] // lax.axis_size("tensor")
-    n = sum(len(group) for group in groups)
-    out_shape = []
-    for group in groups:
-        out_shape.append(shape((len(group), rows, width)))
-        out_shape.append(shape((len(group), rows, width), jnp.float32))
-    out_shape.append(shape((8, 128), jnp.float32))
-    return pl.pallas_call(
-        functools.partial(product_kernel, groups),
-        out_shape=out_shape,
-        in_specs=[IN_HBM, IN_HBM],
-        out_specs=[IN_VMEM] * len(out_shape),
+    n = len(chips)
+    return pl.pallas_call(
+        functools.partial(product_kernel, chips),
+        out_shape=(
+            shape((n, rows, width)),
+            shape((n, rows, width), jnp.float32),
+            shape((8, 128), jnp.float32),
+        ),
+        in_specs=[IN_HBM, IN_HBM] + [ANYWHERE] * len(after),
+        out_specs=[IN_VMEM] * 3,
         scratch_shapes=[
             pltpu.VMEM((rows, depth), jnp.bfloat16),
             pltpu.VMEM((n, depth, 2 * width), jnp.bfloat16),
@@ -148,7 +142,7 @@
         compiler_params=params(mib),
         cost_estimate=cost(4 * n * rows * depth * width, n * (4 * depth * width + 6 * rows * width)),
         name="product",
-    )(attended, out_weight)
+    )(attended, out_weight, *after)
 
 
 def shrink_kernel(distances, down_ref, other_ref, *refs):
@@ -203,7 +197,7 @@
         in_specs=[IN_VMEM] * 4 + [ANYWHERE] * len(after),
         out_specs=[IN_VMEM] * len(groups),
         compiler_params=params(16),
-        cost_estimate=cost(4*CAP*up.size, 4 * up.size),
+        cost_estimate=cost(4 * 10**9, 4 * up.size),
         name="grow",
     )(mine, other, up, up_other, *after)
 
@@ -242,53 +236,62 @@
     )(target, *operands)
 
 
+def gather_kernel(sum_ref, came_ref, out_ref):
+    out_ref[...] = sum_ref[...] + came_ref[...].astype(jnp.float32)
+
+
+def gather(total, came):
+    return pl.pallas_call(
+        gather_kernel,
+        out_shape=shape(total.shape, jnp.float32),
+        in_specs=[IN_VMEM] * 2,
+        out_specs=IN_VMEM,
+        compiler_params=params(16),
+        cost_estimate=cost(total.size, 10 * total.size),
+        name="gather",
+    )(total, came)
+
+
 def staged(attended, out_weight, adapter_down, adapter_up, row_adapter, adapter_slot):
     f32, bf16 = jnp.float32, jnp.bfloat16
     up, down = adapter_up[0], jnp.swapaxes(adapter_down, 1, 2)[0]
     from_y = swap(attended, 2)
     down_other, up_other = swap(down, 1), swap(up, 1)
-    chips = (6, 4, 3, 2, 1, 0)
-    away_first, stay_first, away, stay, token = product(attended, out_weight, ((7, 5), chips), 44)
+    firsts, chips = (7, 6, 5), (4, 3, 2, 1, 0)
+    away_first, stay_first, token = product(attended, out_weight, firsts, 44)
+    came_first = swap(away_first, 1)
+    first = [stay_first[i] + came_first[i].astype(f32) for i in range(3)]
+    go3, go2 = first[0].astype(bf16), first[2].astype(bf16)
     target, outgoing = route(adapter_slot, row_adapter, attended, from_y, token, down_other, up_other)
-    arrived = {k: swap(outgoing[k], 4 * k) for k in (2,3,1)}
+    arrived = {k: swap(outgoing[k], 4 * k) for k in (2, 3, 1)}
     arrived[0] = outgoing[0]
-    away_first, away = once((away_first, away), target)
-    came_first, came = swap(away_first, 1), swap(away, 1)
+    y3, y2 = swap(go3, 2), swap(go2, 2)[None]
+    z3 = swap((first[1] + y3.astype(f32)).astype(bf16), 4)[None]
+    away, stay, _ = product(attended, out_weight, chips, 44, target)
+    came = swap(away, 1)
 
     def base(m):
         return stay[chips.index(m)] + came[chips.index(m)].astype(f32)
 
-    y3 = swap((stay_first[0] + came_first[0].astype(f32)).astype(bf16), 2)
-    y2 = swap((stay_first[1] + came_first[1].astype(f32)).astype(bf16), 2)[None]
+    y1, y0 = swap(base(3).astype(bf16), 2), swap(base(1).astype(bf16), 2)
     mine = shrink(down, down_other, arrived)
-    ready3, go1 = once((y3, base(3).astype(bf16)), mine)
-    z3 = swap((base(6) + ready3.astype(f32)).astype(bf16), 4)[None]
-    y1 = swap(go1, 2)[None]
-    here_chips = (4, 2, 1, 0)
-    groups = (tuple(2 * m for m in here_chips), (10, 6), (12,), (14,))
-    here, over2, over4, over6 = grow(mine, swap(mine, 1), up, up_other, groups, y3, y2)
+    groups = ((8, 0), (10, 2), (12, 4), (14, 6))
+    here, over2, over4, over6 = grow(mine, swap(mine, 1), up, up_other, groups, y2, came)
     over2, over4, over6 = swap(over2, 2), swap(over4, 4), swap(over6, 6)
-
-    def blocks(m):
-        return ((0, chips.index(m)), (1, chips.index(m))), ((2, here_chips.index(m), 0),)
-
-    sums, grown = blocks(4)
+    (ready2,) = join(target, [stay, came, z3, y2], ((((0, 0), (1, 0), (2, 0), (3, 0)), ()),), f32)
+    grown = [here, over2, over4, over6]
     (sum2,) = join(
+        target, [ready2[None]] + grown, ((((0, 0),), tuple((1 + i, 0, 2 * i) for i in range(4))),), bf16
+    )
+    z2 = swap(sum2, 8)
+    (side0,) = join(
         target,
-        [stay, came, here, over2, over4, over6, z3, y2],
-        ((sums + ((6, 0), (7, 0)), grown + ((3, 0, 2), (4, 0, 4), (5, 0, 6))),),
-        bf16,
-    )
-    z2 = swap(sum2, 8)
-    sums, grown = blocks(2)
-    (sum1,) = join(
-        target, [stay, came, here, over2, y1, sum2], ((sums + ((4, 0),), grown + ((3, 1, 2),)),), bf16
-    )
-    z1 = swap(sum1, 4)
-    (go0,) = join(target, [stay, came, here, sum2], (blocks(1),), bf16)
-    y0 = swap(go0, 2)
-    (side0,) = join(target, [stay, came, here], (blocks(0),), f32)
-    total = side0 + y0.astype(f32) + z2.astype(f32) + z1.astype(f32)
+        [stay, came, sum2] + grown,
+        ((((0, 4), (1, 4)), tuple((3 + i, 1, 2 * i) for i in range(4))),),
+        f32,
+    )
+    z1 = swap((base(2) + y1.astype(f32)).astype(bf16), 4)
+    total = gather(side0, z2) + y0.astype(f32) + z1.astype(f32)
     return total.astype(bf16)
 
 

time: 60.7 us -> 62.6 us (1.031)
  waiting for transfers between devices: 27 us -> 29.3 us
  starting transfers between devices: 22.8 us -> 21 us
  Pallas kernels: 8.07 us -> 9.68 us
    ppermute x19, waiting for transfers between devices: 27 us -> 29.3 us  [swap(): return lax.ppermute(value, 'tensor', [(t, t ^ mask) for t in range(count)])]
    pallas_call x3, Pallas kernels: 4.86 us -> 6.75 us  [the longest x2 6.7 us: product(): pl.pallas_call(functools.partial(product_kernel, chips), out_shape=(shape...]
    ppermute x19, starting transfers between devices: 22.8 us -> 21 us  [swap(): return lax.ppermute(value, 'tensor', [(t, t ^ mask) for t in range(count)])]
    pallas_call x4 -> x3, Pallas kernels: 1.31 us -> 1.05 us  [join(): pl.pallas_call(functools.partial(join_kernel, terms), out_shape=[shape((r...]
  transfers between devices with their start and end apart: 19 -> 19, of which waited for: 9 -> 7; matrix products, arithmetic and copies ran while one was open for 0% -> 1% of each run, Pallas kernels for 11% -> 11%
where the time goes in v10:
time: 62.6 us; the launch traced here: 62.5 us
  waiting for transfers between devices  29.3 us (47%)
  starting transfers between devices  21 us (34%)
  Pallas kernels  9.68 us (15%)
  other arithmetic  1.41 us (2%)
  local copies, waits for them, and re-layouts  0.97 us (2%)
    ppermute x19, waiting for transfers between devices, swap(): return lax.ppermute(value, 'tensor', [(t, t ^ mask) for t in range(count)])  29.3 us
    ppermute x19, starting transfers between devices, swap(): return lax.ppermute(value, 'tensor', [(t, t ^ mask) for t in range(count)])  21 us
    pallas_call x2, Pallas kernels, product(): pl.pallas_call(functools.partial(product_kernel, chips), out_shape=(shape...  6.7 us
  transfers between devices with their start and end apart: 19, of which 7 were waited for; matrix products, arithmetic and copies ran while one was open for 1% of the time, Pallas kernels for 11%

profile of v10, /device:TPU:0, one launch (start us, length us, event | category | flops | bytes accessed | tf_op | source)
XLA Modules:
  0.0 62.5 jit_solution(2307599714796770629)
XLA Ops:
  0.0 0.0 copy-start
  0.0 0.9 %copy-done = bf16[256,512]{1,0:T(8,128)(2,1)S(1)} copy-done((bf16[256,512]{1,0:T(8,128)(2,1)S(1)}, bf16[256,512]{1,0:T(8,128)(2,1)}, u32[]{:S(2)}) %copy-start) | copy-done | bytes 262168
  1.0 0.0 copy-start.3
  1.0 0.0 copy-start.4
  1.0 2.7 %product.2 = (bf16[3,256,512]{2,1,0:T(8,128)(2,1)S(1)}, f32[3,256,512]{2,1,0:T(8,128)S(1)}, f32[8,128]{1,0:T(8,128)S(1)}) custom-call(bf16[256,512]{1,0:T(8,128)(2,1)S(1)} %copy-done, bf16[512,8192]{1,0:T(8,128)(2,1)} %weight_hbm.3), custom_call_target="tpu_custom_call" | custom-call | flops 805306368 | bytes 5505024 | tf_op jit(solution)/shard_map/product/pallas_call | solution.py:128
  3.7 0.0 copy-start.1
  3.7 0.0 copy-start.2
  3.7 0.5 collective-permute-start.4
  4.3 0.0 copy-done.3
  4.3 0.1 collective-permute-start.1
  4.3 0.0 copy-done.4
  4.3 0.4 collective-permute-start.2
  4.8 2.6 %collective-permute-start = (bf16[256,512]{1,0:T(8,128)(2,1)S(1)}, bf16[256,512]{1,0:T(8,128)(2,1)S(1)}, u32[]{:S(2)}, u32[]{:S(2)}) collective-permute-start(bf16[256,512]{1,0:T(8,128)(2,1)S(1)} %copy-done), channel_id=1, source_target_pairs={{0,2},{1,3},{2,0},{3,1},{4,6},{5,7},{6,4},{7,5},{8,10},{9,11},{10,... | collective-permute-start | bytes 786440 | tf_op jit(solution)/shard_map/ppermute | solution.py:35
  7.4 0.0 collective-permute-done.4
  7.4 0.2 fusion.3
  7.6 1.7 %collective-permute-start.5 = (bf16[256,512]{1,0:T(8,128)(2,1)S(1)}, bf16[256,512]{1,0:T(8,128)(2,1)S(1)}, u32[]{:S(2)}, u32[]{:S(2)}) collective-permute-start(bf16[256,512]{1,0:T(8,128)(2,1)S(1)} %get-tuple-element.36), channel_id=1, source_target_pairs={{0,2},{1,3},{2,0},{3,1},{4,6},{5,7},{6,4},{7,5},{8,10},{9,11},{10,... | collective-permute-start | bytes 786440 | tf_op jit(solution)/shard_map/ppermute | solution.py:35
  9.3 0.3 collective-permute-start.7
  9.7 4.9 %collective-permute-done.y_ref = bf16[256,512]{1,0:T(8,128)(2,1)S(1)} collective-permute-done((bf16[256,512]{1,0:T(8,128)(2,1)S(1)}, bf16[256,512]{1,0:T(8,128)(2,1)S(1)}, u32[]{:S(2)}, u32[]{:S(2)}) %collective-permute-start) | collective-permute-done | bytes 262176 | tf_op jit(solution)/shard_map/ppermute | solution.py:35
  14.5 0.0 collective-permute-done.1.rest_1_.other_ref
  14.5 0.0 collective-permute-done.2.rest_2_.up_other_ref
  14.5 0.0 copy-done.1
  14.5 0.0 copy-done.2
  14.5 1.2 %route.1 = (s32[1,256]{1,0:T(1,128)S(1)}, bf16[64,1024]{1,0:T(8,128)(2,1)S(1)}, bf16[64,1024]{1,0:T(8,128)(2,1)S(1)}, bf16[64,1024]{1,0:T(8,128)(2,1)S(1)}, bf16[64,1024]{1,0:T(8,128)(2,1)S(1)}) custom-call(s32[16]{0:T(128)S(1)} %copy-done.2, s32[1,256]{1,0:T(1,128)S(1)} %bitcast.28, bf16[256,512]{1,0:T(8,128)(2,1)S(1)} %copy-done, ...), custom_call_target="tpu_custom_call" | custom-call | flops 134217728 | bytes 1048576 | tf_op jit(solution)/shard_map/route/pallas_call | solution.py:88
  15.8 3.1 %collective-permute-start.8 = (bf16[64,1024]{1,0:T(8,128)(2,1)S(1)}, bf16[64,1024]{1,0:T(8,128)(2,1)S(1)}, u32[]{:S(2)}, u32[]{:S(2)}) collective-permute-start(bf16[64,1024]{1,0:T(8,128)(2,1)S(1)} %get-tuple-element.25), channel_id=1, source_target_pairs={{0,8},{1,9},{2,10},{3,11},{4,12},{5,13},{6,14},{7,15},{8,0},{9,1},... | collective-permute-start | bytes 393224 | tf_op jit(solution)/shard_map/ppermute | solution.py:35
  18.8 1.3 %collective-permute-start.9 = (bf16[64,1024]{1,0:T(8,128)(2,1)S(1)}, bf16[64,1024]{1,0:T(8,128)(2,1)S(1)}, u32[]{:S(2)}, u32[]{:S(2)}) collective-permute-start(bf16[64,1024]{1,0:T(8,128)(2,1)S(1)} %get-tuple-element.26), channel_id=1, source_target_pairs={{0,12},{1,13},{2,14},{3,15},{4,8},{5,9},{6,10},{7,11},{8,4},{9,5},... | collective-permute-start | bytes 393224 | tf_op jit(solution)/shard_map/ppermute | solution.py:35
  20.2 0.2 collective-permute-start.10
  20.4 0.0 collective-permute-done.5
  20.4 0.1 fusion.1
  20.5 1.9 %collective-permute-start.6 = (bf16[256,512]{1,0:T(8,128)(2,1)S(1)}, bf16[256,512]{1,0:T(8,128)(2,1)S(1)}, u32[]{:S(2)}, u32[]{:S(2)}) collective-permute-start(bf16[256,512]{1,0:T(8,128)(2,1)S(1)} %fusion.1), channel_id=1, source_target_pairs={{0,4},{1,5},{2,6},{3,7},{4,0},{5,1},{6,2},{7,3},{8,12},{9,13},{10,... | collective-permute-start | bytes 786440 | tf_op jit(solution)/shard_map/ppermute | solution.py:35
  22.4 4.0 %product.3 = (bf16[5,256,512]{2,1,0:T(8,128)(2,1)S(1)}, f32[5,256,512]{2,1,0:T(8,128)S(1)}, f32[8,128]{1,0:T(8,128)}) custom-call(bf16[256,512]{1,0:T(8,128)(2,1)S(1)} %copy-done, bf16[512,8192]{1,0:T(8,128)(2,1)} %weight_hbm.3, s32[1,256]{1,0:T(1,128)S(1)} %get-tuple-element.20.refs_0_.target_ref), custom_call_target="tpu_custom_call" | custom-call | flops 1342177280 | bytes 9175040 | tf_op jit(solution)/shard_map/product/pallas_call | solution.py:128
  26.4 2.2 %collective-permute-done.8.refs_0_ = bf16[64,1024]{1,0:T(8,128)(2,1)S(1)} collective-permute-done((bf16[64,1024]{1,0:T(8,128)(2,1)S(1)}, bf16[64,1024]{1,0:T(8,128)(2,1)S(1)}, u32[]{:S(2)}, u32[]{:S(2)}) %collective-permute-start.8) | collective-permute-done | bytes 131104 | tf_op jit(solution)/shard_map/ppermute | solution.py:35
  28.5 0.0 collective-permute-start.3
  28.5 0.0 collective-permute-done.9.refs_1_
  28.6 1.4 %collective-permute-done.10.refs_2_ = bf16[64,1024]{1,0:T(8,128)(2,1)S(1)} collective-permute-done((bf16[64,1024]{1,0:T(8,128)(2,1)S(1)}, bf16[64,1024]{1,0:T(8,128)(2,1)S(1)}, u32[]{:S(2)}, u32[]{:S(2)}) %collective-permute-start.10) | collective-permute-done | bytes 131104 | tf_op jit(solution)/shard_map/ppermute | solution.py:35
  30.0 0.4 shrink.1.mine_ref
  30.4 0.0 collective-permute-start.11
  30.4 1.2 %collective-permute-done.3.refs_1_ = bf16[5,256,512]{2,1,0:T(8,128)(2,1)S(1)} collective-permute-done((bf16[5,256,512]{2,1,0:T(8,128)(2,1)S(1)}, bf16[5,256,512]{2,1,0:T(8,128)(2,1)S(1)}, u32[]{:S(2)}, u32[]{:S(2)}) %collective-permute-start.3) | collective-permute-done | bytes 1310752 | tf_op jit(solution)/shard_map/ppermute | solution.py:35
  31.6 0.2 fusion.4
  31.8 1.6 %collective-permute-start.17 = (bf16[256,512]{1,0:T(8,128)(2,1)S(1)}, bf16[256,512]{1,0:T(8,128)(2,1)S(1)}, u32[]{:S(2)}, u32[]{:S(2)}) collective-permute-start(bf16[256,512]{1,0:T(8,128)(2,1)S(1)} %get-tuple-element.34), channel_id=1, source_target_pairs={{0,2},{1,3},{2,0},{3,1},{4,6},{5,7},{6,4},{7,5},{8,10},{9,11},{10,... | collective-permute-start | bytes 786440 | tf_op jit(solution)/shard_map/ppermute | solution.py:35
  33.3 0.0 collective-permute-done.7
  33.3 0.0 collective-permute-done.11.other_ref
  33.3 0.3 grow.1
  33.6 0.6 collective-permute-start.12
  34.2 0.2 collective-permute-start.13
  34.4 2.8 %collective-permute-start.14 = (bf16[2,64,512]{2,1,0:T(8,128)(2,1)S(1)}, bf16[2,64,512]{2,1,0:T(8,128)(2,1)S(1)}, u32[]{:S(2)}, u32[]{:S(2)}) collective-permute-start(bf16[2,64,512]{2,1,0:T(8,128)(2,1)S(1)} %get-tuple-element.32), channel_id=1, source_target_pairs={{0,6},{1,7},{2,4},{3,5},{4,2},{5,3},{6,0},{7,1},{8,14},{9,15},{10,... | collective-permute-start | bytes 393224 | tf_op jit(solution)/shard_map/ppermute | solution.py:35
  37.2 0.0 collective-permute-done.6
  37.2 0.5 collective-permute-start.16
  37.7 0.1 join.3
  37.8 8.7 %collective-permute-done.12.refs_2_.refs_4_ = bf16[2,64,512]{2,1,0:T(8,128)(2,1)S(1)} collective-permute-done((bf16[2,64,512]{2,1,0:T(8,128)(2,1)S(1)}, bf16[2,64,512]{2,1,0:T(8,128)(2,1)S(1)}, u32[]{:S(2)}, u32[]{:S(2)}) %collective-permute-start.12) | collective-permute-done | bytes 131104 | tf_op jit(solution)/shard_map/ppermute | solution.py:35
  46.6 0.0 collective-permute-done.13.refs_3_.refs_5_
  46.6 0.0 collective-permute-done.14.refs_4_.refs_6_
  46.6 0.5 join.4.refs_2_
  47.1 1.6 %collective-permute-start.15 = (bf16[256,512]{1,0:T(8,128)(2,1)S(1)}, bf16[256,512]{1,0:T(8,128)(2,1)S(1)}, u32[]{:S(2)}, u32[]{:S(2)}) collective-permute-start(bf16[256,512]{1,0:T(8,128)(2,1)S(1)} %join.4.refs_2_), channel_id=1, source_target_pairs={{0,8},{1,9},{2,10},{3,11},{4,12},{5,13},{6,14},{7,15},{8,0},{9,1},... | collective-permute-start | bytes 786440 | tf_op jit(solution)/shard_map/ppermute | solution.py:35
  48.7 0.0 collective-permute-done.17
  48.7 0.1 fusion
  48.8 1.4 %collective-permute-start.18 = (bf16[256,512]{1,0:T(8,128)(2,1)S(1)}, bf16[256,512]{1,0:T(8,128)(2,1)S(1)}, u32[]{:S(2)}, u32[]{:S(2)}) collective-permute-start(bf16[256,512]{1,0:T(8,128)(2,1)S(1)} %fusion), channel_id=1, source_target_pairs={{0,4},{1,5},{2,6},{3,7},{4,0},{5,1},{6,2},{7,3},{8,12},{9,13},{10,... | collective-permute-start | bytes 786440 | tf_op jit(solution)/shard_map/ppermute | solution.py:35
  50.3 0.5 join.5.sum_ref
  50.7 9.7 %collective-permute-done.15.came_ref = bf16[256,512]{1,0:T(8,128)(2,1)S(1)} collective-permute-done((bf16[256,512]{1,0:T(8,128)(2,1)S(1)}, bf16[256,512]{1,0:T(8,128)(2,1)S(1)}, u32[]{:S(2)}, u32[]{:S(2)}) %collective-permute-start.15) | collective-permute-done | bytes 262176 | tf_op jit(solution)/shard_map/ppermute | solution.py:35
  60.5 0.0 collective-permute-done.16
  60.5 1.1 %collective-permute-done.18 = bf16[256,512]{1,0:T(8,128)(2,1)S(1)} collective-permute-done((bf16[256,512]{1,0:T(8,128)(2,1)S(1)}, bf16[256,512]{1,0:T(8,128)(2,1)S(1)}, u32[]{:S(2)}, u32[]{:S(2)}) %collective-permute-start.18) | collective-permute-done | bytes 262176 | tf_op jit(solution)/shard_map/ppermute | solution.py:35
  61.6 0.8 %add_convert_fusion = bf16[256,512]{1,0:T(8,128)(2,1)} fusion(bf16[256,512]{1,0:T(8,128)(2,1)S(1)} %collective-permute-done.18, f32[256,512]{1,0:T(8,128)S(1)} %gather.1, bf16[256,512]{1,0:T(8,128)(2,1)S(1)} %collective-permute-done.16), kind=kLoop, calls=%fused_computation.4 | loop fusion | flops 655360 | bytes 1310720 | tf_op jit(solution)/shard_map/convert_element_type | solution.py:295
  (1 shorter events, 0.0 us)
Async XLA Ops:
  0.0 0.9 %copy-start = (bf16[256,512]{1,0:T(8,128)(2,1)S(1)}, bf16[256,512]{1,0:T(8,128)(2,1)}, u32[]{:S(2)}) copy-start(bf16[256,512]{1,0:T(8,128)(2,1)} %attended_hbm.3) | copy-start | bytes 786436
  1.0 3.3 %copy-start.3 = (bf16[1,8192,64]{1,2,0:T(8,128)(2,1)S(1)}, bf16[1,8192,64]{1,2,0:T(8,128)(2,1)}, u32[]{:S(2)}) copy-start(bf16[1,8192,64]{1,2,0:T(8,128)(2,1)} %param.8) | copy-start | bytes 3145732
  1.0 3.4 %copy-start.4 = (bf16[1,64,8192]{2,1,0:T(8,128)(2,1)S(1)}, bf16[1,64,8192]{2,1,0:T(8,128)(2,1)}, u32[]{:S(2)}) copy-start(bf16[1,64,8192]{2,1,0:T(8,128)(2,1)} %param.9) | copy-start | bytes 3145732
  3.7 10.8 %copy-start.1 = (s32[256]{0:T(256)S(1)}, s32[256]{0:T(256)}, u32[]{:S(2)}) copy-start(s32[256]{0:T(256)} %param.10) | copy-start | bytes 3076
  3.7 10.8 %copy-start.2 = (s32[16]{0:T(128)S(1)}, s32[16]{0:T(128)}, u32[]{:S(2)}) copy-start(s32[16]{0:T(128)} %slot_hbm.1) | copy-start | bytes 196
  3.7 3.6 %collective-permute-start.4 = (bf16[3,256,512]{2,1,0:T(8,128)(2,1)S(1)}, bf16[3,256,512]{2,1,0:T(8,128)(2,1)S(1)}, u32[]{:S(2)}, u32[]{:S(2)}) collective-permute-start(bf16[3,256,512]{2,1,0:T(8,128)(2,1)S(1)} %get-tuple-element.24), channel_id=1, source_target_pairs={{0,1},{1,0},{2,3},{3,2},{4,5},{5,4},{6,7},{7,6},{8,9},{9,8},{10,11... | collective-permute-start | bytes 2359304 | tf_op jit(solution)/shard_map/ppermute | solution.py:35
  4.3 10.3 %collective-permute-start.1 = (bf16[64,8192]{1,0:T(8,128)(2,1)S(1)}, bf16[64,8192]{1,0:T(8,128)(2,1)S(1)}, u32[]{:S(2)}, u32[]{:S(2)}) collective-permute-start(bf16[64,8192]{1,0:T(8,128)(2,1)S(1)} %bitcast.29), channel_id=1, source_target_pairs={{0,1},{1,0},{2,3},{3,2},{4,5},{5,4},{6,7},{7,6},{8,9},{9,8},{10,11... | collective-permute-start | bytes 3145736 | tf_op jit(solution)/shard_map/ppermute | solution.py:35
  4.3 10.2 %collective-permute-start.2 = (bf16[64,8192]{1,0:T(8,128)(2,1)S(1)}, bf16[64,8192]{1,0:T(8,128)(2,1)S(1)}, u32[]{:S(2)}, u32[]{:S(2)}) collective-permute-start(bf16[64,8192]{1,0:T(8,128)(2,1)S(1)} %bitcast.31), channel_id=1, source_target_pairs={{0,1},{1,0},{2,3},{3,2},{4,5},{5,4},{6,7},{7,6},{8,9},{9,8},{10,11... | collective-permute-start | bytes 3145736 | tf_op jit(solution)/shard_map/ppermute | solution.py:35
  4.8 9.8 %collective-permute-start = (bf16[256,512]{1,0:T(8,128)(2,1)S(1)}, bf16[256,512]{1,0:T(8,128)(2,1)S(1)}, u32[]{:S(2)}, u32[]{:S(2)}) collective-permute-start(bf16[256,512]{1,0:T(8,128)(2,1)S(1)} %copy-done), channel_id=1, source_target_pairs={{0,2},{1,3},{2,0},{3,1},{4,6},{5,7},{6,4},{7,5},{8,10},{9,11},{10,... | collective-permute-start | bytes 786440 | tf_op jit(solution)/shard_map/ppermute | solution.py:35
  7.6 12.9 %collective-permute-start.5 = (bf16[256,512]{1,0:T(8,128)(2,1)S(1)}, bf16[256,512]{1,0:T(8,128)(2,1)S(1)}, u32[]{:S(2)}, u32[]{:S(2)}) collective-permute-start(bf16[256,512]{1,0:T(8,128)(2,1)S(1)} %get-tuple-element.36), channel_id=1, source_target_pairs={{0,2},{1,3},{2,0},{3,1},{4,6},{5,7},{6,4},{7,5},{8,10},{9,11},{10,... | collective-permute-start | bytes 786440 | tf_op jit(solution)/shard_map/ppermute | solution.py:35
  9.3 24.0 %collective-permute-start.7 = (bf16[256,512]{1,0:T(8,128)(2,1)S(1)}, bf16[256,512]{1,0:T(8,128)(2,1)S(1)}, u32[]{:S(2)}, u32[]{:S(2)}) collective-permute-start(bf16[256,512]{1,0:T(8,128)(2,1)S(1)} %get-tuple-element.35), channel_id=1, source_target_pairs={{0,2},{1,3},{2,0},{3,1},{4,6},{5,7},{6,4},{7,5},{8,10},{9,11},{10,... | collective-permute-start | bytes 786440 | tf_op jit(solution)/shard_map/ppermute | solution.py:35
  15.8 12.8 %collective-permute-start.8 = (bf16[64,1024]{1,0:T(8,128)(2,1)S(1)}, bf16[64,1024]{1,0:T(8,128)(2,1)S(1)}, u32[]{:S(2)}, u32[]{:S(2)}) collective-permute-start(bf16[64,1024]{1,0:T(8,128)(2,1)S(1)} %get-tuple-element.25), channel_id=1, source_target_pairs={{0,8},{1,9},{2,10},{3,11},{4,12},{5,13},{6,14},{7,15},{8,0},{9,1},... | collective-permute-start | bytes 393224 | tf_op jit(solution)/shard_map/ppermute | solution.py:35
  18.8 9.7 %collective-permute-start.9 = (bf16[64,1024]{1,0:T(8,128)(2,1)S(1)}, bf16[64,1024]{1,0:T(8,128)(2,1)S(1)}, u32[]{:S(2)}, u32[]{:S(2)}) collective-permute-start(bf16[64,1024]{1,0:T(8,128)(2,1)S(1)} %get-tuple-element.26), channel_id=1, source_target_pairs={{0,12},{1,13},{2,14},{3,15},{4,8},{5,9},{6,10},{7,11},{8,4},{9,5},... | collective-permute-start | bytes 393224 | tf_op jit(solution)/shard_map/ppermute | solution.py:35
  20.2 9.8 %collective-permute-start.10 = (bf16[64,1024]{1,0:T(8,128)(2,1)S(1)}, bf16[64,1024]{1,0:T(8,128)(2,1)S(1)}, u32[]{:S(2)}, u32[]{:S(2)}) collective-permute-start(bf16[64,1024]{1,0:T(8,128)(2,1)S(1)} %get-tuple-element.27), channel_id=1, source_target_pairs={{0,4},{1,5},{2,6},{3,7},{4,0},{5,1},{6,2},{7,3},{8,12},{9,13},{10,... | collective-permute-start | bytes 393224 | tf_op jit(solution)/shard_map/ppermute | solution.py:35
  20.5 16.6 %collective-permute-start.6 = (bf16[256,512]{1,0:T(8,128)(2,1)S(1)}, bf16[256,512]{1,0:T(8,128)(2,1)S(1)}, u32[]{:S(2)}, u32[]{:S(2)}) collective-permute-start(bf16[256,512]{1,0:T(8,128)(2,1)S(1)} %fusion.1), channel_id=1, source_target_pairs={{0,4},{1,5},{2,6},{3,7},{4,0},{5,1},{6,2},{7,3},{8,12},{9,13},{10,... | collective-permute-start | bytes 786440 | tf_op jit(solution)/shard_map/ppermute | solution.py:35
  28.5 3.0 %collective-permute-start.3 = (bf16[5,256,512]{2,1,0:T(8,128)(2,1)S(1)}, bf16[5,256,512]{2,1,0:T(8,128)(2,1)S(1)}, u32[]{:S(2)}, u32[]{:S(2)}) collective-permute-start(bf16[5,256,512]{2,1,0:T(8,128)(2,1)S(1)} %get-tuple-element.22), channel_id=1, source_target_pairs={{0,1},{1,0},{2,3},{3,2},{4,5},{5,4},{6,7},{7,6},{8,9},{9,8},{10,11... | collective-permute-start | bytes 3932168 | tf_op jit(solution)/shard_map/ppermute | solution.py:35
  30.4 3.0 %collective-permute-start.11 = (f32[64,64]{1,0:T(8,128)S(1)}, f32[64,64]{1,0:T(8,128)S(1)}, u32[]{:S(2)}, u32[]{:S(2)}) collective-permute-start(f32[64,64]{1,0:T(8,128)S(1)} %shrink.1.mine_ref), channel_id=1, source_target_pairs={{0,1},{1,0},{2,3},{3,2},{4,5},{5,4},{6,7},{7,6},{8,9},{9,8},{10,11... | collective-permute-start | bytes 49160 | tf_op jit(solution)/shard_map/ppermute | solution.py:35
  31.8 17.0 %collective-permute-start.17 = (bf16[256,512]{1,0:T(8,128)(2,1)S(1)}, bf16[256,512]{1,0:T(8,128)(2,1)S(1)}, u32[]{:S(2)}, u32[]{:S(2)}) collective-permute-start(bf16[256,512]{1,0:T(8,128)(2,1)S(1)} %get-tuple-element.34), channel_id=1, source_target_pairs={{0,2},{1,3},{2,0},{3,1},{4,6},{5,7},{6,4},{7,5},{8,10},{9,11},{10,... | collective-permute-start | bytes 786440 | tf_op jit(solution)/shard_map/ppermute | solution.py:35
  33.6 12.9 %collective-permute-start.12 = (bf16[2,64,512]{2,1,0:T(8,128)(2,1)S(1)}, bf16[2,64,512]{2,1,0:T(8,128)(2,1)S(1)}, u32[]{:S(2)}, u32[]{:S(2)}) collective-permute-start(bf16[2,64,512]{2,1,0:T(8,128)(2,1)S(1)} %get-tuple-element.30), channel_id=1, source_target_pairs={{0,2},{1,3},{2,0},{3,1},{4,6},{5,7},{6,4},{7,5},{8,10},{9,11},{10,... | collective-permute-start | bytes 393224 | tf_op jit(solution)/shard_map/ppermute | solution.py:35
  34.2 12.4 %collective-permute-start.13 = (bf16[2,64,512]{2,1,0:T(8,128)(2,1)S(1)}, bf16[2,64,512]{2,1,0:T(8,128)(2,1)S(1)}, u32[]{:S(2)}, u32[]{:S(2)}) collective-permute-start(bf16[2,64,512]{2,1,0:T(8,128)(2,1)S(1)} %get-tuple-element.31), channel_id=1, source_target_pairs={{0,4},{1,5},{2,6},{3,7},{4,0},{5,1},{6,2},{7,3},{8,12},{9,13},{10,... | collective-permute-start | bytes 393224 | tf_op jit(solution)/shard_map/ppermute | solution.py:35
  34.4 12.2 %collective-permute-start.14 = (bf16[2,64,512]{2,1,0:T(8,128)(2,1)S(1)}, bf16[2,64,512]{2,1,0:T(8,128)(2,1)S(1)}, u32[]{:S(2)}, u32[]{:S(2)}) collective-permute-start(bf16[2,64,512]{2,1,0:T(8,128)(2,1)S(1)} %get-tuple-element.32), channel_id=1, source_target_pairs={{0,6},{1,7},{2,4},{3,5},{4,2},{5,3},{6,0},{7,1},{8,14},{9,15},{10,... | collective-permute-start | bytes 393224 | tf_op jit(solution)/shard_map/ppermute | solution.py:35
  37.2 23.3 %collective-permute-start.16 = (bf16[256,512]{1,0:T(8,128)(2,1)S(1)}, bf16[256,512]{1,0:T(8,128)(2,1)S(1)}, u32[]{:S(2)}, u32[]{:S(2)}) collective-permute-start(bf16[256,512]{1,0:T(8,128)(2,1)S(1)} %get-tuple-element.33), channel_id=1, source_target_pairs={{0,2},{1,3},{2,0},{3,1},{4,6},{5,7},{6,4},{7,5},{8,10},{9,11},{10,... | collective-permute-start | bytes 786440 | tf_op jit(solution)/shard_map/ppermute | solution.py:35
  47.1 13.4 %collective-permute-start.15 = (bf16[256,512]{1,0:T(8,128)(2,1)S(1)}, bf16[256,512]{1,0:T(8,128)(2,1)S(1)}, u32[]{:S(2)}, u32[]{:S(2)}) collective-permute-start(bf16[256,512]{1,0:T(8,128)(2,1)S(1)} %join.4.refs_2_), channel_id=1, source_target_pairs={{0,8},{1,9},{2,10},{3,11},{4,12},{5,13},{6,14},{7,15},{8,0},{9,1},... | collective-permute-start | bytes 786440 | tf_op jit(solution)/shard_map/ppermute | solution.py:35
  48.8 12.8 %collective-permute-start.18 = (bf16[256,512]{1,0:T(8,128)(2,1)S(1)}, bf16[256,512]{1,0:T(8,128)(2,1)S(1)}, u32[]{:S(2)}, u32[]{:S(2)}) collective-permute-start(bf16[256,512]{1,0:T(8,128)(2,1)S(1)} %fusion), channel_id=1, source_target_pairs={{0,4},{1,5},{2,6},{3,7},{4,0},{5,1},{6,2},{7,3},{8,12},{9,13},{10,... | collective-permute-start | bytes 786440 | tf_op jit(solution)/shard_map/ppermute | solution.py:35

commit v11 on v8

--- a/solution.py
+++ b/solution.py
@@ -177,7 +177,7 @@
         in_specs=[IN_VMEM] * (2 + len(arrived)) + [ANYWHERE] * len(after),
         out_specs=IN_VMEM,
         compiler_params=params(16),
-        cost_estimate=cost(40*10**9, 4 * down.size),
+        cost_estimate=cost(40 * 10**9, 4 * down.size),
         name="shrink",
     )(down, other, *arrived.values(), *after)
 
@@ -203,7 +203,7 @@
         in_specs=[IN_VMEM] * 4 + [ANYWHERE] * len(after),
         out_specs=[IN_VMEM] * len(groups),
         compiler_params=params(16),
-        cost_estimate=cost(4*CAP*up.size, 4 * up.size),
+        cost_estimate=cost(4 * CAP * up.size, 4 * up.size),
         name="grow",
     )(mine, other, up, up_other, *after)
 
@@ -242,53 +242,65 @@
     )(target, *operands)
 
 
+def gather_kernel(sum_ref, came_ref, out_ref):
+    out_ref[...] = sum_ref[...] + came_ref[...].astype(jnp.float32)
+
+
+def gather(total, came):
+    return pl.pallas_call(
+        gather_kernel,
+        out_shape=shape(total.shape, jnp.float32),
+        in_specs=[IN_VMEM] * 2,
+        out_specs=IN_VMEM,
+        compiler_params=params(16),
+        cost_estimate=cost(total.size, 10 * total.size),
+        name="gather",
+    )(total, came)
+
+
 def staged(attended, out_weight, adapter_down, adapter_up, row_adapter, adapter_slot):
     f32, bf16 = jnp.float32, jnp.bfloat16
     up, down = adapter_up[0], jnp.swapaxes(adapter_down, 1, 2)[0]
     from_y = swap(attended, 2)
     down_other, up_other = swap(down, 1), swap(up, 1)
-    chips = (6, 4, 3, 2, 1, 0)
-    away_first, stay_first, away, stay, token = product(attended, out_weight, ((7, 5), chips), 44)
-    target, outgoing = route(adapter_slot, row_adapter, attended, from_y, token, down_other, up_other)
-    arrived = {k: swap(outgoing[k], 4 * k) for k in (2,3,1)}
+    firsts, chips = (7, 6, 5), (4, 3, 2, 1, 0)
+    away_first, stay_first, away, stay, token = product(attended, out_weight, (firsts, chips), 44)
+    (away_first,) = once((away_first,), from_y, down_other, up_other)
+    came_first = swap(away_first, 1)
+    first = [stay_first[i] + came_first[i].astype(f32) for i in range(3)]
+    target, outgoing = route(adapter_slot, row_adapter, attended, from_y, token)
+    arrived = {k: swap(outgoing[k], 4 * k) for k in (1, 2, 3)}
     arrived[0] = outgoing[0]
-    away_first, away = once((away_first, away), target)
-    came_first, came = swap(away_first, 1), swap(away, 1)
-
-    def base(m):
-        return stay[chips.index(m)] + came[chips.index(m)].astype(f32)
-
-    y3 = swap((stay_first[0] + came_first[0].astype(f32)).astype(bf16), 2)
-    y2 = swap((stay_first[1] + came_first[1].astype(f32)).astype(bf16), 2)[None]
+    (go3,) = once((first[0].astype(bf16),), target)
+    y3 = swap(go3, 2)
+    (go2,) = once((first[2].astype(bf16),), arrived[1])
+    y2 = swap(go2, 2)[None]
+    z3 = swap((first[1] + y3.astype(f32)).astype(bf16), 4)[None]
+    (away,) = once((away,), target)
+    came = swap(away, 1)
     mine = shrink(down, down_other, arrived)
-    ready3, go1 = once((y3, base(3).astype(bf16)), mine)
-    z3 = swap((base(6) + ready3.astype(f32)).astype(bf16), 4)[None]
-    y1 = swap(go1, 2)[None]
-    here_chips = (4, 2, 1, 0)
-    groups = (tuple(2 * m for m in here_chips), (10, 6), (12,), (14,))
-    here, over2, over4, over6 = grow(mine, swap(mine, 1), up, up_other, groups, y3, y2)
+    groups = ((8, 6, 4, 2, 0), (10,), (12,), (14,))
+    here, over2, over4, over6 = grow(mine, swap(mine, 1), up, up_other, groups, y3, came)
     over2, over4, over6 = swap(over2, 2), swap(over4, 4), swap(over6, 6)
+    (ready2,) = join(target, [stay, came, z3, y2], ((((0, 0), (1, 0), (2, 0), (3, 0)), ()),), f32)
+    grown = [here, over2, over4, over6]
+    (sum2,) = join(
+        target, [ready2[None]] + grown, ((((0, 0),), tuple((1 + i, 0, 2 * i) for i in range(4))),), bf16
+    )
+    z2 = swap(sum2, 8)
 
     def blocks(m):
-        return ((0, chips.index(m)), (1, chips.index(m))), ((2, here_chips.index(m), 0),)
-
-    sums, grown = blocks(4)
-    (sum2,) = join(
-        target,
-        [stay, came, here, over2, over4, over6, z3, y2],
-        ((sums + ((6, 0), (7, 0)), grown + ((3, 0, 2), (4, 0, 4), (5, 0, 6))),),
-        bf16,
-    )
-    z2 = swap(sum2, 8)
-    sums, grown = blocks(2)
-    (sum1,) = join(
-        target, [stay, came, here, over2, y1, sum2], ((sums + ((4, 0),), grown + ((3, 1, 2),)),), bf16
-    )
-    z1 = swap(sum1, 4)
+        return ((0, chips.index(m)), (1, chips.index(m))), ((2, chips.index(m), 0),)
+
+    (go1,) = join(target, [stay, came, here, sum2], (blocks(3),), bf16)
+    y1 = swap(go1, 2)
     (go0,) = join(target, [stay, came, here, sum2], (blocks(1),), bf16)
     y0 = swap(go0, 2)
+    sums, grown = blocks(2)
+    (sum1,) = join(target, [stay, came, here, y1[None], sum2], ((sums + ((3, 0),), grown),), bf16)
+    z1 = swap(sum1, 4)
     (side0,) = join(target, [stay, came, here], (blocks(0),), f32)
-    total = side0 + y0.astype(f32) + z2.astype(f32) + z1.astype(f32)
+    total = gather(side0, z2) + y0.astype(f32) + z1.astype(f32)
     return total.astype(bf16)
 
 

time: 60.7 us -> 59.6 us (0.982)
  starting transfers between devices: 22.8 us -> 21.8 us
  waiting for transfers between devices: 27 us -> 26.3 us
    ppermute x19, starting transfers between devices: 22.8 us -> 21.8 us  [swap(): return lax.ppermute(value, 'tensor', [(t, t ^ mask) for t in range(count)])]
    ppermute x19, waiting for transfers between devices: 27 us -> 26.3 us  [swap(): return lax.ppermute(value, 'tensor', [(t, t ^ mask) for t in range(count)])]
    pallas_call x4 -> x6, Pallas kernels: 1.31 us -> 1.64 us  [join(): pl.pallas_call(functools.partial(join_kernel, terms), out_shape=[shape((r...]
  transfers between devices with their start and end apart: 19 -> 19, of which waited for: 9 -> 11; matrix products, arithmetic and copies ran while one was open for 0% -> 0% of each run, Pallas kernels for 11% -> 13%
where the time goes in v11:
time: 59.6 us; the launch traced here: 59.4 us
  waiting for transfers between devices  26.3 us (44%)
  starting transfers between devices  21.8 us (37%)
  Pallas kernels  8.44 us (14%)
  local copies, waits for them, and re-layouts  1.57 us (3%)
  other arithmetic  1.08 us (2%)
    ppermute x19, waiting for transfers between devices, swap(): return lax.ppermute(value, 'tensor', [(t, t ^ mask) for t in range(count)])  26.3 us
    ppermute x19, starting transfers between devices, swap(): return lax.ppermute(value, 'tensor', [(t, t ^ mask) for t in range(count)])  21.8 us
    pallas_call x1, Pallas kernels, product(): pl.pallas_call(functools.partial(product_kernel, groups), out_shape=out_s...  4.85 us
    pallas_call x6, Pallas kernels, join(): pl.pallas_call(functools.partial(join_kernel, terms), out_shape=[shape((r...  1.64 us
    unnamed x10, local copies, waits for them, and re-layouts  1.57 us
    pallas_call x1, Pallas kernels, route(): pl.pallas_call(functools.partial(route_kernel, count, layers), out_shape=...  1.2 us
  transfers between devices with their start and end apart: 19, of which 11 were waited for; matrix products, arithmetic and copies ran while one was open for 0% of the time, Pallas kernels for 13%

profile of v11, /device:TPU:0, one launch (start us, length us, event | category | flops | bytes accessed | tf_op | source)
XLA Modules:
  0.0 59.4 jit_solution(6412211688370895529)
XLA Ops:
  0.0 0.5 collective-permute-start.2
  0.5 0.1 collective-permute-start.7
  0.5 3.0 %collective-permute-start = (bf16[256,512]{1,0:T(8,128)(2,1)}, bf16[256,512]{1,0:T(8,128)(2,1)S(1)}, u32[]{:S(2)}, u32[]{:S(2)}) collective-permute-start(bf16[256,512]{1,0:T(8,128)(2,1)} %own_ref.1), channel_id=1, source_target_pairs={{0,2},{1,3},{2,0},{3,1},{4,6},{5,7},{6,4},{7,5},{8,10},{9,11},{10,... | collective-permute-start | bytes 786440 | tf_op jit(solution)/shard_map/ppermute | solution.py:35
  3.5 0.0 copy-start.1
  3.5 1.0 %copy-done.1 = bf16[256,512]{1,0:T(8,128)(2,1)S(1)} copy-done((bf16[256,512]{1,0:T(8,128)(2,1)S(1)}, bf16[256,512]{1,0:T(8,128)(2,1)}, u32[]{:S(2)}) %copy-start.1) | copy-done | bytes 262168
  4.5 4.9 %product.1 = (bf16[3,256,512]{2,1,0:T(8,128)(2,1)S(1)}, f32[3,256,512]{2,1,0:T(8,128)S(1)}, bf16[5,256,512]{2,1,0:T(8,128)(2,1)S(1)}, f32[5,256,512]{2,1,0:T(8,128)S(1)}, f32[8,128]{1,0:T(8,128)S(1)}) custom-call(bf16[256,512]{1,0:T(8,128)(2,1)S(1)} %copy-done.1, bf16[512,8192]{1,0:T(8,128)(2,1)} %weight_hbm.1), custom_call_target="tpu_custom_call" | custom-call | flops 2147483648 | bytes 14680064 | tf_op jit(solution)/shard_map/product/pallas_call | solution.py:138
  9.3 0.8 %collective-permute-done.y_ref.refs_1_ = bf16[256,512]{1,0:T(8,128)(2,1)S(1)} collective-permute-done((bf16[256,512]{1,0:T(8,128)(2,1)}, bf16[256,512]{1,0:T(8,128)(2,1)S(1)}, u32[]{:S(2)}, u32[]{:S(2)}) %collective-permute-start) | collective-permute-done | bytes 262176 | tf_op jit(solution)/shard_map/ppermute | solution.py:35
  10.2 0.0 collective-permute-done.2.other_ref.refs_2_
  10.2 0.0 collective-permute-done.7.refs_3_.up_other_ref
  10.2 0.0 copy-start.2
  10.2 0.0 copy-start.3
  10.2 0.1 collective-permute-start.8
  10.3 0.6 copy-done.2
  10.8 0.0 copy-done.3
  10.9 1.2 %route.1 = (s32[1,256]{1,0:T(1,128)S(1)}, bf16[64,1024]{1,0:T(8,128)(2,1)S(1)}, bf16[64,1024]{1,0:T(8,128)(2,1)S(1)}, bf16[64,1024]{1,0:T(8,128)(2,1)S(1)}, bf16[64,1024]{1,0:T(8,128)(2,1)S(1)}) custom-call(s32[16]{0:T(128)S(1)} %copy-done.3, s32[1,256]{1,0:T(1,128)S(1)} %bitcast.23, bf16[256,512]{1,0:T(8,128)(2,1)S(1)} %copy-done.1, ...), custom_call_target="tpu_custom_call" | custom-call | flops 134217728 | bytes 1048576 | tf_op jit(solution)/shard_map/route/pallas_call | solution.py:88
  12.1 0.5 collective-permute-done.8
  12.5 0.2 fusion.2
  12.7 1.8 %collective-permute-start.9 = (bf16[256,512]{1,0:T(8,128)(2,1)S(1)}, bf16[256,512]{1,0:T(8,128)(2,1)S(1)}, u32[]{:S(2)}, u32[]{:S(2)}) collective-permute-start(bf16[256,512]{1,0:T(8,128)(2,1)S(1)} %once.6), channel_id=1, source_target_pairs={{0,2},{1,3},{2,0},{3,1},{4,6},{5,7},{6,4},{7,5},{8,10},{9,11},{10,... | collective-permute-start | bytes 786440 | tf_op jit(solution)/shard_map/ppermute | solution.py:35
  14.5 1.6 %collective-permute-start.3 = (bf16[64,1024]{1,0:T(8,128)(2,1)S(1)}, bf16[64,1024]{1,0:T(8,128)(2,1)S(1)}, u32[]{:S(2)}, u32[]{:S(2)}) collective-permute-start(bf16[64,1024]{1,0:T(8,128)(2,1)S(1)} %get-tuple-element.23), channel_id=1, source_target_pairs={{0,4},{1,5},{2,6},{3,7},{4,0},{5,1},{6,2},{7,3},{8,12},{9,13},{10,... | collective-permute-start | bytes 393224 | tf_op jit(solution)/shard_map/ppermute | solution.py:35
  16.1 0.0 copy-start.4
  16.1 0.0 collective-permute-start.1
  16.1 2.6 %collective-permute-start.4 = (bf16[64,1024]{1,0:T(8,128)(2,1)S(1)}, bf16[64,1024]{1,0:T(8,128)(2,1)S(1)}, u32[]{:S(2)}, u32[]{:S(2)}) collective-permute-start(bf16[64,1024]{1,0:T(8,128)(2,1)S(1)} %get-tuple-element.24), channel_id=1, source_target_pairs={{0,8},{1,9},{2,10},{3,11},{4,12},{5,13},{6,14},{7,15},{8,0},{9,1},... | collective-permute-start | bytes 393224 | tf_op jit(solution)/shard_map/ppermute | solution.py:35
  18.7 0.2 collective-permute-start.5
  18.9 0.9 %collective-permute-done.3.refs_0_.refs_1_ = bf16[64,1024]{1,0:T(8,128)(2,1)S(1)} collective-permute-done((bf16[64,1024]{1,0:T(8,128)(2,1)S(1)}, bf16[64,1024]{1,0:T(8,128)(2,1)S(1)}, u32[]{:S(2)}, u32[]{:S(2)}) %collective-permute-start.3) | collective-permute-done | bytes 131104 | tf_op jit(solution)/shard_map/ppermute | solution.py:35
  19.8 0.4 collective-permute-start.11
  20.1 1.0 %collective-permute-done.9.refs_0_ = bf16[256,512]{1,0:T(8,128)(2,1)S(1)} collective-permute-done((bf16[256,512]{1,0:T(8,128)(2,1)S(1)}, bf16[256,512]{1,0:T(8,128)(2,1)S(1)}, u32[]{:S(2)}, u32[]{:S(2)}) %collective-permute-start.9) | collective-permute-done | bytes 262176 | tf_op jit(solution)/shard_map/ppermute | solution.py:35
  21.2 0.1 fusion
  21.3 1.8 %collective-permute-start.10 = (bf16[256,512]{1,0:T(8,128)(2,1)S(1)}, bf16[256,512]{1,0:T(8,128)(2,1)S(1)}, u32[]{:S(2)}, u32[]{:S(2)}) collective-permute-start(bf16[256,512]{1,0:T(8,128)(2,1)S(1)} %fusion), channel_id=1, source_target_pairs={{0,4},{1,5},{2,6},{3,7},{4,0},{5,1},{6,2},{7,3},{8,12},{9,13},{10,... | collective-permute-start | bytes 786440 | tf_op jit(solution)/shard_map/ppermute | solution.py:35
  23.1 5.9 %collective-permute-done.4.refs_1_ = bf16[64,1024]{1,0:T(8,128)(2,1)S(1)} collective-permute-done((bf16[64,1024]{1,0:T(8,128)(2,1)S(1)}, bf16[64,1024]{1,0:T(8,128)(2,1)S(1)}, u32[]{:S(2)}, u32[]{:S(2)}) %collective-permute-start.4) | collective-permute-done | bytes 131104 | tf_op jit(solution)/shard_map/ppermute | solution.py:35
  29.0 0.0 collective-permute-done.5.refs_2_
  29.0 0.0 copy-done.4
  29.0 0.0 copy-start
  29.0 0.4 shrink.1.mine_ref
  29.4 0.0 collective-permute-start.6
  29.4 1.2 %collective-permute-done.6.other_ref = f32[64,64]{1,0:T(8,128)S(1)} collective-permute-done((f32[64,64]{1,0:T(8,128)S(1)}, f32[64,64]{1,0:T(8,128)S(1)}, u32[]{:S(2)}, u32[]{:S(2)}) %collective-permute-start.6) | collective-permute-done | bytes 16416 | tf_op jit(solution)/shard_map/ppermute | solution.py:35
  30.6 0.0 collective-permute-done.1.refs_1_
  30.6 0.0 copy-done
  30.6 0.3 grow.1
  30.9 0.6 collective-permute-start.12
  31.5 3.0 %collective-permute-start.13 = (bf16[1,64,512]{2,1,0:T(8,128)(2,1)S(1)}, bf16[1,64,512]{2,1,0:T(8,128)(2,1)S(1)}, u32[]{:S(2)}, u32[]{:S(2)}) collective-permute-start(bf16[1,64,512]{2,1,0:T(8,128)(2,1)S(1)} %get-tuple-element.31), channel_id=1, source_target_pairs={{0,4},{1,5},{2,6},{3,7},{4,0},{5,1},{6,2},{7,3},{8,12},{9,13},{10,... | collective-permute-start | bytes 196616 | tf_op jit(solution)/shard_map/ppermute | solution.py:35
  34.5 1.0 %collective-permute-start.14 = (bf16[1,64,512]{2,1,0:T(8,128)(2,1)S(1)}, bf16[1,64,512]{2,1,0:T(8,128)(2,1)S(1)}, u32[]{:S(2)}, u32[]{:S(2)}) collective-permute-start(bf16[1,64,512]{2,1,0:T(8,128)(2,1)S(1)} %get-tuple-element.32), channel_id=1, source_target_pairs={{0,6},{1,7},{2,4},{3,5},{4,2},{5,3},{6,0},{7,1},{8,14},{9,15},{10,... | collective-permute-start | bytes 196616 | tf_op jit(solution)/shard_map/ppermute | solution.py:35
  35.4 0.0 collective-permute-done.11
  35.4 0.0 collective-permute-done.10
  35.4 0.1 join.7
  35.6 0.0 collective-permute-done.12.refs_2_
  35.6 1.2 %collective-permute-done.13.refs_3_ = bf16[1,64,512]{2,1,0:T(8,128)(2,1)S(1)} collective-permute-done((bf16[1,64,512]{2,1,0:T(8,128)(2,1)S(1)}, bf16[1,64,512]{2,1,0:T(8,128)(2,1)S(1)}, u32[]{:S(2)}, u32[]{:S(2)}) %collective-permute-start.13) | collective-permute-done | bytes 65568 | tf_op jit(solution)/shard_map/ppermute | solution.py:35
  36.8 2.8 %collective-permute-done.14.refs_4_ = bf16[1,64,512]{2,1,0:T(8,128)(2,1)S(1)} collective-permute-done((bf16[1,64,512]{2,1,0:T(8,128)(2,1)S(1)}, bf16[1,64,512]{2,1,0:T(8,128)(2,1)S(1)}, u32[]{:S(2)}, u32[]{:S(2)}) %collective-permute-start.14) | collective-permute-done | bytes 65568 | tf_op jit(solution)/shard_map/ppermute | solution.py:35
  39.6 0.5 join.8.refs_3_.refs_4_
  40.1 0.3 join.10
  40.4 1.6 %collective-permute-start.17 = (bf16[256,512]{1,0:T(8,128)(2,1)S(1)}, bf16[256,512]{1,0:T(8,128)(2,1)S(1)}, u32[]{:S(2)}, u32[]{:S(2)}) collective-permute-start(bf16[256,512]{1,0:T(8,128)(2,1)S(1)} %join.10), channel_id=1, source_target_pairs={{0,2},{1,3},{2,0},{3,1},{4,6},{5,7},{6,4},{7,5},{8,10},{9,11},{10,... | collective-permute-start | bytes 786440 | tf_op jit(solution)/shard_map/ppermute | solution.py:35
  42.0 1.4 %collective-permute-start.15 = (bf16[256,512]{1,0:T(8,128)(2,1)S(1)}, bf16[256,512]{1,0:T(8,128)(2,1)S(1)}, u32[]{:S(2)}, u32[]{:S(2)}) collective-permute-start(bf16[256,512]{1,0:T(8,128)(2,1)S(1)} %join.8.refs_3_.refs_4_), channel_id=1, source_target_pairs={{0,8},{1,9},{2,10},{3,11},{4,12},{5,13},{6,14},{7,15},{8,0},{9,1},... | collective-permute-start | bytes 786440 | tf_op jit(solution)/shard_map/ppermute | solution.py:35
  43.3 0.3 join.9
  43.6 1.3 %collective-permute-start.16 = (bf16[256,512]{1,0:T(8,128)(2,1)S(1)}, bf16[256,512]{1,0:T(8,128)(2,1)S(1)}, u32[]{:S(2)}, u32[]{:S(2)}) collective-permute-start(bf16[256,512]{1,0:T(8,128)(2,1)S(1)} %join.9), channel_id=1, source_target_pairs={{0,2},{1,3},{2,0},{3,1},{4,6},{5,7},{6,4},{7,5},{8,10},{9,11},{10,... | collective-permute-start | bytes 786440 | tf_op jit(solution)/shard_map/ppermute | solution.py:35
  44.9 4.8 %collective-permute-done.17 = bf16[256,512]{1,0:T(8,128)(2,1)S(1)} collective-permute-done((bf16[256,512]{1,0:T(8,128)(2,1)S(1)}, bf16[256,512]{1,0:T(8,128)(2,1)S(1)}, u32[]{:S(2)}, u32[]{:S(2)}) %collective-permute-start.17) | collective-permute-done | bytes 262176 | tf_op jit(solution)/shard_map/ppermute | solution.py:35
  49.7 0.3 join.11
  50.0 1.1 %collective-permute-start.18 = (bf16[256,512]{1,0:T(8,128)(2,1)S(1)}, bf16[256,512]{1,0:T(8,128)(2,1)S(1)}, u32[]{:S(2)}, u32[]{:S(2)}) collective-permute-start(bf16[256,512]{1,0:T(8,128)(2,1)S(1)} %join.11), channel_id=1, source_target_pairs={{0,4},{1,5},{2,6},{3,7},{4,0},{5,1},{6,2},{7,3},{8,12},{9,13},{10,... | collective-permute-start | bytes 786440 | tf_op jit(solution)/shard_map/ppermute | solution.py:35
  51.1 0.3 join.6.sum_ref
  51.4 3.6 %collective-permute-done.15.came_ref = bf16[256,512]{1,0:T(8,128)(2,1)S(1)} collective-permute-done((bf16[256,512]{1,0:T(8,128)(2,1)S(1)}, bf16[256,512]{1,0:T(8,128)(2,1)S(1)}, u32[]{:S(2)}, u32[]{:S(2)}) %collective-permute-start.15) | collective-permute-done | bytes 262176 | tf_op jit(solution)/shard_map/ppermute | solution.py:35
  55.0 0.0 collective-permute-done.16
  55.0 3.6 %collective-permute-done.18 = bf16[256,512]{1,0:T(8,128)(2,1)S(1)} collective-permute-done((bf16[256,512]{1,0:T(8,128)(2,1)S(1)}, bf16[256,512]{1,0:T(8,128)(2,1)S(1)}, u32[]{:S(2)}, u32[]{:S(2)}) %collective-permute-start.18) | collective-permute-done | bytes 262176 | tf_op jit(solution)/shard_map/ppermute | solution.py:35
  58.6 0.8 %add_convert_fusion = bf16[256,512]{1,0:T(8,128)(2,1)} fusion(bf16[256,512]{1,0:T(8,128)(2,1)S(1)} %collective-permute-done.18, f32[256,512]{1,0:T(8,128)S(1)} %gather.1, bf16[256,512]{1,0:T(8,128)(2,1)S(1)} %collective-permute-done.16), kind=kLoop, calls=%fused_computation.2 | loop fusion | flops 655360 | bytes 1310720 | tf_op jit(solution)/shard_map/convert_element_type | solution.py:304
  (5 shorter events, 0.1 us)
Async XLA Ops:
  0.0 10.2 %collective-permute-start.2 = (bf16[64,8192]{1,0:T(8,128)(2,1)}, bf16[64,8192]{1,0:T(8,128)(2,1)S(1)}, u32[]{:S(2)}, u32[]{:S(2)}) collective-permute-start(bf16[64,8192]{1,0:T(8,128)(2,1)} %bitcast.24), channel_id=1, source_target_pairs={{0,1},{1,0},{2,3},{3,2},{4,5},{5,4},{6,7},{7,6},{8,9},{9,8},{10,11... | collective-permute-start | bytes 3145736 | tf_op jit(solution)/shard_map/ppermute | solution.py:35
  0.5 9.7 %collective-permute-start.7 = (bf16[64,8192]{1,0:T(8,128)(2,1)}, bf16[64,8192]{1,0:T(8,128)(2,1)S(1)}, u32[]{:S(2)}, u32[]{:S(2)}) collective-permute-start(bf16[64,8192]{1,0:T(8,128)(2,1)} %bitcast.18), channel_id=1, source_target_pairs={{0,1},{1,0},{2,3},{3,2},{4,5},{5,4},{6,7},{7,6},{8,9},{9,8},{10,11... | collective-permute-start | bytes 3145736 | tf_op jit(solution)/shard_map/ppermute | solution.py:35
  0.5 9.6 %collective-permute-start = (bf16[256,512]{1,0:T(8,128)(2,1)}, bf16[256,512]{1,0:T(8,128)(2,1)S(1)}, u32[]{:S(2)}, u32[]{:S(2)}) collective-permute-start(bf16[256,512]{1,0:T(8,128)(2,1)} %own_ref.1), channel_id=1, source_target_pairs={{0,2},{1,3},{2,0},{3,1},{4,6},{5,7},{6,4},{7,5},{8,10},{9,11},{10,... | collective-permute-start | bytes 786440 | tf_op jit(solution)/shard_map/ppermute | solution.py:35
  3.5 1.0 %copy-start.1 = (bf16[256,512]{1,0:T(8,128)(2,1)S(1)}, bf16[256,512]{1,0:T(8,128)(2,1)}, u32[]{:S(2)}) copy-start(bf16[256,512]{1,0:T(8,128)(2,1)} %own_ref.1) | copy-start | bytes 786436
  10.2 0.7 %copy-start.2 = (s32[256]{0:T(256)S(1)}, s32[256]{0:T(256)}, u32[]{:S(2)}) copy-start(s32[256]{0:T(256)} %param.10) | copy-start | bytes 3076
  10.2 0.7 %copy-start.3 = (s32[16]{0:T(128)S(1)}, s32[16]{0:T(128)}, u32[]{:S(2)}) copy-start(s32[16]{0:T(128)} %slot_hbm.1) | copy-start | bytes 196
  10.2 2.4 %collective-permute-start.8 = (bf16[3,256,512]{2,1,0:T(8,128)(2,1)S(1)}, bf16[3,256,512]{2,1,0:T(8,128)(2,1)S(1)}, u32[]{:S(2)}, u32[]{:S(2)}) collective-permute-start(bf16[3,256,512]{2,1,0:T(8,128)(2,1)S(1)} %once.5), channel_id=1, source_target_pairs={{0,1},{1,0},{2,3},{3,2},{4,5},{5,4},{6,7},{7,6},{8,9},{9,8},{10,11... | collective-permute-start | bytes 2359304 | tf_op jit(solution)/shard_map/ppermute | solution.py:35
  12.7 8.5 %collective-permute-start.9 = (bf16[256,512]{1,0:T(8,128)(2,1)S(1)}, bf16[256,512]{1,0:T(8,128)(2,1)S(1)}, u32[]{:S(2)}, u32[]{:S(2)}) collective-permute-start(bf16[256,512]{1,0:T(8,128)(2,1)S(1)} %once.6), channel_id=1, source_target_pairs={{0,2},{1,3},{2,0},{3,1},{4,6},{5,7},{6,4},{7,5},{8,10},{9,11},{10,... | collective-permute-start | bytes 786440 | tf_op jit(solution)/shard_map/ppermute | solution.py:35
  14.5 5.3 %collective-permute-start.3 = (bf16[64,1024]{1,0:T(8,128)(2,1)S(1)}, bf16[64,1024]{1,0:T(8,128)(2,1)S(1)}, u32[]{:S(2)}, u32[]{:S(2)}) collective-permute-start(bf16[64,1024]{1,0:T(8,128)(2,1)S(1)} %get-tuple-element.23), channel_id=1, source_target_pairs={{0,4},{1,5},{2,6},{3,7},{4,0},{5,1},{6,2},{7,3},{8,12},{9,13},{10,... | collective-permute-start | bytes 393224 | tf_op jit(solution)/shard_map/ppermute | solution.py:35
  16.1 12.9 %copy-start.4 = (bf16[1,8192,64]{1,2,0:T(8,128)(2,1)S(1)}, bf16[1,8192,64]{1,2,0:T(8,128)(2,1)}, u32[]{:S(2)}) copy-start(bf16[1,8192,64]{1,2,0:T(8,128)(2,1)} %param.8) | copy-start | bytes 3145732
  16.1 14.5 %collective-permute-start.1 = (bf16[5,256,512]{2,1,0:T(8,128)(2,1)S(1)}, bf16[5,256,512]{2,1,0:T(8,128)(2,1)S(1)}, u32[]{:S(2)}, u32[]{:S(2)}) collective-permute-start(bf16[5,256,512]{2,1,0:T(8,128)(2,1)S(1)} %once.4), channel_id=1, source_target_pairs={{0,1},{1,0},{2,3},{3,2},{4,5},{5,4},{6,7},{7,6},{8,9},{9,8},{10,11... | collective-permute-start | bytes 3932168 | tf_op jit(solution)/shard_map/ppermute | solution.py:35
  16.1 12.9 %collective-permute-start.4 = (bf16[64,1024]{1,0:T(8,128)(2,1)S(1)}, bf16[64,1024]{1,0:T(8,128)(2,1)S(1)}, u32[]{:S(2)}, u32[]{:S(2)}) collective-permute-start(bf16[64,1024]{1,0:T(8,128)(2,1)S(1)} %get-tuple-element.24), channel_id=1, source_target_pairs={{0,8},{1,9},{2,10},{3,11},{4,12},{5,13},{6,14},{7,15},{8,0},{9,1},... | collective-permute-start | bytes 393224 | tf_op jit(solution)/shard_map/ppermute | solution.py:35
  18.7 10.3 %collective-permute-start.5 = (bf16[64,1024]{1,0:T(8,128)(2,1)S(1)}, bf16[64,1024]{1,0:T(8,128)(2,1)S(1)}, u32[]{:S(2)}, u32[]{:S(2)}) collective-permute-start(bf16[64,1024]{1,0:T(8,128)(2,1)S(1)} %get-tuple-element.25), channel_id=1, source_target_pairs={{0,12},{1,13},{2,14},{3,15},{4,8},{5,9},{6,10},{7,11},{8,4},{9,5},... | collective-permute-start | bytes 393224 | tf_op jit(solution)/shard_map/ppermute | solution.py:35
  19.8 15.6 %collective-permute-start.11 = (bf16[256,512]{1,0:T(8,128)(2,1)S(1)}, bf16[256,512]{1,0:T(8,128)(2,1)S(1)}, u32[]{:S(2)}, u32[]{:S(2)}) collective-permute-start(bf16[256,512]{1,0:T(8,128)(2,1)S(1)} %once.7), channel_id=1, source_target_pairs={{0,2},{1,3},{2,0},{3,1},{4,6},{5,7},{6,4},{7,5},{8,10},{9,11},{10,... | collective-permute-start | bytes 786440 | tf_op jit(solution)/shard_map/ppermute | solution.py:35
  21.3 14.1 %collective-permute-start.10 = (bf16[256,512]{1,0:T(8,128)(2,1)S(1)}, bf16[256,512]{1,0:T(8,128)(2,1)S(1)}, u32[]{:S(2)}, u32[]{:S(2)}) collective-permute-start(bf16[256,512]{1,0:T(8,128)(2,1)S(1)} %fusion), channel_id=1, source_target_pairs={{0,4},{1,5},{2,6},{3,7},{4,0},{5,1},{6,2},{7,3},{8,12},{9,13},{10,... | collective-permute-start | bytes 786440 | tf_op jit(solution)/shard_map/ppermute | solution.py:35
  29.0 1.6 %copy-start = (bf16[1,64,8192]{2,1,0:T(8,128)(2,1)S(1)}, bf16[1,64,8192]{2,1,0:T(8,128)(2,1)}, u32[]{:S(2)}) copy-start(bf16[1,64,8192]{2,1,0:T(8,128)(2,1)} %param.9) | copy-start | bytes 3145732
  29.4 1.2 %collective-permute-start.6 = (f32[64,64]{1,0:T(8,128)S(1)}, f32[64,64]{1,0:T(8,128)S(1)}, u32[]{:S(2)}, u32[]{:S(2)}) collective-permute-start(f32[64,64]{1,0:T(8,128)S(1)} %shrink.1.mine_ref), channel_id=1, source_target_pairs={{0,1},{1,0},{2,3},{3,2},{4,5},{5,4},{6,7},{7,6},{8,9},{9,8},{10,11... | collective-permute-start | bytes 49160 | tf_op jit(solution)/shard_map/ppermute | solution.py:35
  30.9 4.7 %collective-permute-start.12 = (bf16[1,64,512]{2,1,0:T(8,128)(2,1)S(1)}, bf16[1,64,512]{2,1,0:T(8,128)(2,1)S(1)}, u32[]{:S(2)}, u32[]{:S(2)}) collective-permute-start(bf16[1,64,512]{2,1,0:T(8,128)(2,1)S(1)} %get-tuple-element.30), channel_id=1, source_target_pairs={{0,2},{1,3},{2,0},{3,1},{4,6},{5,7},{6,4},{7,5},{8,10},{9,11},{10,... | collective-permute-start | bytes 196616 | tf_op jit(solution)/shard_map/ppermute | solution.py:35
  31.5 5.3 %collective-permute-start.13 = (bf16[1,64,512]{2,1,0:T(8,128)(2,1)S(1)}, bf16[1,64,512]{2,1,0:T(8,128)(2,1)S(1)}, u32[]{:S(2)}, u32[]{:S(2)}) collective-permute-start(bf16[1,64,512]{2,1,0:T(8,128)(2,1)S(1)} %get-tuple-element.31), channel_id=1, source_target_pairs={{0,4},{1,5},{2,6},{3,7},{4,0},{5,1},{6,2},{7,3},{8,12},{9,13},{10,... | collective-permute-start | bytes 196616 | tf_op jit(solution)/shard_map/ppermute | solution.py:35
  34.5 5.2 %collective-permute-start.14 = (bf16[1,64,512]{2,1,0:T(8,128)(2,1)S(1)}, bf16[1,64,512]{2,1,0:T(8,128)(2,1)S(1)}, u32[]{:S(2)}, u32[]{:S(2)}) collective-permute-start(bf16[1,64,512]{2,1,0:T(8,128)(2,1)S(1)} %get-tuple-element.32), channel_id=1, source_target_pairs={{0,6},{1,7},{2,4},{3,5},{4,2},{5,3},{6,0},{7,1},{8,14},{9,15},{10,... | collective-permute-start | bytes 196616 | tf_op jit(solution)/shard_map/ppermute | solution.py:35
  40.4 9.3 %collective-permute-start.17 = (bf16[256,512]{1,0:T(8,128)(2,1)S(1)}, bf16[256,512]{1,0:T(8,128)(2,1)S(1)}, u32[]{:S(2)}, u32[]{:S(2)}) collective-permute-start(bf16[256,512]{1,0:T(8,128)(2,1)S(1)} %join.10), channel_id=1, source_target_pairs={{0,2},{1,3},{2,0},{3,1},{4,6},{5,7},{6,4},{7,5},{8,10},{9,11},{10,... | collective-permute-start | bytes 786440 | tf_op jit(solution)/shard_map/ppermute | solution.py:35
  42.0 13.0 %collective-permute-start.15 = (bf16[256,512]{1,0:T(8,128)(2,1)S(1)}, bf16[256,512]{1,0:T(8,128)(2,1)S(1)}, u32[]{:S(2)}, u32[]{:S(2)}) collective-permute-start(bf16[256,512]{1,0:T(8,128)(2,1)S(1)} %join.8.refs_3_.refs_4_), channel_id=1, source_target_pairs={{0,8},{1,9},{2,10},{3,11},{4,12},{5,13},{6,14},{7,15},{8,0},{9,1},... | collective-permute-start | bytes 786440 | tf_op jit(solution)/shard_map/ppermute | solution.py:35
  43.6 11.4 %collective-permute-start.16 = (bf16[256,512]{1,0:T(8,128)(2,1)S(1)}, bf16[256,512]{1,0:T(8,128)(2,1)S(1)}, u32[]{:S(2)}, u32[]{:S(2)}) collective-permute-start(bf16[256,512]{1,0:T(8,128)(2,1)S(1)} %join.9), channel_id=1, source_target_pairs={{0,2},{1,3},{2,0},{3,1},{4,6},{5,7},{6,4},{7,5},{8,10},{9,11},{10,... | collective-permute-start | bytes 786440 | tf_op jit(solution)/shard_map/ppermute | solution.py:35
  50.0 8.7 %collective-permute-start.18 = (bf16[256,512]{1,0:T(8,128)(2,1)S(1)}, bf16[256,512]{1,0:T(8,128)(2,1)S(1)}, u32[]{:S(2)}, u32[]{:S(2)}) collective-permute-start(bf16[256,512]{1,0:T(8,128)(2,1)S(1)} %join.11), channel_id=1, source_target_pairs={{0,4},{1,5},{2,6},{3,7},{4,0},{5,1},{6,2},{7,3},{8,12},{9,13},{10,... | collective-permute-start | bytes 786440 | tf_op jit(solution)/shard_map/ppermute | solution.py:35

commit v12 on v11

--- a/solution.py
+++ b/solution.py
@@ -203,7 +203,7 @@
         in_specs=[IN_VMEM] * 4 + [ANYWHERE] * len(after),
         out_specs=[IN_VMEM] * len(groups),
         compiler_params=params(16),
-        cost_estimate=cost(4 * CAP * up.size, 4 * up.size),
+        cost_estimate=cost(4 * 10**9, 4 * up.size),
         name="grow",
     )(mine, other, up, up_other, *after)
 
@@ -265,22 +265,22 @@
     down_other, up_other = swap(down, 1), swap(up, 1)
     firsts, chips = (7, 6, 5), (4, 3, 2, 1, 0)
     away_first, stay_first, away, stay, token = product(attended, out_weight, (firsts, chips), 44)
-    (away_first,) = once((away_first,), from_y, down_other, up_other)
+    (away_first,) = once((away_first,), from_y)
     came_first = swap(away_first, 1)
     first = [stay_first[i] + came_first[i].astype(f32) for i in range(3)]
-    target, outgoing = route(adapter_slot, row_adapter, attended, from_y, token)
+    target, outgoing = route(adapter_slot, row_adapter, attended, from_y, token, down_other, up_other)
     arrived = {k: swap(outgoing[k], 4 * k) for k in (1, 2, 3)}
     arrived[0] = outgoing[0]
-    (go3,) = once((first[0].astype(bf16),), target)
+    go3 = first[0].astype(bf16)
     y3 = swap(go3, 2)
-    (go2,) = once((first[2].astype(bf16),), arrived[1])
+    (go2,) = once((first[2].astype(bf16),), go3)
     y2 = swap(go2, 2)[None]
     z3 = swap((first[1] + y3.astype(f32)).astype(bf16), 4)[None]
     (away,) = once((away,), target)
     came = swap(away, 1)
     mine = shrink(down, down_other, arrived)
     groups = ((8, 6, 4, 2, 0), (10,), (12,), (14,))
-    here, over2, over4, over6 = grow(mine, swap(mine, 1), up, up_other, groups, y3, came)
+    here, over2, over4, over6 = grow(mine, swap(mine, 1), up, up_other, groups, came)
     over2, over4, over6 = swap(over2, 2), swap(over4, 4), swap(over6, 6)
     (ready2,) = join(target, [stay, came, z3, y2], ((((0, 0), (1, 0), (2, 0), (3, 0)), ()),), f32)
     grown = [here, over2, over4, over6]

time: 59.6 us -> 62.2 us (1.044)
  waiting for transfers between devices: 26.3 us -> 28.3 us
  starting transfers between devices: 21.8 us -> 23.1 us
    ppermute x19, waiting for transfers between devices: 26.3 us -> 28.3 us  [swap(): return lax.ppermute(value, 'tensor', [(t, t ^ mask) for t in range(count)])]
    ppermute x19, starting transfers between devices: 21.8 us -> 23.1 us  [swap(): return lax.ppermute(value, 'tensor', [(t, t ^ mask) for t in range(count)])]
  transfers between devices with their start and end apart: 19 -> 19, of which waited for: 11 -> 9; matrix products, arithmetic and copies ran while one was open for 0% -> 0% of each run, Pallas kernels for 13% -> 12%
where the time goes in v12:
time: 62.2 us; the launch traced here: 62.1 us
  waiting for transfers between devices  28.3 us (45%)
  starting transfers between devices  23.1 us (37%)
  Pallas kernels  8.45 us (14%)
  other arithmetic  1.08 us (2%)
  local copies, waits for them, and re-layouts  1 us (2%)
    ppermute x19, waiting for transfers between devices, swap(): return lax.ppermute(value, 'tensor', [(t, t ^ mask) for t in range(count)])  28.3 us
    ppermute x19, starting transfers between devices, swap(): return lax.ppermute(value, 'tensor', [(t, t ^ mask) for t in range(count)])  23.1 us
    pallas_call x1, Pallas kernels, product(): pl.pallas_call(functools.partial(product_kernel, groups), out_shape=out_s...  4.85 us
    pallas_call x6, Pallas kernels, join(): pl.pallas_call(functools.partial(join_kernel, terms), out_shape=[shape((r...  1.64 us
  transfers between devices with their start and end apart: 19, of which 9 were waited for; matrix products, arithmetic and copies ran while one was open for 0% of the time, Pallas kernels for 12%

profile of v12, /device:TPU:0, one launch (start us, length us, event | category | flops | bytes accessed | tf_op | source)
XLA Modules:
  0.0 62.1 jit_solution(474736506524412576)
XLA Ops:
  0.0 0.5 collective-permute-start.1
  0.5 0.1 collective-permute-start.2
  0.5 3.0 %collective-permute-start = (bf16[256,512]{1,0:T(8,128)(2,1)}, bf16[256,512]{1,0:T(8,128)(2,1)S(1)}, u32[]{:S(2)}, u32[]{:S(2)}) collective-permute-start(bf16[256,512]{1,0:T(8,128)(2,1)} %own_ref.1), channel_id=1, source_target_pairs={{0,2},{1,3},{2,0},{3,1},{4,6},{5,7},{6,4},{7,5},{8,10},{9,11},{10,... | collective-permute-start | bytes 786440 | tf_op jit(solution)/shard_map/ppermute | solution.py:35
  3.5 0.0 copy-start
  3.5 1.0 %copy-done = bf16[256,512]{1,0:T(8,128)(2,1)S(1)} copy-done((bf16[256,512]{1,0:T(8,128)(2,1)S(1)}, bf16[256,512]{1,0:T(8,128)(2,1)}, u32[]{:S(2)}) %copy-start) | copy-done | bytes 262168
  4.5 4.9 %product.1 = (bf16[3,256,512]{2,1,0:T(8,128)(2,1)S(1)}, f32[3,256,512]{2,1,0:T(8,128)S(1)}, bf16[5,256,512]{2,1,0:T(8,128)(2,1)S(1)}, f32[5,256,512]{2,1,0:T(8,128)S(1)}, f32[8,128]{1,0:T(8,128)S(1)}) custom-call(bf16[256,512]{1,0:T(8,128)(2,1)S(1)} %copy-done, bf16[512,8192]{1,0:T(8,128)(2,1)} %weight_hbm.1), custom_call_target="tpu_custom_call" | custom-call | flops 2147483648 | bytes 14680064 | tf_op jit(solution)/shard_map/product/pallas_call | solution.py:138
  9.3 0.0 copy-start.1
  9.3 0.0 copy-start.2
  9.3 0.8 %collective-permute-done.y_ref.refs_1_ = bf16[256,512]{1,0:T(8,128)(2,1)S(1)} collective-permute-done((bf16[256,512]{1,0:T(8,128)(2,1)}, bf16[256,512]{1,0:T(8,128)(2,1)S(1)}, u32[]{:S(2)}, u32[]{:S(2)}) %collective-permute-start) | collective-permute-done | bytes 262176 | tf_op jit(solution)/shard_map/ppermute | solution.py:35
  10.2 0.0 collective-permute-start.8
  10.2 0.0 collective-permute-done.1.rest_1_.other_ref
  10.2 0.0 collective-permute-done.2.rest_2_.up_other_ref
  10.2 0.0 copy-done.1
  10.2 0.0 copy-done.2
  10.2 1.2 %route.1 = (s32[1,256]{1,0:T(1,128)S(1)}, bf16[64,1024]{1,0:T(8,128)(2,1)S(1)}, bf16[64,1024]{1,0:T(8,128)(2,1)S(1)}, bf16[64,1024]{1,0:T(8,128)(2,1)S(1)}, bf16[64,1024]{1,0:T(8,128)(2,1)S(1)}) custom-call(s32[16]{0:T(128)S(1)} %copy-done.2, s32[1,256]{1,0:T(1,128)S(1)} %bitcast.21, bf16[256,512]{1,0:T(8,128)(2,1)S(1)} %copy-done, ...), custom_call_target="tpu_custom_call" | custom-call | flops 134217728 | bytes 1048576 | tf_op jit(solution)/shard_map/route/pallas_call | solution.py:88
  11.4 1.9 %collective-permute-start.4 = (bf16[64,1024]{1,0:T(8,128)(2,1)S(1)}, bf16[64,1024]{1,0:T(8,128)(2,1)S(1)}, u32[]{:S(2)}, u32[]{:S(2)}) collective-permute-start(bf16[64,1024]{1,0:T(8,128)(2,1)S(1)} %get-tuple-element.23), channel_id=1, source_target_pairs={{0,4},{1,5},{2,6},{3,7},{4,0},{5,1},{6,2},{7,3},{8,12},{9,13},{10,... | collective-permute-start | bytes 393224 | tf_op jit(solution)/shard_map/ppermute | solution.py:35
  13.3 2.6 %collective-permute-start.5 = (bf16[64,1024]{1,0:T(8,128)(2,1)S(1)}, bf16[64,1024]{1,0:T(8,128)(2,1)S(1)}, u32[]{:S(2)}, u32[]{:S(2)}) collective-permute-start(bf16[64,1024]{1,0:T(8,128)(2,1)S(1)} %get-tuple-element.24), channel_id=1, source_target_pairs={{0,8},{1,9},{2,10},{3,11},{4,12},{5,13},{6,14},{7,15},{8,0},{9,1},... | collective-permute-start | bytes 393224 | tf_op jit(solution)/shard_map/ppermute | solution.py:35
  15.9 0.0 collective-permute-start.6
  15.9 0.0 collective-permute-done.8
  15.9 0.2 fusion.2
  16.0 1.8 %collective-permute-start.9 = (bf16[256,512]{1,0:T(8,128)(2,1)S(1)}, bf16[256,512]{1,0:T(8,128)(2,1)S(1)}, u32[]{:S(2)}, u32[]{:S(2)}) collective-permute-start(bf16[256,512]{1,0:T(8,128)(2,1)S(1)} %get-tuple-element.34.refs_1_), channel_id=1, source_target_pairs={{0,2},{1,3},{2,0},{3,1},{4,6},{5,7},{6,4},{7,5},{8,10},{9,11},{10,... | collective-permute-start | bytes 786440 | tf_op jit(solution)/shard_map/ppermute | solution.py:35
  17.8 0.0 copy-start.3
  17.8 0.3 collective-permute-start.11
  18.1 1.6 %collective-permute-done.4.refs_0_ = bf16[64,1024]{1,0:T(8,128)(2,1)S(1)} collective-permute-done((bf16[64,1024]{1,0:T(8,128)(2,1)S(1)}, bf16[64,1024]{1,0:T(8,128)(2,1)S(1)}, u32[]{:S(2)}, u32[]{:S(2)}) %collective-permute-start.4) | collective-permute-done | bytes 131104 | tf_op jit(solution)/shard_map/ppermute | solution.py:35
  19.7 0.0 collective-permute-start.3
  19.7 6.5 %collective-permute-done.5.refs_1_ = bf16[64,1024]{1,0:T(8,128)(2,1)S(1)} collective-permute-done((bf16[64,1024]{1,0:T(8,128)(2,1)S(1)}, bf16[64,1024]{1,0:T(8,128)(2,1)S(1)}, u32[]{:S(2)}, u32[]{:S(2)}) %collective-permute-start.5) | collective-permute-done | bytes 131104 | tf_op jit(solution)/shard_map/ppermute | solution.py:35
  26.2 0.0 collective-permute-done.6.refs_2_
  26.2 0.0 copy-done.3
  26.2 0.0 copy-start.4
  26.2 0.4 shrink.1.mine_ref
  26.6 0.0 collective-permute-start.7
  26.6 0.0 collective-permute-done.9
  26.6 0.1 fusion
  26.7 2.7 %collective-permute-start.10 = (bf16[256,512]{1,0:T(8,128)(2,1)S(1)}, bf16[256,512]{1,0:T(8,128)(2,1)S(1)}, u32[]{:S(2)}, u32[]{:S(2)}) collective-permute-start(bf16[256,512]{1,0:T(8,128)(2,1)S(1)} %fusion), channel_id=1, source_target_pairs={{0,4},{1,5},{2,6},{3,7},{4,0},{5,1},{6,2},{7,3},{8,12},{9,13},{10,... | collective-permute-start | bytes 786440 | tf_op jit(solution)/shard_map/ppermute | solution.py:35
  29.4 0.0 collective-permute-done.7.other_ref
  29.4 0.0 collective-permute-done.3.refs_0_.refs_1_
  29.4 0.0 copy-done.4
  29.5 0.3 grow.1
  29.8 1.6 %collective-permute-start.12 = (bf16[1,64,512]{2,1,0:T(8,128)(2,1)S(1)}, bf16[1,64,512]{2,1,0:T(8,128)(2,1)S(1)}, u32[]{:S(2)}, u32[]{:S(2)}) collective-permute-start(bf16[1,64,512]{2,1,0:T(8,128)(2,1)S(1)} %get-tuple-element.30), channel_id=1, source_target_pairs={{0,2},{1,3},{2,0},{3,1},{4,6},{5,7},{6,4},{7,5},{8,10},{9,11},{10,... | collective-permute-start | bytes 196616 | tf_op jit(solution)/shard_map/ppermute | solution.py:35
  31.3 1.0 %collective-permute-start.13 = (bf16[1,64,512]{2,1,0:T(8,128)(2,1)S(1)}, bf16[1,64,512]{2,1,0:T(8,128)(2,1)S(1)}, u32[]{:S(2)}, u32[]{:S(2)}) collective-permute-start(bf16[1,64,512]{2,1,0:T(8,128)(2,1)S(1)} %get-tuple-element.31), channel_id=1, source_target_pairs={{0,4},{1,5},{2,6},{3,7},{4,0},{5,1},{6,2},{7,3},{8,12},{9,13},{10,... | collective-permute-start | bytes 196616 | tf_op jit(solution)/shard_map/ppermute | solution.py:35
  32.3 1.0 %collective-permute-start.14 = (bf16[1,64,512]{2,1,0:T(8,128)(2,1)S(1)}, bf16[1,64,512]{2,1,0:T(8,128)(2,1)S(1)}, u32[]{:S(2)}, u32[]{:S(2)}) collective-permute-start(bf16[1,64,512]{2,1,0:T(8,128)(2,1)S(1)} %get-tuple-element.32), channel_id=1, source_target_pairs={{0,6},{1,7},{2,4},{3,5},{4,2},{5,3},{6,0},{7,1},{8,14},{9,15},{10,... | collective-permute-start | bytes 196616 | tf_op jit(solution)/shard_map/ppermute | solution.py:35
  33.3 0.0 collective-permute-done.11
  33.3 3.3 %collective-permute-done.10 = bf16[256,512]{1,0:T(8,128)(2,1)S(1)} collective-permute-done((bf16[256,512]{1,0:T(8,128)(2,1)S(1)}, bf16[256,512]{1,0:T(8,128)(2,1)S(1)}, u32[]{:S(2)}, u32[]{:S(2)}) %collective-permute-start.10) | collective-permute-done | bytes 262176 | tf_op jit(solution)/shard_map/ppermute | solution.py:35
  36.6 0.1 join.7
  36.7 0.0 collective-permute-done.12.refs_2_
  36.7 1.3 %collective-permute-done.13.refs_3_ = bf16[1,64,512]{2,1,0:T(8,128)(2,1)S(1)} collective-permute-done((bf16[1,64,512]{2,1,0:T(8,128)(2,1)S(1)}, bf16[1,64,512]{2,1,0:T(8,128)(2,1)S(1)}, u32[]{:S(2)}, u32[]{:S(2)}) %collective-permute-start.13) | collective-permute-done | bytes 65568 | tf_op jit(solution)/shard_map/ppermute | solution.py:35
  38.0 2.2 %collective-permute-done.14.refs_4_ = bf16[1,64,512]{2,1,0:T(8,128)(2,1)S(1)} collective-permute-done((bf16[1,64,512]{2,1,0:T(8,128)(2,1)S(1)}, bf16[1,64,512]{2,1,0:T(8,128)(2,1)S(1)}, u32[]{:S(2)}, u32[]{:S(2)}) %collective-permute-start.14) | collective-permute-done | bytes 65568 | tf_op jit(solution)/shard_map/ppermute | solution.py:35
  40.2 0.5 join.8.refs_3_.refs_4_
  40.6 0.3 join.10
  40.9 0.6 collective-permute-start.17
  41.5 2.8 %collective-permute-start.15 = (bf16[256,512]{1,0:T(8,128)(2,1)S(1)}, bf16[256,512]{1,0:T(8,128)(2,1)S(1)}, u32[]{:S(2)}, u32[]{:S(2)}) collective-permute-start(bf16[256,512]{1,0:T(8,128)(2,1)S(1)} %join.8.refs_3_.refs_4_), channel_id=1, source_target_pairs={{0,8},{1,9},{2,10},{3,11},{4,12},{5,13},{6,14},{7,15},{8,0},{9,1},... | collective-permute-start | bytes 786440 | tf_op jit(solution)/shard_map/ppermute | solution.py:35
  44.2 0.3 join.9
  44.5 1.6 %collective-permute-start.16 = (bf16[256,512]{1,0:T(8,128)(2,1)S(1)}, bf16[256,512]{1,0:T(8,128)(2,1)S(1)}, u32[]{:S(2)}, u32[]{:S(2)}) collective-permute-start(bf16[256,512]{1,0:T(8,128)(2,1)S(1)} %join.9), channel_id=1, source_target_pairs={{0,2},{1,3},{2,0},{3,1},{4,6},{5,7},{6,4},{7,5},{8,10},{9,11},{10,... | collective-permute-start | bytes 786440 | tf_op jit(solution)/shard_map/ppermute | solution.py:35
  46.1 4.1 %collective-permute-done.17 = bf16[256,512]{1,0:T(8,128)(2,1)S(1)} collective-permute-done((bf16[256,512]{1,0:T(8,128)(2,1)S(1)}, bf16[256,512]{1,0:T(8,128)(2,1)S(1)}, u32[]{:S(2)}, u32[]{:S(2)}) %collective-permute-start.17) | collective-permute-done | bytes 262176 | tf_op jit(solution)/shard_map/ppermute | solution.py:35
  50.2 0.3 join.11
  50.4 1.8 %collective-permute-start.18 = (bf16[256,512]{1,0:T(8,128)(2,1)S(1)}, bf16[256,512]{1,0:T(8,128)(2,1)S(1)}, u32[]{:S(2)}, u32[]{:S(2)}) collective-permute-start(bf16[256,512]{1,0:T(8,128)(2,1)S(1)} %join.11), channel_id=1, source_target_pairs={{0,4},{1,5},{2,6},{3,7},{4,0},{5,1},{6,2},{7,3},{8,12},{9,13},{10,... | collective-permute-start | bytes 786440 | tf_op jit(solution)/shard_map/ppermute | solution.py:35
  52.3 0.3 join.6.sum_ref
  52.5 3.4 %collective-permute-done.15.came_ref = bf16[256,512]{1,0:T(8,128)(2,1)S(1)} collective-permute-done((bf16[256,512]{1,0:T(8,128)(2,1)S(1)}, bf16[256,512]{1,0:T(8,128)(2,1)S(1)}, u32[]{:S(2)}, u32[]{:S(2)}) %collective-permute-start.15) | collective-permute-done | bytes 262176 | tf_op jit(solution)/shard_map/ppermute | solution.py:35
  56.0 0.0 collective-permute-done.16
  56.0 5.2 %collective-permute-done.18 = bf16[256,512]{1,0:T(8,128)(2,1)S(1)} collective-permute-done((bf16[256,512]{1,0:T(8,128)(2,1)S(1)}, bf16[256,512]{1,0:T(8,128)(2,1)S(1)}, u32[]{:S(2)}, u32[]{:S(2)}) %collective-permute-start.18) | collective-permute-done | bytes 262176 | tf_op jit(solution)/shard_map/ppermute | solution.py:35
  61.3 0.8 %add_convert_fusion = bf16[256,512]{1,0:T(8,128)(2,1)} fusion(bf16[256,512]{1,0:T(8,128)(2,1)S(1)} %collective-permute-done.18, f32[256,512]{1,0:T(8,128)S(1)} %gather.1, bf16[256,512]{1,0:T(8,128)(2,1)S(1)} %collective-permute-done.16), kind=kLoop, calls=%fused_computation.2 | loop fusion | flops 655360 | bytes 1310720 | tf_op jit(solution)/shard_map/convert_element_type | solution.py:304
  (4 shorter events, 0.0 us)
Async XLA Ops:
  0.0 10.2 %collective-permute-start.1 = (bf16[64,8192]{1,0:T(8,128)(2,1)}, bf16[64,8192]{1,0:T(8,128)(2,1)S(1)}, u32[]{:S(2)}, u32[]{:S(2)}) collective-permute-start(bf16[64,8192]{1,0:T(8,128)(2,1)} %bitcast.22), channel_id=1, source_target_pairs={{0,1},{1,0},{2,3},{3,2},{4,5},{5,4},{6,7},{7,6},{8,9},{9,8},{10,11... | collective-permute-start | bytes 3145736 | tf_op jit(solution)/shard_map/ppermute | solution.py:35
  0.5 9.7 %collective-permute-start.2 = (bf16[64,8192]{1,0:T(8,128)(2,1)}, bf16[64,8192]{1,0:T(8,128)(2,1)S(1)}, u32[]{:S(2)}, u32[]{:S(2)}) collective-permute-start(bf16[64,8192]{1,0:T(8,128)(2,1)} %bitcast.24), channel_id=1, source_target_pairs={{0,1},{1,0},{2,3},{3,2},{4,5},{5,4},{6,7},{7,6},{8,9},{9,8},{10,11... | collective-permute-start | bytes 3145736 | tf_op jit(solution)/shard_map/ppermute | solution.py:35
  0.5 9.6 %collective-permute-start = (bf16[256,512]{1,0:T(8,128)(2,1)}, bf16[256,512]{1,0:T(8,128)(2,1)S(1)}, u32[]{:S(2)}, u32[]{:S(2)}) collective-permute-start(bf16[256,512]{1,0:T(8,128)(2,1)} %own_ref.1), channel_id=1, source_target_pairs={{0,2},{1,3},{2,0},{3,1},{4,6},{5,7},{6,4},{7,5},{8,10},{9,11},{10,... | collective-permute-start | bytes 786440 | tf_op jit(solution)/shard_map/ppermute | solution.py:35
  3.5 1.0 %copy-start = (bf16[256,512]{1,0:T(8,128)(2,1)S(1)}, bf16[256,512]{1,0:T(8,128)(2,1)}, u32[]{:S(2)}) copy-start(bf16[256,512]{1,0:T(8,128)(2,1)} %own_ref.1) | copy-start | bytes 786436
  9.3 0.9 %copy-start.1 = (s32[256]{0:T(256)S(1)}, s32[256]{0:T(256)}, u32[]{:S(2)}) copy-start(s32[256]{0:T(256)} %param.10) | copy-start | bytes 3076
  9.3 0.9 %copy-start.2 = (s32[16]{0:T(128)S(1)}, s32[16]{0:T(128)}, u32[]{:S(2)}) copy-start(s32[16]{0:T(128)} %slot_hbm.1) | copy-start | bytes 196
  10.2 5.7 %collective-permute-start.8 = (bf16[3,256,512]{2,1,0:T(8,128)(2,1)S(1)}, bf16[3,256,512]{2,1,0:T(8,128)(2,1)S(1)}, u32[]{:S(2)}, u32[]{:S(2)}) collective-permute-start(bf16[3,256,512]{2,1,0:T(8,128)(2,1)S(1)} %once.4), channel_id=1, source_target_pairs={{0,1},{1,0},{2,3},{3,2},{4,5},{5,4},{6,7},{7,6},{8,9},{9,8},{10,11... | collective-permute-start | bytes 2359304 | tf_op jit(solution)/shard_map/ppermute | solution.py:35
  11.4 8.3 %collective-permute-start.4 = (bf16[64,1024]{1,0:T(8,128)(2,1)S(1)}, bf16[64,1024]{1,0:T(8,128)(2,1)S(1)}, u32[]{:S(2)}, u32[]{:S(2)}) collective-permute-start(bf16[64,1024]{1,0:T(8,128)(2,1)S(1)} %get-tuple-element.23), channel_id=1, source_target_pairs={{0,4},{1,5},{2,6},{3,7},{4,0},{5,1},{6,2},{7,3},{8,12},{9,13},{10,... | collective-permute-start | bytes 393224 | tf_op jit(solution)/shard_map/ppermute | solution.py:35
  13.3 12.9 %collective-permute-start.5 = (bf16[64,1024]{1,0:T(8,128)(2,1)S(1)}, bf16[64,1024]{1,0:T(8,128)(2,1)S(1)}, u32[]{:S(2)}, u32[]{:S(2)}) collective-permute-start(bf16[64,1024]{1,0:T(8,128)(2,1)S(1)} %get-tuple-element.24), channel_id=1, source_target_pairs={{0,8},{1,9},{2,10},{3,11},{4,12},{5,13},{6,14},{7,15},{8,0},{9,1},... | collective-permute-start | bytes 393224 | tf_op jit(solution)/shard_map/ppermute | solution.py:35
  15.9 10.3 %collective-permute-start.6 = (bf16[64,1024]{1,0:T(8,128)(2,1)S(1)}, bf16[64,1024]{1,0:T(8,128)(2,1)S(1)}, u32[]{:S(2)}, u32[]{:S(2)}) collective-permute-start(bf16[64,1024]{1,0:T(8,128)(2,1)S(1)} %get-tuple-element.25), channel_id=1, source_target_pairs={{0,12},{1,13},{2,14},{3,15},{4,8},{5,9},{6,10},{7,11},{8,4},{9,5},... | collective-permute-start | bytes 393224 | tf_op jit(solution)/shard_map/ppermute | solution.py:35
  16.0 10.6 %collective-permute-start.9 = (bf16[256,512]{1,0:T(8,128)(2,1)S(1)}, bf16[256,512]{1,0:T(8,128)(2,1)S(1)}, u32[]{:S(2)}, u32[]{:S(2)}) collective-permute-start(bf16[256,512]{1,0:T(8,128)(2,1)S(1)} %get-tuple-element.34.refs_1_), channel_id=1, source_target_pairs={{0,2},{1,3},{2,0},{3,1},{4,6},{5,7},{6,4},{7,5},{8,10},{9,11},{10,... | collective-permute-start | bytes 786440 | tf_op jit(solution)/shard_map/ppermute | solution.py:35
  17.8 8.3 %copy-start.3 = (bf16[1,8192,64]{1,2,0:T(8,128)(2,1)S(1)}, bf16[1,8192,64]{1,2,0:T(8,128)(2,1)}, u32[]{:S(2)}) copy-start(bf16[1,8192,64]{1,2,0:T(8,128)(2,1)} %param.8) | copy-start | bytes 3145732
  17.8 15.5 %collective-permute-start.11 = (bf16[256,512]{1,0:T(8,128)(2,1)S(1)}, bf16[256,512]{1,0:T(8,128)(2,1)S(1)}, u32[]{:S(2)}, u32[]{:S(2)}) collective-permute-start(bf16[256,512]{1,0:T(8,128)(2,1)S(1)} %once.5), channel_id=1, source_target_pairs={{0,2},{1,3},{2,0},{3,1},{4,6},{5,7},{6,4},{7,5},{8,10},{9,11},{10,... | collective-permute-start | bytes 786440 | tf_op jit(solution)/shard_map/ppermute | solution.py:35
  19.7 9.7 %collective-permute-start.3 = (bf16[5,256,512]{2,1,0:T(8,128)(2,1)S(1)}, bf16[5,256,512]{2,1,0:T(8,128)(2,1)S(1)}, u32[]{:S(2)}, u32[]{:S(2)}) collective-permute-start(bf16[5,256,512]{2,1,0:T(8,128)(2,1)S(1)} %once.3), channel_id=1, source_target_pairs={{0,1},{1,0},{2,3},{3,2},{4,5},{5,4},{6,7},{7,6},{8,9},{9,8},{10,11... | collective-permute-start | bytes 3932168 | tf_op jit(solution)/shard_map/ppermute | solution.py:35
  26.2 3.3 %copy-start.4 = (bf16[1,64,8192]{2,1,0:T(8,128)(2,1)S(1)}, bf16[1,64,8192]{2,1,0:T(8,128)(2,1)}, u32[]{:S(2)}) copy-start(bf16[1,64,8192]{2,1,0:T(8,128)(2,1)} %param.9) | copy-start | bytes 3145732
  26.6 2.9 %collective-permute-start.7 = (f32[64,64]{1,0:T(8,128)S(1)}, f32[64,64]{1,0:T(8,128)S(1)}, u32[]{:S(2)}, u32[]{:S(2)}) collective-permute-start(f32[64,64]{1,0:T(8,128)S(1)} %shrink.1.mine_ref), channel_id=1, source_target_pairs={{0,1},{1,0},{2,3},{3,2},{4,5},{5,4},{6,7},{7,6},{8,9},{9,8},{10,11... | collective-permute-start | bytes 49160 | tf_op jit(solution)/shard_map/ppermute | solution.py:35
  26.7 9.9 %collective-permute-start.10 = (bf16[256,512]{1,0:T(8,128)(2,1)S(1)}, bf16[256,512]{1,0:T(8,128)(2,1)S(1)}, u32[]{:S(2)}, u32[]{:S(2)}) collective-permute-start(bf16[256,512]{1,0:T(8,128)(2,1)S(1)} %fusion), channel_id=1, source_target_pairs={{0,4},{1,5},{2,6},{3,7},{4,0},{5,1},{6,2},{7,3},{8,12},{9,13},{10,... | collective-permute-start | bytes 786440 | tf_op jit(solution)/shard_map/ppermute | solution.py:35
  29.8 7.0 %collective-permute-start.12 = (bf16[1,64,512]{2,1,0:T(8,128)(2,1)S(1)}, bf16[1,64,512]{2,1,0:T(8,128)(2,1)S(1)}, u32[]{:S(2)}, u32[]{:S(2)}) collective-permute-start(bf16[1,64,512]{2,1,0:T(8,128)(2,1)S(1)} %get-tuple-element.30), channel_id=1, source_target_pairs={{0,2},{1,3},{2,0},{3,1},{4,6},{5,7},{6,4},{7,5},{8,10},{9,11},{10,... | collective-permute-start | bytes 196616 | tf_op jit(solution)/shard_map/ppermute | solution.py:35
  31.3 6.7 %collective-permute-start.13 = (bf16[1,64,512]{2,1,0:T(8,128)(2,1)S(1)}, bf16[1,64,512]{2,1,0:T(8,128)(2,1)S(1)}, u32[]{:S(2)}, u32[]{:S(2)}) collective-permute-start(bf16[1,64,512]{2,1,0:T(8,128)(2,1)S(1)} %get-tuple-element.31), channel_id=1, source_target_pairs={{0,4},{1,5},{2,6},{3,7},{4,0},{5,1},{6,2},{7,3},{8,12},{9,13},{10,... | collective-permute-start | bytes 196616 | tf_op jit(solution)/shard_map/ppermute | solution.py:35
  32.3 7.8 %collective-permute-start.14 = (bf16[1,64,512]{2,1,0:T(8,128)(2,1)S(1)}, bf16[1,64,512]{2,1,0:T(8,128)(2,1)S(1)}, u32[]{:S(2)}, u32[]{:S(2)}) collective-permute-start(bf16[1,64,512]{2,1,0:T(8,128)(2,1)S(1)} %get-tuple-element.32), channel_id=1, source_target_pairs={{0,6},{1,7},{2,4},{3,5},{4,2},{5,3},{6,0},{7,1},{8,14},{9,15},{10,... | collective-permute-start | bytes 196616 | tf_op jit(solution)/shard_map/ppermute | solution.py:35
  40.9 9.3 %collective-permute-start.17 = (bf16[256,512]{1,0:T(8,128)(2,1)S(1)}, bf16[256,512]{1,0:T(8,128)(2,1)S(1)}, u32[]{:S(2)}, u32[]{:S(2)}) collective-permute-start(bf16[256,512]{1,0:T(8,128)(2,1)S(1)} %join.10), channel_id=1, source_target_pairs={{0,2},{1,3},{2,0},{3,1},{4,6},{5,7},{6,4},{7,5},{8,10},{9,11},{10,... | collective-permute-start | bytes 786440 | tf_op jit(solution)/shard_map/ppermute | solution.py:35
  41.5 14.5 %collective-permute-start.15 = (bf16[256,512]{1,0:T(8,128)(2,1)S(1)}, bf16[256,512]{1,0:T(8,128)(2,1)S(1)}, u32[]{:S(2)}, u32[]{:S(2)}) collective-permute-start(bf16[256,512]{1,0:T(8,128)(2,1)S(1)} %join.8.refs_3_.refs_4_), channel_id=1, source_target_pairs={{0,8},{1,9},{2,10},{3,11},{4,12},{5,13},{6,14},{7,15},{8,0},{9,1},... | collective-permute-start | bytes 786440 | tf_op jit(solution)/shard_map/ppermute | solution.py:35
  44.5 11.5 %collective-permute-start.16 = (bf16[256,512]{1,0:T(8,128)(2,1)S(1)}, bf16[256,512]{1,0:T(8,128)(2,1)S(1)}, u32[]{:S(2)}, u32[]{:S(2)}) collective-permute-start(bf16[256,512]{1,0:T(8,128)(2,1)S(1)} %join.9), channel_id=1, source_target_pairs={{0,2},{1,3},{2,0},{3,1},{4,6},{5,7},{6,4},{7,5},{8,10},{9,11},{10,... | collective-permute-start | bytes 786440 | tf_op jit(solution)/shard_map/ppermute | solution.py:35
  50.4 10.8 %collective-permute-start.18 = (bf16[256,512]{1,0:T(8,128)(2,1)S(1)}, bf16[256,512]{1,0:T(8,128)(2,1)S(1)}, u32[]{:S(2)}, u32[]{:S(2)}) collective-permute-start(bf16[256,512]{1,0:T(8,128)(2,1)S(1)} %join.11), channel_id=1, source_target_pairs={{0,4},{1,5},{2,6},{3,7},{4,0},{5,1},{6,2},{7,3},{8,12},{9,13},{10,... | collective-permute-start | bytes 786440 | tf_op jit(solution)/shard_map/ppermute | solution.py:35

commit v13 on v12

--- a/solution.py
+++ b/solution.py
@@ -203,7 +203,7 @@
         in_specs=[IN_VMEM] * 4 + [ANYWHERE] * len(after),
         out_specs=[IN_VMEM] * len(groups),
         compiler_params=params(16),
-        cost_estimate=cost(4 * 10**9, 4 * up.size),
+        cost_estimate=cost(4 * CAP * up.size, 4 * up.size),
         name="grow",
     )(mine, other, up, up_other, *after)
 
@@ -278,8 +278,10 @@
     z3 = swap((first[1] + y3.astype(f32)).astype(bf16), 4)[None]
     (away,) = once((away,), target)
     came = swap(away, 1)
+    go1 = (stay[1] + came[1].astype(f32)).astype(bf16)
+    y1 = swap(go1, 2)[None]
     mine = shrink(down, down_other, arrived)
-    groups = ((8, 6, 4, 2, 0), (10,), (12,), (14,))
+    groups = ((8, 4, 2, 0), (10, 6), (12,), (14,))
     here, over2, over4, over6 = grow(mine, swap(mine, 1), up, up_other, groups, came)
     over2, over4, over6 = swap(over2, 2), swap(over4, 4), swap(over6, 6)
     (ready2,) = join(target, [stay, came, z3, y2], ((((0, 0), (1, 0), (2, 0), (3, 0)), ()),), f32)
@@ -290,14 +292,14 @@
     z2 = swap(sum2, 8)
 
     def blocks(m):
-        return ((0, chips.index(m)), (1, chips.index(m))), ((2, chips.index(m), 0),)
-
-    (go1,) = join(target, [stay, came, here, sum2], (blocks(3),), bf16)
-    y1 = swap(go1, 2)
+        return ((0, chips.index(m)), (1, chips.index(m))), ((2, (4, 2, 1, 0).index(m), 0),)
+
     (go0,) = join(target, [stay, came, here, sum2], (blocks(1),), bf16)
     y0 = swap(go0, 2)
-    sums, grown = blocks(2)
-    (sum1,) = join(target, [stay, came, here, y1[None], sum2], ((sums + ((3, 0),), grown),), bf16)
+    sums, own = blocks(2)
+    (sum1,) = join(
+        target, [stay, came, here, over2, y1, sum2], ((sums + ((4, 0),), own + ((3, 1, 2),)),), bf16
+    )
     z1 = swap(sum1, 4)
     (side0,) = join(target, [stay, came, here], (blocks(0),), f32)
     total = gather(side0, z2) + y0.astype(f32) + z1.astype(f32)

time: 62.2 us -> 55.9 us (0.90)
  waiting for transfers between devices: 28.3 us -> 21.6 us
    ppermute x19, waiting for transfers between devices: 28.3 us -> 21.6 us  [swap(): return lax.ppermute(value, 'tensor', [(t, t ^ mask) for t in range(count)])]
    pallas_call x6 -> x5, Pallas kernels: 1.64 us -> 1.44 us  [join(): pl.pallas_call(functools.partial(join_kernel, terms), out_shape=[shape((r...]
  transfers between devices with their start and end apart: 19 -> 19, of which waited for: 9 -> 9; matrix products, arithmetic and copies ran while one was open for 0% -> 1% of each run, Pallas kernels for 12% -> 15%
where the time goes in v13:
time: 55.9 us; the launch traced here: 55.8 us
  starting transfers between devices  23.6 us (42%)
  waiting for transfers between devices  21.6 us (39%)
  Pallas kernels  8.24 us (15%)
  other arithmetic  1.21 us (2%)
  local copies, waits for them, and re-layouts  1 us (2%)
    ppermute x19, starting transfers between devices, swap(): return lax.ppermute(value, 'tensor', [(t, t ^ mask) for t in range(count)])  23.6 us
    ppermute x19, waiting for transfers between devices, swap(): return lax.ppermute(value, 'tensor', [(t, t ^ mask) for t in range(count)])  21.6 us
    pallas_call x1, Pallas kernels, product(): pl.pallas_call(functools.partial(product_kernel, groups), out_shape=out_s...  4.85 us
    pallas_call x5, Pallas kernels, join(): pl.pallas_call(functools.partial(join_kernel, terms), out_shape=[shape((r...  1.44 us
    pallas_call x1, Pallas kernels, route(): pl.pallas_call(functools.partial(route_kernel, count, layers), out_shape=...  1.21 us
  transfers between devices with their start and end apart: 19, of which 9 were waited for; matrix products, arithmetic and copies ran while one was open for 1% of the time, Pallas kernels for 15%

profile of v13, /device:TPU:0, one launch (start us, length us, event | category | flops | bytes accessed | tf_op | source)
XLA Modules:
  0.0 55.8 jit_solution(7759660917632354167)
XLA Ops:
  0.0 0.5 collective-permute-start.1
  0.5 0.1 collective-permute-start.2
  0.5 3.0 %collective-permute-start = (bf16[256,512]{1,0:T(8,128)(2,1)}, bf16[256,512]{1,0:T(8,128)(2,1)S(1)}, u32[]{:S(2)}, u32[]{:S(2)}) collective-permute-start(bf16[256,512]{1,0:T(8,128)(2,1)} %own_ref.1), channel_id=1, source_target_pairs={{0,2},{1,3},{2,0},{3,1},{4,6},{5,7},{6,4},{7,5},{8,10},{9,11},{10,... | collective-permute-start | bytes 786440 | tf_op jit(solution)/shard_map/ppermute | solution.py:35
  3.5 0.0 copy-start.1
  3.5 1.0 %copy-done.1 = bf16[256,512]{1,0:T(8,128)(2,1)S(1)} copy-done((bf16[256,512]{1,0:T(8,128)(2,1)S(1)}, bf16[256,512]{1,0:T(8,128)(2,1)}, u32[]{:S(2)}) %copy-start.1) | copy-done | bytes 262168
  4.5 4.9 %product.1 = (bf16[3,256,512]{2,1,0:T(8,128)(2,1)S(1)}, f32[3,256,512]{2,1,0:T(8,128)S(1)}, bf16[5,256,512]{2,1,0:T(8,128)(2,1)S(1)}, f32[5,256,512]{2,1,0:T(8,128)S(1)}, f32[8,128]{1,0:T(8,128)S(1)}) custom-call(bf16[256,512]{1,0:T(8,128)(2,1)S(1)} %copy-done.1, bf16[512,8192]{1,0:T(8,128)(2,1)} %weight_hbm.1), custom_call_target="tpu_custom_call" | custom-call | flops 2147483648 | bytes 14680064 | tf_op jit(solution)/shard_map/product/pallas_call | solution.py:138
  9.3 0.0 copy-start.2
  9.3 0.0 copy-start.3
  9.3 0.8 %collective-permute-done.y_ref.refs_1_ = bf16[256,512]{1,0:T(8,128)(2,1)S(1)} collective-permute-done((bf16[256,512]{1,0:T(8,128)(2,1)}, bf16[256,512]{1,0:T(8,128)(2,1)S(1)}, u32[]{:S(2)}, u32[]{:S(2)}) %collective-permute-start) | collective-permute-done | bytes 262176 | tf_op jit(solution)/shard_map/ppermute | solution.py:35
  10.2 0.0 collective-permute-start.8
  10.2 0.0 collective-permute-done.1.rest_1_.other_ref
  10.2 0.0 collective-permute-done.2.rest_2_.up_other_ref
  10.2 0.0 copy-done.2
  10.2 0.0 copy-done.3
  10.2 1.2 %route.1 = (s32[1,256]{1,0:T(1,128)S(1)}, bf16[64,1024]{1,0:T(8,128)(2,1)S(1)}, bf16[64,1024]{1,0:T(8,128)(2,1)S(1)}, bf16[64,1024]{1,0:T(8,128)(2,1)S(1)}, bf16[64,1024]{1,0:T(8,128)(2,1)S(1)}) custom-call(s32[16]{0:T(128)S(1)} %copy-done.3, s32[1,256]{1,0:T(1,128)S(1)} %bitcast.25, bf16[256,512]{1,0:T(8,128)(2,1)S(1)} %copy-done.1, ...), custom_call_target="tpu_custom_call" | custom-call | flops 134217728 | bytes 1048576 | tf_op jit(solution)/shard_map/route/pallas_call | solution.py:88
  11.4 0.6 %collective-permute-start.3 = (bf16[5,256,512]{2,1,0:T(8,128)(2,1)S(1)}, bf16[5,256,512]{2,1,0:T(8,128)(2,1)S(1)}, u32[]{:S(2)}, u32[]{:S(2)}) collective-permute-start(bf16[5,256,512]{2,1,0:T(8,128)(2,1)S(1)} %once.3), channel_id=1, source_target_pairs={{0,1},{1,0},{2,3},{3,2},{4,5},{5,4},{6,7},{7,6},{8,9},{9,8},{10,11... | collective-permute-start | bytes 3932168 | tf_op jit(solution)/shard_map/ppermute | solution.py:35
  12.0 0.5 collective-permute-done.8
  12.4 0.2 fusion.2
  12.6 1.8 %collective-permute-start.9 = (bf16[256,512]{1,0:T(8,128)(2,1)S(1)}, bf16[256,512]{1,0:T(8,128)(2,1)S(1)}, u32[]{:S(2)}, u32[]{:S(2)}) collective-permute-start(bf16[256,512]{1,0:T(8,128)(2,1)S(1)} %get-tuple-element.34.refs_1_), channel_id=1, source_target_pairs={{0,2},{1,3},{2,0},{3,1},{4,6},{5,7},{6,4},{7,5},{8,10},{9,11},{10,... | collective-permute-start | bytes 786440 | tf_op jit(solution)/shard_map/ppermute | solution.py:35
  14.5 1.6 %collective-permute-start.4 = (bf16[64,1024]{1,0:T(8,128)(2,1)S(1)}, bf16[64,1024]{1,0:T(8,128)(2,1)S(1)}, u32[]{:S(2)}, u32[]{:S(2)}) collective-permute-start(bf16[64,1024]{1,0:T(8,128)(2,1)S(1)} %get-tuple-element.23), channel_id=1, source_target_pairs={{0,4},{1,5},{2,6},{3,7},{4,0},{5,1},{6,2},{7,3},{8,12},{9,13},{10,... | collective-permute-start | bytes 393224 | tf_op jit(solution)/shard_map/ppermute | solution.py:35
  16.0 2.6 %collective-permute-start.5 = (bf16[64,1024]{1,0:T(8,128)(2,1)S(1)}, bf16[64,1024]{1,0:T(8,128)(2,1)S(1)}, u32[]{:S(2)}, u32[]{:S(2)}) collective-permute-start(bf16[64,1024]{1,0:T(8,128)(2,1)S(1)} %get-tuple-element.24), channel_id=1, source_target_pairs={{0,8},{1,9},{2,10},{3,11},{4,12},{5,13},{6,14},{7,15},{8,0},{9,1},... | collective-permute-start | bytes 393224 | tf_op jit(solution)/shard_map/ppermute | solution.py:35
  18.6 0.2 collective-permute-start.6
  18.8 0.0 copy-start.4
  18.8 2.2 %collective-permute-done.9 = bf16[256,512]{1,0:T(8,128)(2,1)S(1)} collective-permute-done((bf16[256,512]{1,0:T(8,128)(2,1)S(1)}, bf16[256,512]{1,0:T(8,128)(2,1)S(1)}, u32[]{:S(2)}, u32[]{:S(2)}) %collective-permute-start.9) | collective-permute-done | bytes 262176 | tf_op jit(solution)/shard_map/ppermute | solution.py:35
  21.1 1.7 %collective-permute-start.11 = (bf16[256,512]{1,0:T(8,128)(2,1)S(1)}, bf16[256,512]{1,0:T(8,128)(2,1)S(1)}, u32[]{:S(2)}, u32[]{:S(2)}) collective-permute-start(bf16[256,512]{1,0:T(8,128)(2,1)S(1)} %once.5), channel_id=1, source_target_pairs={{0,2},{1,3},{2,0},{3,1},{4,6},{5,7},{6,4},{7,5},{8,10},{9,11},{10,... | collective-permute-start | bytes 786440 | tf_op jit(solution)/shard_map/ppermute | solution.py:35
  22.8 0.1 fusion
  22.9 0.0 collective-permute-done.3.refs_0_.refs_1_
  22.9 1.6 %collective-permute-start.10 = (bf16[256,512]{1,0:T(8,128)(2,1)S(1)}, bf16[256,512]{1,0:T(8,128)(2,1)S(1)}, u32[]{:S(2)}, u32[]{:S(2)}) collective-permute-start(bf16[256,512]{1,0:T(8,128)(2,1)S(1)} %fusion), channel_id=1, source_target_pairs={{0,4},{1,5},{2,6},{3,7},{4,0},{5,1},{6,2},{7,3},{8,12},{9,13},{10,... | collective-permute-start | bytes 786440 | tf_op jit(solution)/shard_map/ppermute | solution.py:35
  24.6 0.1 fusion.3
  24.7 0.0 collective-permute-done.4.refs_0_
  24.7 0.6 %collective-permute-start.17 = (bf16[256,512]{1,0:T(8,128)(2,1)S(1)}, bf16[256,512]{1,0:T(8,128)(2,1)S(1)}, u32[]{:S(2)}, u32[]{:S(2)}) collective-permute-start(bf16[256,512]{1,0:T(8,128)(2,1)S(1)} %fusion.3), channel_id=1, source_target_pairs={{0,2},{1,3},{2,0},{3,1},{4,6},{5,7},{6,4},{7,5},{8,10},{9,11},{10,... | collective-permute-start | bytes 786440 | tf_op jit(solution)/shard_map/ppermute | solution.py:35
  25.2 3.8 %collective-permute-done.5.refs_1_ = bf16[64,1024]{1,0:T(8,128)(2,1)S(1)} collective-permute-done((bf16[64,1024]{1,0:T(8,128)(2,1)S(1)}, bf16[64,1024]{1,0:T(8,128)(2,1)S(1)}, u32[]{:S(2)}, u32[]{:S(2)}) %collective-permute-start.5) | collective-permute-done | bytes 131104 | tf_op jit(solution)/shard_map/ppermute | solution.py:35
  29.0 0.0 collective-permute-done.6.refs_2_
  29.0 0.0 copy-done.4
  29.0 0.0 copy-start
  29.0 0.4 shrink.1.mine_ref
  29.4 0.0 collective-permute-start.7
  29.4 1.2 %collective-permute-done.7.other_ref = f32[64,64]{1,0:T(8,128)S(1)} collective-permute-done((f32[64,64]{1,0:T(8,128)S(1)}, f32[64,64]{1,0:T(8,128)S(1)}, u32[]{:S(2)}, u32[]{:S(2)}) %collective-permute-start.7) | collective-permute-done | bytes 16416 | tf_op jit(solution)/shard_map/ppermute | solution.py:35
  30.7 0.0 copy-done
  30.7 0.3 grow.1
  31.0 0.6 %collective-permute-start.12 = (bf16[2,64,512]{2,1,0:T(8,128)(2,1)S(1)}, bf16[2,64,512]{2,1,0:T(8,128)(2,1)S(1)}, u32[]{:S(2)}, u32[]{:S(2)}) collective-permute-start(bf16[2,64,512]{2,1,0:T(8,128)(2,1)S(1)} %get-tuple-element.30), channel_id=1, source_target_pairs={{0,2},{1,3},{2,0},{3,1},{4,6},{5,7},{6,4},{7,5},{8,10},{9,11},{10,... | collective-permute-start | bytes 393224 | tf_op jit(solution)/shard_map/ppermute | solution.py:35
  31.5 2.0 %collective-permute-start.13 = (bf16[1,64,512]{2,1,0:T(8,128)(2,1)S(1)}, bf16[1,64,512]{2,1,0:T(8,128)(2,1)S(1)}, u32[]{:S(2)}, u32[]{:S(2)}) collective-permute-start(bf16[1,64,512]{2,1,0:T(8,128)(2,1)S(1)} %get-tuple-element.31), channel_id=1, source_target_pairs={{0,4},{1,5},{2,6},{3,7},{4,0},{5,1},{6,2},{7,3},{8,12},{9,13},{10,... | collective-permute-start | bytes 196616 | tf_op jit(solution)/shard_map/ppermute | solution.py:35
  33.5 0.0 collective-permute-done.11
  33.5 1.0 %collective-permute-start.14 = (bf16[1,64,512]{2,1,0:T(8,128)(2,1)S(1)}, bf16[1,64,512]{2,1,0:T(8,128)(2,1)S(1)}, u32[]{:S(2)}, u32[]{:S(2)}) collective-permute-start(bf16[1,64,512]{2,1,0:T(8,128)(2,1)S(1)} %get-tuple-element.32), channel_id=1, source_target_pairs={{0,6},{1,7},{2,4},{3,5},{4,2},{5,3},{6,0},{7,1},{8,14},{9,15},{10,... | collective-permute-start | bytes 196616 | tf_op jit(solution)/shard_map/ppermute | solution.py:35
  34.5 0.0 collective-permute-done.10
  34.5 0.1 join.6
  34.6 1.2 %collective-permute-done.13.refs_3_ = bf16[1,64,512]{2,1,0:T(8,128)(2,1)S(1)} collective-permute-done((bf16[1,64,512]{2,1,0:T(8,128)(2,1)S(1)}, bf16[1,64,512]{2,1,0:T(8,128)(2,1)S(1)}, u32[]{:S(2)}, u32[]{:S(2)}) %collective-permute-start.13) | collective-permute-done | bytes 65568 | tf_op jit(solution)/shard_map/ppermute | solution.py:35
  35.8 2.8 %collective-permute-done.14.refs_4_ = bf16[1,64,512]{2,1,0:T(8,128)(2,1)S(1)} collective-permute-done((bf16[1,64,512]{2,1,0:T(8,128)(2,1)S(1)}, bf16[1,64,512]{2,1,0:T(8,128)(2,1)S(1)}, u32[]{:S(2)}, u32[]{:S(2)}) %collective-permute-start.14) | collective-permute-done | bytes 65568 | tf_op jit(solution)/shard_map/ppermute | solution.py:35
  38.7 0.0 collective-permute-done.12.refs_2_.refs_3_
  38.7 0.5 join.7.refs_3_.refs_5_
  39.1 2.6 %collective-permute-start.15 = (bf16[256,512]{1,0:T(8,128)(2,1)S(1)}, bf16[256,512]{1,0:T(8,128)(2,1)S(1)}, u32[]{:S(2)}, u32[]{:S(2)}) collective-permute-start(bf16[256,512]{1,0:T(8,128)(2,1)S(1)} %join.7.refs_3_.refs_5_), channel_id=1, source_target_pairs={{0,8},{1,9},{2,10},{3,11},{4,12},{5,13},{6,14},{7,15},{8,0},{9,1},... | collective-permute-start | bytes 786440 | tf_op jit(solution)/shard_map/ppermute | solution.py:35
  41.8 0.3 join.8
  42.0 1.6 %collective-permute-start.16 = (bf16[256,512]{1,0:T(8,128)(2,1)S(1)}, bf16[256,512]{1,0:T(8,128)(2,1)S(1)}, u32[]{:S(2)}, u32[]{:S(2)}) collective-permute-start(bf16[256,512]{1,0:T(8,128)(2,1)S(1)} %join.8), channel_id=1, source_target_pairs={{0,2},{1,3},{2,0},{3,1},{4,6},{5,7},{6,4},{7,5},{8,10},{9,11},{10,... | collective-permute-start | bytes 786440 | tf_op jit(solution)/shard_map/ppermute | solution.py:35
  43.6 0.0 collective-permute-done.17
  43.6 0.3 join.9
  44.0 1.6 %collective-permute-start.18 = (bf16[256,512]{1,0:T(8,128)(2,1)S(1)}, bf16[256,512]{1,0:T(8,128)(2,1)S(1)}, u32[]{:S(2)}, u32[]{:S(2)}) collective-permute-start(bf16[256,512]{1,0:T(8,128)(2,1)S(1)} %join.9), channel_id=1, source_target_pairs={{0,4},{1,5},{2,6},{3,7},{4,0},{5,1},{6,2},{7,3},{8,12},{9,13},{10,... | collective-permute-start | bytes 786440 | tf_op jit(solution)/shard_map/ppermute | solution.py:35
  45.6 0.3 join.5.sum_ref
  45.9 7.5 %collective-permute-done.15.came_ref = bf16[256,512]{1,0:T(8,128)(2,1)S(1)} collective-permute-done((bf16[256,512]{1,0:T(8,128)(2,1)S(1)}, bf16[256,512]{1,0:T(8,128)(2,1)S(1)}, u32[]{:S(2)}, u32[]{:S(2)}) %collective-permute-start.15) | collective-permute-done | bytes 262176 | tf_op jit(solution)/shard_map/ppermute | solution.py:35
  53.4 0.0 collective-permute-done.16
  53.4 1.6 %collective-permute-done.18 = bf16[256,512]{1,0:T(8,128)(2,1)S(1)} collective-permute-done((bf16[256,512]{1,0:T(8,128)(2,1)S(1)}, bf16[256,512]{1,0:T(8,128)(2,1)S(1)}, u32[]{:S(2)}, u32[]{:S(2)}) %collective-permute-start.18) | collective-permute-done | bytes 262176 | tf_op jit(solution)/shard_map/ppermute | solution.py:35
  55.0 0.8 %add_convert_fusion = bf16[256,512]{1,0:T(8,128)(2,1)} fusion(bf16[256,512]{1,0:T(8,128)(2,1)S(1)} %collective-permute-done.18, f32[256,512]{1,0:T(8,128)S(1)} %gather.1, bf16[256,512]{1,0:T(8,128)(2,1)S(1)} %collective-permute-done.16), kind=kLoop, calls=%fused_computation.2 | loop fusion | flops 655360 | bytes 1310720 | tf_op jit(solution)/shard_map/convert_element_type | solution.py:306
  (4 shorter events, 0.0 us)
Async XLA Ops:
  0.0 10.2 %collective-permute-start.1 = (bf16[64,8192]{1,0:T(8,128)(2,1)}, bf16[64,8192]{1,0:T(8,128)(2,1)S(1)}, u32[]{:S(2)}, u32[]{:S(2)}) collective-permute-start(bf16[64,8192]{1,0:T(8,128)(2,1)} %bitcast.26), channel_id=1, source_target_pairs={{0,1},{1,0},{2,3},{3,2},{4,5},{5,4},{6,7},{7,6},{8,9},{9,8},{10,11... | collective-permute-start | bytes 3145736 | tf_op jit(solution)/shard_map/ppermute | solution.py:35
  0.5 9.7 %collective-permute-start.2 = (bf16[64,8192]{1,0:T(8,128)(2,1)}, bf16[64,8192]{1,0:T(8,128)(2,1)S(1)}, u32[]{:S(2)}, u32[]{:S(2)}) collective-permute-start(bf16[64,8192]{1,0:T(8,128)(2,1)} %bitcast.20), channel_id=1, source_target_pairs={{0,1},{1,0},{2,3},{3,2},{4,5},{5,4},{6,7},{7,6},{8,9},{9,8},{10,11... | collective-permute-start | bytes 3145736 | tf_op jit(solution)/shard_map/ppermute | solution.py:35
  0.5 9.6 %collective-permute-start = (bf16[256,512]{1,0:T(8,128)(2,1)}, bf16[256,512]{1,0:T(8,128)(2,1)S(1)}, u32[]{:S(2)}, u32[]{:S(2)}) collective-permute-start(bf16[256,512]{1,0:T(8,128)(2,1)} %own_ref.1), channel_id=1, source_target_pairs={{0,2},{1,3},{2,0},{3,1},{4,6},{5,7},{6,4},{7,5},{8,10},{9,11},{10,... | collective-permute-start | bytes 786440 | tf_op jit(solution)/shard_map/ppermute | solution.py:35
  3.5 1.0 %copy-start.1 = (bf16[256,512]{1,0:T(8,128)(2,1)S(1)}, bf16[256,512]{1,0:T(8,128)(2,1)}, u32[]{:S(2)}) copy-start(bf16[256,512]{1,0:T(8,128)(2,1)} %own_ref.1) | copy-start | bytes 786436
  9.3 0.9 %copy-start.2 = (s32[256]{0:T(256)S(1)}, s32[256]{0:T(256)}, u32[]{:S(2)}) copy-start(s32[256]{0:T(256)} %param.10) | copy-start | bytes 3076
  9.3 0.9 %copy-start.3 = (s32[16]{0:T(128)S(1)}, s32[16]{0:T(128)}, u32[]{:S(2)}) copy-start(s32[16]{0:T(128)} %slot_hbm.1) | copy-start | bytes 196
  10.2 2.3 %collective-permute-start.8 = (bf16[3,256,512]{2,1,0:T(8,128)(2,1)S(1)}, bf16[3,256,512]{2,1,0:T(8,128)(2,1)S(1)}, u32[]{:S(2)}, u32[]{:S(2)}) collective-permute-start(bf16[3,256,512]{2,1,0:T(8,128)(2,1)S(1)} %once.4), channel_id=1, source_target_pairs={{0,1},{1,0},{2,3},{3,2},{4,5},{5,4},{6,7},{7,6},{8,9},{9,8},{10,11... | collective-permute-start | bytes 2359304 | tf_op jit(solution)/shard_map/ppermute | solution.py:35
  11.4 11.5 %collective-permute-start.3 = (bf16[5,256,512]{2,1,0:T(8,128)(2,1)S(1)}, bf16[5,256,512]{2,1,0:T(8,128)(2,1)S(1)}, u32[]{:S(2)}, u32[]{:S(2)}) collective-permute-start(bf16[5,256,512]{2,1,0:T(8,128)(2,1)S(1)} %once.3), channel_id=1, source_target_pairs={{0,1},{1,0},{2,3},{3,2},{4,5},{5,4},{6,7},{7,6},{8,9},{9,8},{10,11... | collective-permute-start | bytes 3932168 | tf_op jit(solution)/shard_map/ppermute | solution.py:35
  12.6 8.4 %collective-permute-start.9 = (bf16[256,512]{1,0:T(8,128)(2,1)S(1)}, bf16[256,512]{1,0:T(8,128)(2,1)S(1)}, u32[]{:S(2)}, u32[]{:S(2)}) collective-permute-start(bf16[256,512]{1,0:T(8,128)(2,1)S(1)} %get-tuple-element.34.refs_1_), channel_id=1, source_target_pairs={{0,2},{1,3},{2,0},{3,1},{4,6},{5,7},{6,4},{7,5},{8,10},{9,11},{10,... | collective-permute-start | bytes 786440 | tf_op jit(solution)/shard_map/ppermute | solution.py:35
  14.5 10.2 %collective-permute-start.4 = (bf16[64,1024]{1,0:T(8,128)(2,1)S(1)}, bf16[64,1024]{1,0:T(8,128)(2,1)S(1)}, u32[]{:S(2)}, u32[]{:S(2)}) collective-permute-start(bf16[64,1024]{1,0:T(8,128)(2,1)S(1)} %get-tuple-element.23), channel_id=1, source_target_pairs={{0,4},{1,5},{2,6},{3,7},{4,0},{5,1},{6,2},{7,3},{8,12},{9,13},{10,... | collective-permute-start | bytes 393224 | tf_op jit(solution)/shard_map/ppermute | solution.py:35
  16.0 13.0 %collective-permute-start.5 = (bf16[64,1024]{1,0:T(8,128)(2,1)S(1)}, bf16[64,1024]{1,0:T(8,128)(2,1)S(1)}, u32[]{:S(2)}, u32[]{:S(2)}) collective-permute-start(bf16[64,1024]{1,0:T(8,128)(2,1)S(1)} %get-tuple-element.24), channel_id=1, source_target_pairs={{0,8},{1,9},{2,10},{3,11},{4,12},{5,13},{6,14},{7,15},{8,0},{9,1},... | collective-permute-start | bytes 393224 | tf_op jit(solution)/shard_map/ppermute | solution.py:35
  18.6 10.4 %collective-permute-start.6 = (bf16[64,1024]{1,0:T(8,128)(2,1)S(1)}, bf16[64,1024]{1,0:T(8,128)(2,1)S(1)}, u32[]{:S(2)}, u32[]{:S(2)}) collective-permute-start(bf16[64,1024]{1,0:T(8,128)(2,1)S(1)} %get-tuple-element.25), channel_id=1, source_target_pairs={{0,12},{1,13},{2,14},{3,15},{4,8},{5,9},{6,10},{7,11},{8,4},{9,5},... | collective-permute-start | bytes 393224 | tf_op jit(solution)/shard_map/ppermute | solution.py:35
  18.8 10.2 %copy-start.4 = (bf16[1,8192,64]{1,2,0:T(8,128)(2,1)S(1)}, bf16[1,8192,64]{1,2,0:T(8,128)(2,1)}, u32[]{:S(2)}) copy-start(bf16[1,8192,64]{1,2,0:T(8,128)(2,1)} %param.8) | copy-start | bytes 3145732
  21.1 12.4 %collective-permute-start.11 = (bf16[256,512]{1,0:T(8,128)(2,1)S(1)}, bf16[256,512]{1,0:T(8,128)(2,1)S(1)}, u32[]{:S(2)}, u32[]{:S(2)}) collective-permute-start(bf16[256,512]{1,0:T(8,128)(2,1)S(1)} %once.5), channel_id=1, source_target_pairs={{0,2},{1,3},{2,0},{3,1},{4,6},{5,7},{6,4},{7,5},{8,10},{9,11},{10,... | collective-permute-start | bytes 786440 | tf_op jit(solution)/shard_map/ppermute | solution.py:35
  22.9 11.6 %collective-permute-start.10 = (bf16[256,512]{1,0:T(8,128)(2,1)S(1)}, bf16[256,512]{1,0:T(8,128)(2,1)S(1)}, u32[]{:S(2)}, u32[]{:S(2)}) collective-permute-start(bf16[256,512]{1,0:T(8,128)(2,1)S(1)} %fusion), channel_id=1, source_target_pairs={{0,4},{1,5},{2,6},{3,7},{4,0},{5,1},{6,2},{7,3},{8,12},{9,13},{10,... | collective-permute-start | bytes 786440 | tf_op jit(solution)/shard_map/ppermute | solution.py:35
  24.7 19.0 %collective-permute-start.17 = (bf16[256,512]{1,0:T(8,128)(2,1)S(1)}, bf16[256,512]{1,0:T(8,128)(2,1)S(1)}, u32[]{:S(2)}, u32[]{:S(2)}) collective-permute-start(bf16[256,512]{1,0:T(8,128)(2,1)S(1)} %fusion.3), channel_id=1, source_target_pairs={{0,2},{1,3},{2,0},{3,1},{4,6},{5,7},{6,4},{7,5},{8,10},{9,11},{10,... | collective-permute-start | bytes 786440 | tf_op jit(solution)/shard_map/ppermute | solution.py:35
  29.0 1.6 %copy-start = (bf16[1,64,8192]{2,1,0:T(8,128)(2,1)S(1)}, bf16[1,64,8192]{2,1,0:T(8,128)(2,1)}, u32[]{:S(2)}) copy-start(bf16[1,64,8192]{2,1,0:T(8,128)(2,1)} %param.9) | copy-start | bytes 3145732
  29.4 1.2 %collective-permute-start.7 = (f32[64,64]{1,0:T(8,128)S(1)}, f32[64,64]{1,0:T(8,128)S(1)}, u32[]{:S(2)}, u32[]{:S(2)}) collective-permute-start(f32[64,64]{1,0:T(8,128)S(1)} %shrink.1.mine_ref), channel_id=1, source_target_pairs={{0,1},{1,0},{2,3},{3,2},{4,5},{5,4},{6,7},{7,6},{8,9},{9,8},{10,11... | collective-permute-start | bytes 49160 | tf_op jit(solution)/shard_map/ppermute | solution.py:35
  31.0 7.7 %collective-permute-start.12 = (bf16[2,64,512]{2,1,0:T(8,128)(2,1)S(1)}, bf16[2,64,512]{2,1,0:T(8,128)(2,1)S(1)}, u32[]{:S(2)}, u32[]{:S(2)}) collective-permute-start(bf16[2,64,512]{2,1,0:T(8,128)(2,1)S(1)} %get-tuple-element.30), channel_id=1, source_target_pairs={{0,2},{1,3},{2,0},{3,1},{4,6},{5,7},{6,4},{7,5},{8,10},{9,11},{10,... | collective-permute-start | bytes 393224 | tf_op jit(solution)/shard_map/ppermute | solution.py:35
  31.5 4.3 %collective-permute-start.13 = (bf16[1,64,512]{2,1,0:T(8,128)(2,1)S(1)}, bf16[1,64,512]{2,1,0:T(8,128)(2,1)S(1)}, u32[]{:S(2)}, u32[]{:S(2)}) collective-permute-start(bf16[1,64,512]{2,1,0:T(8,128)(2,1)S(1)} %get-tuple-element.31), channel_id=1, source_target_pairs={{0,4},{1,5},{2,6},{3,7},{4,0},{5,1},{6,2},{7,3},{8,12},{9,13},{10,... | collective-permute-start | bytes 196616 | tf_op jit(solution)/shard_map/ppermute | solution.py:35
  33.5 5.2 %collective-permute-start.14 = (bf16[1,64,512]{2,1,0:T(8,128)(2,1)S(1)}, bf16[1,64,512]{2,1,0:T(8,128)(2,1)S(1)}, u32[]{:S(2)}, u32[]{:S(2)}) collective-permute-start(bf16[1,64,512]{2,1,0:T(8,128)(2,1)S(1)} %get-tuple-element.32), channel_id=1, source_target_pairs={{0,6},{1,7},{2,4},{3,5},{4,2},{5,3},{6,0},{7,1},{8,14},{9,15},{10,... | collective-permute-start | bytes 196616 | tf_op jit(solution)/shard_map/ppermute | solution.py:35
  39.1 14.2 %collective-permute-start.15 = (bf16[256,512]{1,0:T(8,128)(2,1)S(1)}, bf16[256,512]{1,0:T(8,128)(2,1)S(1)}, u32[]{:S(2)}, u32[]{:S(2)}) collective-permute-start(bf16[256,512]{1,0:T(8,128)(2,1)S(1)} %join.7.refs_3_.refs_5_), channel_id=1, source_target_pairs={{0,8},{1,9},{2,10},{3,11},{4,12},{5,13},{6,14},{7,15},{8,0},{9,1},... | collective-permute-start | bytes 786440 | tf_op jit(solution)/shard_map/ppermute | solution.py:35
  42.0 11.4 %collective-permute-start.16 = (bf16[256,512]{1,0:T(8,128)(2,1)S(1)}, bf16[256,512]{1,0:T(8,128)(2,1)S(1)}, u32[]{:S(2)}, u32[]{:S(2)}) collective-permute-start(bf16[256,512]{1,0:T(8,128)(2,1)S(1)} %join.8), channel_id=1, source_target_pairs={{0,2},{1,3},{2,0},{3,1},{4,6},{5,7},{6,4},{7,5},{8,10},{9,11},{10,... | collective-permute-start | bytes 786440 | tf_op jit(solution)/shard_map/ppermute | solution.py:35
  44.0 11.0 %collective-permute-start.18 = (bf16[256,512]{1,0:T(8,128)(2,1)S(1)}, bf16[256,512]{1,0:T(8,128)(2,1)S(1)}, u32[]{:S(2)}, u32[]{:S(2)}) collective-permute-start(bf16[256,512]{1,0:T(8,128)(2,1)S(1)} %join.9), channel_id=1, source_target_pairs={{0,4},{1,5},{2,6},{3,7},{4,0},{5,1},{6,2},{7,3},{8,12},{9,13},{10,... | collective-permute-start | bytes 786440 | tf_op jit(solution)/shard_map/ppermute | solution.py:35

commit v14 on v13

--- a/solution.py
+++ b/solution.py
@@ -282,27 +282,29 @@
     y1 = swap(go1, 2)[None]
     mine = shrink(down, down_other, arrived)
     groups = ((8, 4, 2, 0), (10, 6), (12,), (14,))
-    here, over2, over4, over6 = grow(mine, swap(mine, 1), up, up_other, groups, came)
-    over2, over4, over6 = swap(over2, 2), swap(over4, 4), swap(over6, 6)
+    here, over2, over4, over6 = grow(mine, swap(mine, 1), up, up_other, groups, came, y2)
+    over6, over4, over2 = swap(over6, 6), swap(over4, 4), swap(over2, 2)
     (ready2,) = join(target, [stay, came, z3, y2], ((((0, 0), (1, 0), (2, 0), (3, 0)), ()),), f32)
-    grown = [here, over2, over4, over6]
     (sum2,) = join(
-        target, [ready2[None]] + grown, ((((0, 0),), tuple((1 + i, 0, 2 * i) for i in range(4))),), bf16
+        target,
+        [ready2[None], over6, over4, over2, here],
+        ((((0, 0),), ((1, 0, 6), (2, 0, 4), (3, 0, 2), (4, 0, 0))),),
+        bf16,
     )
     z2 = swap(sum2, 8)
 
     def blocks(m):
         return ((0, chips.index(m)), (1, chips.index(m))), ((2, (4, 2, 1, 0).index(m), 0),)
 
-    (go0,) = join(target, [stay, came, here, sum2], (blocks(1),), bf16)
-    y0 = swap(go0, 2)
     sums, own = blocks(2)
     (sum1,) = join(
         target, [stay, came, here, over2, y1, sum2], ((sums + ((4, 0),), own + ((3, 1, 2),)),), bf16
     )
     z1 = swap(sum1, 4)
+    (go0,) = join(target, [stay, came, here, sum1], (blocks(1),), bf16)
+    y0 = swap(go0, 2)
     (side0,) = join(target, [stay, came, here], (blocks(0),), f32)
-    total = gather(side0, z2) + y0.astype(f32) + z1.astype(f32)
+    total = gather(gather(side0, z2), z1) + y0.astype(f32)
     return total.astype(bf16)
 
 

time: 55.9 us -> 55.2 us (0.987)
  waiting for transfers between devices: 21.6 us -> 20.9 us
    ppermute x19, waiting for transfers between devices: 21.6 us -> 20.9 us  [swap(): return lax.ppermute(value, 'tensor', [(t, t ^ mask) for t in range(count)])]
where the time goes in v14:
time: 55.2 us; the launch traced here: 55 us
  starting transfers between devices  23.5 us (43%)
  waiting for transfers between devices  20.9 us (38%)
  Pallas kernels  8.3 us (15%)
  other arithmetic  1.12 us (2%)
  local copies, waits for them, and re-layouts  1 us (2%)
    ppermute x19, starting transfers between devices, swap(): return lax.ppermute(value, 'tensor', [(t, t ^ mask) for t in range(count)])  23.5 us
    ppermute x19, waiting for transfers between devices, swap(): return lax.ppermute(value, 'tensor', [(t, t ^ mask) for t in range(count)])  20.9 us
    pallas_call x1, Pallas kernels, product(): pl.pallas_call(functools.partial(product_kernel, groups), out_shape=out_s...  4.85 us
    pallas_call x5, Pallas kernels, join(): pl.pallas_call(functools.partial(join_kernel, terms), out_shape=[shape((r...  1.45 us
    pallas_call x1, Pallas kernels, route(): pl.pallas_call(functools.partial(route_kernel, count, layers), out_shape=...  1.21 us
  transfers between devices with their start and end apart: 19, of which 9 were waited for; matrix products, arithmetic and copies ran while one was open for 1% of the time, Pallas kernels for 15%

profile of v14, /device:TPU:0, one launch (start us, length us, event | category | flops | bytes accessed | tf_op | source)
XLA Modules:
  0.0 55.0 jit_solution(8802060232471025460)
XLA Ops:
  0.0 0.5 collective-permute-start.1
  0.5 0.1 collective-permute-start.2
  0.5 3.0 %collective-permute-start = (bf16[256,512]{1,0:T(8,128)(2,1)}, bf16[256,512]{1,0:T(8,128)(2,1)S(1)}, u32[]{:S(2)}, u32[]{:S(2)}) collective-permute-start(bf16[256,512]{1,0:T(8,128)(2,1)} %own_ref.1), channel_id=1, source_target_pairs={{0,2},{1,3},{2,0},{3,1},{4,6},{5,7},{6,4},{7,5},{8,10},{9,11},{10,... | collective-permute-start | bytes 786440 | tf_op jit(solution)/shard_map/ppermute | solution.py:35
  3.5 0.0 copy-start.1
  3.5 1.0 %copy-done.1 = bf16[256,512]{1,0:T(8,128)(2,1)S(1)} copy-done((bf16[256,512]{1,0:T(8,128)(2,1)S(1)}, bf16[256,512]{1,0:T(8,128)(2,1)}, u32[]{:S(2)}) %copy-start.1) | copy-done | bytes 262168
  4.5 4.9 %product.1 = (bf16[3,256,512]{2,1,0:T(8,128)(2,1)S(1)}, f32[3,256,512]{2,1,0:T(8,128)S(1)}, bf16[5,256,512]{2,1,0:T(8,128)(2,1)S(1)}, f32[5,256,512]{2,1,0:T(8,128)S(1)}, f32[8,128]{1,0:T(8,128)S(1)}) custom-call(bf16[256,512]{1,0:T(8,128)(2,1)S(1)} %copy-done.1, bf16[512,8192]{1,0:T(8,128)(2,1)} %weight_hbm.1), custom_call_target="tpu_custom_call" | custom-call | flops 2147483648 | bytes 14680064 | tf_op jit(solution)/shard_map/product/pallas_call | solution.py:138
  9.3 0.0 copy-start.2
  9.3 0.0 copy-start.3
  9.3 0.8 %collective-permute-done.y_ref.refs_1_ = bf16[256,512]{1,0:T(8,128)(2,1)S(1)} collective-permute-done((bf16[256,512]{1,0:T(8,128)(2,1)}, bf16[256,512]{1,0:T(8,128)(2,1)S(1)}, u32[]{:S(2)}, u32[]{:S(2)}) %collective-permute-start) | collective-permute-done | bytes 262176 | tf_op jit(solution)/shard_map/ppermute | solution.py:35
  10.2 0.0 collective-permute-start.8
  10.2 0.0 collective-permute-done.1.rest_1_.other_ref
  10.2 0.0 collective-permute-done.2.rest_2_.up_other_ref
  10.2 0.0 copy-done.2
  10.2 0.0 copy-done.3
  10.2 1.2 %route.1 = (s32[1,256]{1,0:T(1,128)S(1)}, bf16[64,1024]{1,0:T(8,128)(2,1)S(1)}, bf16[64,1024]{1,0:T(8,128)(2,1)S(1)}, bf16[64,1024]{1,0:T(8,128)(2,1)S(1)}, bf16[64,1024]{1,0:T(8,128)(2,1)S(1)}) custom-call(s32[16]{0:T(128)S(1)} %copy-done.3, s32[1,256]{1,0:T(1,128)S(1)} %bitcast.26, bf16[256,512]{1,0:T(8,128)(2,1)S(1)} %copy-done.1, ...), custom_call_target="tpu_custom_call" | custom-call | flops 134217728 | bytes 1048576 | tf_op jit(solution)/shard_map/route/pallas_call | solution.py:88
  11.4 0.6 %collective-permute-start.3 = (bf16[5,256,512]{2,1,0:T(8,128)(2,1)S(1)}, bf16[5,256,512]{2,1,0:T(8,128)(2,1)S(1)}, u32[]{:S(2)}, u32[]{:S(2)}) collective-permute-start(bf16[5,256,512]{2,1,0:T(8,128)(2,1)S(1)} %once.3), channel_id=1, source_target_pairs={{0,1},{1,0},{2,3},{3,2},{4,5},{5,4},{6,7},{7,6},{8,9},{9,8},{10,11... | collective-permute-start | bytes 3932168 | tf_op jit(solution)/shard_map/ppermute | solution.py:35
  12.0 0.5 collective-permute-done.8
  12.4 0.2 fusion.2
  12.6 1.8 %collective-permute-start.10 = (bf16[256,512]{1,0:T(8,128)(2,1)S(1)}, bf16[256,512]{1,0:T(8,128)(2,1)S(1)}, u32[]{:S(2)}, u32[]{:S(2)}) collective-permute-start(bf16[256,512]{1,0:T(8,128)(2,1)S(1)} %get-tuple-element.33.refs_1_), channel_id=1, source_target_pairs={{0,2},{1,3},{2,0},{3,1},{4,6},{5,7},{6,4},{7,5},{8,10},{9,11},{10,... | collective-permute-start | bytes 786440 | tf_op jit(solution)/shard_map/ppermute | solution.py:35
  14.4 1.6 %collective-permute-start.4 = (bf16[64,1024]{1,0:T(8,128)(2,1)S(1)}, bf16[64,1024]{1,0:T(8,128)(2,1)S(1)}, u32[]{:S(2)}, u32[]{:S(2)}) collective-permute-start(bf16[64,1024]{1,0:T(8,128)(2,1)S(1)} %get-tuple-element.23), channel_id=1, source_target_pairs={{0,4},{1,5},{2,6},{3,7},{4,0},{5,1},{6,2},{7,3},{8,12},{9,13},{10,... | collective-permute-start | bytes 393224 | tf_op jit(solution)/shard_map/ppermute | solution.py:35
  16.0 2.6 %collective-permute-start.5 = (bf16[64,1024]{1,0:T(8,128)(2,1)S(1)}, bf16[64,1024]{1,0:T(8,128)(2,1)S(1)}, u32[]{:S(2)}, u32[]{:S(2)}) collective-permute-start(bf16[64,1024]{1,0:T(8,128)(2,1)S(1)} %get-tuple-element.24), channel_id=1, source_target_pairs={{0,8},{1,9},{2,10},{3,11},{4,12},{5,13},{6,14},{7,15},{8,0},{9,1},... | collective-permute-start | bytes 393224 | tf_op jit(solution)/shard_map/ppermute | solution.py:35
  18.6 0.2 collective-permute-start.6
  18.8 0.0 copy-start.4
  18.8 2.2 %collective-permute-done.10 = bf16[256,512]{1,0:T(8,128)(2,1)S(1)} collective-permute-done((bf16[256,512]{1,0:T(8,128)(2,1)S(1)}, bf16[256,512]{1,0:T(8,128)(2,1)S(1)}, u32[]{:S(2)}, u32[]{:S(2)}) %collective-permute-start.10) | collective-permute-done | bytes 262176 | tf_op jit(solution)/shard_map/ppermute | solution.py:35
  21.0 1.7 %collective-permute-start.9 = (bf16[256,512]{1,0:T(8,128)(2,1)S(1)}, bf16[256,512]{1,0:T(8,128)(2,1)S(1)}, u32[]{:S(2)}, u32[]{:S(2)}) collective-permute-start(bf16[256,512]{1,0:T(8,128)(2,1)S(1)} %once.5), channel_id=1, source_target_pairs={{0,2},{1,3},{2,0},{3,1},{4,6},{5,7},{6,4},{7,5},{8,10},{9,11},{10,... | collective-permute-start | bytes 786440 | tf_op jit(solution)/shard_map/ppermute | solution.py:35
  22.8 0.1 fusion
  22.9 0.0 collective-permute-done.3.refs_0_.refs_1_
  22.9 1.6 %collective-permute-start.11 = (bf16[256,512]{1,0:T(8,128)(2,1)S(1)}, bf16[256,512]{1,0:T(8,128)(2,1)S(1)}, u32[]{:S(2)}, u32[]{:S(2)}) collective-permute-start(bf16[256,512]{1,0:T(8,128)(2,1)S(1)} %fusion), channel_id=1, source_target_pairs={{0,4},{1,5},{2,6},{3,7},{4,0},{5,1},{6,2},{7,3},{8,12},{9,13},{10,... | collective-permute-start | bytes 786440 | tf_op jit(solution)/shard_map/ppermute | solution.py:35
  24.5 0.1 fusion.3
  24.6 0.0 collective-permute-done.4.refs_0_
  24.6 0.6 %collective-permute-start.16 = (bf16[256,512]{1,0:T(8,128)(2,1)S(1)}, bf16[256,512]{1,0:T(8,128)(2,1)S(1)}, u32[]{:S(2)}, u32[]{:S(2)}) collective-permute-start(bf16[256,512]{1,0:T(8,128)(2,1)S(1)} %fusion.3), channel_id=1, source_target_pairs={{0,2},{1,3},{2,0},{3,1},{4,6},{5,7},{6,4},{7,5},{8,10},{9,11},{10,... | collective-permute-start | bytes 786440 | tf_op jit(solution)/shard_map/ppermute | solution.py:35
  25.2 3.8 %collective-permute-done.5.refs_1_ = bf16[64,1024]{1,0:T(8,128)(2,1)S(1)} collective-permute-done((bf16[64,1024]{1,0:T(8,128)(2,1)S(1)}, bf16[64,1024]{1,0:T(8,128)(2,1)S(1)}, u32[]{:S(2)}, u32[]{:S(2)}) %collective-permute-start.5) | collective-permute-done | bytes 131104 | tf_op jit(solution)/shard_map/ppermute | solution.py:35
  29.0 0.0 collective-permute-done.6.refs_2_
  29.0 0.0 copy-done.4
  29.0 0.0 copy-start
  29.0 0.4 shrink.1.mine_ref
  29.4 0.0 collective-permute-start.7
  29.4 1.2 %collective-permute-done.7.other_ref = f32[64,64]{1,0:T(8,128)S(1)} collective-permute-done((f32[64,64]{1,0:T(8,128)S(1)}, f32[64,64]{1,0:T(8,128)S(1)}, u32[]{:S(2)}, u32[]{:S(2)}) %collective-permute-start.7) | collective-permute-done | bytes 16416 | tf_op jit(solution)/shard_map/ppermute | solution.py:35
  30.6 0.0 collective-permute-done.9
  30.6 0.0 copy-done
  30.6 0.3 grow.1
  30.9 1.5 %collective-permute-start.14 = (bf16[2,64,512]{2,1,0:T(8,128)(2,1)S(1)}, bf16[2,64,512]{2,1,0:T(8,128)(2,1)S(1)}, u32[]{:S(2)}, u32[]{:S(2)}) collective-permute-start(bf16[2,64,512]{2,1,0:T(8,128)(2,1)S(1)} %get-tuple-element.32), channel_id=1, source_target_pairs={{0,2},{1,3},{2,0},{3,1},{4,6},{5,7},{6,4},{7,5},{8,10},{9,11},{10,... | collective-permute-start | bytes 393224 | tf_op jit(solution)/shard_map/ppermute | solution.py:35
  32.4 2.0 %collective-permute-start.12 = (bf16[1,64,512]{2,1,0:T(8,128)(2,1)S(1)}, bf16[1,64,512]{2,1,0:T(8,128)(2,1)S(1)}, u32[]{:S(2)}, u32[]{:S(2)}) collective-permute-start(bf16[1,64,512]{2,1,0:T(8,128)(2,1)S(1)} %get-tuple-element.30), channel_id=1, source_target_pairs={{0,6},{1,7},{2,4},{3,5},{4,2},{5,3},{6,0},{7,1},{8,14},{9,15},{10,... | collective-permute-start | bytes 196616 | tf_op jit(solution)/shard_map/ppermute | solution.py:35
  34.4 0.1 collective-permute-start.13
  34.5 0.0 collective-permute-done.11
  34.5 0.1 join.6
  34.6 3.5 %collective-permute-done.12.refs_1_ = bf16[1,64,512]{2,1,0:T(8,128)(2,1)S(1)} collective-permute-done((bf16[1,64,512]{2,1,0:T(8,128)(2,1)S(1)}, bf16[1,64,512]{2,1,0:T(8,128)(2,1)S(1)}, u32[]{:S(2)}, u32[]{:S(2)}) %collective-permute-start.12) | collective-permute-done | bytes 65568 | tf_op jit(solution)/shard_map/ppermute | solution.py:35
  38.1 0.6 %collective-permute-done.13.refs_2_ = bf16[1,64,512]{2,1,0:T(8,128)(2,1)S(1)} collective-permute-done((bf16[1,64,512]{2,1,0:T(8,128)(2,1)S(1)}, bf16[1,64,512]{2,1,0:T(8,128)(2,1)S(1)}, u32[]{:S(2)}, u32[]{:S(2)}) %collective-permute-start.13) | collective-permute-done | bytes 65568 | tf_op jit(solution)/shard_map/ppermute | solution.py:35
  38.7 0.0 collective-permute-done.14.refs_3_
  38.7 0.5 join.7.refs_5_
  39.2 2.6 %collective-permute-start.15 = (bf16[256,512]{1,0:T(8,128)(2,1)S(1)}, bf16[256,512]{1,0:T(8,128)(2,1)S(1)}, u32[]{:S(2)}, u32[]{:S(2)}) collective-permute-start(bf16[256,512]{1,0:T(8,128)(2,1)S(1)} %join.7.refs_5_), channel_id=1, source_target_pairs={{0,8},{1,9},{2,10},{3,11},{4,12},{5,13},{6,14},{7,15},{8,0},{9,1},... | collective-permute-start | bytes 786440 | tf_op jit(solution)/shard_map/ppermute | solution.py:35
  41.7 0.0 collective-permute-done.16
  41.7 0.3 join.8.refs_3_
  42.1 1.6 %collective-permute-start.17 = (bf16[256,512]{1,0:T(8,128)(2,1)S(1)}, bf16[256,512]{1,0:T(8,128)(2,1)S(1)}, u32[]{:S(2)}, u32[]{:S(2)}) collective-permute-start(bf16[256,512]{1,0:T(8,128)(2,1)S(1)} %join.8.refs_3_), channel_id=1, source_target_pairs={{0,4},{1,5},{2,6},{3,7},{4,0},{5,1},{6,2},{7,3},{8,12},{9,13},{10,... | collective-permute-start | bytes 786440 | tf_op jit(solution)/shard_map/ppermute | solution.py:35
  43.7 0.3 join.9
  44.0 1.6 %collective-permute-start.18 = (bf16[256,512]{1,0:T(8,128)(2,1)S(1)}, bf16[256,512]{1,0:T(8,128)(2,1)S(1)}, u32[]{:S(2)}, u32[]{:S(2)}) collective-permute-start(bf16[256,512]{1,0:T(8,128)(2,1)S(1)} %join.9), channel_id=1, source_target_pairs={{0,2},{1,3},{2,0},{3,1},{4,6},{5,7},{6,4},{7,5},{8,10},{9,11},{10,... | collective-permute-start | bytes 786440 | tf_op jit(solution)/shard_map/ppermute | solution.py:35
  45.6 0.3 join.5.sum_ref
  45.8 7.7 %collective-permute-done.15.came_ref = bf16[256,512]{1,0:T(8,128)(2,1)S(1)} collective-permute-done((bf16[256,512]{1,0:T(8,128)(2,1)S(1)}, bf16[256,512]{1,0:T(8,128)(2,1)S(1)}, u32[]{:S(2)}, u32[]{:S(2)}) %collective-permute-start.15) | collective-permute-done | bytes 262176 | tf_op jit(solution)/shard_map/ppermute | solution.py:35
  53.6 0.6 %collective-permute-done.17.came_ref = bf16[256,512]{1,0:T(8,128)(2,1)S(1)} collective-permute-done((bf16[256,512]{1,0:T(8,128)(2,1)S(1)}, bf16[256,512]{1,0:T(8,128)(2,1)S(1)}, u32[]{:S(2)}, u32[]{:S(2)}) %collective-permute-start.17) | collective-permute-done | bytes 262176 | tf_op jit(solution)/shard_map/ppermute | solution.py:35
  54.2 0.0 collective-permute-done.18
  54.2 0.8 %add_convert_fusion = bf16[256,512]{1,0:T(8,128)(2,1)} fusion(f32[256,512]{1,0:T(8,128)S(1)} %gather.3, bf16[256,512]{1,0:T(8,128)(2,1)S(1)} %collective-permute-done.18), kind=kLoop, calls=%fused_computation.2 | loop fusion | flops 393216 | bytes 1048576 | tf_op jit(solution)/shard_map/convert_element_type | solution.py:308
  (5 shorter events, 0.1 us)
Async XLA Ops:
  0.0 10.2 %collective-permute-start.1 = (bf16[64,8192]{1,0:T(8,128)(2,1)}, bf16[64,8192]{1,0:T(8,128)(2,1)S(1)}, u32[]{:S(2)}, u32[]{:S(2)}) collective-permute-start(bf16[64,8192]{1,0:T(8,128)(2,1)} %bitcast.27), channel_id=1, source_target_pairs={{0,1},{1,0},{2,3},{3,2},{4,5},{5,4},{6,7},{7,6},{8,9},{9,8},{10,11... | collective-permute-start | bytes 3145736 | tf_op jit(solution)/shard_map/ppermute | solution.py:35
  0.5 9.7 %collective-permute-start.2 = (bf16[64,8192]{1,0:T(8,128)(2,1)}, bf16[64,8192]{1,0:T(8,128)(2,1)S(1)}, u32[]{:S(2)}, u32[]{:S(2)}) collective-permute-start(bf16[64,8192]{1,0:T(8,128)(2,1)} %bitcast.20), channel_id=1, source_target_pairs={{0,1},{1,0},{2,3},{3,2},{4,5},{5,4},{6,7},{7,6},{8,9},{9,8},{10,11... | collective-permute-start | bytes 3145736 | tf_op jit(solution)/shard_map/ppermute | solution.py:35
  0.5 9.6 %collective-permute-start = (bf16[256,512]{1,0:T(8,128)(2,1)}, bf16[256,512]{1,0:T(8,128)(2,1)S(1)}, u32[]{:S(2)}, u32[]{:S(2)}) collective-permute-start(bf16[256,512]{1,0:T(8,128)(2,1)} %own_ref.1), channel_id=1, source_target_pairs={{0,2},{1,3},{2,0},{3,1},{4,6},{5,7},{6,4},{7,5},{8,10},{9,11},{10,... | collective-permute-start | bytes 786440 | tf_op jit(solution)/shard_map/ppermute | solution.py:35
  3.5 1.0 %copy-start.1 = (bf16[256,512]{1,0:T(8,128)(2,1)S(1)}, bf16[256,512]{1,0:T(8,128)(2,1)}, u32[]{:S(2)}) copy-start(bf16[256,512]{1,0:T(8,128)(2,1)} %own_ref.1) | copy-start | bytes 786436
  9.3 0.9 %copy-start.2 = (s32[256]{0:T(256)S(1)}, s32[256]{0:T(256)}, u32[]{:S(2)}) copy-start(s32[256]{0:T(256)} %param.10) | copy-start | bytes 3076
  9.3 0.9 %copy-start.3 = (s32[16]{0:T(128)S(1)}, s32[16]{0:T(128)}, u32[]{:S(2)}) copy-start(s32[16]{0:T(128)} %slot_hbm.1) | copy-start | bytes 196
  10.2 2.3 %collective-permute-start.8 = (bf16[3,256,512]{2,1,0:T(8,128)(2,1)S(1)}, bf16[3,256,512]{2,1,0:T(8,128)(2,1)S(1)}, u32[]{:S(2)}, u32[]{:S(2)}) collective-permute-start(bf16[3,256,512]{2,1,0:T(8,128)(2,1)S(1)} %once.4), channel_id=1, source_target_pairs={{0,1},{1,0},{2,3},{3,2},{4,5},{5,4},{6,7},{7,6},{8,9},{9,8},{10,11... | collective-permute-start | bytes 2359304 | tf_op jit(solution)/shard_map/ppermute | solution.py:35
  11.4 11.5 %collective-permute-start.3 = (bf16[5,256,512]{2,1,0:T(8,128)(2,1)S(1)}, bf16[5,256,512]{2,1,0:T(8,128)(2,1)S(1)}, u32[]{:S(2)}, u32[]{:S(2)}) collective-permute-start(bf16[5,256,512]{2,1,0:T(8,128)(2,1)S(1)} %once.3), channel_id=1, source_target_pairs={{0,1},{1,0},{2,3},{3,2},{4,5},{5,4},{6,7},{7,6},{8,9},{9,8},{10,11... | collective-permute-start | bytes 3932168 | tf_op jit(solution)/shard_map/ppermute | solution.py:35
  12.6 8.4 %collective-permute-start.10 = (bf16[256,512]{1,0:T(8,128)(2,1)S(1)}, bf16[256,512]{1,0:T(8,128)(2,1)S(1)}, u32[]{:S(2)}, u32[]{:S(2)}) collective-permute-start(bf16[256,512]{1,0:T(8,128)(2,1)S(1)} %get-tuple-element.33.refs_1_), channel_id=1, source_target_pairs={{0,2},{1,3},{2,0},{3,1},{4,6},{5,7},{6,4},{7,5},{8,10},{9,11},{10,... | collective-permute-start | bytes 786440 | tf_op jit(solution)/shard_map/ppermute | solution.py:35
  14.4 10.2 %collective-permute-start.4 = (bf16[64,1024]{1,0:T(8,128)(2,1)S(1)}, bf16[64,1024]{1,0:T(8,128)(2,1)S(1)}, u32[]{:S(2)}, u32[]{:S(2)}) collective-permute-start(bf16[64,1024]{1,0:T(8,128)(2,1)S(1)} %get-tuple-element.23), channel_id=1, source_target_pairs={{0,4},{1,5},{2,6},{3,7},{4,0},{5,1},{6,2},{7,3},{8,12},{9,13},{10,... | collective-permute-start | bytes 393224 | tf_op jit(solution)/shard_map/ppermute | solution.py:35
  16.0 13.0 %collective-permute-start.5 = (bf16[64,1024]{1,0:T(8,128)(2,1)S(1)}, bf16[64,1024]{1,0:T(8,128)(2,1)S(1)}, u32[]{:S(2)}, u32[]{:S(2)}) collective-permute-start(bf16[64,1024]{1,0:T(8,128)(2,1)S(1)} %get-tuple-element.24), channel_id=1, source_target_pairs={{0,8},{1,9},{2,10},{3,11},{4,12},{5,13},{6,14},{7,15},{8,0},{9,1},... | collective-permute-start | bytes 393224 | tf_op jit(solution)/shard_map/ppermute | solution.py:35
  18.6 10.4 %collective-permute-start.6 = (bf16[64,1024]{1,0:T(8,128)(2,1)S(1)}, bf16[64,1024]{1,0:T(8,128)(2,1)S(1)}, u32[]{:S(2)}, u32[]{:S(2)}) collective-permute-start(bf16[64,1024]{1,0:T(8,128)(2,1)S(1)} %get-tuple-element.25), channel_id=1, source_target_pairs={{0,12},{1,13},{2,14},{3,15},{4,8},{5,9},{6,10},{7,11},{8,4},{9,5},... | collective-permute-start | bytes 393224 | tf_op jit(solution)/shard_map/ppermute | solution.py:35
  18.8 10.2 %copy-start.4 = (bf16[1,8192,64]{1,2,0:T(8,128)(2,1)S(1)}, bf16[1,8192,64]{1,2,0:T(8,128)(2,1)}, u32[]{:S(2)}) copy-start(bf16[1,8192,64]{1,2,0:T(8,128)(2,1)} %param.8) | copy-start | bytes 3145732
  21.0 9.6 %collective-permute-start.9 = (bf16[256,512]{1,0:T(8,128)(2,1)S(1)}, bf16[256,512]{1,0:T(8,128)(2,1)S(1)}, u32[]{:S(2)}, u32[]{:S(2)}) collective-permute-start(bf16[256,512]{1,0:T(8,128)(2,1)S(1)} %once.5), channel_id=1, source_target_pairs={{0,2},{1,3},{2,0},{3,1},{4,6},{5,7},{6,4},{7,5},{8,10},{9,11},{10,... | collective-permute-start | bytes 786440 | tf_op jit(solution)/shard_map/ppermute | solution.py:35
  22.9 11.6 %collective-permute-start.11 = (bf16[256,512]{1,0:T(8,128)(2,1)S(1)}, bf16[256,512]{1,0:T(8,128)(2,1)S(1)}, u32[]{:S(2)}, u32[]{:S(2)}) collective-permute-start(bf16[256,512]{1,0:T(8,128)(2,1)S(1)} %fusion), channel_id=1, source_target_pairs={{0,4},{1,5},{2,6},{3,7},{4,0},{5,1},{6,2},{7,3},{8,12},{9,13},{10,... | collective-permute-start | bytes 786440 | tf_op jit(solution)/shard_map/ppermute | solution.py:35
  24.6 17.1 %collective-permute-start.16 = (bf16[256,512]{1,0:T(8,128)(2,1)S(1)}, bf16[256,512]{1,0:T(8,128)(2,1)S(1)}, u32[]{:S(2)}, u32[]{:S(2)}) collective-permute-start(bf16[256,512]{1,0:T(8,128)(2,1)S(1)} %fusion.3), channel_id=1, source_target_pairs={{0,2},{1,3},{2,0},{3,1},{4,6},{5,7},{6,4},{7,5},{8,10},{9,11},{10,... | collective-permute-start | bytes 786440 | tf_op jit(solution)/shard_map/ppermute | solution.py:35
  29.0 1.6 %copy-start = (bf16[1,64,8192]{2,1,0:T(8,128)(2,1)S(1)}, bf16[1,64,8192]{2,1,0:T(8,128)(2,1)}, u32[]{:S(2)}) copy-start(bf16[1,64,8192]{2,1,0:T(8,128)(2,1)} %param.9) | copy-start | bytes 3145732
  29.4 1.2 %collective-permute-start.7 = (f32[64,64]{1,0:T(8,128)S(1)}, f32[64,64]{1,0:T(8,128)S(1)}, u32[]{:S(2)}, u32[]{:S(2)}) collective-permute-start(f32[64,64]{1,0:T(8,128)S(1)} %shrink.1.mine_ref), channel_id=1, source_target_pairs={{0,1},{1,0},{2,3},{3,2},{4,5},{5,4},{6,7},{7,6},{8,9},{9,8},{10,11... | collective-permute-start | bytes 49160 | tf_op jit(solution)/shard_map/ppermute | solution.py:35
  30.9 7.8 %collective-permute-start.14 = (bf16[2,64,512]{2,1,0:T(8,128)(2,1)S(1)}, bf16[2,64,512]{2,1,0:T(8,128)(2,1)S(1)}, u32[]{:S(2)}, u32[]{:S(2)}) collective-permute-start(bf16[2,64,512]{2,1,0:T(8,128)(2,1)S(1)} %get-tuple-element.32), channel_id=1, source_target_pairs={{0,2},{1,3},{2,0},{3,1},{4,6},{5,7},{6,4},{7,5},{8,10},{9,11},{10,... | collective-permute-start | bytes 393224 | tf_op jit(solution)/shard_map/ppermute | solution.py:35
  32.4 5.7 %collective-permute-start.12 = (bf16[1,64,512]{2,1,0:T(8,128)(2,1)S(1)}, bf16[1,64,512]{2,1,0:T(8,128)(2,1)S(1)}, u32[]{:S(2)}, u32[]{:S(2)}) collective-permute-start(bf16[1,64,512]{2,1,0:T(8,128)(2,1)S(1)} %get-tuple-element.30), channel_id=1, source_target_pairs={{0,6},{1,7},{2,4},{3,5},{4,2},{5,3},{6,0},{7,1},{8,14},{9,15},{10,... | collective-permute-start | bytes 196616 | tf_op jit(solution)/shard_map/ppermute | solution.py:35
  34.4 4.3 %collective-permute-start.13 = (bf16[1,64,512]{2,1,0:T(8,128)(2,1)S(1)}, bf16[1,64,512]{2,1,0:T(8,128)(2,1)S(1)}, u32[]{:S(2)}, u32[]{:S(2)}) collective-permute-start(bf16[1,64,512]{2,1,0:T(8,128)(2,1)S(1)} %get-tuple-element.31), channel_id=1, source_target_pairs={{0,4},{1,5},{2,6},{3,7},{4,0},{5,1},{6,2},{7,3},{8,12},{9,13},{10,... | collective-permute-start | bytes 196616 | tf_op jit(solution)/shard_map/ppermute | solution.py:35
  39.2 14.4 %collective-permute-start.15 = (bf16[256,512]{1,0:T(8,128)(2,1)S(1)}, bf16[256,512]{1,0:T(8,128)(2,1)S(1)}, u32[]{:S(2)}, u32[]{:S(2)}) collective-permute-start(bf16[256,512]{1,0:T(8,128)(2,1)S(1)} %join.7.refs_5_), channel_id=1, source_target_pairs={{0,8},{1,9},{2,10},{3,11},{4,12},{5,13},{6,14},{7,15},{8,0},{9,1},... | collective-permute-start | bytes 786440 | tf_op jit(solution)/shard_map/ppermute | solution.py:35
  42.1 12.1 %collective-permute-start.17 = (bf16[256,512]{1,0:T(8,128)(2,1)S(1)}, bf16[256,512]{1,0:T(8,128)(2,1)S(1)}, u32[]{:S(2)}, u32[]{:S(2)}) collective-permute-start(bf16[256,512]{1,0:T(8,128)(2,1)S(1)} %join.8.refs_3_), channel_id=1, source_target_pairs={{0,4},{1,5},{2,6},{3,7},{4,0},{5,1},{6,2},{7,3},{8,12},{9,13},{10,... | collective-permute-start | bytes 786440 | tf_op jit(solution)/shard_map/ppermute | solution.py:35
  44.0 10.3 %collective-permute-start.18 = (bf16[256,512]{1,0:T(8,128)(2,1)S(1)}, bf16[256,512]{1,0:T(8,128)(2,1)S(1)}, u32[]{:S(2)}, u32[]{:S(2)}) collective-permute-start(bf16[256,512]{1,0:T(8,128)(2,1)S(1)} %join.9), channel_id=1, source_target_pairs={{0,2},{1,3},{2,0},{3,1},{4,6},{5,7},{6,4},{7,5},{8,10},{9,11},{10,... | collective-permute-start | bytes 786440 | tf_op jit(solution)/shard_map/ppermute | solution.py:35

commit v15 on v14

--- a/solution.py
+++ b/solution.py
@@ -263,28 +263,25 @@
     up, down = adapter_up[0], jnp.swapaxes(adapter_down, 1, 2)[0]
     from_y = swap(attended, 2)
     down_other, up_other = swap(down, 1), swap(up, 1)
-    firsts, chips = (7, 6, 5), (4, 3, 2, 1, 0)
+    firsts, chips = (7, 5, 6), (4, 3, 2, 1, 0)
     away_first, stay_first, away, stay, token = product(attended, out_weight, (firsts, chips), 44)
     (away_first,) = once((away_first,), from_y)
     came_first = swap(away_first, 1)
-    first = [stay_first[i] + came_first[i].astype(f32) for i in range(3)]
     target, outgoing = route(adapter_slot, row_adapter, attended, from_y, token, down_other, up_other)
-    arrived = {k: swap(outgoing[k], 4 * k) for k in (1, 2, 3)}
+    arrived = {k: swap(outgoing[k], 4 * k) for k in (2, 3, 1)}
     arrived[0] = outgoing[0]
-    go3 = first[0].astype(bf16)
-    y3 = swap(go3, 2)
-    (go2,) = once((first[2].astype(bf16),), go3)
-    y2 = swap(go2, 2)[None]
-    z3 = swap((first[1] + y3.astype(f32)).astype(bf16), 4)[None]
+    ys = swap((stay_first[:2] + came_first[:2].astype(f32)).astype(bf16), 2)
+    last = stay_first[2] + came_first[2].astype(f32) + ys[0].astype(f32)
+    z3 = swap(last.astype(bf16), 4)[None]
     (away,) = once((away,), target)
     came = swap(away, 1)
     go1 = (stay[1] + came[1].astype(f32)).astype(bf16)
     y1 = swap(go1, 2)[None]
     mine = shrink(down, down_other, arrived)
     groups = ((8, 4, 2, 0), (10, 6), (12,), (14,))
-    here, over2, over4, over6 = grow(mine, swap(mine, 1), up, up_other, groups, came, y2)
+    here, over2, over4, over6 = grow(mine, swap(mine, 1), up, up_other, groups, came, ys)
     over6, over4, over2 = swap(over6, 6), swap(over4, 4), swap(over2, 2)
-    (ready2,) = join(target, [stay, came, z3, y2], ((((0, 0), (1, 0), (2, 0), (3, 0)), ()),), f32)
+    (ready2,) = join(target, [stay, came, z3, ys], ((((0, 0), (1, 0), (2, 0), (3, 1)), ()),), f32)
     (sum2,) = join(
         target,
         [ready2[None], over6, over4, over2, here],

time: 55.2 us -> 57.5 us (1.042)
  waiting for transfers between devices: 20.9 us -> 24.9 us
  starting transfers between devices: 23.5 us -> 21.8 us
    ppermute x19 -> x18, waiting for transfers between devices: 20.9 us -> 24.9 us  [swap(): return lax.ppermute(value, 'tensor', [(t, t ^ mask) for t in range(count)])]
    ppermute x19 -> x18, starting transfers between devices: 23.5 us -> 21.8 us  [swap(): return lax.ppermute(value, 'tensor', [(t, t ^ mask) for t in range(count)])]
  transfers between devices with their start and end apart: 19 -> 18, of which waited for: 9 -> 9; matrix products, arithmetic and copies ran while one was open for 1% -> 1% of each run, Pallas kernels for 15% -> 14%
where the time goes in v15:
time: 57.5 us; the launch traced here: 57.4 us
  waiting for transfers between devices  24.9 us (43%)
  starting transfers between devices  21.8 us (38%)
  Pallas kernels  8.29 us (14%)
  other arithmetic  1.17 us (2%)
  local copies, waits for them, and re-layouts  1.01 us (2%)
    ppermute x18, waiting for transfers between devices, swap(): return lax.ppermute(value, 'tensor', [(t, t ^ mask) for t in range(count)])  24.9 us
    ppermute x18, starting transfers between devices, swap(): return lax.ppermute(value, 'tensor', [(t, t ^ mask) for t in range(count)])  21.8 us
    pallas_call x1, Pallas kernels, product(): pl.pallas_call(functools.partial(product_kernel, groups), out_shape=out_s...  4.85 us
    pallas_call x5, Pallas kernels, join(): pl.pallas_call(functools.partial(join_kernel, terms), out_shape=[shape((r...  1.45 us
    pallas_call x1, Pallas kernels, route(): pl.pallas_call(functools.partial(route_kernel, count, layers), out_shape=...  1.21 us
  transfers between devices with their start and end apart: 18, of which 9 were waited for; matrix products, arithmetic and copies ran while one was open for 1% of the time, Pallas kernels for 14%

profile of v15, /device:TPU:0, one launch (start us, length us, event | category | flops | bytes accessed | tf_op | source)
XLA Modules:
  0.0 57.4 jit_solution(1607140538564631621)
XLA Ops:
  0.0 0.5 collective-permute-start.1
  0.5 0.1 collective-permute-start.2
  0.5 3.0 %collective-permute-start = (bf16[256,512]{1,0:T(8,128)(2,1)}, bf16[256,512]{1,0:T(8,128)(2,1)S(1)}, u32[]{:S(2)}, u32[]{:S(2)}) collective-permute-start(bf16[256,512]{1,0:T(8,128)(2,1)} %own_ref.1), channel_id=1, source_target_pairs={{0,2},{1,3},{2,0},{3,1},{4,6},{5,7},{6,4},{7,5},{8,10},{9,11},{10,... | collective-permute-start | bytes 786440 | tf_op jit(solution)/shard_map/ppermute | solution.py:35
  3.5 0.0 copy-start.1
  3.5 1.0 %copy-done.1 = bf16[256,512]{1,0:T(8,128)(2,1)S(1)} copy-done((bf16[256,512]{1,0:T(8,128)(2,1)S(1)}, bf16[256,512]{1,0:T(8,128)(2,1)}, u32[]{:S(2)}) %copy-start.1) | copy-done | bytes 262168
  4.5 4.9 %product.1 = (bf16[3,256,512]{2,1,0:T(8,128)(2,1)S(1)}, f32[3,256,512]{2,1,0:T(8,128)S(1)}, bf16[5,256,512]{2,1,0:T(8,128)(2,1)S(1)}, f32[5,256,512]{2,1,0:T(8,128)S(1)}, f32[8,128]{1,0:T(8,128)S(1)}) custom-call(bf16[256,512]{1,0:T(8,128)(2,1)S(1)} %copy-done.1, bf16[512,8192]{1,0:T(8,128)(2,1)} %weight_hbm.1), custom_call_target="tpu_custom_call" | custom-call | flops 2147483648 | bytes 14680064 | tf_op jit(solution)/shard_map/product/pallas_call | solution.py:138
  9.3 0.0 copy-start.2
  9.3 0.0 copy-start.3
  9.3 0.8 %collective-permute-done.y_ref.refs_1_ = bf16[256,512]{1,0:T(8,128)(2,1)S(1)} collective-permute-done((bf16[256,512]{1,0:T(8,128)(2,1)}, bf16[256,512]{1,0:T(8,128)(2,1)S(1)}, u32[]{:S(2)}, u32[]{:S(2)}) %collective-permute-start) | collective-permute-done | bytes 262176 | tf_op jit(solution)/shard_map/ppermute | solution.py:35
  10.2 0.0 collective-permute-start.8
  10.2 0.0 collective-permute-done.1.rest_1_.other_ref
  10.2 0.0 collective-permute-done.2.rest_2_.up_other_ref
  10.2 0.0 copy-done.2
  10.2 0.0 copy-done.3
  10.2 1.2 %route.1 = (s32[1,256]{1,0:T(1,128)S(1)}, bf16[64,1024]{1,0:T(8,128)(2,1)S(1)}, bf16[64,1024]{1,0:T(8,128)(2,1)S(1)}, bf16[64,1024]{1,0:T(8,128)(2,1)S(1)}, bf16[64,1024]{1,0:T(8,128)(2,1)S(1)}) custom-call(s32[16]{0:T(128)S(1)} %copy-done.3, s32[1,256]{1,0:T(1,128)S(1)} %bitcast.17, bf16[256,512]{1,0:T(8,128)(2,1)S(1)} %copy-done.1, ...), custom_call_target="tpu_custom_call" | custom-call | flops 134217728 | bytes 1048576 | tf_op jit(solution)/shard_map/route/pallas_call | solution.py:88
  11.4 0.6 collective-permute-start.3
  12.0 0.5 collective-permute-done.8
  12.4 0.2 add_convert_fusion
  12.6 0.0 copy-start.4
  12.7 1.8 %collective-permute-start.9 = (bf16[2,256,512]{2,1,0:T(8,128)(2,1)S(1)}, bf16[2,256,512]{2,1,0:T(8,128)(2,1)S(1)}, u32[]{:S(2)}, u32[]{:S(2)}) collective-permute-start(bf16[2,256,512]{2,1,0:T(8,128)(2,1)S(1)} %add_convert_fusion), channel_id=1, source_target_pairs={{0,2},{1,3},{2,0},{3,1},{4,6},{5,7},{6,4},{7,5},{8,10},{9,11},{10,... | collective-permute-start | bytes 1572872 | tf_op jit(solution)/shard_map/ppermute | solution.py:35
  14.5 2.6 %collective-permute-start.4 = (bf16[64,1024]{1,0:T(8,128)(2,1)S(1)}, bf16[64,1024]{1,0:T(8,128)(2,1)S(1)}, u32[]{:S(2)}, u32[]{:S(2)}) collective-permute-start(bf16[64,1024]{1,0:T(8,128)(2,1)S(1)} %get-tuple-element.23), channel_id=1, source_target_pairs={{0,8},{1,9},{2,10},{3,11},{4,12},{5,13},{6,14},{7,15},{8,0},{9,1},... | collective-permute-start | bytes 393224 | tf_op jit(solution)/shard_map/ppermute | solution.py:35
  17.1 1.3 %collective-permute-start.5 = (bf16[64,1024]{1,0:T(8,128)(2,1)S(1)}, bf16[64,1024]{1,0:T(8,128)(2,1)S(1)}, u32[]{:S(2)}, u32[]{:S(2)}) collective-permute-start(bf16[64,1024]{1,0:T(8,128)(2,1)S(1)} %get-tuple-element.24), channel_id=1, source_target_pairs={{0,12},{1,13},{2,14},{3,15},{4,8},{5,9},{6,10},{7,11},{8,4},{9,5},... | collective-permute-start | bytes 393224 | tf_op jit(solution)/shard_map/ppermute | solution.py:35
  18.4 0.2 collective-permute-start.6
  18.6 8.1 %collective-permute-done.9.refs_1_.refs_3_ = bf16[2,256,512]{2,1,0:T(8,128)(2,1)S(1)} collective-permute-done((bf16[2,256,512]{2,1,0:T(8,128)(2,1)S(1)}, bf16[2,256,512]{2,1,0:T(8,128)(2,1)S(1)}, u32[]{:S(2)}, u32[]{:S(2)}) %collective-permute-start.9) | collective-permute-done | bytes 524320 | tf_op jit(solution)/shard_map/ppermute | solution.py:35
  26.7 0.1 fusion
  26.8 1.9 %collective-permute-start.10 = (bf16[256,512]{1,0:T(8,128)(2,1)S(1)}, bf16[256,512]{1,0:T(8,128)(2,1)S(1)}, u32[]{:S(2)}, u32[]{:S(2)}) collective-permute-start(bf16[256,512]{1,0:T(8,128)(2,1)S(1)} %fusion), channel_id=1, source_target_pairs={{0,4},{1,5},{2,6},{3,7},{4,0},{5,1},{6,2},{7,3},{8,12},{9,13},{10,... | collective-permute-start | bytes 786440 | tf_op jit(solution)/shard_map/ppermute | solution.py:35
  28.7 0.0 collective-permute-done.3.refs_0_.refs_1_
  28.7 0.1 fusion.1
  28.8 1.6 %collective-permute-start.15 = (bf16[256,512]{1,0:T(8,128)(2,1)S(1)}, bf16[256,512]{1,0:T(8,128)(2,1)S(1)}, u32[]{:S(2)}, u32[]{:S(2)}) collective-permute-start(bf16[256,512]{1,0:T(8,128)(2,1)S(1)} %fusion.1), channel_id=1, source_target_pairs={{0,2},{1,3},{2,0},{3,1},{4,6},{5,7},{6,4},{7,5},{8,10},{9,11},{10,... | collective-permute-start | bytes 786440 | tf_op jit(solution)/shard_map/ppermute | solution.py:35
  30.3 0.0 collective-permute-done.4.refs_0_
  30.3 0.0 collective-permute-done.5.refs_1_
  30.4 0.0 collective-permute-done.6.refs_2_
  30.4 0.0 copy-done.4
  30.4 0.0 copy-start
  30.4 0.4 shrink.1.mine_ref
  30.8 0.0 collective-permute-start.7
  30.8 1.2 %collective-permute-done.7.other_ref = f32[64,64]{1,0:T(8,128)S(1)} collective-permute-done((f32[64,64]{1,0:T(8,128)S(1)}, f32[64,64]{1,0:T(8,128)S(1)}, u32[]{:S(2)}, u32[]{:S(2)}) %collective-permute-start.7) | collective-permute-done | bytes 16416 | tf_op jit(solution)/shard_map/ppermute | solution.py:35
  32.0 0.0 copy-done
  32.0 0.3 grow.1
  32.3 0.6 %collective-permute-start.13 = (bf16[2,64,512]{2,1,0:T(8,128)(2,1)S(1)}, bf16[2,64,512]{2,1,0:T(8,128)(2,1)S(1)}, u32[]{:S(2)}, u32[]{:S(2)}) collective-permute-start(bf16[2,64,512]{2,1,0:T(8,128)(2,1)S(1)} %get-tuple-element.32), channel_id=1, source_target_pairs={{0,2},{1,3},{2,0},{3,1},{4,6},{5,7},{6,4},{7,5},{8,10},{9,11},{10,... | collective-permute-start | bytes 393224 | tf_op jit(solution)/shard_map/ppermute | solution.py:35
  32.9 1.4 %collective-permute-start.11 = (bf16[1,64,512]{2,1,0:T(8,128)(2,1)S(1)}, bf16[1,64,512]{2,1,0:T(8,128)(2,1)S(1)}, u32[]{:S(2)}, u32[]{:S(2)}) collective-permute-start(bf16[1,64,512]{2,1,0:T(8,128)(2,1)S(1)} %get-tuple-element.30), channel_id=1, source_target_pairs={{0,6},{1,7},{2,4},{3,5},{4,2},{5,3},{6,0},{7,1},{8,14},{9,15},{10,... | collective-permute-start | bytes 196616 | tf_op jit(solution)/shard_map/ppermute | solution.py:35
  34.3 1.6 %collective-permute-start.12 = (bf16[1,64,512]{2,1,0:T(8,128)(2,1)S(1)}, bf16[1,64,512]{2,1,0:T(8,128)(2,1)S(1)}, u32[]{:S(2)}, u32[]{:S(2)}) collective-permute-start(bf16[1,64,512]{2,1,0:T(8,128)(2,1)S(1)} %get-tuple-element.31), channel_id=1, source_target_pairs={{0,4},{1,5},{2,6},{3,7},{4,0},{5,1},{6,2},{7,3},{8,12},{9,13},{10,... | collective-permute-start | bytes 196616 | tf_op jit(solution)/shard_map/ppermute | solution.py:35
  35.9 0.0 collective-permute-done.10
  35.9 0.1 join.6
  36.0 2.4 %collective-permute-done.11.refs_1_ = bf16[1,64,512]{2,1,0:T(8,128)(2,1)S(1)} collective-permute-done((bf16[1,64,512]{2,1,0:T(8,128)(2,1)S(1)}, bf16[1,64,512]{2,1,0:T(8,128)(2,1)S(1)}, u32[]{:S(2)}, u32[]{:S(2)}) %collective-permute-start.11) | collective-permute-done | bytes 65568 | tf_op jit(solution)/shard_map/ppermute | solution.py:35
  38.4 0.7 %collective-permute-done.12.refs_2_ = bf16[1,64,512]{2,1,0:T(8,128)(2,1)S(1)} collective-permute-done((bf16[1,64,512]{2,1,0:T(8,128)(2,1)S(1)}, bf16[1,64,512]{2,1,0:T(8,128)(2,1)S(1)}, u32[]{:S(2)}, u32[]{:S(2)}) %collective-permute-start.12) | collective-permute-done | bytes 65568 | tf_op jit(solution)/shard_map/ppermute | solution.py:35
  39.1 1.2 %collective-permute-done.13.refs_3_ = bf16[2,64,512]{2,1,0:T(8,128)(2,1)S(1)} collective-permute-done((bf16[2,64,512]{2,1,0:T(8,128)(2,1)S(1)}, bf16[2,64,512]{2,1,0:T(8,128)(2,1)S(1)}, u32[]{:S(2)}, u32[]{:S(2)}) %collective-permute-start.13) | collective-permute-done | bytes 131104 | tf_op jit(solution)/shard_map/ppermute | solution.py:35
  40.3 0.5 join.7.refs_5_
  40.8 2.7 %collective-permute-start.14 = (bf16[256,512]{1,0:T(8,128)(2,1)S(1)}, bf16[256,512]{1,0:T(8,128)(2,1)S(1)}, u32[]{:S(2)}, u32[]{:S(2)}) collective-permute-start(bf16[256,512]{1,0:T(8,128)(2,1)S(1)} %join.7.refs_5_), channel_id=1, source_target_pairs={{0,8},{1,9},{2,10},{3,11},{4,12},{5,13},{6,14},{7,15},{8,0},{9,1},... | collective-permute-start | bytes 786440 | tf_op jit(solution)/shard_map/ppermute | solution.py:35
  43.4 0.0 collective-permute-done.15
  43.4 0.3 join.8.refs_3_
  43.7 0.5 collective-permute-start.16
  44.3 0.3 join.9
  44.5 1.6 %collective-permute-start.17 = (bf16[256,512]{1,0:T(8,128)(2,1)S(1)}, bf16[256,512]{1,0:T(8,128)(2,1)S(1)}, u32[]{:S(2)}, u32[]{:S(2)}) collective-permute-start(bf16[256,512]{1,0:T(8,128)(2,1)S(1)} %join.9), channel_id=1, source_target_pairs={{0,2},{1,3},{2,0},{3,1},{4,6},{5,7},{6,4},{7,5},{8,10},{9,11},{10,... | collective-permute-start | bytes 786440 | tf_op jit(solution)/shard_map/ppermute | solution.py:35
  46.1 0.3 join.5.sum_ref
  46.4 8.4 %collective-permute-done.14.came_ref = bf16[256,512]{1,0:T(8,128)(2,1)S(1)} collective-permute-done((bf16[256,512]{1,0:T(8,128)(2,1)S(1)}, bf16[256,512]{1,0:T(8,128)(2,1)S(1)}, u32[]{:S(2)}, u32[]{:S(2)}) %collective-permute-start.14) | collective-permute-done | bytes 262176 | tf_op jit(solution)/shard_map/ppermute | solution.py:35
  54.8 1.7 %collective-permute-done.16.came_ref = bf16[256,512]{1,0:T(8,128)(2,1)S(1)} collective-permute-done((bf16[256,512]{1,0:T(8,128)(2,1)S(1)}, bf16[256,512]{1,0:T(8,128)(2,1)S(1)}, u32[]{:S(2)}, u32[]{:S(2)}) %collective-permute-start.16) | collective-permute-done | bytes 262176 | tf_op jit(solution)/shard_map/ppermute | solution.py:35
  56.6 0.0 collective-permute-done.17
  56.6 0.8 %add_convert_fusion.1 = bf16[256,512]{1,0:T(8,128)(2,1)} fusion(f32[256,512]{1,0:T(8,128)S(1)} %gather.3, bf16[256,512]{1,0:T(8,128)(2,1)S(1)} %collective-permute-done.17), kind=kLoop, calls=%fused_computation.1 | loop fusion | flops 393216 | bytes 1048576 | tf_op jit(solution)/shard_map/convert_element_type | solution.py:305
  (4 shorter events, 0.1 us)
Async XLA Ops:
  0.0 10.2 %collective-permute-start.1 = (bf16[64,8192]{1,0:T(8,128)(2,1)}, bf16[64,8192]{1,0:T(8,128)(2,1)S(1)}, u32[]{:S(2)}, u32[]{:S(2)}) collective-permute-start(bf16[64,8192]{1,0:T(8,128)(2,1)} %bitcast.18), channel_id=1, source_target_pairs={{0,1},{1,0},{2,3},{3,2},{4,5},{5,4},{6,7},{7,6},{8,9},{9,8},{10,11... | collective-permute-start | bytes 3145736 | tf_op jit(solution)/shard_map/ppermute | solution.py:35
  0.5 9.7 %collective-permute-start.2 = (bf16[64,8192]{1,0:T(8,128)(2,1)}, bf16[64,8192]{1,0:T(8,128)(2,1)S(1)}, u32[]{:S(2)}, u32[]{:S(2)}) collective-permute-start(bf16[64,8192]{1,0:T(8,128)(2,1)} %bitcast.13), channel_id=1, source_target_pairs={{0,1},{1,0},{2,3},{3,2},{4,5},{5,4},{6,7},{7,6},{8,9},{9,8},{10,11... | collective-permute-start | bytes 3145736 | tf_op jit(solution)/shard_map/ppermute | solution.py:35
  0.5 9.6 %collective-permute-start = (bf16[256,512]{1,0:T(8,128)(2,1)}, bf16[256,512]{1,0:T(8,128)(2,1)S(1)}, u32[]{:S(2)}, u32[]{:S(2)}) collective-permute-start(bf16[256,512]{1,0:T(8,128)(2,1)} %own_ref.1), channel_id=1, source_target_pairs={{0,2},{1,3},{2,0},{3,1},{4,6},{5,7},{6,4},{7,5},{8,10},{9,11},{10,... | collective-permute-start | bytes 786440 | tf_op jit(solution)/shard_map/ppermute | solution.py:35
  3.5 1.0 %copy-start.1 = (bf16[256,512]{1,0:T(8,128)(2,1)S(1)}, bf16[256,512]{1,0:T(8,128)(2,1)}, u32[]{:S(2)}) copy-start(bf16[256,512]{1,0:T(8,128)(2,1)} %own_ref.1) | copy-start | bytes 786436
  9.3 0.9 %copy-start.2 = (s32[256]{0:T(256)S(1)}, s32[256]{0:T(256)}, u32[]{:S(2)}) copy-start(s32[256]{0:T(256)} %param.10) | copy-start | bytes 3076
  9.3 0.9 %copy-start.3 = (s32[16]{0:T(128)S(1)}, s32[16]{0:T(128)}, u32[]{:S(2)}) copy-start(s32[16]{0:T(128)} %slot_hbm.1) | copy-start | bytes 196
  10.2 2.3 %collective-permute-start.8 = (bf16[3,256,512]{2,1,0:T(8,128)(2,1)S(1)}, bf16[3,256,512]{2,1,0:T(8,128)(2,1)S(1)}, u32[]{:S(2)}, u32[]{:S(2)}) collective-permute-start(bf16[3,256,512]{2,1,0:T(8,128)(2,1)S(1)} %once.3), channel_id=1, source_target_pairs={{0,1},{1,0},{2,3},{3,2},{4,5},{5,4},{6,7},{7,6},{8,9},{9,8},{10,11... | collective-permute-start | bytes 2359304 | tf_op jit(solution)/shard_map/ppermute | solution.py:35
  11.4 17.3 %collective-permute-start.3 = (bf16[5,256,512]{2,1,0:T(8,128)(2,1)S(1)}, bf16[5,256,512]{2,1,0:T(8,128)(2,1)S(1)}, u32[]{:S(2)}, u32[]{:S(2)}) collective-permute-start(bf16[5,256,512]{2,1,0:T(8,128)(2,1)S(1)} %once.2), channel_id=1, source_target_pairs={{0,1},{1,0},{2,3},{3,2},{4,5},{5,4},{6,7},{7,6},{8,9},{9,8},{10,11... | collective-permute-start | bytes 3932168 | tf_op jit(solution)/shard_map/ppermute | solution.py:35
  12.6 17.7 %copy-start.4 = (bf16[1,8192,64]{1,2,0:T(8,128)(2,1)S(1)}, bf16[1,8192,64]{1,2,0:T(8,128)(2,1)}, u32[]{:S(2)}) copy-start(bf16[1,8192,64]{1,2,0:T(8,128)(2,1)} %param.8) | copy-start | bytes 3145732
  12.7 14.0 %collective-permute-start.9 = (bf16[2,256,512]{2,1,0:T(8,128)(2,1)S(1)}, bf16[2,256,512]{2,1,0:T(8,128)(2,1)S(1)}, u32[]{:S(2)}, u32[]{:S(2)}) collective-permute-start(bf16[2,256,512]{2,1,0:T(8,128)(2,1)S(1)} %add_convert_fusion), channel_id=1, source_target_pairs={{0,2},{1,3},{2,0},{3,1},{4,6},{5,7},{6,4},{7,5},{8,10},{9,11},{10,... | collective-permute-start | bytes 1572872 | tf_op jit(solution)/shard_map/ppermute | solution.py:35
  14.5 15.9 %collective-permute-start.4 = (bf16[64,1024]{1,0:T(8,128)(2,1)S(1)}, bf16[64,1024]{1,0:T(8,128)(2,1)S(1)}, u32[]{:S(2)}, u32[]{:S(2)}) collective-permute-start(bf16[64,1024]{1,0:T(8,128)(2,1)S(1)} %get-tuple-element.23), channel_id=1, source_target_pairs={{0,8},{1,9},{2,10},{3,11},{4,12},{5,13},{6,14},{7,15},{8,0},{9,1},... | collective-permute-start | bytes 393224 | tf_op jit(solution)/shard_map/ppermute | solution.py:35
  17.1 13.3 %collective-permute-start.5 = (bf16[64,1024]{1,0:T(8,128)(2,1)S(1)}, bf16[64,1024]{1,0:T(8,128)(2,1)S(1)}, u32[]{:S(2)}, u32[]{:S(2)}) collective-permute-start(bf16[64,1024]{1,0:T(8,128)(2,1)S(1)} %get-tuple-element.24), channel_id=1, source_target_pairs={{0,12},{1,13},{2,14},{3,15},{4,8},{5,9},{6,10},{7,11},{8,4},{9,5},... | collective-permute-start | bytes 393224 | tf_op jit(solution)/shard_map/ppermute | solution.py:35
  18.4 11.9 %collective-permute-start.6 = (bf16[64,1024]{1,0:T(8,128)(2,1)S(1)}, bf16[64,1024]{1,0:T(8,128)(2,1)S(1)}, u32[]{:S(2)}, u32[]{:S(2)}) collective-permute-start(bf16[64,1024]{1,0:T(8,128)(2,1)S(1)} %get-tuple-element.25), channel_id=1, source_target_pairs={{0,4},{1,5},{2,6},{3,7},{4,0},{5,1},{6,2},{7,3},{8,12},{9,13},{10,... | collective-permute-start | bytes 393224 | tf_op jit(solution)/shard_map/ppermute | solution.py:35
  26.8 9.1 %collective-permute-start.10 = (bf16[256,512]{1,0:T(8,128)(2,1)S(1)}, bf16[256,512]{1,0:T(8,128)(2,1)S(1)}, u32[]{:S(2)}, u32[]{:S(2)}) collective-permute-start(bf16[256,512]{1,0:T(8,128)(2,1)S(1)} %fusion), channel_id=1, source_target_pairs={{0,4},{1,5},{2,6},{3,7},{4,0},{5,1},{6,2},{7,3},{8,12},{9,13},{10,... | collective-permute-start | bytes 786440 | tf_op jit(solution)/shard_map/ppermute | solution.py:35
  28.8 14.6 %collective-permute-start.15 = (bf16[256,512]{1,0:T(8,128)(2,1)S(1)}, bf16[256,512]{1,0:T(8,128)(2,1)S(1)}, u32[]{:S(2)}, u32[]{:S(2)}) collective-permute-start(bf16[256,512]{1,0:T(8,128)(2,1)S(1)} %fusion.1), channel_id=1, source_target_pairs={{0,2},{1,3},{2,0},{3,1},{4,6},{5,7},{6,4},{7,5},{8,10},{9,11},{10,... | collective-permute-start | bytes 786440 | tf_op jit(solution)/shard_map/ppermute | solution.py:35
  30.4 1.6 %copy-start = (bf16[1,64,8192]{2,1,0:T(8,128)(2,1)S(1)}, bf16[1,64,8192]{2,1,0:T(8,128)(2,1)}, u32[]{:S(2)}) copy-start(bf16[1,64,8192]{2,1,0:T(8,128)(2,1)} %param.9) | copy-start | bytes 3145732
  30.8 1.2 %collective-permute-start.7 = (f32[64,64]{1,0:T(8,128)S(1)}, f32[64,64]{1,0:T(8,128)S(1)}, u32[]{:S(2)}, u32[]{:S(2)}) collective-permute-start(f32[64,64]{1,0:T(8,128)S(1)} %shrink.1.mine_ref), channel_id=1, source_target_pairs={{0,1},{1,0},{2,3},{3,2},{4,5},{5,4},{6,7},{7,6},{8,9},{9,8},{10,11... | collective-permute-start | bytes 49160 | tf_op jit(solution)/shard_map/ppermute | solution.py:35
  32.3 8.0 %collective-permute-start.13 = (bf16[2,64,512]{2,1,0:T(8,128)(2,1)S(1)}, bf16[2,64,512]{2,1,0:T(8,128)(2,1)S(1)}, u32[]{:S(2)}, u32[]{:S(2)}) collective-permute-start(bf16[2,64,512]{2,1,0:T(8,128)(2,1)S(1)} %get-tuple-element.32), channel_id=1, source_target_pairs={{0,2},{1,3},{2,0},{3,1},{4,6},{5,7},{6,4},{7,5},{8,10},{9,11},{10,... | collective-permute-start | bytes 393224 | tf_op jit(solution)/shard_map/ppermute | solution.py:35
  32.9 5.5 %collective-permute-start.11 = (bf16[1,64,512]{2,1,0:T(8,128)(2,1)S(1)}, bf16[1,64,512]{2,1,0:T(8,128)(2,1)S(1)}, u32[]{:S(2)}, u32[]{:S(2)}) collective-permute-start(bf16[1,64,512]{2,1,0:T(8,128)(2,1)S(1)} %get-tuple-element.30), channel_id=1, source_target_pairs={{0,6},{1,7},{2,4},{3,5},{4,2},{5,3},{6,0},{7,1},{8,14},{9,15},{10,... | collective-permute-start | bytes 196616 | tf_op jit(solution)/shard_map/ppermute | solution.py:35
  34.3 4.8 %collective-permute-start.12 = (bf16[1,64,512]{2,1,0:T(8,128)(2,1)S(1)}, bf16[1,64,512]{2,1,0:T(8,128)(2,1)S(1)}, u32[]{:S(2)}, u32[]{:S(2)}) collective-permute-start(bf16[1,64,512]{2,1,0:T(8,128)(2,1)S(1)} %get-tuple-element.31), channel_id=1, source_target_pairs={{0,4},{1,5},{2,6},{3,7},{4,0},{5,1},{6,2},{7,3},{8,12},{9,13},{10,... | collective-permute-start | bytes 196616 | tf_op jit(solution)/shard_map/ppermute | solution.py:35
  40.8 14.0 %collective-permute-start.14 = (bf16[256,512]{1,0:T(8,128)(2,1)S(1)}, bf16[256,512]{1,0:T(8,128)(2,1)S(1)}, u32[]{:S(2)}, u32[]{:S(2)}) collective-permute-start(bf16[256,512]{1,0:T(8,128)(2,1)S(1)} %join.7.refs_5_), channel_id=1, source_target_pairs={{0,8},{1,9},{2,10},{3,11},{4,12},{5,13},{6,14},{7,15},{8,0},{9,1},... | collective-permute-start | bytes 786440 | tf_op jit(solution)/shard_map/ppermute | solution.py:35
  43.7 12.8 %collective-permute-start.16 = (bf16[256,512]{1,0:T(8,128)(2,1)S(1)}, bf16[256,512]{1,0:T(8,128)(2,1)S(1)}, u32[]{:S(2)}, u32[]{:S(2)}) collective-permute-start(bf16[256,512]{1,0:T(8,128)(2,1)S(1)} %join.8.refs_3_), channel_id=1, source_target_pairs={{0,4},{1,5},{2,6},{3,7},{4,0},{5,1},{6,2},{7,3},{8,12},{9,13},{10,... | collective-permute-start | bytes 786440 | tf_op jit(solution)/shard_map/ppermute | solution.py:35
  44.5 12.0 %collective-permute-start.17 = (bf16[256,512]{1,0:T(8,128)(2,1)S(1)}, bf16[256,512]{1,0:T(8,128)(2,1)S(1)}, u32[]{:S(2)}, u32[]{:S(2)}) collective-permute-start(bf16[256,512]{1,0:T(8,128)(2,1)S(1)} %join.9), channel_id=1, source_target_pairs={{0,2},{1,3},{2,0},{3,1},{4,6},{5,7},{6,4},{7,5},{8,10},{9,11},{10,... | collective-permute-start | bytes 786440 | tf_op jit(solution)/shard_map/ppermute | solution.py:35

commit v16 on v14

--- a/solution.py
+++ b/solution.py
@@ -269,7 +269,7 @@
     came_first = swap(away_first, 1)
     first = [stay_first[i] + came_first[i].astype(f32) for i in range(3)]
     target, outgoing = route(adapter_slot, row_adapter, attended, from_y, token, down_other, up_other)
-    arrived = {k: swap(outgoing[k], 4 * k) for k in (1, 2, 3)}
+    arrived = {k: swap(outgoing[k], 4 * k) for k in (2, 3, 1)}
     arrived[0] = outgoing[0]
     go3 = first[0].astype(bf16)
     y3 = swap(go3, 2)

time: 55.2 us -> 55.4 us (level)
  transfers between devices with their start and end apart: 19 -> 19, of which waited for: 9 -> 11; matrix products, arithmetic and copies ran while one was open for 1% -> 1% of each run, Pallas kernels for 15% -> 15%
where the time goes in v16:
time: 55.4 us; the launch traced here: 55.2 us
  starting transfers between devices  23.3 us (42%)
  waiting for transfers between devices  21.3 us (38%)
  Pallas kernels  8.29 us (15%)
  other arithmetic  1.13 us (2%)
  local copies, waits for them, and re-layouts  1 us (2%)
    ppermute x19, starting transfers between devices, swap(): return lax.ppermute(value, 'tensor', [(t, t ^ mask) for t in range(count)])  23.3 us
    ppermute x19, waiting for transfers between devices, swap(): return lax.ppermute(value, 'tensor', [(t, t ^ mask) for t in range(count)])  21.3 us
    pallas_call x1, Pallas kernels, product(): pl.pallas_call(functools.partial(product_kernel, groups), out_shape=out_s...  4.85 us
    pallas_call x5, Pallas kernels, join(): pl.pallas_call(functools.partial(join_kernel, terms), out_shape=[shape((r...  1.45 us
    pallas_call x1, Pallas kernels, route(): pl.pallas_call(functools.partial(route_kernel, count, layers), out_shape=...  1.21 us
  transfers between devices with their start and end apart: 19, of which 11 were waited for; matrix products, arithmetic and copies ran while one was open for 1% of the time, Pallas kernels for 15%

profile of v16, /device:TPU:0, one launch (start us, length us, event | category | flops | bytes accessed | tf_op | source)
XLA Modules:
  0.0 55.2 jit_solution(2623907211925998465)
XLA Ops:
  0.0 0.5 collective-permute-start.1
  0.5 0.1 collective-permute-start.2
  0.5 3.0 %collective-permute-start = (bf16[256,512]{1,0:T(8,128)(2,1)}, bf16[256,512]{1,0:T(8,128)(2,1)S(1)}, u32[]{:S(2)}, u32[]{:S(2)}) collective-permute-start(bf16[256,512]{1,0:T(8,128)(2,1)} %own_ref.1), channel_id=1, source_target_pairs={{0,2},{1,3},{2,0},{3,1},{4,6},{5,7},{6,4},{7,5},{8,10},{9,11},{10,... | collective-permute-start | bytes 786440 | tf_op jit(solution)/shard_map/ppermute | solution.py:35
  3.5 0.0 copy-start.1
  3.5 1.0 %copy-done.1 = bf16[256,512]{1,0:T(8,128)(2,1)S(1)} copy-done((bf16[256,512]{1,0:T(8,128)(2,1)S(1)}, bf16[256,512]{1,0:T(8,128)(2,1)}, u32[]{:S(2)}) %copy-start.1) | copy-done | bytes 262168
  4.5 4.9 %product.1 = (bf16[3,256,512]{2,1,0:T(8,128)(2,1)S(1)}, f32[3,256,512]{2,1,0:T(8,128)S(1)}, bf16[5,256,512]{2,1,0:T(8,128)(2,1)S(1)}, f32[5,256,512]{2,1,0:T(8,128)S(1)}, f32[8,128]{1,0:T(8,128)S(1)}) custom-call(bf16[256,512]{1,0:T(8,128)(2,1)S(1)} %copy-done.1, bf16[512,8192]{1,0:T(8,128)(2,1)} %weight_hbm.1), custom_call_target="tpu_custom_call" | custom-call | flops 2147483648 | bytes 14680064 | tf_op jit(solution)/shard_map/product/pallas_call | solution.py:138
  9.3 0.0 copy-start.2
  9.3 0.0 copy-start.3
  9.3 0.8 %collective-permute-done.y_ref.refs_1_ = bf16[256,512]{1,0:T(8,128)(2,1)S(1)} collective-permute-done((bf16[256,512]{1,0:T(8,128)(2,1)}, bf16[256,512]{1,0:T(8,128)(2,1)S(1)}, u32[]{:S(2)}, u32[]{:S(2)}) %collective-permute-start) | collective-permute-done | bytes 262176 | tf_op jit(solution)/shard_map/ppermute | solution.py:35
  10.2 0.0 collective-permute-start.8
  10.2 0.0 collective-permute-done.1.rest_1_.other_ref
  10.2 0.0 collective-permute-done.2.rest_2_.up_other_ref
  10.2 0.0 copy-done.2
  10.2 0.0 copy-done.3
  10.2 1.2 %route.1 = (s32[1,256]{1,0:T(1,128)S(1)}, bf16[64,1024]{1,0:T(8,128)(2,1)S(1)}, bf16[64,1024]{1,0:T(8,128)(2,1)S(1)}, bf16[64,1024]{1,0:T(8,128)(2,1)S(1)}, bf16[64,1024]{1,0:T(8,128)(2,1)S(1)}) custom-call(s32[16]{0:T(128)S(1)} %copy-done.3, s32[1,256]{1,0:T(1,128)S(1)} %bitcast.26, bf16[256,512]{1,0:T(8,128)(2,1)S(1)} %copy-done.1, ...), custom_call_target="tpu_custom_call" | custom-call | flops 134217728 | bytes 1048576 | tf_op jit(solution)/shard_map/route/pallas_call | solution.py:88
  11.4 0.6 %collective-permute-start.3 = (bf16[5,256,512]{2,1,0:T(8,128)(2,1)S(1)}, bf16[5,256,512]{2,1,0:T(8,128)(2,1)S(1)}, u32[]{:S(2)}, u32[]{:S(2)}) collective-permute-start(bf16[5,256,512]{2,1,0:T(8,128)(2,1)S(1)} %once.3), channel_id=1, source_target_pairs={{0,1},{1,0},{2,3},{3,2},{4,5},{5,4},{6,7},{7,6},{8,9},{9,8},{10,11... | collective-permute-start | bytes 3932168 | tf_op jit(solution)/shard_map/ppermute | solution.py:35
  12.0 0.5 collective-permute-done.8
  12.4 0.2 fusion.2
  12.6 1.8 %collective-permute-start.10 = (bf16[256,512]{1,0:T(8,128)(2,1)S(1)}, bf16[256,512]{1,0:T(8,128)(2,1)S(1)}, u32[]{:S(2)}, u32[]{:S(2)}) collective-permute-start(bf16[256,512]{1,0:T(8,128)(2,1)S(1)} %get-tuple-element.33.refs_1_), channel_id=1, source_target_pairs={{0,2},{1,3},{2,0},{3,1},{4,6},{5,7},{6,4},{7,5},{8,10},{9,11},{10,... | collective-permute-start | bytes 786440 | tf_op jit(solution)/shard_map/ppermute | solution.py:35
  14.4 2.6 %collective-permute-start.4 = (bf16[64,1024]{1,0:T(8,128)(2,1)S(1)}, bf16[64,1024]{1,0:T(8,128)(2,1)S(1)}, u32[]{:S(2)}, u32[]{:S(2)}) collective-permute-start(bf16[64,1024]{1,0:T(8,128)(2,1)S(1)} %get-tuple-element.23), channel_id=1, source_target_pairs={{0,8},{1,9},{2,10},{3,11},{4,12},{5,13},{6,14},{7,15},{8,0},{9,1},... | collective-permute-start | bytes 393224 | tf_op jit(solution)/shard_map/ppermute | solution.py:35
  17.0 1.3 %collective-permute-start.5 = (bf16[64,1024]{1,0:T(8,128)(2,1)S(1)}, bf16[64,1024]{1,0:T(8,128)(2,1)S(1)}, u32[]{:S(2)}, u32[]{:S(2)}) collective-permute-start(bf16[64,1024]{1,0:T(8,128)(2,1)S(1)} %get-tuple-element.24), channel_id=1, source_target_pairs={{0,12},{1,13},{2,14},{3,15},{4,8},{5,9},{6,10},{7,11},{8,4},{9,5},... | collective-permute-start | bytes 393224 | tf_op jit(solution)/shard_map/ppermute | solution.py:35
  18.4 0.2 collective-permute-start.6
  18.6 0.0 copy-start.4
  18.6 2.4 %collective-permute-done.10 = bf16[256,512]{1,0:T(8,128)(2,1)S(1)} collective-permute-done((bf16[256,512]{1,0:T(8,128)(2,1)S(1)}, bf16[256,512]{1,0:T(8,128)(2,1)S(1)}, u32[]{:S(2)}, u32[]{:S(2)}) %collective-permute-start.10) | collective-permute-done | bytes 262176 | tf_op jit(solution)/shard_map/ppermute | solution.py:35
  21.0 1.7 %collective-permute-start.9 = (bf16[256,512]{1,0:T(8,128)(2,1)S(1)}, bf16[256,512]{1,0:T(8,128)(2,1)S(1)}, u32[]{:S(2)}, u32[]{:S(2)}) collective-permute-start(bf16[256,512]{1,0:T(8,128)(2,1)S(1)} %once.5), channel_id=1, source_target_pairs={{0,2},{1,3},{2,0},{3,1},{4,6},{5,7},{6,4},{7,5},{8,10},{9,11},{10,... | collective-permute-start | bytes 786440 | tf_op jit(solution)/shard_map/ppermute | solution.py:35
  22.8 0.1 fusion
  22.9 0.0 collective-permute-done.3.refs_0_.refs_1_
  22.9 1.6 %collective-permute-start.11 = (bf16[256,512]{1,0:T(8,128)(2,1)S(1)}, bf16[256,512]{1,0:T(8,128)(2,1)S(1)}, u32[]{:S(2)}, u32[]{:S(2)}) collective-permute-start(bf16[256,512]{1,0:T(8,128)(2,1)S(1)} %fusion), channel_id=1, source_target_pairs={{0,4},{1,5},{2,6},{3,7},{4,0},{5,1},{6,2},{7,3},{8,12},{9,13},{10,... | collective-permute-start | bytes 786440 | tf_op jit(solution)/shard_map/ppermute | solution.py:35
  24.5 0.1 fusion.3
  24.6 2.7 %collective-permute-done.4.refs_0_ = bf16[64,1024]{1,0:T(8,128)(2,1)S(1)} collective-permute-done((bf16[64,1024]{1,0:T(8,128)(2,1)S(1)}, bf16[64,1024]{1,0:T(8,128)(2,1)S(1)}, u32[]{:S(2)}, u32[]{:S(2)}) %collective-permute-start.4) | collective-permute-done | bytes 131104 | tf_op jit(solution)/shard_map/ppermute | solution.py:35
  27.4 0.3 collective-permute-start.16
  27.6 0.0 collective-permute-done.5.refs_1_
  27.6 1.2 %collective-permute-done.6.refs_2_ = bf16[64,1024]{1,0:T(8,128)(2,1)S(1)} collective-permute-done((bf16[64,1024]{1,0:T(8,128)(2,1)S(1)}, bf16[64,1024]{1,0:T(8,128)(2,1)S(1)}, u32[]{:S(2)}, u32[]{:S(2)}) %collective-permute-start.6) | collective-permute-done | bytes 131104 | tf_op jit(solution)/shard_map/ppermute | solution.py:35
  28.8 0.0 copy-done.4
  28.8 0.0 copy-start
  28.8 0.4 shrink.1.mine_ref
  29.2 0.0 collective-permute-start.7
  29.2 1.2 %collective-permute-done.7.other_ref = f32[64,64]{1,0:T(8,128)S(1)} collective-permute-done((f32[64,64]{1,0:T(8,128)S(1)}, f32[64,64]{1,0:T(8,128)S(1)}, u32[]{:S(2)}, u32[]{:S(2)}) %collective-permute-start.7) | collective-permute-done | bytes 16416 | tf_op jit(solution)/shard_map/ppermute | solution.py:35
  30.5 0.0 collective-permute-done.9
  30.5 0.0 copy-done
  30.5 0.3 grow.1
  30.8 1.6 %collective-permute-start.14 = (bf16[2,64,512]{2,1,0:T(8,128)(2,1)S(1)}, bf16[2,64,512]{2,1,0:T(8,128)(2,1)S(1)}, u32[]{:S(2)}, u32[]{:S(2)}) collective-permute-start(bf16[2,64,512]{2,1,0:T(8,128)(2,1)S(1)} %get-tuple-element.32), channel_id=1, source_target_pairs={{0,2},{1,3},{2,0},{3,1},{4,6},{5,7},{6,4},{7,5},{8,10},{9,11},{10,... | collective-permute-start | bytes 393224 | tf_op jit(solution)/shard_map/ppermute | solution.py:35
  32.4 1.1 %collective-permute-start.12 = (bf16[1,64,512]{2,1,0:T(8,128)(2,1)S(1)}, bf16[1,64,512]{2,1,0:T(8,128)(2,1)S(1)}, u32[]{:S(2)}, u32[]{:S(2)}) collective-permute-start(bf16[1,64,512]{2,1,0:T(8,128)(2,1)S(1)} %get-tuple-element.30), channel_id=1, source_target_pairs={{0,6},{1,7},{2,4},{3,5},{4,2},{5,3},{6,0},{7,1},{8,14},{9,15},{10,... | collective-permute-start | bytes 196616 | tf_op jit(solution)/shard_map/ppermute | solution.py:35
  33.5 0.8 %collective-permute-start.13 = (bf16[1,64,512]{2,1,0:T(8,128)(2,1)S(1)}, bf16[1,64,512]{2,1,0:T(8,128)(2,1)S(1)}, u32[]{:S(2)}, u32[]{:S(2)}) collective-permute-start(bf16[1,64,512]{2,1,0:T(8,128)(2,1)S(1)} %get-tuple-element.31), channel_id=1, source_target_pairs={{0,4},{1,5},{2,6},{3,7},{4,0},{5,1},{6,2},{7,3},{8,12},{9,13},{10,... | collective-permute-start | bytes 196616 | tf_op jit(solution)/shard_map/ppermute | solution.py:35
  34.3 0.0 collective-permute-done.11
  34.3 0.1 join.6
  34.4 3.2 %collective-permute-done.12.refs_1_ = bf16[1,64,512]{2,1,0:T(8,128)(2,1)S(1)} collective-permute-done((bf16[1,64,512]{2,1,0:T(8,128)(2,1)S(1)}, bf16[1,64,512]{2,1,0:T(8,128)(2,1)S(1)}, u32[]{:S(2)}, u32[]{:S(2)}) %collective-permute-start.12) | collective-permute-done | bytes 65568 | tf_op jit(solution)/shard_map/ppermute | solution.py:35
  37.6 0.1 collective-permute-done.13.refs_2_
  37.7 0.6 %collective-permute-done.14.refs_3_ = bf16[2,64,512]{2,1,0:T(8,128)(2,1)S(1)} collective-permute-done((bf16[2,64,512]{2,1,0:T(8,128)(2,1)S(1)}, bf16[2,64,512]{2,1,0:T(8,128)(2,1)S(1)}, u32[]{:S(2)}, u32[]{:S(2)}) %collective-permute-start.14) | collective-permute-done | bytes 131104 | tf_op jit(solution)/shard_map/ppermute | solution.py:35
  38.4 0.5 join.7.refs_5_
  38.8 2.9 %collective-permute-start.15 = (bf16[256,512]{1,0:T(8,128)(2,1)S(1)}, bf16[256,512]{1,0:T(8,128)(2,1)S(1)}, u32[]{:S(2)}, u32[]{:S(2)}) collective-permute-start(bf16[256,512]{1,0:T(8,128)(2,1)S(1)} %join.7.refs_5_), channel_id=1, source_target_pairs={{0,8},{1,9},{2,10},{3,11},{4,12},{5,13},{6,14},{7,15},{8,0},{9,1},... | collective-permute-start | bytes 786440 | tf_op jit(solution)/shard_map/ppermute | solution.py:35
  41.7 0.0 collective-permute-done.16
  41.7 0.3 join.8.refs_3_
  42.1 1.6 %collective-permute-start.17 = (bf16[256,512]{1,0:T(8,128)(2,1)S(1)}, bf16[256,512]{1,0:T(8,128)(2,1)S(1)}, u32[]{:S(2)}, u32[]{:S(2)}) collective-permute-start(bf16[256,512]{1,0:T(8,128)(2,1)S(1)} %join.8.refs_3_), channel_id=1, source_target_pairs={{0,4},{1,5},{2,6},{3,7},{4,0},{5,1},{6,2},{7,3},{8,12},{9,13},{10,... | collective-permute-start | bytes 786440 | tf_op jit(solution)/shard_map/ppermute | solution.py:35
  43.7 0.3 join.9
  44.0 1.6 %collective-permute-start.18 = (bf16[256,512]{1,0:T(8,128)(2,1)S(1)}, bf16[256,512]{1,0:T(8,128)(2,1)S(1)}, u32[]{:S(2)}, u32[]{:S(2)}) collective-permute-start(bf16[256,512]{1,0:T(8,128)(2,1)S(1)} %join.9), channel_id=1, source_target_pairs={{0,2},{1,3},{2,0},{3,1},{4,6},{5,7},{6,4},{7,5},{8,10},{9,11},{10,... | collective-permute-start | bytes 786440 | tf_op jit(solution)/shard_map/ppermute | solution.py:35
  45.6 0.3 join.5.sum_ref
  45.8 7.7 %collective-permute-done.15.came_ref = bf16[256,512]{1,0:T(8,128)(2,1)S(1)} collective-permute-done((bf16[256,512]{1,0:T(8,128)(2,1)S(1)}, bf16[256,512]{1,0:T(8,128)(2,1)S(1)}, u32[]{:S(2)}, u32[]{:S(2)}) %collective-permute-start.15) | collective-permute-done | bytes 262176 | tf_op jit(solution)/shard_map/ppermute | solution.py:35
  53.6 0.8 %collective-permute-done.17.came_ref = bf16[256,512]{1,0:T(8,128)(2,1)S(1)} collective-permute-done((bf16[256,512]{1,0:T(8,128)(2,1)S(1)}, bf16[256,512]{1,0:T(8,128)(2,1)S(1)}, u32[]{:S(2)}, u32[]{:S(2)}) %collective-permute-start.17) | collective-permute-done | bytes 262176 | tf_op jit(solution)/shard_map/ppermute | solution.py:35
  54.4 0.0 collective-permute-done.18
  54.4 0.8 %add_convert_fusion = bf16[256,512]{1,0:T(8,128)(2,1)} fusion(f32[256,512]{1,0:T(8,128)S(1)} %gather.3, bf16[256,512]{1,0:T(8,128)(2,1)S(1)} %collective-permute-done.18), kind=kLoop, calls=%fused_computation.2 | loop fusion | flops 393216 | bytes 1048576 | tf_op jit(solution)/shard_map/convert_element_type | solution.py:308
  (5 shorter events, 0.1 us)
Async XLA Ops:
  0.0 10.2 %collective-permute-start.1 = (bf16[64,8192]{1,0:T(8,128)(2,1)}, bf16[64,8192]{1,0:T(8,128)(2,1)S(1)}, u32[]{:S(2)}, u32[]{:S(2)}) collective-permute-start(bf16[64,8192]{1,0:T(8,128)(2,1)} %bitcast.27), channel_id=1, source_target_pairs={{0,1},{1,0},{2,3},{3,2},{4,5},{5,4},{6,7},{7,6},{8,9},{9,8},{10,11... | collective-permute-start | bytes 3145736 | tf_op jit(solution)/shard_map/ppermute | solution.py:35
  0.5 9.7 %collective-permute-start.2 = (bf16[64,8192]{1,0:T(8,128)(2,1)}, bf16[64,8192]{1,0:T(8,128)(2,1)S(1)}, u32[]{:S(2)}, u32[]{:S(2)}) collective-permute-start(bf16[64,8192]{1,0:T(8,128)(2,1)} %bitcast.20), channel_id=1, source_target_pairs={{0,1},{1,0},{2,3},{3,2},{4,5},{5,4},{6,7},{7,6},{8,9},{9,8},{10,11... | collective-permute-start | bytes 3145736 | tf_op jit(solution)/shard_map/ppermute | solution.py:35
  0.5 9.6 %collective-permute-start = (bf16[256,512]{1,0:T(8,128)(2,1)}, bf16[256,512]{1,0:T(8,128)(2,1)S(1)}, u32[]{:S(2)}, u32[]{:S(2)}) collective-permute-start(bf16[256,512]{1,0:T(8,128)(2,1)} %own_ref.1), channel_id=1, source_target_pairs={{0,2},{1,3},{2,0},{3,1},{4,6},{5,7},{6,4},{7,5},{8,10},{9,11},{10,... | collective-permute-start | bytes 786440 | tf_op jit(solution)/shard_map/ppermute | solution.py:35
  3.5 1.0 %copy-start.1 = (bf16[256,512]{1,0:T(8,128)(2,1)S(1)}, bf16[256,512]{1,0:T(8,128)(2,1)}, u32[]{:S(2)}) copy-start(bf16[256,512]{1,0:T(8,128)(2,1)} %own_ref.1) | copy-start | bytes 786436
  9.3 0.9 %copy-start.2 = (s32[256]{0:T(256)S(1)}, s32[256]{0:T(256)}, u32[]{:S(2)}) copy-start(s32[256]{0:T(256)} %param.10) | copy-start | bytes 3076
  9.3 0.9 %copy-start.3 = (s32[16]{0:T(128)S(1)}, s32[16]{0:T(128)}, u32[]{:S(2)}) copy-start(s32[16]{0:T(128)} %slot_hbm.1) | copy-start | bytes 196
  10.2 2.3 %collective-permute-start.8 = (bf16[3,256,512]{2,1,0:T(8,128)(2,1)S(1)}, bf16[3,256,512]{2,1,0:T(8,128)(2,1)S(1)}, u32[]{:S(2)}, u32[]{:S(2)}) collective-permute-start(bf16[3,256,512]{2,1,0:T(8,128)(2,1)S(1)} %once.4), channel_id=1, source_target_pairs={{0,1},{1,0},{2,3},{3,2},{4,5},{5,4},{6,7},{7,6},{8,9},{9,8},{10,11... | collective-permute-start | bytes 2359304 | tf_op jit(solution)/shard_map/ppermute | solution.py:35
  11.4 11.5 %collective-permute-start.3 = (bf16[5,256,512]{2,1,0:T(8,128)(2,1)S(1)}, bf16[5,256,512]{2,1,0:T(8,128)(2,1)S(1)}, u32[]{:S(2)}, u32[]{:S(2)}) collective-permute-start(bf16[5,256,512]{2,1,0:T(8,128)(2,1)S(1)} %once.3), channel_id=1, source_target_pairs={{0,1},{1,0},{2,3},{3,2},{4,5},{5,4},{6,7},{7,6},{8,9},{9,8},{10,11... | collective-permute-start | bytes 3932168 | tf_op jit(solution)/shard_map/ppermute | solution.py:35
  12.6 8.4 %collective-permute-start.10 = (bf16[256,512]{1,0:T(8,128)(2,1)S(1)}, bf16[256,512]{1,0:T(8,128)(2,1)S(1)}, u32[]{:S(2)}, u32[]{:S(2)}) collective-permute-start(bf16[256,512]{1,0:T(8,128)(2,1)S(1)} %get-tuple-element.33.refs_1_), channel_id=1, source_target_pairs={{0,2},{1,3},{2,0},{3,1},{4,6},{5,7},{6,4},{7,5},{8,10},{9,11},{10,... | collective-permute-start | bytes 786440 | tf_op jit(solution)/shard_map/ppermute | solution.py:35
  14.4 12.9 %collective-permute-start.4 = (bf16[64,1024]{1,0:T(8,128)(2,1)S(1)}, bf16[64,1024]{1,0:T(8,128)(2,1)S(1)}, u32[]{:S(2)}, u32[]{:S(2)}) collective-permute-start(bf16[64,1024]{1,0:T(8,128)(2,1)S(1)} %get-tuple-element.23), channel_id=1, source_target_pairs={{0,8},{1,9},{2,10},{3,11},{4,12},{5,13},{6,14},{7,15},{8,0},{9,1},... | collective-permute-start | bytes 393224 | tf_op jit(solution)/shard_map/ppermute | solution.py:35
  17.0 10.6 %collective-permute-start.5 = (bf16[64,1024]{1,0:T(8,128)(2,1)S(1)}, bf16[64,1024]{1,0:T(8,128)(2,1)S(1)}, u32[]{:S(2)}, u32[]{:S(2)}) collective-permute-start(bf16[64,1024]{1,0:T(8,128)(2,1)S(1)} %get-tuple-element.24), channel_id=1, source_target_pairs={{0,12},{1,13},{2,14},{3,15},{4,8},{5,9},{6,10},{7,11},{8,4},{9,5},... | collective-permute-start | bytes 393224 | tf_op jit(solution)/shard_map/ppermute | solution.py:35
  18.4 10.5 %collective-permute-start.6 = (bf16[64,1024]{1,0:T(8,128)(2,1)S(1)}, bf16[64,1024]{1,0:T(8,128)(2,1)S(1)}, u32[]{:S(2)}, u32[]{:S(2)}) collective-permute-start(bf16[64,1024]{1,0:T(8,128)(2,1)S(1)} %get-tuple-element.25), channel_id=1, source_target_pairs={{0,4},{1,5},{2,6},{3,7},{4,0},{5,1},{6,2},{7,3},{8,12},{9,13},{10,... | collective-permute-start | bytes 393224 | tf_op jit(solution)/shard_map/ppermute | solution.py:35
  18.6 10.2 %copy-start.4 = (bf16[1,8192,64]{1,2,0:T(8,128)(2,1)S(1)}, bf16[1,8192,64]{1,2,0:T(8,128)(2,1)}, u32[]{:S(2)}) copy-start(bf16[1,8192,64]{1,2,0:T(8,128)(2,1)} %param.8) | copy-start | bytes 3145732
  21.0 9.4 %collective-permute-start.9 = (bf16[256,512]{1,0:T(8,128)(2,1)S(1)}, bf16[256,512]{1,0:T(8,128)(2,1)S(1)}, u32[]{:S(2)}, u32[]{:S(2)}) collective-permute-start(bf16[256,512]{1,0:T(8,128)(2,1)S(1)} %once.5), channel_id=1, source_target_pairs={{0,2},{1,3},{2,0},{3,1},{4,6},{5,7},{6,4},{7,5},{8,10},{9,11},{10,... | collective-permute-start | bytes 786440 | tf_op jit(solution)/shard_map/ppermute | solution.py:35
  22.9 11.4 %collective-permute-start.11 = (bf16[256,512]{1,0:T(8,128)(2,1)S(1)}, bf16[256,512]{1,0:T(8,128)(2,1)S(1)}, u32[]{:S(2)}, u32[]{:S(2)}) collective-permute-start(bf16[256,512]{1,0:T(8,128)(2,1)S(1)} %fusion), channel_id=1, source_target_pairs={{0,4},{1,5},{2,6},{3,7},{4,0},{5,1},{6,2},{7,3},{8,12},{9,13},{10,... | collective-permute-start | bytes 786440 | tf_op jit(solution)/shard_map/ppermute | solution.py:35
  27.4 14.4 %collective-permute-start.16 = (bf16[256,512]{1,0:T(8,128)(2,1)S(1)}, bf16[256,512]{1,0:T(8,128)(2,1)S(1)}, u32[]{:S(2)}, u32[]{:S(2)}) collective-permute-start(bf16[256,512]{1,0:T(8,128)(2,1)S(1)} %fusion.3), channel_id=1, source_target_pairs={{0,2},{1,3},{2,0},{3,1},{4,6},{5,7},{6,4},{7,5},{8,10},{9,11},{10,... | collective-permute-start | bytes 786440 | tf_op jit(solution)/shard_map/ppermute | solution.py:35
  28.8 1.6 %copy-start = (bf16[1,64,8192]{2,1,0:T(8,128)(2,1)S(1)}, bf16[1,64,8192]{2,1,0:T(8,128)(2,1)}, u32[]{:S(2)}) copy-start(bf16[1,64,8192]{2,1,0:T(8,128)(2,1)} %param.9) | copy-start | bytes 3145732
  29.2 1.2 %collective-permute-start.7 = (f32[64,64]{1,0:T(8,128)S(1)}, f32[64,64]{1,0:T(8,128)S(1)}, u32[]{:S(2)}, u32[]{:S(2)}) collective-permute-start(f32[64,64]{1,0:T(8,128)S(1)} %shrink.1.mine_ref), channel_id=1, source_target_pairs={{0,1},{1,0},{2,3},{3,2},{4,5},{5,4},{6,7},{7,6},{8,9},{9,8},{10,11... | collective-permute-start | bytes 49160 | tf_op jit(solution)/shard_map/ppermute | solution.py:35
  30.8 7.6 %collective-permute-start.14 = (bf16[2,64,512]{2,1,0:T(8,128)(2,1)S(1)}, bf16[2,64,512]{2,1,0:T(8,128)(2,1)S(1)}, u32[]{:S(2)}, u32[]{:S(2)}) collective-permute-start(bf16[2,64,512]{2,1,0:T(8,128)(2,1)S(1)} %get-tuple-element.32), channel_id=1, source_target_pairs={{0,2},{1,3},{2,0},{3,1},{4,6},{5,7},{6,4},{7,5},{8,10},{9,11},{10,... | collective-permute-start | bytes 393224 | tf_op jit(solution)/shard_map/ppermute | solution.py:35
  32.4 5.3 %collective-permute-start.12 = (bf16[1,64,512]{2,1,0:T(8,128)(2,1)S(1)}, bf16[1,64,512]{2,1,0:T(8,128)(2,1)S(1)}, u32[]{:S(2)}, u32[]{:S(2)}) collective-permute-start(bf16[1,64,512]{2,1,0:T(8,128)(2,1)S(1)} %get-tuple-element.30), channel_id=1, source_target_pairs={{0,6},{1,7},{2,4},{3,5},{4,2},{5,3},{6,0},{7,1},{8,14},{9,15},{10,... | collective-permute-start | bytes 196616 | tf_op jit(solution)/shard_map/ppermute | solution.py:35
  33.5 4.3 %collective-permute-start.13 = (bf16[1,64,512]{2,1,0:T(8,128)(2,1)S(1)}, bf16[1,64,512]{2,1,0:T(8,128)(2,1)S(1)}, u32[]{:S(2)}, u32[]{:S(2)}) collective-permute-start(bf16[1,64,512]{2,1,0:T(8,128)(2,1)S(1)} %get-tuple-element.31), channel_id=1, source_target_pairs={{0,4},{1,5},{2,6},{3,7},{4,0},{5,1},{6,2},{7,3},{8,12},{9,13},{10,... | collective-permute-start | bytes 196616 | tf_op jit(solution)/shard_map/ppermute | solution.py:35
  38.8 14.7 %collective-permute-start.15 = (bf16[256,512]{1,0:T(8,128)(2,1)S(1)}, bf16[256,512]{1,0:T(8,128)(2,1)S(1)}, u32[]{:S(2)}, u32[]{:S(2)}) collective-permute-start(bf16[256,512]{1,0:T(8,128)(2,1)S(1)} %join.7.refs_5_), channel_id=1, source_target_pairs={{0,8},{1,9},{2,10},{3,11},{4,12},{5,13},{6,14},{7,15},{8,0},{9,1},... | collective-permute-start | bytes 786440 | tf_op jit(solution)/shard_map/ppermute | solution.py:35
  42.1 12.3 %collective-permute-start.17 = (bf16[256,512]{1,0:T(8,128)(2,1)S(1)}, bf16[256,512]{1,0:T(8,128)(2,1)S(1)}, u32[]{:S(2)}, u32[]{:S(2)}) collective-permute-start(bf16[256,512]{1,0:T(8,128)(2,1)S(1)} %join.8.refs_3_), channel_id=1, source_target_pairs={{0,4},{1,5},{2,6},{3,7},{4,0},{5,1},{6,2},{7,3},{8,12},{9,13},{10,... | collective-permute-start | bytes 786440 | tf_op jit(solution)/shard_map/ppermute | solution.py:35
  44.0 10.5 %collective-permute-start.18 = (bf16[256,512]{1,0:T(8,128)(2,1)S(1)}, bf16[256,512]{1,0:T(8,128)(2,1)S(1)}, u32[]{:S(2)}, u32[]{:S(2)}) collective-permute-start(bf16[256,512]{1,0:T(8,128)(2,1)S(1)} %join.9), channel_id=1, source_target_pairs={{0,2},{1,3},{2,0},{3,1},{4,6},{5,7},{6,4},{7,5},{8,10},{9,11},{10,... | collective-permute-start | bytes 786440 | tf_op jit(solution)/shard_map/ppermute | solution.py:35

commit v17 on v16

--- a/solution.py
+++ b/solution.py
@@ -268,7 +268,7 @@
     (away_first,) = once((away_first,), from_y)
     came_first = swap(away_first, 1)
     first = [stay_first[i] + came_first[i].astype(f32) for i in range(3)]
-    target, outgoing = route(adapter_slot, row_adapter, attended, from_y, token, down_other, up_other)
+    target, outgoing = route(adapter_slot, row_adapter, attended, from_y, token, came_first, down_other, up_other)
     arrived = {k: swap(outgoing[k], 4 * k) for k in (2, 3, 1)}
     arrived[0] = outgoing[0]
     go3 = first[0].astype(bf16)

time: 55.4 us -> 56.2 us (1.014)
  waiting for transfers between devices: 21.3 us -> 22.5 us
    ppermute x19, waiting for transfers between devices: 21.3 us -> 22.5 us  [swap(): return lax.ppermute(value, 'tensor', [(t, t ^ mask) for t in range(count)])]
  transfers between devices with their start and end apart: 19 -> 19, of which waited for: 11 -> 11; matrix products, arithmetic and copies ran while one was open for 1% -> 1% of each run, Pallas kernels for 15% -> 13%
where the time goes in v17:
time: 56.2 us; the launch traced here: 56.1 us
  starting transfers between devices  23 us (41%)
  waiting for transfers between devices  22.5 us (40%)
  Pallas kernels  8.29 us (15%)
  other arithmetic  1.17 us (2%)
  local copies, waits for them, and re-layouts  0.97 us (2%)
    ppermute x19, starting transfers between devices, swap(): return lax.ppermute(value, 'tensor', [(t, t ^ mask) for t in range(count)])  23 us
    ppermute x19, waiting for transfers between devices, swap(): return lax.ppermute(value, 'tensor', [(t, t ^ mask) for t in range(count)])  22.5 us
    pallas_call x1, Pallas kernels, product(): pl.pallas_call(functools.partial(product_kernel, groups), out_shape=out_s...  4.85 us
    pallas_call x5, Pallas kernels, join(): pl.pallas_call(functools.partial(join_kernel, terms), out_shape=[shape((r...  1.45 us
    pallas_call x1, Pallas kernels, route(): pl.pallas_call(functools.partial(route_kernel, count, layers), out_shape=...  1.2 us
  transfers between devices with their start and end apart: 19, of which 11 were waited for; matrix products, arithmetic and copies ran while one was open for 1% of the time, Pallas kernels for 13%

profile of v17, /device:TPU:0, one launch (start us, length us, event | category | flops | bytes accessed | tf_op | source)
XLA Modules:
  0.0 56.1 jit_solution(9822141634039356795)
XLA Ops:
  0.0 3.0 %collective-permute-start = (bf16[256,512]{1,0:T(8,128)(2,1)}, bf16[256,512]{1,0:T(8,128)(2,1)S(1)}, u32[]{:S(2)}, u32[]{:S(2)}) collective-permute-start(bf16[256,512]{1,0:T(8,128)(2,1)} %own_ref.1), channel_id=1, source_target_pairs={{0,2},{1,3},{2,0},{3,1},{4,6},{5,7},{6,4},{7,5},{8,10},{9,11},{10,... | collective-permute-start | bytes 786440 | tf_op jit(solution)/shard_map/ppermute | solution.py:35
  3.0 0.0 collective-permute-start.2
  3.0 0.5 collective-permute-start.3
  3.5 0.0 copy-start.1
  3.5 0.9 %copy-done.1 = bf16[256,512]{1,0:T(8,128)(2,1)S(1)} copy-done((bf16[256,512]{1,0:T(8,128)(2,1)S(1)}, bf16[256,512]{1,0:T(8,128)(2,1)}, u32[]{:S(2)}) %copy-start.1) | copy-done | bytes 262168
  4.4 4.9 %product.1 = (bf16[3,256,512]{2,1,0:T(8,128)(2,1)S(1)}, f32[3,256,512]{2,1,0:T(8,128)S(1)}, bf16[5,256,512]{2,1,0:T(8,128)(2,1)S(1)}, f32[5,256,512]{2,1,0:T(8,128)S(1)}, f32[8,128]{1,0:T(8,128)S(1)}) custom-call(bf16[256,512]{1,0:T(8,128)(2,1)S(1)} %copy-done.1, bf16[512,8192]{1,0:T(8,128)(2,1)} %weight_hbm.1), custom_call_target="tpu_custom_call" | custom-call | flops 2147483648 | bytes 14680064 | tf_op jit(solution)/shard_map/product/pallas_call | solution.py:138
  9.3 0.0 copy-start.2
  9.3 0.0 copy-start.3
  9.3 0.2 collective-permute-done.refs_1_.y_ref
  9.5 0.0 collective-permute-start.1
  9.5 0.0 collective-permute-done.2.rest_2_.other_ref
  9.5 0.0 collective-permute-done.3.rest_3_.up_other_ref
  9.5 2.3 %collective-permute-done.1.rest_1_ = bf16[3,256,512]{2,1,0:T(8,128)(2,1)S(1)} collective-permute-done((bf16[3,256,512]{2,1,0:T(8,128)(2,1)S(1)}, bf16[3,256,512]{2,1,0:T(8,128)(2,1)S(1)}, u32[]{:S(2)}, u32[]{:S(2)}) %collective-permute-start.1) | collective-permute-done | bytes 786464 | tf_op jit(solution)/shard_map/ppermute | solution.py:35
  11.8 0.0 copy-done.2
  11.8 0.0 copy-done.3
  11.8 1.2 %route.1 = (s32[1,256]{1,0:T(1,128)S(1)}, bf16[64,1024]{1,0:T(8,128)(2,1)S(1)}, bf16[64,1024]{1,0:T(8,128)(2,1)S(1)}, bf16[64,1024]{1,0:T(8,128)(2,1)S(1)}, bf16[64,1024]{1,0:T(8,128)(2,1)S(1)}) custom-call(s32[16]{0:T(128)S(1)} %copy-done.3, s32[1,256]{1,0:T(1,128)S(1)} %bitcast.26, bf16[256,512]{1,0:T(8,128)(2,1)S(1)} %copy-done.1, ...), custom_call_target="tpu_custom_call" | custom-call | flops 134217728 | bytes 1048576 | tf_op jit(solution)/shard_map/route/pallas_call | solution.py:88
  13.0 0.2 collective-permute-start.4
  13.2 0.2 fusion.2
  13.4 1.8 %collective-permute-start.10 = (bf16[256,512]{1,0:T(8,128)(2,1)S(1)}, bf16[256,512]{1,0:T(8,128)(2,1)S(1)}, u32[]{:S(2)}, u32[]{:S(2)}) collective-permute-start(bf16[256,512]{1,0:T(8,128)(2,1)S(1)} %get-tuple-element.33.refs_1_), channel_id=1, source_target_pairs={{0,2},{1,3},{2,0},{3,1},{4,6},{5,7},{6,4},{7,5},{8,10},{9,11},{10,... | collective-permute-start | bytes 786440 | tf_op jit(solution)/shard_map/ppermute | solution.py:35
  15.2 2.6 %collective-permute-start.5 = (bf16[64,1024]{1,0:T(8,128)(2,1)S(1)}, bf16[64,1024]{1,0:T(8,128)(2,1)S(1)}, u32[]{:S(2)}, u32[]{:S(2)}) collective-permute-start(bf16[64,1024]{1,0:T(8,128)(2,1)S(1)} %get-tuple-element.24), channel_id=1, source_target_pairs={{0,8},{1,9},{2,10},{3,11},{4,12},{5,13},{6,14},{7,15},{8,0},{9,1},... | collective-permute-start | bytes 393224 | tf_op jit(solution)/shard_map/ppermute | solution.py:35
  17.8 1.3 %collective-permute-start.6 = (bf16[64,1024]{1,0:T(8,128)(2,1)S(1)}, bf16[64,1024]{1,0:T(8,128)(2,1)S(1)}, u32[]{:S(2)}, u32[]{:S(2)}) collective-permute-start(bf16[64,1024]{1,0:T(8,128)(2,1)S(1)} %get-tuple-element.25), channel_id=1, source_target_pairs={{0,12},{1,13},{2,14},{3,15},{4,8},{5,9},{6,10},{7,11},{8,4},{9,5},... | collective-permute-start | bytes 393224 | tf_op jit(solution)/shard_map/ppermute | solution.py:35
  19.2 0.2 collective-permute-start.7
  19.4 0.0 copy-start.4
  19.4 2.7 %collective-permute-done.10 = bf16[256,512]{1,0:T(8,128)(2,1)S(1)} collective-permute-done((bf16[256,512]{1,0:T(8,128)(2,1)S(1)}, bf16[256,512]{1,0:T(8,128)(2,1)S(1)}, u32[]{:S(2)}, u32[]{:S(2)}) %collective-permute-start.10) | collective-permute-done | bytes 262176 | tf_op jit(solution)/shard_map/ppermute | solution.py:35
  22.1 1.7 %collective-permute-start.9 = (bf16[256,512]{1,0:T(8,128)(2,1)S(1)}, bf16[256,512]{1,0:T(8,128)(2,1)S(1)}, u32[]{:S(2)}, u32[]{:S(2)}) collective-permute-start(bf16[256,512]{1,0:T(8,128)(2,1)S(1)} %once.5), channel_id=1, source_target_pairs={{0,2},{1,3},{2,0},{3,1},{4,6},{5,7},{6,4},{7,5},{8,10},{9,11},{10,... | collective-permute-start | bytes 786440 | tf_op jit(solution)/shard_map/ppermute | solution.py:35
  23.8 0.1 fusion
  23.9 0.0 collective-permute-done.4.refs_0_.refs_1_
  23.9 1.6 %collective-permute-start.11 = (bf16[256,512]{1,0:T(8,128)(2,1)S(1)}, bf16[256,512]{1,0:T(8,128)(2,1)S(1)}, u32[]{:S(2)}, u32[]{:S(2)}) collective-permute-start(bf16[256,512]{1,0:T(8,128)(2,1)S(1)} %fusion), channel_id=1, source_target_pairs={{0,4},{1,5},{2,6},{3,7},{4,0},{5,1},{6,2},{7,3},{8,12},{9,13},{10,... | collective-permute-start | bytes 786440 | tf_op jit(solution)/shard_map/ppermute | solution.py:35
  25.6 0.1 fusion.3
  25.6 2.5 %collective-permute-done.5.refs_0_ = bf16[64,1024]{1,0:T(8,128)(2,1)S(1)} collective-permute-done((bf16[64,1024]{1,0:T(8,128)(2,1)S(1)}, bf16[64,1024]{1,0:T(8,128)(2,1)S(1)}, u32[]{:S(2)}, u32[]{:S(2)}) %collective-permute-start.5) | collective-permute-done | bytes 131104 | tf_op jit(solution)/shard_map/ppermute | solution.py:35
  28.1 0.3 collective-permute-start.16
  28.4 0.0 collective-permute-done.6.refs_1_
  28.4 1.4 %collective-permute-done.7.refs_2_ = bf16[64,1024]{1,0:T(8,128)(2,1)S(1)} collective-permute-done((bf16[64,1024]{1,0:T(8,128)(2,1)S(1)}, bf16[64,1024]{1,0:T(8,128)(2,1)S(1)}, u32[]{:S(2)}, u32[]{:S(2)}) %collective-permute-start.7) | collective-permute-done | bytes 131104 | tf_op jit(solution)/shard_map/ppermute | solution.py:35
  29.8 0.0 copy-done.4
  29.8 0.0 copy-start
  29.8 0.4 shrink.1.mine_ref
  30.2 0.0 collective-permute-start.8
  30.2 1.2 %collective-permute-done.8.other_ref = f32[64,64]{1,0:T(8,128)S(1)} collective-permute-done((f32[64,64]{1,0:T(8,128)S(1)}, f32[64,64]{1,0:T(8,128)S(1)}, u32[]{:S(2)}, u32[]{:S(2)}) %collective-permute-start.8) | collective-permute-done | bytes 16416 | tf_op jit(solution)/shard_map/ppermute | solution.py:35
  31.4 0.0 collective-permute-done.9
  31.4 0.0 copy-done
  31.4 0.3 grow.1
  31.7 1.7 %collective-permute-start.14 = (bf16[2,64,512]{2,1,0:T(8,128)(2,1)S(1)}, bf16[2,64,512]{2,1,0:T(8,128)(2,1)S(1)}, u32[]{:S(2)}, u32[]{:S(2)}) collective-permute-start(bf16[2,64,512]{2,1,0:T(8,128)(2,1)S(1)} %get-tuple-element.32), channel_id=1, source_target_pairs={{0,2},{1,3},{2,0},{3,1},{4,6},{5,7},{6,4},{7,5},{8,10},{9,11},{10,... | collective-permute-start | bytes 393224 | tf_op jit(solution)/shard_map/ppermute | solution.py:35
  33.4 1.1 %collective-permute-start.12 = (bf16[1,64,512]{2,1,0:T(8,128)(2,1)S(1)}, bf16[1,64,512]{2,1,0:T(8,128)(2,1)S(1)}, u32[]{:S(2)}, u32[]{:S(2)}) collective-permute-start(bf16[1,64,512]{2,1,0:T(8,128)(2,1)S(1)} %get-tuple-element.30), channel_id=1, source_target_pairs={{0,6},{1,7},{2,4},{3,5},{4,2},{5,3},{6,0},{7,1},{8,14},{9,15},{10,... | collective-permute-start | bytes 196616 | tf_op jit(solution)/shard_map/ppermute | solution.py:35
  34.5 0.8 %collective-permute-start.13 = (bf16[1,64,512]{2,1,0:T(8,128)(2,1)S(1)}, bf16[1,64,512]{2,1,0:T(8,128)(2,1)S(1)}, u32[]{:S(2)}, u32[]{:S(2)}) collective-permute-start(bf16[1,64,512]{2,1,0:T(8,128)(2,1)S(1)} %get-tuple-element.31), channel_id=1, source_target_pairs={{0,4},{1,5},{2,6},{3,7},{4,0},{5,1},{6,2},{7,3},{8,12},{9,13},{10,... | collective-permute-start | bytes 196616 | tf_op jit(solution)/shard_map/ppermute | solution.py:35
  35.3 0.0 collective-permute-done.11
  35.3 0.1 join.6
  35.4 3.3 %collective-permute-done.12.refs_1_ = bf16[1,64,512]{2,1,0:T(8,128)(2,1)S(1)} collective-permute-done((bf16[1,64,512]{2,1,0:T(8,128)(2,1)S(1)}, bf16[1,64,512]{2,1,0:T(8,128)(2,1)S(1)}, u32[]{:S(2)}, u32[]{:S(2)}) %collective-permute-start.12) | collective-permute-done | bytes 65568 | tf_op jit(solution)/shard_map/ppermute | solution.py:35
  38.7 0.1 collective-permute-done.13.refs_2_
  38.7 0.9 %collective-permute-done.14.refs_3_ = bf16[2,64,512]{2,1,0:T(8,128)(2,1)S(1)} collective-permute-done((bf16[2,64,512]{2,1,0:T(8,128)(2,1)S(1)}, bf16[2,64,512]{2,1,0:T(8,128)(2,1)S(1)}, u32[]{:S(2)}, u32[]{:S(2)}) %collective-permute-start.14) | collective-permute-done | bytes 131104 | tf_op jit(solution)/shard_map/ppermute | solution.py:35
  39.7 0.5 join.7.refs_5_
  40.1 2.9 %collective-permute-start.15 = (bf16[256,512]{1,0:T(8,128)(2,1)S(1)}, bf16[256,512]{1,0:T(8,128)(2,1)S(1)}, u32[]{:S(2)}, u32[]{:S(2)}) collective-permute-start(bf16[256,512]{1,0:T(8,128)(2,1)S(1)} %join.7.refs_5_), channel_id=1, source_target_pairs={{0,8},{1,9},{2,10},{3,11},{4,12},{5,13},{6,14},{7,15},{8,0},{9,1},... | collective-permute-start | bytes 786440 | tf_op jit(solution)/shard_map/ppermute | solution.py:35
  43.0 0.0 collective-permute-done.16
  43.0 0.3 join.8.refs_3_
  43.3 1.6 %collective-permute-start.17 = (bf16[256,512]{1,0:T(8,128)(2,1)S(1)}, bf16[256,512]{1,0:T(8,128)(2,1)S(1)}, u32[]{:S(2)}, u32[]{:S(2)}) collective-permute-start(bf16[256,512]{1,0:T(8,128)(2,1)S(1)} %join.8.refs_3_), channel_id=1, source_target_pairs={{0,4},{1,5},{2,6},{3,7},{4,0},{5,1},{6,2},{7,3},{8,12},{9,13},{10,... | collective-permute-start | bytes 786440 | tf_op jit(solution)/shard_map/ppermute | solution.py:35
  45.0 0.3 join.9
  45.3 1.6 %collective-permute-start.18 = (bf16[256,512]{1,0:T(8,128)(2,1)S(1)}, bf16[256,512]{1,0:T(8,128)(2,1)S(1)}, u32[]{:S(2)}, u32[]{:S(2)}) collective-permute-start(bf16[256,512]{1,0:T(8,128)(2,1)S(1)} %join.9), channel_id=1, source_target_pairs={{0,2},{1,3},{2,0},{3,1},{4,6},{5,7},{6,4},{7,5},{8,10},{9,11},{10,... | collective-permute-start | bytes 786440 | tf_op jit(solution)/shard_map/ppermute | solution.py:35
  46.8 0.3 join.5.sum_ref
  47.1 7.4 %collective-permute-done.15.came_ref = bf16[256,512]{1,0:T(8,128)(2,1)S(1)} collective-permute-done((bf16[256,512]{1,0:T(8,128)(2,1)S(1)}, bf16[256,512]{1,0:T(8,128)(2,1)S(1)}, u32[]{:S(2)}, u32[]{:S(2)}) %collective-permute-start.15) | collective-permute-done | bytes 262176 | tf_op jit(solution)/shard_map/ppermute | solution.py:35
  54.6 0.6 %collective-permute-done.17.came_ref = bf16[256,512]{1,0:T(8,128)(2,1)S(1)} collective-permute-done((bf16[256,512]{1,0:T(8,128)(2,1)S(1)}, bf16[256,512]{1,0:T(8,128)(2,1)S(1)}, u32[]{:S(2)}, u32[]{:S(2)}) %collective-permute-start.17) | collective-permute-done | bytes 262176 | tf_op jit(solution)/shard_map/ppermute | solution.py:35
  55.3 0.0 collective-permute-done.18
  55.3 0.8 %add_convert_fusion = bf16[256,512]{1,0:T(8,128)(2,1)} fusion(f32[256,512]{1,0:T(8,128)S(1)} %gather.3, bf16[256,512]{1,0:T(8,128)(2,1)S(1)} %collective-permute-done.18), kind=kLoop, calls=%fused_computation.2 | loop fusion | flops 393216 | bytes 1048576 | tf_op jit(solution)/shard_map/convert_element_type | solution.py:308
  (5 shorter events, 0.1 us)
Async XLA Ops:
  0.0 9.5 %collective-permute-start = (bf16[256,512]{1,0:T(8,128)(2,1)}, bf16[256,512]{1,0:T(8,128)(2,1)S(1)}, u32[]{:S(2)}, u32[]{:S(2)}) collective-permute-start(bf16[256,512]{1,0:T(8,128)(2,1)} %own_ref.1), channel_id=1, source_target_pairs={{0,2},{1,3},{2,0},{3,1},{4,6},{5,7},{6,4},{7,5},{8,10},{9,11},{10,... | collective-permute-start | bytes 786440 | tf_op jit(solution)/shard_map/ppermute | solution.py:35
  3.0 6.5 %collective-permute-start.2 = (bf16[64,8192]{1,0:T(8,128)(2,1)}, bf16[64,8192]{1,0:T(8,128)(2,1)S(1)}, u32[]{:S(2)}, u32[]{:S(2)}) collective-permute-start(bf16[64,8192]{1,0:T(8,128)(2,1)} %bitcast.27), channel_id=1, source_target_pairs={{0,1},{1,0},{2,3},{3,2},{4,5},{5,4},{6,7},{7,6},{8,9},{9,8},{10,11... | collective-permute-start | bytes 3145736 | tf_op jit(solution)/shard_map/ppermute | solution.py:35
  3.0 6.5 %collective-permute-start.3 = (bf16[64,8192]{1,0:T(8,128)(2,1)}, bf16[64,8192]{1,0:T(8,128)(2,1)S(1)}, u32[]{:S(2)}, u32[]{:S(2)}) collective-permute-start(bf16[64,8192]{1,0:T(8,128)(2,1)} %bitcast.20), channel_id=1, source_target_pairs={{0,1},{1,0},{2,3},{3,2},{4,5},{5,4},{6,7},{7,6},{8,9},{9,8},{10,11... | collective-permute-start | bytes 3145736 | tf_op jit(solution)/shard_map/ppermute | solution.py:35
  3.5 0.9 %copy-start.1 = (bf16[256,512]{1,0:T(8,128)(2,1)S(1)}, bf16[256,512]{1,0:T(8,128)(2,1)}, u32[]{:S(2)}) copy-start(bf16[256,512]{1,0:T(8,128)(2,1)} %own_ref.1) | copy-start | bytes 786436
  9.3 2.5 %copy-start.2 = (s32[256]{0:T(256)S(1)}, s32[256]{0:T(256)}, u32[]{:S(2)}) copy-start(s32[256]{0:T(256)} %param.10) | copy-start | bytes 3076
  9.3 2.5 %copy-start.3 = (s32[16]{0:T(128)S(1)}, s32[16]{0:T(128)}, u32[]{:S(2)}) copy-start(s32[16]{0:T(128)} %slot_hbm.1) | copy-start | bytes 196
  9.5 2.3 %collective-permute-start.1 = (bf16[3,256,512]{2,1,0:T(8,128)(2,1)S(1)}, bf16[3,256,512]{2,1,0:T(8,128)(2,1)S(1)}, u32[]{:S(2)}, u32[]{:S(2)}) collective-permute-start(bf16[3,256,512]{2,1,0:T(8,128)(2,1)S(1)} %once.3), channel_id=1, source_target_pairs={{0,1},{1,0},{2,3},{3,2},{4,5},{5,4},{6,7},{7,6},{8,9},{9,8},{10,11... | collective-permute-start | bytes 2359304 | tf_op jit(solution)/shard_map/ppermute | solution.py:35
  13.0 10.9 %collective-permute-start.4 = (bf16[5,256,512]{2,1,0:T(8,128)(2,1)S(1)}, bf16[5,256,512]{2,1,0:T(8,128)(2,1)S(1)}, u32[]{:S(2)}, u32[]{:S(2)}) collective-permute-start(bf16[5,256,512]{2,1,0:T(8,128)(2,1)S(1)} %once.4), channel_id=1, source_target_pairs={{0,1},{1,0},{2,3},{3,2},{4,5},{5,4},{6,7},{7,6},{8,9},{9,8},{10,11... | collective-permute-start | bytes 3932168 | tf_op jit(solution)/shard_map/ppermute | solution.py:35
  13.4 8.7 %collective-permute-start.10 = (bf16[256,512]{1,0:T(8,128)(2,1)S(1)}, bf16[256,512]{1,0:T(8,128)(2,1)S(1)}, u32[]{:S(2)}, u32[]{:S(2)}) collective-permute-start(bf16[256,512]{1,0:T(8,128)(2,1)S(1)} %get-tuple-element.33.refs_1_), channel_id=1, source_target_pairs={{0,2},{1,3},{2,0},{3,1},{4,6},{5,7},{6,4},{7,5},{8,10},{9,11},{10,... | collective-permute-start | bytes 786440 | tf_op jit(solution)/shard_map/ppermute | solution.py:35
  15.2 12.9 %collective-permute-start.5 = (bf16[64,1024]{1,0:T(8,128)(2,1)S(1)}, bf16[64,1024]{1,0:T(8,128)(2,1)S(1)}, u32[]{:S(2)}, u32[]{:S(2)}) collective-permute-start(bf16[64,1024]{1,0:T(8,128)(2,1)S(1)} %get-tuple-element.24), channel_id=1, source_target_pairs={{0,8},{1,9},{2,10},{3,11},{4,12},{5,13},{6,14},{7,15},{8,0},{9,1},... | collective-permute-start | bytes 393224 | tf_op jit(solution)/shard_map/ppermute | solution.py:35
  17.8 10.6 %collective-permute-start.6 = (bf16[64,1024]{1,0:T(8,128)(2,1)S(1)}, bf16[64,1024]{1,0:T(8,128)(2,1)S(1)}, u32[]{:S(2)}, u32[]{:S(2)}) collective-permute-start(bf16[64,1024]{1,0:T(8,128)(2,1)S(1)} %get-tuple-element.25), channel_id=1, source_target_pairs={{0,12},{1,13},{2,14},{3,15},{4,8},{5,9},{6,10},{7,11},{8,4},{9,5},... | collective-permute-start | bytes 393224 | tf_op jit(solution)/shard_map/ppermute | solution.py:35
  19.2 10.6 %collective-permute-start.7 = (bf16[64,1024]{1,0:T(8,128)(2,1)S(1)}, bf16[64,1024]{1,0:T(8,128)(2,1)S(1)}, u32[]{:S(2)}, u32[]{:S(2)}) collective-permute-start(bf16[64,1024]{1,0:T(8,128)(2,1)S(1)} %get-tuple-element.26), channel_id=1, source_target_pairs={{0,4},{1,5},{2,6},{3,7},{4,0},{5,1},{6,2},{7,3},{8,12},{9,13},{10,... | collective-permute-start | bytes 393224 | tf_op jit(solution)/shard_map/ppermute | solution.py:35
  19.4 10.4 %copy-start.4 = (bf16[1,8192,64]{1,2,0:T(8,128)(2,1)S(1)}, bf16[1,8192,64]{1,2,0:T(8,128)(2,1)}, u32[]{:S(2)}) copy-start(bf16[1,8192,64]{1,2,0:T(8,128)(2,1)} %param.8) | copy-start | bytes 3145732
  22.1 9.4 %collective-permute-start.9 = (bf16[256,512]{1,0:T(8,128)(2,1)S(1)}, bf16[256,512]{1,0:T(8,128)(2,1)S(1)}, u32[]{:S(2)}, u32[]{:S(2)}) collective-permute-start(bf16[256,512]{1,0:T(8,128)(2,1)S(1)} %once.5), channel_id=1, source_target_pairs={{0,2},{1,3},{2,0},{3,1},{4,6},{5,7},{6,4},{7,5},{8,10},{9,11},{10,... | collective-permute-start | bytes 786440 | tf_op jit(solution)/shard_map/ppermute | solution.py:35
  23.9 11.4 %collective-permute-start.11 = (bf16[256,512]{1,0:T(8,128)(2,1)S(1)}, bf16[256,512]{1,0:T(8,128)(2,1)S(1)}, u32[]{:S(2)}, u32[]{:S(2)}) collective-permute-start(bf16[256,512]{1,0:T(8,128)(2,1)S(1)} %fusion), channel_id=1, source_target_pairs={{0,4},{1,5},{2,6},{3,7},{4,0},{5,1},{6,2},{7,3},{8,12},{9,13},{10,... | collective-permute-start | bytes 786440 | tf_op jit(solution)/shard_map/ppermute | solution.py:35
  28.1 14.9 %collective-permute-start.16 = (bf16[256,512]{1,0:T(8,128)(2,1)S(1)}, bf16[256,512]{1,0:T(8,128)(2,1)S(1)}, u32[]{:S(2)}, u32[]{:S(2)}) collective-permute-start(bf16[256,512]{1,0:T(8,128)(2,1)S(1)} %fusion.3), channel_id=1, source_target_pairs={{0,2},{1,3},{2,0},{3,1},{4,6},{5,7},{6,4},{7,5},{8,10},{9,11},{10,... | collective-permute-start | bytes 786440 | tf_op jit(solution)/shard_map/ppermute | solution.py:35
  29.8 1.6 %copy-start = (bf16[1,64,8192]{2,1,0:T(8,128)(2,1)S(1)}, bf16[1,64,8192]{2,1,0:T(8,128)(2,1)}, u32[]{:S(2)}) copy-start(bf16[1,64,8192]{2,1,0:T(8,128)(2,1)} %param.9) | copy-start | bytes 3145732
  30.2 1.2 %collective-permute-start.8 = (f32[64,64]{1,0:T(8,128)S(1)}, f32[64,64]{1,0:T(8,128)S(1)}, u32[]{:S(2)}, u32[]{:S(2)}) collective-permute-start(f32[64,64]{1,0:T(8,128)S(1)} %shrink.1.mine_ref), channel_id=1, source_target_pairs={{0,1},{1,0},{2,3},{3,2},{4,5},{5,4},{6,7},{7,6},{8,9},{9,8},{10,11... | collective-permute-start | bytes 49160 | tf_op jit(solution)/shard_map/ppermute | solution.py:35
  31.7 7.9 %collective-permute-start.14 = (bf16[2,64,512]{2,1,0:T(8,128)(2,1)S(1)}, bf16[2,64,512]{2,1,0:T(8,128)(2,1)S(1)}, u32[]{:S(2)}, u32[]{:S(2)}) collective-permute-start(bf16[2,64,512]{2,1,0:T(8,128)(2,1)S(1)} %get-tuple-element.32), channel_id=1, source_target_pairs={{0,2},{1,3},{2,0},{3,1},{4,6},{5,7},{6,4},{7,5},{8,10},{9,11},{10,... | collective-permute-start | bytes 393224 | tf_op jit(solution)/shard_map/ppermute | solution.py:35
  33.4 5.3 %collective-permute-start.12 = (bf16[1,64,512]{2,1,0:T(8,128)(2,1)S(1)}, bf16[1,64,512]{2,1,0:T(8,128)(2,1)S(1)}, u32[]{:S(2)}, u32[]{:S(2)}) collective-permute-start(bf16[1,64,512]{2,1,0:T(8,128)(2,1)S(1)} %get-tuple-element.30), channel_id=1, source_target_pairs={{0,6},{1,7},{2,4},{3,5},{4,2},{5,3},{6,0},{7,1},{8,14},{9,15},{10,... | collective-permute-start | bytes 196616 | tf_op jit(solution)/shard_map/ppermute | solution.py:35
  34.5 4.3 %collective-permute-start.13 = (bf16[1,64,512]{2,1,0:T(8,128)(2,1)S(1)}, bf16[1,64,512]{2,1,0:T(8,128)(2,1)S(1)}, u32[]{:S(2)}, u32[]{:S(2)}) collective-permute-start(bf16[1,64,512]{2,1,0:T(8,128)(2,1)S(1)} %get-tuple-element.31), channel_id=1, source_target_pairs={{0,4},{1,5},{2,6},{3,7},{4,0},{5,1},{6,2},{7,3},{8,12},{9,13},{10,... | collective-permute-start | bytes 196616 | tf_op jit(solution)/shard_map/ppermute | solution.py:35
  40.1 14.4 %collective-permute-start.15 = (bf16[256,512]{1,0:T(8,128)(2,1)S(1)}, bf16[256,512]{1,0:T(8,128)(2,1)S(1)}, u32[]{:S(2)}, u32[]{:S(2)}) collective-permute-start(bf16[256,512]{1,0:T(8,128)(2,1)S(1)} %join.7.refs_5_), channel_id=1, source_target_pairs={{0,8},{1,9},{2,10},{3,11},{4,12},{5,13},{6,14},{7,15},{8,0},{9,1},... | collective-permute-start | bytes 786440 | tf_op jit(solution)/shard_map/ppermute | solution.py:35
  43.3 11.9 %collective-permute-start.17 = (bf16[256,512]{1,0:T(8,128)(2,1)S(1)}, bf16[256,512]{1,0:T(8,128)(2,1)S(1)}, u32[]{:S(2)}, u32[]{:S(2)}) collective-permute-start(bf16[256,512]{1,0:T(8,128)(2,1)S(1)} %join.8.refs_3_), channel_id=1, source_target_pairs={{0,4},{1,5},{2,6},{3,7},{4,0},{5,1},{6,2},{7,3},{8,12},{9,13},{10,... | collective-permute-start | bytes 786440 | tf_op jit(solution)/shard_map/ppermute | solution.py:35
  45.3 10.0 %collective-permute-start.18 = (bf16[256,512]{1,0:T(8,128)(2,1)S(1)}, bf16[256,512]{1,0:T(8,128)(2,1)S(1)}, u32[]{:S(2)}, u32[]{:S(2)}) collective-permute-start(bf16[256,512]{1,0:T(8,128)(2,1)S(1)} %join.9), channel_id=1, source_target_pairs={{0,2},{1,3},{2,0},{3,1},{4,6},{5,7},{6,4},{7,5},{8,10},{9,11},{10,... | collective-permute-start | bytes 786440 | tf_op jit(solution)/shard_map/ppermute | solution.py:35

commit v18 on v16

--- a/solution.py
+++ b/solution.py
@@ -269,7 +269,7 @@
     came_first = swap(away_first, 1)
     first = [stay_first[i] + came_first[i].astype(f32) for i in range(3)]
     target, outgoing = route(adapter_slot, row_adapter, attended, from_y, token, down_other, up_other)
-    arrived = {k: swap(outgoing[k], 4 * k) for k in (2, 3, 1)}
+    arrived = {k: swap(outgoing[k], 4 * k) for k in (1, 3, 2)}
     arrived[0] = outgoing[0]
     go3 = first[0].astype(bf16)
     y3 = swap(go3, 2)

time: 55.4 us -> 55.5 us (level)
  waiting for transfers between devices: 21.3 us -> 22.1 us
  starting transfers between devices: 23.3 us -> 22.7 us
    ppermute x19, waiting for transfers between devices: 21.3 us -> 22.1 us  [swap(): return lax.ppermute(value, 'tensor', [(t, t ^ mask) for t in range(count)])]
    ppermute x19, starting transfers between devices: 23.3 us -> 22.7 us  [swap(): return lax.ppermute(value, 'tensor', [(t, t ^ mask) for t in range(count)])]
where the time goes in v18:
time: 55.5 us; the launch traced here: 55.4 us
  starting transfers between devices  22.7 us (41%)
  waiting for transfers between devices  22.1 us (40%)
  Pallas kernels  8.3 us (15%)
  other arithmetic  1.13 us (2%)
  local copies, waits for them, and re-layouts  1 us (2%)
    ppermute x19, starting transfers between devices, swap(): return lax.ppermute(value, 'tensor', [(t, t ^ mask) for t in range(count)])  22.7 us
    ppermute x19, waiting for transfers between devices, swap(): return lax.ppermute(value, 'tensor', [(t, t ^ mask) for t in range(count)])  22.1 us
    pallas_call x1, Pallas kernels, product(): pl.pallas_call(functools.partial(product_kernel, groups), out_shape=out_s...  4.85 us
    pallas_call x5, Pallas kernels, join(): pl.pallas_call(functools.partial(join_kernel, terms), out_shape=[shape((r...  1.46 us
    pallas_call x1, Pallas kernels, route(): pl.pallas_call(functools.partial(route_kernel, count, layers), out_shape=...  1.21 us
  transfers between devices with their start and end apart: 19, of which 11 were waited for; matrix products, arithmetic and copies ran while one was open for 1% of the time, Pallas kernels for 15%

profile of v18, /device:TPU:0, one launch (start us, length us, event | category | flops | bytes accessed | tf_op | source)
XLA Modules:
  0.0 55.4 jit_solution(7269537348278265484)
XLA Ops:
  0.0 0.5 collective-permute-start.1
  0.5 0.1 collective-permute-start.2
  0.5 3.0 %collective-permute-start = (bf16[256,512]{1,0:T(8,128)(2,1)}, bf16[256,512]{1,0:T(8,128)(2,1)S(1)}, u32[]{:S(2)}, u32[]{:S(2)}) collective-permute-start(bf16[256,512]{1,0:T(8,128)(2,1)} %own_ref.1), channel_id=1, source_target_pairs={{0,2},{1,3},{2,0},{3,1},{4,6},{5,7},{6,4},{7,5},{8,10},{9,11},{10,... | collective-permute-start | bytes 786440 | tf_op jit(solution)/shard_map/ppermute | solution.py:35
  3.5 0.0 copy-start.1
  3.5 1.0 %copy-done.1 = bf16[256,512]{1,0:T(8,128)(2,1)S(1)} copy-done((bf16[256,512]{1,0:T(8,128)(2,1)S(1)}, bf16[256,512]{1,0:T(8,128)(2,1)}, u32[]{:S(2)}) %copy-start.1) | copy-done | bytes 262168
  4.5 4.9 %product.1 = (bf16[3,256,512]{2,1,0:T(8,128)(2,1)S(1)}, f32[3,256,512]{2,1,0:T(8,128)S(1)}, bf16[5,256,512]{2,1,0:T(8,128)(2,1)S(1)}, f32[5,256,512]{2,1,0:T(8,128)S(1)}, f32[8,128]{1,0:T(8,128)S(1)}) custom-call(bf16[256,512]{1,0:T(8,128)(2,1)S(1)} %copy-done.1, bf16[512,8192]{1,0:T(8,128)(2,1)} %weight_hbm.1), custom_call_target="tpu_custom_call" | custom-call | flops 2147483648 | bytes 14680064 | tf_op jit(solution)/shard_map/product/pallas_call | solution.py:138
  9.3 0.0 copy-start.2
  9.3 0.0 copy-start.3
  9.3 0.8 %collective-permute-done.y_ref.refs_1_ = bf16[256,512]{1,0:T(8,128)(2,1)S(1)} collective-permute-done((bf16[256,512]{1,0:T(8,128)(2,1)}, bf16[256,512]{1,0:T(8,128)(2,1)S(1)}, u32[]{:S(2)}, u32[]{:S(2)}) %collective-permute-start) | collective-permute-done | bytes 262176 | tf_op jit(solution)/shard_map/ppermute | solution.py:35
  10.2 0.0 collective-permute-start.8
  10.2 0.0 collective-permute-done.1.rest_1_.other_ref
  10.2 0.0 collective-permute-done.2.rest_2_.up_other_ref
  10.2 0.0 copy-done.2
  10.2 0.0 copy-done.3
  10.2 1.2 %route.1 = (s32[1,256]{1,0:T(1,128)S(1)}, bf16[64,1024]{1,0:T(8,128)(2,1)S(1)}, bf16[64,1024]{1,0:T(8,128)(2,1)S(1)}, bf16[64,1024]{1,0:T(8,128)(2,1)S(1)}, bf16[64,1024]{1,0:T(8,128)(2,1)S(1)}) custom-call(s32[16]{0:T(128)S(1)} %copy-done.3, s32[1,256]{1,0:T(1,128)S(1)} %bitcast.26, bf16[256,512]{1,0:T(8,128)(2,1)S(1)} %copy-done.1, ...), custom_call_target="tpu_custom_call" | custom-call | flops 134217728 | bytes 1048576 | tf_op jit(solution)/shard_map/route/pallas_call | solution.py:88
  11.4 0.6 %collective-permute-start.3 = (bf16[5,256,512]{2,1,0:T(8,128)(2,1)S(1)}, bf16[5,256,512]{2,1,0:T(8,128)(2,1)S(1)}, u32[]{:S(2)}, u32[]{:S(2)}) collective-permute-start(bf16[5,256,512]{2,1,0:T(8,128)(2,1)S(1)} %once.3), channel_id=1, source_target_pairs={{0,1},{1,0},{2,3},{3,2},{4,5},{5,4},{6,7},{7,6},{8,9},{9,8},{10,11... | collective-permute-start | bytes 3932168 | tf_op jit(solution)/shard_map/ppermute | solution.py:35
  12.0 0.5 collective-permute-done.8
  12.4 0.2 fusion.2
  12.6 1.8 %collective-permute-start.10 = (bf16[256,512]{1,0:T(8,128)(2,1)S(1)}, bf16[256,512]{1,0:T(8,128)(2,1)S(1)}, u32[]{:S(2)}, u32[]{:S(2)}) collective-permute-start(bf16[256,512]{1,0:T(8,128)(2,1)S(1)} %get-tuple-element.33.refs_1_), channel_id=1, source_target_pairs={{0,2},{1,3},{2,0},{3,1},{4,6},{5,7},{6,4},{7,5},{8,10},{9,11},{10,... | collective-permute-start | bytes 786440 | tf_op jit(solution)/shard_map/ppermute | solution.py:35
  14.4 1.6 %collective-permute-start.4 = (bf16[64,1024]{1,0:T(8,128)(2,1)S(1)}, bf16[64,1024]{1,0:T(8,128)(2,1)S(1)}, u32[]{:S(2)}, u32[]{:S(2)}) collective-permute-start(bf16[64,1024]{1,0:T(8,128)(2,1)S(1)} %get-tuple-element.23), channel_id=1, source_target_pairs={{0,4},{1,5},{2,6},{3,7},{4,0},{5,1},{6,2},{7,3},{8,12},{9,13},{10,... | collective-permute-start | bytes 393224 | tf_op jit(solution)/shard_map/ppermute | solution.py:35
  16.0 2.5 %collective-permute-start.5 = (bf16[64,1024]{1,0:T(8,128)(2,1)S(1)}, bf16[64,1024]{1,0:T(8,128)(2,1)S(1)}, u32[]{:S(2)}, u32[]{:S(2)}) collective-permute-start(bf16[64,1024]{1,0:T(8,128)(2,1)S(1)} %get-tuple-element.24), channel_id=1, source_target_pairs={{0,12},{1,13},{2,14},{3,15},{4,8},{5,9},{6,10},{7,11},{8,4},{9,5},... | collective-permute-start | bytes 393224 | tf_op jit(solution)/shard_map/ppermute | solution.py:35
  18.5 0.1 collective-permute-start.6
  18.6 0.0 copy-start.4
  18.6 2.4 %collective-permute-done.10 = bf16[256,512]{1,0:T(8,128)(2,1)S(1)} collective-permute-done((bf16[256,512]{1,0:T(8,128)(2,1)S(1)}, bf16[256,512]{1,0:T(8,128)(2,1)S(1)}, u32[]{:S(2)}, u32[]{:S(2)}) %collective-permute-start.10) | collective-permute-done | bytes 262176 | tf_op jit(solution)/shard_map/ppermute | solution.py:35
  21.0 1.7 %collective-permute-start.9 = (bf16[256,512]{1,0:T(8,128)(2,1)S(1)}, bf16[256,512]{1,0:T(8,128)(2,1)S(1)}, u32[]{:S(2)}, u32[]{:S(2)}) collective-permute-start(bf16[256,512]{1,0:T(8,128)(2,1)S(1)} %once.5), channel_id=1, source_target_pairs={{0,2},{1,3},{2,0},{3,1},{4,6},{5,7},{6,4},{7,5},{8,10},{9,11},{10,... | collective-permute-start | bytes 786440 | tf_op jit(solution)/shard_map/ppermute | solution.py:35
  22.8 0.1 fusion
  22.9 0.0 collective-permute-done.3.refs_0_.refs_1_
  22.9 1.6 %collective-permute-start.11 = (bf16[256,512]{1,0:T(8,128)(2,1)S(1)}, bf16[256,512]{1,0:T(8,128)(2,1)S(1)}, u32[]{:S(2)}, u32[]{:S(2)}) collective-permute-start(bf16[256,512]{1,0:T(8,128)(2,1)S(1)} %fusion), channel_id=1, source_target_pairs={{0,4},{1,5},{2,6},{3,7},{4,0},{5,1},{6,2},{7,3},{8,12},{9,13},{10,... | collective-permute-start | bytes 786440 | tf_op jit(solution)/shard_map/ppermute | solution.py:35
  24.5 0.1 fusion.3
  24.6 0.0 collective-permute-done.4.refs_0_
  24.6 0.6 %collective-permute-start.16 = (bf16[256,512]{1,0:T(8,128)(2,1)S(1)}, bf16[256,512]{1,0:T(8,128)(2,1)S(1)}, u32[]{:S(2)}, u32[]{:S(2)}) collective-permute-start(bf16[256,512]{1,0:T(8,128)(2,1)S(1)} %fusion.3), channel_id=1, source_target_pairs={{0,2},{1,3},{2,0},{3,1},{4,6},{5,7},{6,4},{7,5},{8,10},{9,11},{10,... | collective-permute-start | bytes 786440 | tf_op jit(solution)/shard_map/ppermute | solution.py:35
  25.2 0.5 collective-permute-done.5.refs_1_
  25.7 4.6 %collective-permute-done.6.refs_2_ = bf16[64,1024]{1,0:T(8,128)(2,1)S(1)} collective-permute-done((bf16[64,1024]{1,0:T(8,128)(2,1)S(1)}, bf16[64,1024]{1,0:T(8,128)(2,1)S(1)}, u32[]{:S(2)}, u32[]{:S(2)}) %collective-permute-start.6) | collective-permute-done | bytes 131104 | tf_op jit(solution)/shard_map/ppermute | solution.py:35
  30.4 0.0 copy-done.4
  30.4 0.0 copy-start
  30.4 0.4 shrink.1.mine_ref
  30.8 0.0 collective-permute-start.7
  30.8 1.2 %collective-permute-done.7.other_ref = f32[64,64]{1,0:T(8,128)S(1)} collective-permute-done((f32[64,64]{1,0:T(8,128)S(1)}, f32[64,64]{1,0:T(8,128)S(1)}, u32[]{:S(2)}, u32[]{:S(2)}) %collective-permute-start.7) | collective-permute-done | bytes 16416 | tf_op jit(solution)/shard_map/ppermute | solution.py:35
  32.0 0.0 collective-permute-done.9
  32.0 0.0 copy-done
  32.0 0.3 grow.1
  32.3 0.6 %collective-permute-start.14 = (bf16[2,64,512]{2,1,0:T(8,128)(2,1)S(1)}, bf16[2,64,512]{2,1,0:T(8,128)(2,1)S(1)}, u32[]{:S(2)}, u32[]{:S(2)}) collective-permute-start(bf16[2,64,512]{2,1,0:T(8,128)(2,1)S(1)} %get-tuple-element.32), channel_id=1, source_target_pairs={{0,2},{1,3},{2,0},{3,1},{4,6},{5,7},{6,4},{7,5},{8,10},{9,11},{10,... | collective-permute-start | bytes 393224 | tf_op jit(solution)/shard_map/ppermute | solution.py:35
  32.9 1.0 %collective-permute-start.12 = (bf16[1,64,512]{2,1,0:T(8,128)(2,1)S(1)}, bf16[1,64,512]{2,1,0:T(8,128)(2,1)S(1)}, u32[]{:S(2)}, u32[]{:S(2)}) collective-permute-start(bf16[1,64,512]{2,1,0:T(8,128)(2,1)S(1)} %get-tuple-element.30), channel_id=1, source_target_pairs={{0,6},{1,7},{2,4},{3,5},{4,2},{5,3},{6,0},{7,1},{8,14},{9,15},{10,... | collective-permute-start | bytes 196616 | tf_op jit(solution)/shard_map/ppermute | solution.py:35
  33.9 1.9 %collective-permute-start.13 = (bf16[1,64,512]{2,1,0:T(8,128)(2,1)S(1)}, bf16[1,64,512]{2,1,0:T(8,128)(2,1)S(1)}, u32[]{:S(2)}, u32[]{:S(2)}) collective-permute-start(bf16[1,64,512]{2,1,0:T(8,128)(2,1)S(1)} %get-tuple-element.31), channel_id=1, source_target_pairs={{0,4},{1,5},{2,6},{3,7},{4,0},{5,1},{6,2},{7,3},{8,12},{9,13},{10,... | collective-permute-start | bytes 196616 | tf_op jit(solution)/shard_map/ppermute | solution.py:35
  35.8 0.0 collective-permute-done.11
  35.8 0.1 join.6
  36.0 2.4 %collective-permute-done.12.refs_1_ = bf16[1,64,512]{2,1,0:T(8,128)(2,1)S(1)} collective-permute-done((bf16[1,64,512]{2,1,0:T(8,128)(2,1)S(1)}, bf16[1,64,512]{2,1,0:T(8,128)(2,1)S(1)}, u32[]{:S(2)}, u32[]{:S(2)}) %collective-permute-start.12) | collective-permute-done | bytes 65568 | tf_op jit(solution)/shard_map/ppermute | solution.py:35
  38.4 0.7 %collective-permute-done.13.refs_2_ = bf16[1,64,512]{2,1,0:T(8,128)(2,1)S(1)} collective-permute-done((bf16[1,64,512]{2,1,0:T(8,128)(2,1)S(1)}, bf16[1,64,512]{2,1,0:T(8,128)(2,1)S(1)}, u32[]{:S(2)}, u32[]{:S(2)}) %collective-permute-start.13) | collective-permute-done | bytes 65568 | tf_op jit(solution)/shard_map/ppermute | solution.py:35
  39.1 0.2 collective-permute-done.14.refs_3_
  39.3 0.5 join.7.refs_5_
  39.8 2.0 %collective-permute-start.15 = (bf16[256,512]{1,0:T(8,128)(2,1)S(1)}, bf16[256,512]{1,0:T(8,128)(2,1)S(1)}, u32[]{:S(2)}, u32[]{:S(2)}) collective-permute-start(bf16[256,512]{1,0:T(8,128)(2,1)S(1)} %join.7.refs_5_), channel_id=1, source_target_pairs={{0,8},{1,9},{2,10},{3,11},{4,12},{5,13},{6,14},{7,15},{8,0},{9,1},... | collective-permute-start | bytes 786440 | tf_op jit(solution)/shard_map/ppermute | solution.py:35
  41.8 0.0 collective-permute-done.16
  41.8 0.3 join.8.refs_3_
  42.2 1.5 %collective-permute-start.17 = (bf16[256,512]{1,0:T(8,128)(2,1)S(1)}, bf16[256,512]{1,0:T(8,128)(2,1)S(1)}, u32[]{:S(2)}, u32[]{:S(2)}) collective-permute-start(bf16[256,512]{1,0:T(8,128)(2,1)S(1)} %join.8.refs_3_), channel_id=1, source_target_pairs={{0,4},{1,5},{2,6},{3,7},{4,0},{5,1},{6,2},{7,3},{8,12},{9,13},{10,... | collective-permute-start | bytes 786440 | tf_op jit(solution)/shard_map/ppermute | solution.py:35
  43.7 0.3 join.9
  44.0 1.6 %collective-permute-start.18 = (bf16[256,512]{1,0:T(8,128)(2,1)S(1)}, bf16[256,512]{1,0:T(8,128)(2,1)S(1)}, u32[]{:S(2)}, u32[]{:S(2)}) collective-permute-start(bf16[256,512]{1,0:T(8,128)(2,1)S(1)} %join.9), channel_id=1, source_target_pairs={{0,2},{1,3},{2,0},{3,1},{4,6},{5,7},{6,4},{7,5},{8,10},{9,11},{10,... | collective-permute-start | bytes 786440 | tf_op jit(solution)/shard_map/ppermute | solution.py:35
  45.6 0.3 join.5.sum_ref
  45.8 8.2 %collective-permute-done.15.came_ref = bf16[256,512]{1,0:T(8,128)(2,1)S(1)} collective-permute-done((bf16[256,512]{1,0:T(8,128)(2,1)S(1)}, bf16[256,512]{1,0:T(8,128)(2,1)S(1)}, u32[]{:S(2)}, u32[]{:S(2)}) %collective-permute-start.15) | collective-permute-done | bytes 262176 | tf_op jit(solution)/shard_map/ppermute | solution.py:35
  54.1 0.4 collective-permute-done.17.came_ref
  54.6 0.0 collective-permute-done.18
  54.6 0.8 %add_convert_fusion = bf16[256,512]{1,0:T(8,128)(2,1)} fusion(f32[256,512]{1,0:T(8,128)S(1)} %gather.3, bf16[256,512]{1,0:T(8,128)(2,1)S(1)} %collective-permute-done.18), kind=kLoop, calls=%fused_computation.2 | loop fusion | flops 393216 | bytes 1048576 | tf_op jit(solution)/shard_map/convert_element_type | solution.py:308
  (5 shorter events, 0.1 us)
Async XLA Ops:
  0.0 10.2 %collective-permute-start.1 = (bf16[64,8192]{1,0:T(8,128)(2,1)}, bf16[64,8192]{1,0:T(8,128)(2,1)S(1)}, u32[]{:S(2)}, u32[]{:S(2)}) collective-permute-start(bf16[64,8192]{1,0:T(8,128)(2,1)} %bitcast.27), channel_id=1, source_target_pairs={{0,1},{1,0},{2,3},{3,2},{4,5},{5,4},{6,7},{7,6},{8,9},{9,8},{10,11... | collective-permute-start | bytes 3145736 | tf_op jit(solution)/shard_map/ppermute | solution.py:35
  0.5 9.7 %collective-permute-start.2 = (bf16[64,8192]{1,0:T(8,128)(2,1)}, bf16[64,8192]{1,0:T(8,128)(2,1)S(1)}, u32[]{:S(2)}, u32[]{:S(2)}) collective-permute-start(bf16[64,8192]{1,0:T(8,128)(2,1)} %bitcast.20), channel_id=1, source_target_pairs={{0,1},{1,0},{2,3},{3,2},{4,5},{5,4},{6,7},{7,6},{8,9},{9,8},{10,11... | collective-permute-start | bytes 3145736 | tf_op jit(solution)/shard_map/ppermute | solution.py:35
  0.5 9.6 %collective-permute-start = (bf16[256,512]{1,0:T(8,128)(2,1)}, bf16[256,512]{1,0:T(8,128)(2,1)S(1)}, u32[]{:S(2)}, u32[]{:S(2)}) collective-permute-start(bf16[256,512]{1,0:T(8,128)(2,1)} %own_ref.1), channel_id=1, source_target_pairs={{0,2},{1,3},{2,0},{3,1},{4,6},{5,7},{6,4},{7,5},{8,10},{9,11},{10,... | collective-permute-start | bytes 786440 | tf_op jit(solution)/shard_map/ppermute | solution.py:35
  3.5 1.0 %copy-start.1 = (bf16[256,512]{1,0:T(8,128)(2,1)S(1)}, bf16[256,512]{1,0:T(8,128)(2,1)}, u32[]{:S(2)}) copy-start(bf16[256,512]{1,0:T(8,128)(2,1)} %own_ref.1) | copy-start | bytes 786436
  9.3 0.9 %copy-start.2 = (s32[256]{0:T(256)S(1)}, s32[256]{0:T(256)}, u32[]{:S(2)}) copy-start(s32[256]{0:T(256)} %param.10) | copy-start | bytes 3076
  9.3 0.9 %copy-start.3 = (s32[16]{0:T(128)S(1)}, s32[16]{0:T(128)}, u32[]{:S(2)}) copy-start(s32[16]{0:T(128)} %slot_hbm.1) | copy-start | bytes 196
  10.2 2.3 %collective-permute-start.8 = (bf16[3,256,512]{2,1,0:T(8,128)(2,1)S(1)}, bf16[3,256,512]{2,1,0:T(8,128)(2,1)S(1)}, u32[]{:S(2)}, u32[]{:S(2)}) collective-permute-start(bf16[3,256,512]{2,1,0:T(8,128)(2,1)S(1)} %once.4), channel_id=1, source_target_pairs={{0,1},{1,0},{2,3},{3,2},{4,5},{5,4},{6,7},{7,6},{8,9},{9,8},{10,11... | collective-permute-start | bytes 2359304 | tf_op jit(solution)/shard_map/ppermute | solution.py:35
  11.4 11.5 %collective-permute-start.3 = (bf16[5,256,512]{2,1,0:T(8,128)(2,1)S(1)}, bf16[5,256,512]{2,1,0:T(8,128)(2,1)S(1)}, u32[]{:S(2)}, u32[]{:S(2)}) collective-permute-start(bf16[5,256,512]{2,1,0:T(8,128)(2,1)S(1)} %once.3), channel_id=1, source_target_pairs={{0,1},{1,0},{2,3},{3,2},{4,5},{5,4},{6,7},{7,6},{8,9},{9,8},{10,11... | collective-permute-start | bytes 3932168 | tf_op jit(solution)/shard_map/ppermute | solution.py:35
  12.6 8.4 %collective-permute-start.10 = (bf16[256,512]{1,0:T(8,128)(2,1)S(1)}, bf16[256,512]{1,0:T(8,128)(2,1)S(1)}, u32[]{:S(2)}, u32[]{:S(2)}) collective-permute-start(bf16[256,512]{1,0:T(8,128)(2,1)S(1)} %get-tuple-element.33.refs_1_), channel_id=1, source_target_pairs={{0,2},{1,3},{2,0},{3,1},{4,6},{5,7},{6,4},{7,5},{8,10},{9,11},{10,... | collective-permute-start | bytes 786440 | tf_op jit(solution)/shard_map/ppermute | solution.py:35
  14.4 10.2 %collective-permute-start.4 = (bf16[64,1024]{1,0:T(8,128)(2,1)S(1)}, bf16[64,1024]{1,0:T(8,128)(2,1)S(1)}, u32[]{:S(2)}, u32[]{:S(2)}) collective-permute-start(bf16[64,1024]{1,0:T(8,128)(2,1)S(1)} %get-tuple-element.23), channel_id=1, source_target_pairs={{0,4},{1,5},{2,6},{3,7},{4,0},{5,1},{6,2},{7,3},{8,12},{9,13},{10,... | collective-permute-start | bytes 393224 | tf_op jit(solution)/shard_map/ppermute | solution.py:35
  16.0 9.7 %collective-permute-start.5 = (bf16[64,1024]{1,0:T(8,128)(2,1)S(1)}, bf16[64,1024]{1,0:T(8,128)(2,1)S(1)}, u32[]{:S(2)}, u32[]{:S(2)}) collective-permute-start(bf16[64,1024]{1,0:T(8,128)(2,1)S(1)} %get-tuple-element.24), channel_id=1, source_target_pairs={{0,12},{1,13},{2,14},{3,15},{4,8},{5,9},{6,10},{7,11},{8,4},{9,5},... | collective-permute-start | bytes 393224 | tf_op jit(solution)/shard_map/ppermute | solution.py:35
  18.5 11.9 %collective-permute-start.6 = (bf16[64,1024]{1,0:T(8,128)(2,1)S(1)}, bf16[64,1024]{1,0:T(8,128)(2,1)S(1)}, u32[]{:S(2)}, u32[]{:S(2)}) collective-permute-start(bf16[64,1024]{1,0:T(8,128)(2,1)S(1)} %get-tuple-element.25), channel_id=1, source_target_pairs={{0,8},{1,9},{2,10},{3,11},{4,12},{5,13},{6,14},{7,15},{8,0},{9,1},... | collective-permute-start | bytes 393224 | tf_op jit(solution)/shard_map/ppermute | solution.py:35
  18.6 11.8 %copy-start.4 = (bf16[1,8192,64]{1,2,0:T(8,128)(2,1)S(1)}, bf16[1,8192,64]{1,2,0:T(8,128)(2,1)}, u32[]{:S(2)}) copy-start(bf16[1,8192,64]{1,2,0:T(8,128)(2,1)} %param.8) | copy-start | bytes 3145732
  21.0 11.0 %collective-permute-start.9 = (bf16[256,512]{1,0:T(8,128)(2,1)S(1)}, bf16[256,512]{1,0:T(8,128)(2,1)S(1)}, u32[]{:S(2)}, u32[]{:S(2)}) collective-permute-start(bf16[256,512]{1,0:T(8,128)(2,1)S(1)} %once.5), channel_id=1, source_target_pairs={{0,2},{1,3},{2,0},{3,1},{4,6},{5,7},{6,4},{7,5},{8,10},{9,11},{10,... | collective-permute-start | bytes 786440 | tf_op jit(solution)/shard_map/ppermute | solution.py:35
  22.9 13.0 %collective-permute-start.11 = (bf16[256,512]{1,0:T(8,128)(2,1)S(1)}, bf16[256,512]{1,0:T(8,128)(2,1)S(1)}, u32[]{:S(2)}, u32[]{:S(2)}) collective-permute-start(bf16[256,512]{1,0:T(8,128)(2,1)S(1)} %fusion), channel_id=1, source_target_pairs={{0,4},{1,5},{2,6},{3,7},{4,0},{5,1},{6,2},{7,3},{8,12},{9,13},{10,... | collective-permute-start | bytes 786440 | tf_op jit(solution)/shard_map/ppermute | solution.py:35
  24.6 17.2 %collective-permute-start.16 = (bf16[256,512]{1,0:T(8,128)(2,1)S(1)}, bf16[256,512]{1,0:T(8,128)(2,1)S(1)}, u32[]{:S(2)}, u32[]{:S(2)}) collective-permute-start(bf16[256,512]{1,0:T(8,128)(2,1)S(1)} %fusion.3), channel_id=1, source_target_pairs={{0,2},{1,3},{2,0},{3,1},{4,6},{5,7},{6,4},{7,5},{8,10},{9,11},{10,... | collective-permute-start | bytes 786440 | tf_op jit(solution)/shard_map/ppermute | solution.py:35
  30.4 1.6 %copy-start = (bf16[1,64,8192]{2,1,0:T(8,128)(2,1)S(1)}, bf16[1,64,8192]{2,1,0:T(8,128)(2,1)}, u32[]{:S(2)}) copy-start(bf16[1,64,8192]{2,1,0:T(8,128)(2,1)} %param.9) | copy-start | bytes 3145732
  30.8 1.2 %collective-permute-start.7 = (f32[64,64]{1,0:T(8,128)S(1)}, f32[64,64]{1,0:T(8,128)S(1)}, u32[]{:S(2)}, u32[]{:S(2)}) collective-permute-start(f32[64,64]{1,0:T(8,128)S(1)} %shrink.1.mine_ref), channel_id=1, source_target_pairs={{0,1},{1,0},{2,3},{3,2},{4,5},{5,4},{6,7},{7,6},{8,9},{9,8},{10,11... | collective-permute-start | bytes 49160 | tf_op jit(solution)/shard_map/ppermute | solution.py:35
  32.3 7.0 %collective-permute-start.14 = (bf16[2,64,512]{2,1,0:T(8,128)(2,1)S(1)}, bf16[2,64,512]{2,1,0:T(8,128)(2,1)S(1)}, u32[]{:S(2)}, u32[]{:S(2)}) collective-permute-start(bf16[2,64,512]{2,1,0:T(8,128)(2,1)S(1)} %get-tuple-element.32), channel_id=1, source_target_pairs={{0,2},{1,3},{2,0},{3,1},{4,6},{5,7},{6,4},{7,5},{8,10},{9,11},{10,... | collective-permute-start | bytes 393224 | tf_op jit(solution)/shard_map/ppermute | solution.py:35
  32.9 5.5 %collective-permute-start.12 = (bf16[1,64,512]{2,1,0:T(8,128)(2,1)S(1)}, bf16[1,64,512]{2,1,0:T(8,128)(2,1)S(1)}, u32[]{:S(2)}, u32[]{:S(2)}) collective-permute-start(bf16[1,64,512]{2,1,0:T(8,128)(2,1)S(1)} %get-tuple-element.30), channel_id=1, source_target_pairs={{0,6},{1,7},{2,4},{3,5},{4,2},{5,3},{6,0},{7,1},{8,14},{9,15},{10,... | collective-permute-start | bytes 196616 | tf_op jit(solution)/shard_map/ppermute | solution.py:35
  33.9 5.2 %collective-permute-start.13 = (bf16[1,64,512]{2,1,0:T(8,128)(2,1)S(1)}, bf16[1,64,512]{2,1,0:T(8,128)(2,1)S(1)}, u32[]{:S(2)}, u32[]{:S(2)}) collective-permute-start(bf16[1,64,512]{2,1,0:T(8,128)(2,1)S(1)} %get-tuple-element.31), channel_id=1, source_target_pairs={{0,4},{1,5},{2,6},{3,7},{4,0},{5,1},{6,2},{7,3},{8,12},{9,13},{10,... | collective-permute-start | bytes 196616 | tf_op jit(solution)/shard_map/ppermute | solution.py:35
  39.8 14.2 %collective-permute-start.15 = (bf16[256,512]{1,0:T(8,128)(2,1)S(1)}, bf16[256,512]{1,0:T(8,128)(2,1)S(1)}, u32[]{:S(2)}, u32[]{:S(2)}) collective-permute-start(bf16[256,512]{1,0:T(8,128)(2,1)S(1)} %join.7.refs_5_), channel_id=1, source_target_pairs={{0,8},{1,9},{2,10},{3,11},{4,12},{5,13},{6,14},{7,15},{8,0},{9,1},... | collective-permute-start | bytes 786440 | tf_op jit(solution)/shard_map/ppermute | solution.py:35
  42.2 12.3 %collective-permute-start.17 = (bf16[256,512]{1,0:T(8,128)(2,1)S(1)}, bf16[256,512]{1,0:T(8,128)(2,1)S(1)}, u32[]{:S(2)}, u32[]{:S(2)}) collective-permute-start(bf16[256,512]{1,0:T(8,128)(2,1)S(1)} %join.8.refs_3_), channel_id=1, source_target_pairs={{0,4},{1,5},{2,6},{3,7},{4,0},{5,1},{6,2},{7,3},{8,12},{9,13},{10,... | collective-permute-start | bytes 786440 | tf_op jit(solution)/shard_map/ppermute | solution.py:35
  44.0 10.6 %collective-permute-start.18 = (bf16[256,512]{1,0:T(8,128)(2,1)S(1)}, bf16[256,512]{1,0:T(8,128)(2,1)S(1)}, u32[]{:S(2)}, u32[]{:S(2)}) collective-permute-start(bf16[256,512]{1,0:T(8,128)(2,1)S(1)} %join.9), channel_id=1, source_target_pairs={{0,2},{1,3},{2,0},{3,1},{4,6},{5,7},{6,4},{7,5},{8,10},{9,11},{10,... | collective-permute-start | bytes 786440 | tf_op jit(solution)/shard_map/ppermute | solution.py:35
